TPU v7x, 32 devices: a whole 2x2x4 slice. The times are simulated.
32 devices in a mesh: dp: 8 (over z, x), tensor: 4 (over y, core).
Axes of the slice: x: 2, y: 2, z: 4, core: 2. Of those that a mesh axis runs over, the one named last changes fastest.
Arguments:
- tokens: bfloat16 [16384, 1024], P(('dp', 'tensor')), may hold values from -6 to 6
- cotangent: bfloat16 [16384, 1024], P(('dp', 'tensor')), may hold values from -6 to 6
- lengths: int32 [8, 8], P('dp'), may hold values from 1 to 1024, 2048 in all within a row
- projection_weight: float32 [1024, 8, 512], P('dp', 'tensor'), may hold values from -0.1875 to 0.1875
- w_out: float32 [16, 128, 1024], P('tensor', 'dp'), may hold values from -1 to 1
- w_gate_up: float32 [1024, 2, 3072], P('dp', None, 'tensor'), may hold values from -0.1875 to 0.1875
- w_down: float32 [24, 128, 1024], P('tensor', 'dp'), may hold values from -0.109375 to 0.109375
- gains: float32 [2304], P('dp'), may hold values from 0.5 to 1.5
- first_moment_projection: float32 [1024, 8, 512], P('dp', 'tensor'), may hold values from -64 to 64
- first_out: float32 [16, 128, 1024], P('tensor', 'dp'), may hold values from -14 to 14
- first_gate_up: float32 [1024, 2, 3072], P('dp', None, 'tensor'), may hold values from -32 to 32
- first_down: float32 [24, 128, 1024], P('tensor', 'dp'), may hold values from -48 to 48
- first_gains: float32 [2304], P('dp'), may hold values from -160 to 160
- second_moment_projection: float32 [1024, 8, 512], P('dp', 'tensor'), may hold values from 557.056 to 2211.84
- second_out: float32 [16, 128, 1024], P('tensor', 'dp'), may hold values from 19.6608 to 77.0048
- second_gate_up: float32 [1024, 2, 3072], P('dp', None, 'tensor'), may hold values from 137.6256 to 557.056
- second_down: float32 [24, 128, 1024], P('tensor', 'dp'), may hold values from 311.296 to 1245.184
- second_gains: float32 [2304], P('dp'), may hold values from 819.2 to 32768
Outputs:
- block_out: bfloat16 [16384, 1024], P(('dp', 'tensor'))
- grad_tokens: float32 [16384, 1024], P(('dp', 'tensor'))
- next_w_qkv: float32 [1024, 8, 512], P('dp', 'tensor')
- next_w_out: float32 [16, 128, 1024], P('tensor', 'dp')
- next_w_gate_up: float32 [1024, 2, 3072], P('dp', None, 'tensor')
- next_w_down: float32 [24, 128, 1024], P('tensor', 'dp')
- next_gains: float32 [2304], P('dp')
- next_first_qkv: float32 [1024, 8, 512], P('dp', 'tensor')
- next_first_out: float32 [16, 128, 1024], P('tensor', 'dp')
- next_first_gate_up: float32 [1024, 2, 3072], P('dp', None, 'tensor')
- next_first_down: float32 [24, 128, 1024], P('tensor', 'dp')
- next_first_gains: float32 [2304], P('dp')
- next_second_qkv: float32 [1024, 8, 512], P('dp', 'tensor')
- next_second_out: float32 [16, 128, 1024], P('tensor', 'dp')
- next_second_gate_up: float32 [1024, 2, 3072], P('dp', None, 'tensor')
- next_second_down: float32 [24, 128, 1024], P('tensor', 'dp')
- next_second_gains: float32 [2304], P('dp')
Inputs may be any that keep to these rules, and one draw needn't show every extreme that they name: Each row holds the lengths of the 8 documents of one index of dp, in order; they sum to 2048, and in every row one of them is exactly 1024.
All inputs are finite; a program needn't handle non-finite values.
Results may differ from a plain program's by a relative error of at most 0.017.
Values may be sent and summed in bfloat16 or wider, within the bound.
No kernel may reach another device: no remote copies, remote signals or barrier semaphores. Data moves between devices by JAX's collectives and lax.ppermute only.
A program may use at most 192 MiB of HBM per device.

v0:
```python
import jax
import jax.numpy as jnp
from jax import lax
from jax.sharding import PartitionSpec as P

MODEL_WIDTH = 1024
QUERY_HEADS = 16
KEY_VALUE_HEADS = 8
HEAD_SIZE = 128
FF = 3072
STEP = 10


EPS = 1e-06
THETA = 1000000.0
BETA_ONE = 0.9
BETA_TWO = 0.95
ADAM_EPS = 1e-08
DECAY = 0.1


def norm_rows(values, scales):
    return values * lax.rsqrt(jnp.mean(values * values, axis=-1, keepdims=True) + EPS) * scales


def rotate(values, cosine_table, sine_table):
    middle_at = values.shape[-1] // 2
    first_half = values[..., :middle_at]
    second_half = values[..., middle_at:]
    return jnp.concatenate(
        [
            first_half * cosine_table - second_half * sine_table,
            second_half * cosine_table + first_half * sine_table,
        ],
        axis=-1,
    )


def layout(lengths, row_total_count):
    doc_ends = jnp.cumsum(lengths)
    starts = doc_ends - lengths
    index_of_row = jnp.arange(row_total_count, dtype=jnp.int32)
    document_label = jnp.sum((index_of_row[:, None] >= doc_ends[None, :]).astype(jnp.int32), axis=1)
    member = document_label[:, None] == jnp.arange(lengths.shape[0], dtype=jnp.int32)[None, :]
    offset = jnp.sum(jnp.where(member, starts[None, :], 0), axis=1)
    return (document_label, index_of_row - offset, index_of_row)


def angles(position):
    freq_index = jnp.arange(HEAD_SIZE // 2, dtype=jnp.float32)
    inverse = THETA ** (-2.0 * freq_index / HEAD_SIZE)
    turned = position.astype(jnp.float32)[:, None] * inverse[None, :]
    return (jnp.cos(turned), jnp.sin(turned))


def adamw_update(master, moment_one, moment_two, gradient, step_rate, decay_rate):
    next_one = BETA_ONE * moment_one + (1.0 - BETA_ONE) * gradient
    next_two = BETA_TWO * moment_two + (1.0 - BETA_TWO) * gradient * gradient
    one_hat = next_one / (1.0 - BETA_ONE**STEP)
    two_hat = next_two / (1.0 - BETA_TWO**STEP)
    next_master = master - step_rate * (
        one_hat / (jnp.sqrt(two_hat) + ADAM_EPS) + decay_rate * master
    )
    return (next_one, next_two, next_master)


def swiglu(gating, upward):
    return gating * jax.nn.sigmoid(gating) * upward


def per_device(
    tokens,
    cotangent,
    lengths,
    projection_weight,
    w_out,
    w_gate_up,
    w_down,
    gains,
    first_moment_projection,
    first_out,
    first_gate_up,
    first_down,
    first_gains,
    second_moment_projection,
    second_out,
    second_gate_up,
    second_down,
    second_gains,
):
    tensor_count = lax.axis_size("tensor")
    local_rows = tokens.shape[0]
    group_rows = local_rows * tensor_count
    query_group_width = QUERY_HEADS // KEY_VALUE_HEADS
    score_scale = HEAD_SIZE ** (-0.5)
    lowered = tuple(
        (
            master.astype(jnp.bfloat16)
            for master in (projection_weight, w_out, w_gate_up, w_down, gains)
        )
    )
    full_qkv, full_out, full_gate_up, full_down, full_gains = (
        lax.all_gather(lowered[0], "dp", axis=0, tiled=True),
        lax.all_gather(lowered[1], "dp", axis=1, tiled=True),
        lax.all_gather(lowered[2], "dp", axis=0, tiled=True),
        lax.all_gather(lowered[3], "dp", axis=1, tiled=True),
        lax.all_gather(lowered[4], "dp", axis=0, tiled=True),
    )
    gains_all = full_gains.astype(jnp.float32)
    gain_attn = gains_all[:MODEL_WIDTH]
    gain_mlp = gains_all[MODEL_WIDTH : 2 * MODEL_WIDTH]
    gain_query = gains_all[2 * MODEL_WIDTH : 2 * MODEL_WIDTH + HEAD_SIZE]
    gain_key = gains_all[2 * MODEL_WIDTH + HEAD_SIZE :]
    kv_local = full_qkv.shape[1]
    document_label, position, index_of_row = layout(lengths[0], group_rows)
    cosine_table, sine_table = angles(position)
    rows_float = tokens.astype(jnp.float32)
    attention_normed = norm_rows(rows_float, gain_attn).astype(jnp.bfloat16)
    gathered_one = lax.all_gather(attention_normed, "tensor", axis=0, tiled=True)
    qkv_matrix = full_qkv.reshape(MODEL_WIDTH, -1)
    projected_unrotated = jnp.dot(
        gathered_one, qkv_matrix, preferred_element_type=jnp.float32
    ).reshape(group_rows, kv_local, query_group_width + 2, HEAD_SIZE)

    def heads_in(raw_heads, scale_query, scale_key):
        query_rows = rotate(
            norm_rows(raw_heads[:, :, :query_group_width], scale_query),
            cosine_table[:, None, None, :],
            sine_table[:, None, None, :],
        )
        keys_out = rotate(
            norm_rows(raw_heads[:, :, query_group_width], scale_key),
            cosine_table[:, None, :],
            sine_table[:, None, :],
        )
        return (query_rows, keys_out)

    (queries_float, keys_float), heads_back = jax.vjp(
        heads_in, projected_unrotated, gain_query, gain_key
    )
    queries_low = queries_float.astype(jnp.bfloat16)
    keys_low = keys_float.astype(jnp.bfloat16)
    values_low = projected_unrotated[:, :, query_group_width + 1].astype(jnp.bfloat16)
    rows_per_block = min(512, group_rows)
    block_number = group_rows // rows_per_block
    query_blocks = queries_low.reshape(
        block_number, rows_per_block, kv_local, query_group_width, HEAD_SIZE
    )
    seg_blocks = document_label.reshape(block_number, rows_per_block)
    index_blocks = index_of_row.reshape(block_number, rows_per_block)

    def masked_scores(query_block, seg_block, index_block):
        scores = (
            jnp.einsum("qjgd,kjd->jgqk", query_block, keys_low, preferred_element_type=jnp.float32)
            * score_scale
        )
        allowed = (seg_block[:, None] == document_label[None, :]) & (
            index_block[:, None] >= index_of_row[None, :]
        )
        return (scores, allowed)

    def attention_apply(pieces):
        query_block, seg_block, index_block = pieces
        scores, allowed = masked_scores(query_block, seg_block, index_block)
        scores = jnp.where(allowed, scores, -1e30)
        highest = jnp.max(scores, axis=-1, keepdims=True)
        exponent = jnp.exp(scores - highest)
        totals = jnp.sum(exponent, axis=-1, keepdims=True)
        shares = (exponent / totals).astype(jnp.bfloat16)
        attention_blend = jnp.einsum(
            "jgqk,kjd->qjgd", shares, values_low, preferred_element_type=jnp.float32
        )
        return (attention_blend, highest + jnp.log(totals))

    mixture_blocks, log_totals = lax.map(attention_apply, (query_blocks, seg_blocks, index_blocks))
    heads_out = mixture_blocks.reshape(group_rows, -1).astype(jnp.bfloat16)
    out_matrix = full_out.reshape(-1, MODEL_WIDTH)
    part_rows = heads_out
    attn_rows = lax.psum_scatter(
        jnp.dot(part_rows, out_matrix, preferred_element_type=jnp.float32).astype(jnp.bfloat16),
        "tensor",
        scatter_dimension=0,
        tiled=True,
    ).astype(jnp.float32)
    middle = rows_float + attn_rows
    normed_two = norm_rows(middle, gain_mlp).astype(jnp.bfloat16)
    feature_rows = lax.all_gather(normed_two, "tensor", axis=0, tiled=True)
    gate_up_matrix = full_gate_up.reshape(MODEL_WIDTH, -1)
    down_matrix = full_down.reshape(-1, MODEL_WIDTH)
    feature_count = feature_rows.shape[0]
    gate_up = jnp.dot(feature_rows, gate_up_matrix, preferred_element_type=jnp.float32).reshape(
        feature_count, 2, -1
    )
    hidden_float, swiglu_back = jax.vjp(swiglu, gate_up[:, 0], gate_up[:, 1])
    hidden = hidden_float.astype(jnp.bfloat16)
    part_rows = hidden
    mlp_rows = lax.psum_scatter(
        jnp.dot(part_rows, down_matrix, preferred_element_type=jnp.float32).astype(jnp.bfloat16),
        "tensor",
        scatter_dimension=0,
        tiled=True,
    ).astype(jnp.float32)
    block_out = (middle + mlp_rows).astype(jnp.bfloat16)
    grad_output = cotangent.astype(jnp.float32)
    grad_all = lax.all_gather(cotangent, "tensor", axis=0, tiled=True)
    grad_hidden = jnp.dot(grad_all, down_matrix.T, preferred_element_type=jnp.float32)
    grad_down = jnp.dot(hidden.T, grad_all, preferred_element_type=jnp.float32)
    grad_gating, grad_upward = swiglu_back(grad_hidden)
    grad_gate_up = (
        jnp.stack([grad_gating, grad_upward], axis=1)
        .astype(jnp.bfloat16)
        .reshape(feature_count, -1)
    )
    grad_gate_up_w = jnp.dot(feature_rows.T, grad_gate_up, preferred_element_type=jnp.float32)
    part_rows = grad_gate_up
    grad_normed_two = lax.psum_scatter(
        jnp.dot(part_rows, gate_up_matrix.T, preferred_element_type=jnp.float32).astype(
            jnp.bfloat16
        ),
        "tensor",
        scatter_dimension=0,
        tiled=True,
    ).astype(jnp.float32)
    unused_two, norm_two_back = jax.vjp(norm_rows, middle, gain_mlp)
    grad_middle_part, grad_gain_mlp = norm_two_back(grad_normed_two)
    grad_middle = grad_output + grad_middle_part
    grad_middle_low = grad_middle.astype(jnp.bfloat16)
    grad_middle_all = lax.all_gather(grad_middle_low, "tensor", axis=0, tiled=True)
    grad_heads = jnp.dot(grad_middle_all, out_matrix.T, preferred_element_type=jnp.float32).astype(
        jnp.bfloat16
    )
    grad_out_w = jnp.dot(heads_out.T, grad_middle_all, preferred_element_type=jnp.float32)
    grad_head_blocks = grad_heads.reshape(
        block_number, rows_per_block, kv_local, query_group_width, HEAD_SIZE
    )

    def attend_back(running, pieces):
        grad_keys, grad_values = running
        query_block, seg_block, index_block, log_block, grad_block = pieces
        scores, allowed = masked_scores(query_block, seg_block, index_block)
        shares_float = jnp.where(allowed, jnp.exp(scores - log_block), 0.0)
        shares = shares_float.astype(jnp.bfloat16)
        grad_shares = jnp.einsum(
            "qjgd,kjd->jgqk", grad_block, values_low, preferred_element_type=jnp.float32
        )
        across = jnp.sum(shares_float * grad_shares, axis=-1, keepdims=True)
        grad_scores = (shares_float * (grad_shares - across)).astype(jnp.bfloat16)
        grad_values = grad_values + jnp.einsum(
            "jgqk,qjgd->kjd", shares, grad_block, preferred_element_type=jnp.float32
        )
        grad_keys = (
            grad_keys
            + jnp.einsum(
                "jgqk,qjgd->kjd", grad_scores, query_block, preferred_element_type=jnp.float32
            )
            * score_scale
        )
        grad_query = (
            jnp.einsum("jgqk,kjd->qjgd", grad_scores, keys_low, preferred_element_type=jnp.float32)
            * score_scale
        )
        return ((grad_keys, grad_values), grad_query)

    zero_keys = jnp.zeros((group_rows, kv_local, HEAD_SIZE), jnp.float32)
    (grad_keys, grad_values), grad_query_blocks = lax.scan(
        attend_back,
        (zero_keys, zero_keys),
        (query_blocks, seg_blocks, index_blocks, log_totals, grad_head_blocks),
    )
    grad_queries = grad_query_blocks.reshape(group_rows, kv_local, query_group_width, HEAD_SIZE)
    grad_raw, grad_gain_query, grad_gain_key = heads_back((grad_queries, grad_keys))
    grad_qkv = (
        jnp.concatenate(
            [grad_raw[:, :, : query_group_width + 1], grad_values[:, :, None, :]], axis=2
        )
        .astype(jnp.bfloat16)
        .reshape(group_rows, -1)
    )
    grad_qkv_w = jnp.dot(gathered_one.T, grad_qkv, preferred_element_type=jnp.float32)
    part_rows = grad_qkv
    grad_normed_one = lax.psum_scatter(
        jnp.dot(part_rows, qkv_matrix.T, preferred_element_type=jnp.float32).astype(jnp.bfloat16),
        "tensor",
        scatter_dimension=0,
        tiled=True,
    ).astype(jnp.float32)
    unused_one, norm_one_back = jax.vjp(norm_rows, rows_float, gain_attn)
    grad_rows_part, grad_gain_attn = norm_one_back(grad_normed_one)
    grad_tokens = grad_middle + grad_rows_part
    grad_gains = jnp.concatenate([grad_gain_attn, grad_gain_mlp, grad_gain_query, grad_gain_key])
    sum_qkv, sum_out, sum_gate_up, sum_down, gain_part = (
        lax.psum_scatter(grad_qkv_w.reshape(full_qkv.shape), "dp", scatter_dimension=0, tiled=True),
        lax.psum_scatter(grad_out_w.reshape(full_out.shape), "dp", scatter_dimension=1, tiled=True),
        lax.psum_scatter(
            grad_gate_up_w.reshape(full_gate_up.shape), "dp", scatter_dimension=0, tiled=True
        ),
        lax.psum_scatter(grad_down.reshape(full_down.shape), "dp", scatter_dimension=1, tiled=True),
        lax.psum_scatter(grad_gains, "dp", scatter_dimension=0, tiled=True),
    )
    sum_gains = lax.psum(gain_part, "tensor")
    upd_qkv = adamw_update(
        projection_weight,
        first_moment_projection,
        second_moment_projection,
        sum_qkv,
        2.0 * MODEL_WIDTH ** (-0.5),
        DECAY,
    )
    upd_out = adamw_update(
        w_out,
        first_out,
        second_out,
        sum_out,
        2.0 * (QUERY_HEADS * HEAD_SIZE // 64) ** (-0.5),
        DECAY,
    )
    upd_gate_up = adamw_update(
        w_gate_up, first_gate_up, second_gate_up, sum_gate_up, 2.0 * MODEL_WIDTH ** (-0.5), DECAY
    )
    upd_down = adamw_update(w_down, first_down, second_down, sum_down, 2.0 * FF ** (-0.5), DECAY)
    upd_gains = adamw_update(gains, first_gains, second_gains, sum_gains, 0.5, 0.0)
    return (
        block_out,
        grad_tokens,
        upd_qkv[2],
        upd_out[2],
        upd_gate_up[2],
        upd_down[2],
        upd_gains[2],
        upd_qkv[0],
        upd_out[0],
        upd_gate_up[0],
        upd_down[0],
        upd_gains[0],
        upd_qkv[1],
        upd_out[1],
        upd_gate_up[1],
        upd_down[1],
        upd_gains[1],
    )


def solution(mesh):
    return jax.shard_map(
        per_device,
        mesh=mesh,
        in_specs=(
            P(("dp", "tensor"), None),
            P(("dp", "tensor"), None),
            P("dp", None),
            P("dp", "tensor", None),
            P("tensor", "dp", None),
            P("dp", None, "tensor"),
            P("tensor", "dp", None),
            P("dp"),
            P("dp", "tensor", None),
            P("tensor", "dp", None),
            P("dp", None, "tensor"),
            P("tensor", "dp", None),
            P("dp"),
            P("dp", "tensor", None),
            P("tensor", "dp", None),
            P("dp", None, "tensor"),
            P("tensor", "dp", None),
            P("dp"),
        ),
        out_specs=(
            P(("dp", "tensor"), None),
            P(("dp", "tensor"), None),
            P("dp", "tensor", None),
            P("tensor", "dp", None),
            P("dp", None, "tensor"),
            P("tensor", "dp", None),
            P("dp"),
            P("dp", "tensor", None),
            P("tensor", "dp", None),
            P("dp", None, "tensor"),
            P("tensor", "dp", None),
            P("dp"),
            P("dp", "tensor", None),
            P("tensor", "dp", None),
            P("dp", None, "tensor"),
            P("tensor", "dp", None),
            P("dp"),
        ),
        check_vma=False,
    )
```

profile of v0, /device:TPU:0, one launch (start us, length us, event | category | flops | bytes accessed | tf_op | source)
XLA Modules:
  0.0 1234.3 jit_solution(10228143967330496179)
XLA Ops:
  12.2 23.5 %all-reduce.6 = bf16[2304]{0:T(1024)(128)(2,1)S(1)} all-reduce(bf16[2304]{0:T(1024)(128)(2,1)S(1)} %dynamic-update-slice), channel_id=1, replica_groups=mesh['dp'=8,'tensor'=4] {'dp'}, use_global_device_ids=true, to_apply=%add.6 | all-reduce | flops 2304 | bytes 9216
  44.7 18.3 %all-gather.11.cloned.1.call-done = bf16[1024,2,512]{2,1,0:T(2,128)(2,1)} async-done(((bf16[128,2,512]{2,1,0:T(2,128)(2,1)}), bf16[1024,2,512]{2,1,0:T(2,128)(2,1)}) %all-gather.11.cloned.1.call-update) | async-done | bytes 2097168 | tf_op jit(solution)/shard_map/all_gather | solution.py:103
  70.5 27.6 %all-gather.9.cloned.1.call-done = bf16[2048,1024]{1,0:T(8,128)(2,1)} async-done(((bf16[512,1024]{1,0:T(8,128)(2,1)}), bf16[2048,1024]{1,0:T(8,128)(2,1)}) %all-gather.9.cloned.1.call-update) | async-done | bytes 4194320 | tf_op jit(solution)/shard_map/all_gather | solution.py:119
  136.3 70.8 %while.28 = (s32[]{:T(128)}, bf16[4,512,2,2,128]{4,1,3,2,0:T(8,128)(2,1)}, f32[4,2,2,512,1]{3,2,1,4,0:T(2,128)}, s32[4,512]{1,0:T(4,128)S(1)}, s32[2048]{0:T(102...) while((s32[]{:T(128)}, ...), condition=%wide.region_9.10_spmd.clone, body=%wide.region_6.9_spmd.clone.sunk | while | flops 2200958976 | bytes 75059384 | solution.py:175
  224.9 42.7 %reduce-scatter.9.cloned.1.call-done = bf16[512,1024]{1,0:T(8,128)(2,1)} async-done(((bf16[2048,1024]{1,0:T(8,128)(2,1)}), bf16[512,1024]{1,0:T(8,128)(2,1)}) %reduce-scatter.9.cloned.1.call-update) | async-done | bytes 1048592 | tf_op jit(solution)/shard_map/reduce_scatter | solution.py:179
  272.7 58.3 %all-gather.17.cloned.1.call-done = bf16[1024,2,768]{2,0,1:T(8,128)(2,1)} async-done(((bf16[128,2,768]{2,0,1:T(8,128)(2,1)}), bf16[1024,2,768]{2,0,1:T(8,128)(2,1)}) %all-gather.17.cloned.1.call-update) | async-done | bytes 3145744 | tf_op jit(solution)/shard_map/all_gather | solution.py:105
  335.9 30.3 %all-gather.15.cloned.1.call-done = bf16[2048,1024]{1,0:T(8,128)(2,1)} async-done(((bf16[512,1024]{1,0:T(8,128)(2,1)}), bf16[2048,1024]{1,0:T(8,128)(2,1)}) %all-gather.15.cloned.1.call-update) | async-done | bytes 4194320 | tf_op jit(solution)/shard_map/all_gather | solution.py:187
  383.7 18.6 %all-gather.21.cloned.1.call-done = bf16[2048,1024]{1,0:T(8,128)(2,1)} async-done(((bf16[512,1024]{1,0:T(8,128)(2,1)}), bf16[2048,1024]{1,0:T(8,128)(2,1)}) %all-gather.21.cloned.1.call-update) | async-done | bytes 4194320 | tf_op jit(solution)/shard_map/all_gather | solution.py:205
  410.8 74.8 %reduce-scatter.23.cloned.1.call-done = f32[6,16,1024]{2,1,0:T(8,128)} async-done(((f32[6,128,1024]{2,1,0:T(8,128)}), f32[6,16,1024]{2,1,0:T(8,128)}) %reduce-scatter.23.cloned.1.call-update) | async-done | bytes 393232 | tf_op jit(solution)/shard_map/reduce_scatter | solution.py:297
  487.9 44.1 %all-gather.19.cloned.1.call-done = bf16[6,128,1024]{2,1,0:T(8,128)(2,1)} async-done(((bf16[6,16,1024]{2,1,0:T(8,128)(2,1)}), bf16[6,128,1024]{2,1,0:T(8,128)(2,1)}) %all-gather.19.cloned.1.call-update) | async-done | bytes 1572880 | tf_op jit(solution)/shard_map/all_gather | solution.py:106
  532.0 10.9 fusion.53
  554.1 43.4 %reduce-scatter.13.cloned.1.call-done = bf16[512,1024]{1,0:T(8,128)(2,1)} async-done(((bf16[2048,1024]{1,0:T(8,128)(2,1)}), bf16[512,1024]{1,0:T(8,128)(2,1)}) %reduce-scatter.13.cloned.1.call-update) | async-done | bytes 1048592 | tf_op jit(solution)/shard_map/reduce_scatter | solution.py:216
  607.7 12.6 %fusion.54 = f32[1024,2,768]{2,0,1:T(8,128)} fusion(bf16[2048,1024]{1,0:T(8,128)(2,1)} %all-gather.15.cloned.1.call-done, bf16[2048,1,768]{0,2,1:T(8,128)(2,1)} %copy-done.76, bf16[2048,1,768]{0,2,1:T(8,128)(2,1)} %copy-done.75), kind=kOutput, calls=%fused_computation.71 | convolution fusion | flops 6455033856 | bytes 16777216 | tf_op jit(solution)/shard_map/dot_general | solution.py:214
  620.3 17.9 %all-gather.23.cloned.1.call-done = bf16[2048,1024]{1,0:T(8,128)(2,1)} async-done(((bf16[512,1024]{1,0:T(8,128)(2,1)}), bf16[2048,1024]{1,0:T(8,128)(2,1)}) %all-gather.23.cloned.1.call-update) | async-done | bytes 4194320 | tf_op jit(solution)/shard_map/all_gather | solution.py:228
  645.2 308.5 %while.29 = (s32[]{:T(128)}, f32[2048,2,128]{0,2,1:T(8,128)}, f32[2048,2,128]{0,2,1:T(8,128)}, f32[4,512,2,2,128]{1,0,4,2,3:T(4,128)}, bf16[4,512,2,2,128]{4,1,3...) while((s32[]{:T(128)}, f32[2048,2,128]{0,2,1:T(8,128)}, ...), condition=%wide.region_17.18_spmd.clone, body=%wide.region_15.17_spmd.clone.sunk | while | flops 5437650944 | bytes 233910528 | solution.py:265
  666.2 12.6 %fusion.164 = (f32[2,2,512]{2,1,0:T(2,128)S(1)}, f32[2,512,2,2048]{3,1,2,0:T(8,128)}) fusion(f32[2,512,2,2048]{3,1,2,0:T(8,128)} %copy-done, f32[2,2,512]{2,1,0:T(2,128)S(1)} %dynamic-slice_bitcast_fusion.2, pred[512,2048]{1,0:T(8,128)(4,1)S(1)} %fusion.163, bf16[2048,2,128]{2,0,1:T(8,128)(2,1)} %get-tuple-element.664, ...), kind=kOutput, calls=%fused_computation.26.clone.1 | convolution fusion | flops 1094711296 | bytes 36192256 | tf_op jit(solution)/shard_map/while/body/eval_jaxpr/qjgd,kjd->jgqk/dot_general | solution.py:243
  678.8 12.3 fusion.165
  701.2 21.2 %dynamic_update_slice.21 = f32[4,512,2,2,128]{1,0,4,2,3:T(4,128)} dynamic-update-slice(f32[4,512,2,2,128]{1,0,4,2,3:T(4,128)} %get-tuple-element.642, f32[1,512,2,2,128]{1,0,4,2,3:T(1,128)} %copy.240, s32[]{:T(128)S(6)} %copy.258, s32[]{:T(128)} %constant.46.clone.1..sunk, s32[]{:T(128)} %constant.46.clone.1..sunk, s32[]{:T(128)} %constant.46.clone.1..sunk, s32[]{:T(128)} %constant.46.clone.1..sunk) | dynamic-update-slice | bytes 2097156 | tf_op jit(solution)/shard_map/while/body/jit(dynamic_update_index_in_dim)/dynamic_update_slice | solution.py:175
  743.6 12.6 %fusion.164 = (f32[2,2,512]{2,1,0:T(2,128)S(1)}, f32[2,512,2,2048]{3,1,2,0:T(8,128)}) fusion(f32[2,512,2,2048]{3,1,2,0:T(8,128)} %copy-done, f32[2,2,512]{2,1,0:T(2,128)S(1)} %dynamic-slice_bitcast_fusion.2, pred[512,2048]{1,0:T(8,128)(4,1)S(1)} %fusion.163, bf16[2048,2,128]{2,0,1:T(8,128)(2,1)} %get-tuple-element.664, ...), kind=kOutput, calls=%fused_computation.26.clone.1 | convolution fusion | flops 1094711296 | bytes 36192256 | tf_op jit(solution)/shard_map/while/body/eval_jaxpr/qjgd,kjd->jgqk/dot_general | solution.py:243
  756.2 12.2 fusion.165
  778.4 21.1 %dynamic_update_slice.21 = f32[4,512,2,2,128]{1,0,4,2,3:T(4,128)} dynamic-update-slice(f32[4,512,2,2,128]{1,0,4,2,3:T(4,128)} %get-tuple-element.642, f32[1,512,2,2,128]{1,0,4,2,3:T(1,128)} %copy.240, s32[]{:T(128)S(6)} %copy.258, s32[]{:T(128)} %constant.46.clone.1..sunk, s32[]{:T(128)} %constant.46.clone.1..sunk, s32[]{:T(128)} %constant.46.clone.1..sunk, s32[]{:T(128)} %constant.46.clone.1..sunk) | dynamic-update-slice | bytes 2097156 | tf_op jit(solution)/shard_map/while/body/jit(dynamic_update_index_in_dim)/dynamic_update_slice | solution.py:175
  820.7 12.5 %fusion.164 = (f32[2,2,512]{2,1,0:T(2,128)S(1)}, f32[2,512,2,2048]{3,1,2,0:T(8,128)}) fusion(f32[2,512,2,2048]{3,1,2,0:T(8,128)} %copy-done, f32[2,2,512]{2,1,0:T(2,128)S(1)} %dynamic-slice_bitcast_fusion.2, pred[512,2048]{1,0:T(8,128)(4,1)S(1)} %fusion.163, bf16[2048,2,128]{2,0,1:T(8,128)(2,1)} %get-tuple-element.664, ...), kind=kOutput, calls=%fused_computation.26.clone.1 | convolution fusion | flops 1094711296 | bytes 36192256 | tf_op jit(solution)/shard_map/while/body/eval_jaxpr/qjgd,kjd->jgqk/dot_general | solution.py:243
  833.2 12.1 fusion.165
  855.3 21.1 %dynamic_update_slice.21 = f32[4,512,2,2,128]{1,0,4,2,3:T(4,128)} dynamic-update-slice(f32[4,512,2,2,128]{1,0,4,2,3:T(4,128)} %get-tuple-element.642, f32[1,512,2,2,128]{1,0,4,2,3:T(1,128)} %copy.240, s32[]{:T(128)S(6)} %copy.258, s32[]{:T(128)} %constant.46.clone.1..sunk, s32[]{:T(128)} %constant.46.clone.1..sunk, s32[]{:T(128)} %constant.46.clone.1..sunk, s32[]{:T(128)} %constant.46.clone.1..sunk) | dynamic-update-slice | bytes 2097156 | tf_op jit(solution)/shard_map/while/body/jit(dynamic_update_index_in_dim)/dynamic_update_slice | solution.py:175
  897.6 12.5 %fusion.164 = (f32[2,2,512]{2,1,0:T(2,128)S(1)}, f32[2,512,2,2048]{3,1,2,0:T(8,128)}) fusion(f32[2,512,2,2048]{3,1,2,0:T(8,128)} %copy-done, f32[2,2,512]{2,1,0:T(2,128)S(1)} %dynamic-slice_bitcast_fusion.2, pred[512,2048]{1,0:T(8,128)(4,1)S(1)} %fusion.163, bf16[2048,2,128]{2,0,1:T(8,128)(2,1)} %get-tuple-element.664, ...), kind=kOutput, calls=%fused_computation.26.clone.1 | convolution fusion | flops 1094711296 | bytes 36192256 | tf_op jit(solution)/shard_map/while/body/eval_jaxpr/qjgd,kjd->jgqk/dot_general | solution.py:243
  910.1 12.1 fusion.165
  932.2 21.1 %dynamic_update_slice.21 = f32[4,512,2,2,128]{1,0,4,2,3:T(4,128)} dynamic-update-slice(f32[4,512,2,2,128]{1,0,4,2,3:T(4,128)} %get-tuple-element.642, f32[1,512,2,2,128]{1,0,4,2,3:T(1,128)} %copy.240, s32[]{:T(128)S(6)} %copy.258, s32[]{:T(128)} %constant.46.clone.1..sunk, s32[]{:T(128)} %constant.46.clone.1..sunk, s32[]{:T(128)} %constant.46.clone.1..sunk, s32[]{:T(128)} %constant.46.clone.1..sunk) | dynamic-update-slice | bytes 2097156 | tf_op jit(solution)/shard_map/while/body/jit(dynamic_update_index_in_dim)/dynamic_update_slice | solution.py:175
  1003.0 10.3 convolution_convert_fusion.1
  1021.2 17.7 %reduce-scatter.19.cloned.1.call-done = f32[4,16,1024]{2,1,0:T(8,128)} async-done(((f32[4,128,1024]{2,1,0:T(8,128)}), f32[4,16,1024]{2,1,0:T(8,128)}) %reduce-scatter.19.cloned.1.call-update) | async-done | bytes 262160 | tf_op jit(solution)/shard_map/reduce_scatter | solution.py:293
  1040.9 88.6 %reduce-scatter.17.cloned.1.call-done = f32[128,2,512]{2,0,1:T(8,128)} async-done(((f32[1024,2,512]{2,0,1:T(8,128)}), f32[128,2,512]{2,0,1:T(8,128)}) %reduce-scatter.17.cloned.1.call-update) | async-done | bytes 524304 | tf_op jit(solution)/shard_map/reduce_scatter | solution.py:292
  1135.1 41.2 %reduce-scatter.15.cloned.1.call-done = bf16[512,1024]{1,0:T(8,128)(2,1)} async-done(((bf16[2048,1024]{1,0:T(8,128)(2,1)}), bf16[512,1024]{1,0:T(8,128)(2,1)}) %reduce-scatter.15.cloned.1.call-update) | async-done | bytes 1048592 | tf_op jit(solution)/shard_map/reduce_scatter | solution.py:281
  1178.5 37.1 %all-reduce.7 = f32[2304]{0:T(1024)S(1)} all-reduce(f32[2304]{0:T(1024)S(1)} %pad_maximum_fusion.2), channel_id=10, replica_groups=mesh['dp'=8,'tensor'=4] {'dp'}, use_global_device_ids=true, to_apply=%region_30.31.clone | all-reduce | flops 2304 | bytes 18432
  (379 shorter events, 415.6 us)
Async XLA Ops:
  7.2 55.8 %all-gather.11.cloned.1.call-start = ((), (), s32[]{:S(2)}) async-start(), calls=%async_computation.9 | async-start | bytes 2359296 | tf_op jit(solution)/shard_map/all_gather | solution.py:103
  9.2 88.9 %all-gather.9.cloned.1.call-start = ((), (), s32[]{:S(2)}) async-start(), calls=%async_computation.8 | async-start | bytes 5242880 | tf_op jit(solution)/shard_map/all_gather | solution.py:119
  41.5 175.2 %all-gather.13.cloned.1.call-start = ((), (), s32[]{:S(2)}) async-start(), calls=%async_computation.10 | async-start | bytes 1179648 | tf_op jit(solution)/shard_map/all_gather | solution.py:104
  42.3 225.4 %reduce-scatter.9.cloned.1.call-start = ((), (), s32[]{:S(2)}) async-start(), calls=%async_computation.11 | async-start | bytes 5242880 | tf_op jit(solution)/shard_map/reduce_scatter | solution.py:179
  222.9 108.0 %all-gather.17.cloned.1.call-start = ((), (), s32[]{:S(2)}) async-start(), calls=%async_computation.13 | async-start | bytes 3538944 | tf_op jit(solution)/shard_map/all_gather | solution.py:105
  224.8 141.3 %all-gather.15.cloned.1.call-start = ((), (), s32[]{:S(2)}) async-start(), calls=%async_computation.12 | async-start | bytes 5242880 | tf_op jit(solution)/shard_map/all_gather | solution.py:187
  269.3 331.0 %copy-start.53 = (f32[512]{0:T(512)}, f32[512]{0:T(512)S(1)}, u32[]{:S(2)}) copy-start(f32[512]{0:T(512)S(1)} %fusion.97) | copy-start | bytes 6148
  271.9 130.4 %all-gather.21.cloned.1.call-start = ((), (), s32[]{:S(2)}) async-start(), calls=%async_computation.16 | async-start | bytes 5242880 | tf_op jit(solution)/shard_map/all_gather | solution.py:205
  272.7 212.9 %reduce-scatter.23.cloned.1.call-start = ((), (), s32[]{:S(2)}) async-start(), calls=%async_computation.23 | async-start | bytes 3538944 | tf_op jit(solution)/shard_map/reduce_scatter | solution.py:297
  402.3 83.2 %copy-start.37 = (f32[6,16,1024]{2,1,0:T(8,128)S(1)}, f32[6,16,1024]{2,1,0:T(8,128)}, u32[]{:S(2)}) copy-start(f32[6,16,1024]{2,1,0:T(8,128)} %param.33) | copy-start | bytes 1179652
  402.3 83.2 %copy-start.38 = (f32[6,16,1024]{2,1,0:T(8,128)S(1)}, f32[6,16,1024]{2,1,0:T(8,128)}, u32[]{:S(2)}) copy-start(f32[6,16,1024]{2,1,0:T(8,128)} %param.38) | copy-start | bytes 1179652
  410.7 121.3 %all-gather.19.cloned.1.call-start = ((), (), s32[]{:S(2)}) async-start(), calls=%async_computation.14 | async-start | bytes 1769472 | tf_op jit(solution)/shard_map/all_gather | solution.py:106
  487.9 109.6 %reduce-scatter.13.cloned.1.call-start = ((), (), s32[]{:S(2)}) async-start(), calls=%async_computation.17 | async-start | bytes 5242880 | tf_op jit(solution)/shard_map/reduce_scatter | solution.py:216
  554.0 84.2 %all-gather.23.cloned.1.call-start = ((), (), s32[]{:S(2)}) async-start(), calls=%async_computation.18 | async-start | bytes 5242880 | tf_op jit(solution)/shard_map/all_gather | solution.py:228
  603.6 410.6 %reduce-scatter.21.cloned.1.call-start = ((), (), s32[]{:S(2)}) async-start(), calls=%async_computation.22 | async-start | bytes 7077888 | tf_op jit(solution)/shard_map/reduce_scatter | solution.py:294
  620.3 418.6 %reduce-scatter.19.cloned.1.call-start = ((), (), s32[]{:S(2)}) async-start(), calls=%async_computation.21 | async-start | bytes 2359296 | tf_op jit(solution)/shard_map/reduce_scatter | solution.py:293
  970.2 159.3 %reduce-scatter.17.cloned.1.call-start = ((), (), s32[]{:S(2)}) async-start(), calls=%async_computation.20 | async-start | bytes 4718592 | tf_op jit(solution)/shard_map/reduce_scatter | solution.py:292
  991.4 184.8 %reduce-scatter.15.cloned.1.call-start = ((), (), s32[]{:S(2)}) async-start(), calls=%async_computation.19 | async-start | bytes 5242880 | tf_op jit(solution)/shard_map/reduce_scatter | solution.py:281
  1001.6 221.7 %reduce-scatter.11.cloned.1.call-start = ((), (), s32[]{:S(2)}) async-start(), calls=%async_computation.15 | async-start | bytes 5242880 | tf_op jit(solution)/shard_map/reduce_scatter | solution.py:197
  1021.2 155.1 %copy-start.6 = (bf16[512,1024]{1,0:T(8,128)(2,1)S(1)}, bf16[512,1024]{1,0:T(8,128)(2,1)}, u32[]{:S(2)}) copy-start(bf16[512,1024]{1,0:T(8,128)(2,1)} %param.22) | copy-start | bytes 3145732
  1021.2 155.1 %copy-start.52 = (f32[1024]{0:T(1024)S(1)}, f32[1024]{0:T(1024)}, u32[]{:S(2)}) copy-start(f32[1024]{0:T(1024)} %copy-done.51) | copy-start | bytes 12292
  1021.2 155.1 %copy-start.56 = (f32[512]{0:T(512)S(1)}, f32[512]{0:T(512)}, u32[]{:S(2)}) copy-start(f32[512]{0:T(512)} %copy-done.55) | copy-start | bytes 6148
  1040.8 137.6 %copy-start.63 = (f32[1024]{0:T(1024)S(1)}, f32[1024]{0:T(1024)}, u32[]{:S(2)}) copy-start(f32[1024]{0:T(1024)} %get-tuple-element.361) | copy-start | bytes 12292
  1040.8 180.9 %copy-start.60 = (f32[512]{0:T(512)S(1)}, f32[512]{0:T(512)}, u32[]{:S(2)}) copy-start(f32[512]{0:T(512)} %copy-done.59) | copy-start | bytes 6148
  1040.8 180.9 %copy-start.68 = (f32[288]{0:T(512)S(1)}, f32[288]{0:T(512)}, u32[]{:S(2)}) copy-start(f32[288]{0:T(512)} %param.29) | copy-start | bytes 3460
  1040.8 180.9 %copy-start.69 = (f32[288]{0:T(512)S(1)}, f32[288]{0:T(512)}, u32[]{:S(2)}) copy-start(f32[288]{0:T(512)} %param.34) | copy-start | bytes 3460
  1040.9 180.9 %copy-start.70 = (f32[288]{0:T(512)S(1)}, f32[288]{0:T(512)}, u32[]{:S(2)}) copy-start(f32[288]{0:T(512)} %param.39) | copy-start | bytes 3460
  1040.9 182.5 %copy-start.9 = (bf16[512,1024]{1,0:T(8,128)(2,1)S(1)}, bf16[512,1024]{1,0:T(8,128)(2,1)}, u32[]{:S(2)}) copy-start(bf16[512,1024]{1,0:T(8,128)(2,1)} %reduce-scatter.9.cloned.1.call-done) | copy-start | bytes 3145732
  1040.9 182.4 %copy-start.19 = (bf16[512,1024]{1,0:T(8,128)(2,1)S(1)}, bf16[512,1024]{1,0:T(8,128)(2,1)}, u32[]{:S(2)}) copy-start(bf16[512,1024]{1,0:T(8,128)(2,1)} %param.23) | copy-start | bytes 3145732
  1040.9 182.4 %copy-start.48 = (f32[1024]{0:T(1024)S(1)}, f32[1024]{0:T(1024)}, u32[]{:S(2)}) copy-start(f32[1024]{0:T(1024)} %get-tuple-element.445) | copy-start | bytes 12292
  1040.9 182.4 %copy-start.54 = (f32[512]{0:T(512)S(1)}, f32[512]{0:T(512)}, u32[]{:S(2)}) copy-start(f32[512]{0:T(512)} %copy-done.53) | copy-start | bytes 6148
  1040.9 182.4 %copy-start.58 = (f32[512]{0:T(512)S(1)}, f32[512]{0:T(512)}, u32[]{:S(2)}) copy-start(f32[512]{0:T(512)} %copy-done.57) | copy-start | bytes 6148
  (78 other events, 1088.6 us)
Sparse Core Ops, SparseCore 0:
  10.7 52.2 all-gather.10
  65.1 32.9 all-gather.8
  100.9 40.1 all-gather.12
  223.0 44.5 reduce-scatter.8
  270.5 60.4 all-gather.16
  333.0 33.0 all-gather.14
  367.8 34.4 all-gather.20
  410.9 74.6 reduce-scatter.22
  488.6 43.4 all-gather.18
  554.2 43.3 reduce-scatter.12
  603.8 34.4 all-gather.22
  641.7 117.9 reduce-scatter.20
  970.3 68.5 reduce-scatter.18
  1042.4 87.0 reduce-scatter.16
  1132.0 44.2 reduce-scatter.14
  1178.7 44.6 reduce-scatter.10
where the time goes:
time: 1250 us; the launch traced here: 1230 us
  waiting for transfers between devices  525 us (42%)
  matrix products  256 us (20%)
  local copies, waits for them, and re-layouts  224 us (18%)
  other arithmetic  144 us (12%)
  blocking collectives  66.7 us (5%)
  between operations  16.5 us (1%)
    dynamic_update_slice x8, local copies, waits for them, and re-layouts, per_device(): lax.map(attention_apply, (query_blocks, seg_blocks, index_blocks))  99.6 us
    reduce_scatter x1, waiting for transfers between devices, per_device(): lax.psum_scatter(grad_qkv_w.reshape(full_qkv.shape), 'dp', scatter_dimens...  88.6 us
    reduce_scatter x1, waiting for transfers between devices, per_device(): lax.psum_scatter(grad_down.reshape(full_down.shape), 'dp', scatter_dimens...  74.8 us
    unnamed x2, blocking collectives  60.5 us
    all_gather x1, waiting for transfers between devices, per_device(): lax.all_gather(lowered[2], 'dp', axis=0, tiled=True)  58.3 us
    dot_general x4, matrix products, attend_back(): jnp.einsum('qjgd,kjd->jgqk', grad_block, values_low, preferred_element_ty...  50.2 us
    convert_element_type x4, other arithmetic, attend_back(): grad_scores = (shares_float * (grad_shares - across)).astype(jnp.bfloat16)  48.6 us
    all_gather x1, waiting for transfers between devices, per_device(): lax.all_gather(lowered[3], 'dp', axis=1, tiled=True)  44.1 us
  transfers between devices with their start and end apart: 16, of which 14 were waited for; matrix products, arithmetic and copies ran while one was open for 43% of the time, Pallas kernels for 0%

commit v1 on v0

v1 whole, which is shorter than its diff:
```python
import jax
import jax.numpy as jnp
from jax import lax
from jax.experimental import pallas as pl
from jax.experimental.pallas import tpu as pltpu
from jax.sharding import PartitionSpec as P

MODEL_WIDTH = 1024
QUERY_HEADS = 16
KEY_VALUE_HEADS = 8
HEAD_SIZE = 128
FF = 3072
STEP = 10

EPS = 1e-06
THETA = 1000000.0
BETA_ONE = 0.9
BETA_TWO = 0.95
ADAM_EPS = 1e-08
DECAY = 0.1

GROUP = QUERY_HEADS // KEY_VALUE_HEADS
SLOTS = GROUP + 2
SCALE = HEAD_SIZE ** (-0.5)
LOG2E = 1.4426950408889634
BLOCK = 256
VMEM_LIMIT = 56 * 1024 * 1024
F32 = jnp.float32
BF16 = jnp.bfloat16


def norm_rows(values, scales):
    return values * lax.rsqrt(jnp.mean(values * values, axis=-1, keepdims=True) + EPS) * scales


def norm_back(values, scales, grad):
    r = lax.rsqrt(jnp.mean(values * values, axis=-1, keepdims=True) + EPS)
    u = grad * scales
    back = r * u - values * (r * r * r) * jnp.mean(u * values, axis=-1, keepdims=True)
    return back, jnp.sum(grad * values * r, axis=0)


def adamw_update(master, moment_one, moment_two, gradient, step_rate, decay_rate):
    next_one = BETA_ONE * moment_one + (1.0 - BETA_ONE) * gradient
    next_two = BETA_TWO * moment_two + (1.0 - BETA_TWO) * gradient * gradient
    one_hat = next_one / (1.0 - BETA_ONE**STEP)
    two_hat = next_two / (1.0 - BETA_TWO**STEP)
    next_master = master - step_rate * (
        one_hat / (jnp.sqrt(two_hat) + ADAM_EPS) + decay_rate * master
    )
    return (next_one, next_two, next_master)


def nt(a, b):
    return lax.dot_general(a, b, (((1,), (1,)), ((), ())), preferred_element_type=F32)


def nn(a, b):
    return jnp.dot(a, b, preferred_element_type=F32)


def head_rotated(x, gain, cos, sin):
    r = lax.rsqrt(jnp.mean(x * x, axis=-1, keepdims=True) + EPS)
    y = x * r * gain
    return y * cos + pltpu.roll(y, HEAD_SIZE // 2, 1) * sin


def head_back(x, gain, cos, sin, grad):
    r = lax.rsqrt(jnp.mean(x * x, axis=-1, keepdims=True) + EPS)
    turned = grad * cos - pltpu.roll(grad, HEAD_SIZE // 2, 1) * sin
    u = turned * gain
    back = r * u - x * (r * r * r) * jnp.mean(u * x, axis=-1, keepdims=True)
    return back, jnp.sum(turned * x * r, axis=0, keepdims=True)


def block_at(index, flip):
    return pl.ds(pl.multiple_of((index ^ flip) * BLOCK, BLOCK), BLOCK)


def allowed_block(key_block, query_block, start):
    keys = key_block * BLOCK + lax.broadcasted_iota(jnp.int32, (BLOCK, BLOCK), 0)
    queries = query_block * BLOCK + lax.broadcasted_iota(jnp.int32, (BLOCK, BLOCK), 1)
    return (keys >= start) & (keys <= queries)


def attend_kernel(info, qkv, cos, sin, gain_q, gain_k, start, out, logs, qs, ks, vt):
    blocks = qkv.shape[0] // BLOCK
    flip = info[blocks]

    def prepare(i, _):
        rows = pl.ds(pl.multiple_of(i * BLOCK, BLOCK), BLOCK)
        c, s = cos[rows, :], sin[rows, :]
        for h in range(GROUP):
            x = qkv[rows, h * HEAD_SIZE : (h + 1) * HEAD_SIZE]
            qs[h, rows, :] = head_rotated(x, gain_q[...], c, s).astype(BF16)
        x = qkv[rows, GROUP * HEAD_SIZE : (GROUP + 1) * HEAD_SIZE]
        ks[rows, :] = head_rotated(x, gain_k[...], c, s).astype(BF16)
        x = qkv[rows, (GROUP + 1) * HEAD_SIZE :]
        vt[:, rows] = x.T.astype(BF16)
        return 0

    lax.fori_loop(0, blocks, prepare, 0)

    def one_block(b, _):
        here = block_at(b, flip)
        first = start[:, here]
        queries = [qs[h, here, :] for h in range(GROUP)]

        def keys_step(kb, carry):
            there = block_at(kb, flip)
            k, v = ks[there, :], vt[:, there]
            allowed = allowed_block(kb, b, first)
            after = []
            for h in range(GROUP):
                total, blend = carry[h]
                p = jnp.where(allowed, jnp.exp2(nt(k, queries[h]) * (SCALE * LOG2E)), 0.0)
                after.append(
                    (total + jnp.sum(p, axis=0, keepdims=True), blend + nn(v, p.astype(BF16)))
                )
            return tuple(after)

        zero = (jnp.zeros((1, BLOCK), F32), jnp.zeros((HEAD_SIZE, BLOCK), F32))
        done = lax.fori_loop(info[b], b + 1, keys_step, (zero,) * GROUP)
        for h in range(GROUP):
            total, blend = done[h]
            out[here, h * HEAD_SIZE : (h + 1) * HEAD_SIZE] = (blend / total).T.astype(BF16)
            logs[0, h : h + 1, here] = jnp.log2(total)
        return 0

    lax.fori_loop(0, blocks, one_block, 0)


def attend_back_kernel(
    info, qkv, cos, sin, gain_q, gain_k, start, logs, out, grad_out,
    grad_qkv, grad_gains, qs, ks, kt, vs, grad_k, grad_v,
):
    blocks = qkv.shape[0] // BLOCK
    flip = info[blocks]
    grad_gains[...] = jnp.zeros(grad_gains.shape, F32)

    def prepare(i, _):
        rows = pl.ds(pl.multiple_of(i * BLOCK, BLOCK), BLOCK)
        c, s = cos[rows, :], sin[rows, :]
        for h in range(GROUP):
            x = qkv[rows, h * HEAD_SIZE : (h + 1) * HEAD_SIZE]
            qs[h, rows, :] = head_rotated(x, gain_q[...], c, s).astype(BF16)
        x = qkv[rows, GROUP * HEAD_SIZE : (GROUP + 1) * HEAD_SIZE]
        turned = head_rotated(x, gain_k[...], c, s)
        ks[rows, :] = turned.astype(BF16)
        kt[:, rows] = turned.T.astype(BF16)
        vs[rows, :] = qkv[rows, (GROUP + 1) * HEAD_SIZE :].astype(BF16)
        grad_k[rows, :] = jnp.zeros((BLOCK, HEAD_SIZE), F32)
        grad_v[rows, :] = jnp.zeros((BLOCK, HEAD_SIZE), F32)
        return 0

    lax.fori_loop(0, blocks, prepare, 0)

    def one_block(b, _):
        here = block_at(b, flip)
        first = start[:, here]
        queries, gradients, across, log = [], [], [], []
        for h in range(GROUP):
            lanes = slice(h * HEAD_SIZE, (h + 1) * HEAD_SIZE)
            g = grad_out[here, lanes]
            queries.append(qs[h, here, :])
            gradients.append(g)
            both = g.astype(F32) * out[here, lanes].astype(F32)
            across.append(jnp.sum(both.T, axis=0, keepdims=True))
            log.append(logs[0, h : h + 1, here])

        def keys_step(kb, carry):
            there = block_at(kb, flip)
            k, v, k_turned = ks[there, :], vs[there, :], kt[:, there]
            allowed = allowed_block(kb, b, first)
            after, add_k, add_v = [], 0.0, 0.0
            for h in range(GROUP):
                s = nt(k, queries[h])
                p = jnp.where(allowed, jnp.exp2(s * (SCALE * LOG2E) - log[h]), 0.0)
                d = (p * (nt(v, gradients[h]) - across[h])).astype(BF16)
                add_v = add_v + nn(p.astype(BF16), gradients[h])
                add_k = add_k + nn(d, queries[h])
                after.append(carry[h] + nn(k_turned, d))
            grad_k[there, :] += add_k
            grad_v[there, :] += add_v
            return tuple(after)

        zero = jnp.zeros((HEAD_SIZE, BLOCK), F32)
        done = lax.fori_loop(info[b], b + 1, keys_step, (zero,) * GROUP)
        c, s = cos[here, :], sin[here, :]
        for h in range(GROUP):
            lanes = slice(h * HEAD_SIZE, (h + 1) * HEAD_SIZE)
            back, gain = head_back(qkv[here, lanes], gain_q[...], c, s, done[h].T * SCALE)
            grad_qkv[here, lanes] = back.astype(BF16)
            grad_gains[0, 0:1, :] += gain
        return 0

    lax.fori_loop(0, blocks, one_block, 0)

    def finish(i, _):
        rows = pl.ds(pl.multiple_of(i * BLOCK, BLOCK), BLOCK)
        lanes = slice(GROUP * HEAD_SIZE, (GROUP + 1) * HEAD_SIZE)
        back, gain = head_back(
            qkv[rows, lanes], gain_k[...], cos[rows, :], sin[rows, :], grad_k[rows, :] * SCALE
        )
        grad_qkv[rows, lanes] = back.astype(BF16)
        grad_gains[0, 1:2, :] += gain
        grad_qkv[rows, (GROUP + 1) * HEAD_SIZE :] = grad_v[rows, :].astype(BF16)
        return 0

    lax.fori_loop(0, blocks, finish, 0)


def whole(shape):
    return pl.BlockSpec(shape, lambda j, info: (0,) * len(shape))


def attend(info, qkv, cos, sin, gain_q, gain_k, start):
    rows = qkv.shape[0]
    heads = qkv.shape[1] // (SLOTS * HEAD_SIZE)
    per_head = lambda width: pl.BlockSpec((rows, width), lambda j, info: (0, j))
    return pl.pallas_call(
        attend_kernel,
        grid_spec=pltpu.PrefetchScalarGridSpec(
            num_scalar_prefetch=1,
            grid=(heads,),
            in_specs=[
                per_head(SLOTS * HEAD_SIZE),
                whole((rows, HEAD_SIZE)),
                whole((rows, HEAD_SIZE)),
                whole((1, HEAD_SIZE)),
                whole((1, HEAD_SIZE)),
                whole((1, rows)),
            ],
            out_specs=[
                per_head(GROUP * HEAD_SIZE),
                pl.BlockSpec((1, GROUP, rows), lambda j, info: (j, 0, 0)),
            ],
            scratch_shapes=[
                pltpu.VMEM((GROUP, rows, HEAD_SIZE), BF16),
                pltpu.VMEM((rows, HEAD_SIZE), BF16),
                pltpu.VMEM((HEAD_SIZE, rows), BF16),
            ],
        ),
        out_shape=[
            jax.ShapeDtypeStruct((rows, heads * GROUP * HEAD_SIZE), BF16),
            jax.ShapeDtypeStruct((heads, GROUP, rows), F32),
        ],
        compiler_params=pltpu.CompilerParams(
            dimension_semantics=("arbitrary",), vmem_limit_bytes=VMEM_LIMIT
        ),
        cost_estimate=pl.CostEstimate(
            flops=8_000_000_000, bytes_accessed=14_000_000, transcendentals=6_000_000
        ),
        name="attend",
    )(info, qkv, cos, sin, gain_q, gain_k, start)


def attend_back(info, qkv, cos, sin, gain_q, gain_k, start, logs, out, grad_out):
    rows = qkv.shape[0]
    heads = qkv.shape[1] // (SLOTS * HEAD_SIZE)
    per_head = lambda width: pl.BlockSpec((rows, width), lambda j, info: (0, j))
    return pl.pallas_call(
        attend_back_kernel,
        grid_spec=pltpu.PrefetchScalarGridSpec(
            num_scalar_prefetch=1,
            grid=(heads,),
            in_specs=[
                per_head(SLOTS * HEAD_SIZE),
                whole((rows, HEAD_SIZE)),
                whole((rows, HEAD_SIZE)),
                whole((1, HEAD_SIZE)),
                whole((1, HEAD_SIZE)),
                whole((1, rows)),
                pl.BlockSpec((1, GROUP, rows), lambda j, info: (j, 0, 0)),
                per_head(GROUP * HEAD_SIZE),
                per_head(GROUP * HEAD_SIZE),
            ],
            out_specs=[
                per_head(SLOTS * HEAD_SIZE),
                pl.BlockSpec((1, 2, HEAD_SIZE), lambda j, info: (j, 0, 0)),
            ],
            scratch_shapes=[
                pltpu.VMEM((GROUP, rows, HEAD_SIZE), BF16),
                pltpu.VMEM((rows, HEAD_SIZE), BF16),
                pltpu.VMEM((HEAD_SIZE, rows), BF16),
                pltpu.VMEM((rows, HEAD_SIZE), BF16),
                pltpu.VMEM((rows, HEAD_SIZE), F32),
                pltpu.VMEM((rows, HEAD_SIZE), F32),
            ],
        ),
        out_shape=[
            jax.ShapeDtypeStruct((rows, qkv.shape[1]), BF16),
            jax.ShapeDtypeStruct((heads, 2, HEAD_SIZE), F32),
        ],
        compiler_params=pltpu.CompilerParams(
            dimension_semantics=("arbitrary",), vmem_limit_bytes=VMEM_LIMIT
        ),
        cost_estimate=pl.CostEstimate(
            flops=20_000_000_000, bytes_accessed=20_000_000, transcendentals=6_000_000
        ),
        name="attend_back",
    )(info, qkv, cos, sin, gain_q, gain_k, start, logs, out, grad_out)


def flipped(value, axis, bit):
    return lax.ppermute(value, axis, [(i, i ^ bit) for i in range(lax.axis_size(axis))])


def gathered(value):
    across = flipped(value, "tensor", 2)
    beside = flipped(value, "tensor", 1)
    return [value, beside, across, flipped(across, "tensor", 1)]


def scattered(parts):
    near = parts[2].astype(F32) + flipped(parts[3], "tensor", 1).astype(F32)
    across = flipped(near.astype(BF16), "tensor", 2)
    own = parts[0].astype(F32) + flipped(parts[1], "tensor", 1).astype(F32)
    return own + across.astype(F32)


def per_device(
    tokens, cotangent, lengths,
    projection_weight, w_out, w_gate_up, w_down, gains,
    first_moment_projection, first_out, first_gate_up, first_down, first_gains,
    second_moment_projection, second_out, second_gate_up, second_down, second_gains,
):
    shards = lax.axis_size("tensor")
    spread = lax.axis_size("dp")
    me = lax.axis_index("tensor")
    local_rows = tokens.shape[0]
    rows = local_rows * shards
    blocks = rows // BLOCK
    kv_local = projection_weight.shape[1]
    hidden_local = w_gate_up.shape[2]
    out_heads, out_depth = w_out.shape[0], w_out.shape[1]
    down_blocks, down_depth = w_down.shape[0], w_down.shape[1]
    depth = projection_weight.shape[0]
    gain_count = gains.shape[0]

    pack_one = jnp.concatenate(
        [
            projection_weight.astype(BF16).reshape(depth, -1),
            w_out.astype(BF16).reshape(-1, MODEL_WIDTH),
            jnp.pad(gains.astype(BF16)[None, :], ((0, 15), (0, MODEL_WIDTH - gain_count))),
        ],
        axis=0,
    )
    half = MODEL_WIDTH // 2
    pieces = 2 * hidden_local // half
    pack_two = jnp.concatenate(
        [
            w_gate_up.astype(BF16).reshape(depth, pieces, half).swapaxes(0, 1).reshape(-1, half),
            w_down.astype(BF16).reshape(-1, 2, half).swapaxes(0, 1).reshape(-1, half),
        ],
        axis=0,
    )
    full_one = lax.all_gather(pack_one, "dp", axis=0, tiled=False)
    full_two = lax.all_gather(pack_two, "dp", axis=0, tiled=False)
    qkv_matrix = full_one[:, :depth].reshape(MODEL_WIDTH, -1)
    out_matrix = (
        full_one[:, depth : depth + out_heads * out_depth]
        .reshape(spread, out_heads, out_depth, MODEL_WIDTH)
        .swapaxes(0, 1)
        .reshape(-1, MODEL_WIDTH)
    )
    gains_all = full_one[:, depth + out_heads * out_depth, :gain_count].reshape(-1).astype(F32)
    gate_up_matrix = (
        full_two[:, : pieces * depth]
        .reshape(spread, pieces, depth, half)
        .swapaxes(1, 2)
        .reshape(MODEL_WIDTH, -1)
    )
    down_matrix = (
        full_two[:, pieces * depth :]
        .reshape(spread, 2, down_blocks, down_depth, half)
        .transpose(2, 0, 3, 1, 4)
        .reshape(-1, MODEL_WIDTH)
    )
    gain_attn = gains_all[:MODEL_WIDTH]
    gain_mlp = gains_all[MODEL_WIDTH : 2 * MODEL_WIDTH]
    gain_query = gains_all[2 * MODEL_WIDTH : 2 * MODEL_WIDTH + HEAD_SIZE]
    gain_key = gains_all[2 * MODEL_WIDTH + HEAD_SIZE :]

    doc_ends = jnp.cumsum(lengths[0])
    doc_starts = doc_ends - lengths[0]

    def start_of(index):
        return jnp.max(
            jnp.where(index[:, None] >= doc_starts[None, :], doc_starts[None, :], 0), axis=1
        )

    order = me ^ jnp.arange(shards, dtype=jnp.int32)
    index_of_row = (
        order[:, None] * local_rows + jnp.arange(local_rows, dtype=jnp.int32)[None, :]
    ).reshape(-1)
    start_of_row = start_of(index_of_row)
    position = index_of_row - start_of_row
    inverse = THETA ** (-2.0 * jnp.arange(HEAD_SIZE // 2, dtype=F32) / HEAD_SIZE)
    turned = position.astype(F32)[:, None] * inverse[None, :]
    cosine, sine = jnp.cos(turned), jnp.sin(turned)
    cos = jnp.concatenate([cosine, cosine], axis=1)
    sin = jnp.concatenate([-sine, sine], axis=1)
    block_starts = start_of(jnp.arange(blocks, dtype=jnp.int32) * BLOCK) // BLOCK
    info = jnp.concatenate([block_starts, (me * (local_rows // BLOCK))[None]]).astype(jnp.int32)
    start_row = start_of_row[None, :]

    rows_float = tokens.astype(F32)
    tokens_all = jnp.concatenate(gathered(tokens), axis=0)
    normed_one = norm_rows(tokens_all.astype(F32), gain_attn).astype(BF16)
    qkv = nn(normed_one, qkv_matrix)
    heads_args = (info, qkv, cos, sin, gain_query[None, :], gain_key[None, :], start_row)
    heads_out, logs = attend(*heads_args)

    def shard(value, i):
        return value[i * local_rows : (i + 1) * local_rows]

    def partial_sums(product):
        return scattered([shard(product, i) for i in range(shards)])

    attn_rows = partial_sums(nn(heads_out, out_matrix).astype(BF16))
    middle = rows_float + attn_rows

    normed_two_own = norm_rows(middle, gain_mlp).astype(BF16)
    normed_two = jnp.concatenate(gathered(normed_two_own), axis=0)
    grad_all = jnp.concatenate(gathered(cotangent), axis=0)
    gate_up = nn(normed_two, gate_up_matrix)
    gate, up = gate_up[:, :hidden_local], gate_up[:, hidden_local:]
    gate_sig = jax.nn.sigmoid(gate)
    hidden = (gate * gate_sig * up).astype(BF16)
    grad_hidden = nt(grad_all, down_matrix)
    grad_gate = grad_hidden * up * (gate_sig + gate * gate_sig * (1.0 - gate_sig))
    grad_up = grad_hidden * gate * gate_sig
    grad_gate_up = jnp.concatenate([grad_gate.astype(BF16), grad_up.astype(BF16)], axis=1)
    grad_normed_two = partial_sums(nt(grad_gate_up, gate_up_matrix).astype(BF16))
    grad_middle_part, grad_gain_mlp = norm_back(middle, gain_mlp, grad_normed_two)
    grad_middle = cotangent.astype(F32) + grad_middle_part
    grad_middle_all = jnp.concatenate(gathered(grad_middle.astype(BF16)), axis=0)

    def over_rows(a, b):
        return lax.dot_general(a, b, (((0,), (0,)), ((), ())), preferred_element_type=F32)

    grad_down = over_rows(hidden, grad_all).astype(BF16)
    sum_down = lax.psum_scatter(
        grad_down.reshape(down_blocks, -1, MODEL_WIDTH), "dp", scatter_dimension=1, tiled=True
    ).astype(F32)
    grad_gate_up_w = over_rows(normed_two, grad_gate_up).astype(BF16)
    sum_gate_up = lax.psum_scatter(
        grad_gate_up_w, "dp", scatter_dimension=0, tiled=True
    ).astype(F32)
    mlp_rows = partial_sums(nn(hidden, down_matrix).astype(BF16))
    block_out = (middle + mlp_rows).astype(BF16)

    grad_heads = nt(grad_middle_all, out_matrix).astype(BF16)
    grad_out_w = over_rows(heads_out, grad_middle_all).astype(BF16)
    sum_out = lax.psum_scatter(
        grad_out_w.reshape(out_heads, -1, MODEL_WIDTH), "dp", scatter_dimension=1, tiled=True
    ).astype(F32)
    grad_qkv, grad_head_gains = attend_back(*heads_args, logs, heads_out, grad_heads)
    grad_qkv_w = over_rows(normed_one, grad_qkv)
    sum_qkv = lax.psum_scatter(
        grad_qkv_w.astype(BF16), "dp", scatter_dimension=0, tiled=True
    ).astype(F32)
    grad_normed_one = partial_sums(nt(grad_qkv, qkv_matrix).astype(BF16))
    grad_rows_part, _ = norm_back(rows_float, gain_attn, grad_normed_one)
    grad_tokens = grad_middle + grad_rows_part

    grad_gain_attn = jnp.sum(qkv_matrix.astype(F32) * grad_qkv_w, axis=1) / gain_attn
    gain_sums = jnp.concatenate(
        [grad_gain_attn, grad_gain_mlp, jnp.sum(grad_head_gains, axis=0).reshape(-1)]
    )
    for axis in ("tensor", "dp"):
        bit = 1
        while bit < lax.axis_size(axis):
            gain_sums = gain_sums + flipped(gain_sums, axis, bit)
            bit *= 2
    sum_gains = lax.dynamic_slice(
        gain_sums, (lax.axis_index("dp") * gain_count,), (gain_count,)
    )

    upd_qkv = adamw_update(
        projection_weight, first_moment_projection, second_moment_projection,
        sum_qkv.reshape(projection_weight.shape), 2.0 * MODEL_WIDTH ** (-0.5), DECAY,
    )
    upd_out = adamw_update(
        w_out, first_out, second_out, sum_out,
        2.0 * (QUERY_HEADS * HEAD_SIZE // 64) ** (-0.5), DECAY,
    )
    upd_gate_up = adamw_update(
        w_gate_up, first_gate_up, second_gate_up, sum_gate_up.reshape(w_gate_up.shape),
        2.0 * MODEL_WIDTH ** (-0.5), DECAY,
    )
    upd_down = adamw_update(w_down, first_down, second_down, sum_down, 2.0 * FF ** (-0.5), DECAY)
    upd_gains = adamw_update(gains, first_gains, second_gains, sum_gains, 0.5, 0.0)
    updates = (upd_qkv, upd_out, upd_gate_up, upd_down, upd_gains)
    return (
        block_out,
        grad_tokens,
        *(update[2] for update in updates),
        *(update[0] for update in updates),
        *(update[1] for update in updates),
    )


def solution(mesh):
    weights = (
        P("dp", "tensor", None),
        P("tensor", "dp", None),
        P("dp", None, "tensor"),
        P("tensor", "dp", None),
        P("dp"),
    )
    batch = P(("dp", "tensor"), None)
    return jax.shard_map(
        per_device,
        mesh=mesh,
        in_specs=(batch, batch, P("dp", None), *weights, *weights, *weights),
        out_specs=(batch, batch, *weights, *weights, *weights),
        check_vma=False,
    )
```

time: 1250 us -> 568 us (0.45)
  waiting for transfers between devices: 525 us -> 235 us
  local copies, waits for them, and re-layouts: 224 us -> 47.6 us
  matrix products: 256 us -> 101 us
  other arithmetic: 144 us -> 45.8 us
  Pallas kernels: 0 us -> 86 us
  blocking collectives: 66.7 us -> 0 us
  starting transfers between devices: 0.66 us -> 32.4 us
    reduce_scatter x8 -> x3, waiting for transfers between devices: 309 us -> 0.01 us  [the longest x1 0.01 us: per_device(): lax.psum_scatter(grad_down.reshape(down_blocks, -1, MODEL_WIDTH), 'dp', s...]
    all_gather x8 -> x2, waiting for transfers between devices: 215 us -> 31.3 us  [the longest x1 31.3 us: per_device(): full_one = lax.all_gather(pack_one, 'dp', axis=0, tiled=False)]
    ppermute x0 -> x29, waiting for transfers between devices: none -> 172 us  [flipped(): lax.ppermute(value, axis, [(i, i ^ bit) for i in range(lax.axis_size(axis...]
    dot_general x40 -> x12, matrix products: 256 us -> 101 us  [the longest x4 35 us: nt(): lax.dot_general(a, b, (((1,), (1,)), ((), ())), preferred_element_type=F32)]
    dynamic_update_slice x8 -> x0, local copies, waits for them, and re-layouts: 99.6 us -> none  [per_device(): lax.map(attention_apply, (query_blocks, seg_blocks, index_blocks))]
    pallas_call x0 -> x2, Pallas kernels: none -> 86 us  [the longest x1 50.2 us: attend_back(): pl.pallas_call(attend_back_kernel, grid_spec=pltpu.PrefetchScalarGridSpec...]
    unnamed x2 -> x0, blocking collectives: 60.5 us -> none
    convert_element_type x13 -> x12, other arithmetic: 64.1 us -> 16.1 us  [the longest x4 7.13 us: scattered(): across = flipped(near.astype(BF16), 'tensor', 2)]
  transfers between devices with their start and end apart: 16 -> 35, of which waited for: 14 -> 15; matrix products, arithmetic and copies ran while one was open for 43% -> 25% of each run, Pallas kernels for 0% -> 15%
where the time goes in v1:
time: 568 us; the launch traced here: 563 us
  waiting for transfers between devices  235 us (41%)
  matrix products  101 us (18%)
  Pallas kernels  86 us (15%)
  local copies, waits for them, and re-layouts  47.6 us (8%)
  other arithmetic  45.8 us (8%)
  starting transfers between devices  32.4 us (6%)
  between operations  15.2 us (3%)
    ppermute x29, waiting for transfers between devices, flipped(): lax.ppermute(value, axis, [(i, i ^ bit) for i in range(lax.axis_size(axis...  172 us
    pallas_call x1, Pallas kernels, attend_back(): pl.pallas_call(attend_back_kernel, grid_spec=pltpu.PrefetchScalarGridSpec...  50.2 us
    pallas_call x1, Pallas kernels, attend(): pl.pallas_call(attend_kernel, grid_spec=pltpu.PrefetchScalarGridSpec(num_...  35.8 us
    dot_general x4, matrix products, nt(): lax.dot_general(a, b, (((1,), (1,)), ((), ())), preferred_element_type=F32)  35 us
    dot_general x4, matrix products, over_rows(): lax.dot_general(a, b, (((0,), (0,)), ((), ())), preferred_element_type=F32)  33.9 us
    dot_general x4, matrix products, nn(): return jnp.dot(a, b, preferred_element_type=F32)  32.2 us
    ppermute x29, starting transfers between devices, flipped(): lax.ppermute(value, axis, [(i, i ^ bit) for i in range(lax.axis_size(axis...  31.9 us
    all_gather x1, waiting for transfers between devices, per_device(): full_one = lax.all_gather(pack_one, 'dp', axis=0, tiled=False)  31.3 us
  transfers between devices with their start and end apart: 35, of which 15 were waited for; matrix products, arithmetic and copies ran while one was open for 25% of the time, Pallas kernels for 15%

profile of v1, /device:TPU:0, one launch (start us, length us, event | category | flops | bytes accessed | tf_op | source)
XLA Modules:
  0.0 562.9 jit_solution(17563283175207129854)
XLA Ops:
  17.4 20.1 %collective-permute-done.1 = bf16[512,1024]{1,0:T(8,128)(2,1)S(1)} collective-permute-done((bf16[512,1024]{1,0:T(8,128)(2,1)}, bf16[512,1024]{1,0:T(8,128)(2,1)S(1)}, u32[]{:S(2)}, u32[]{:S(2)}) %collective-permute-start.1) | collective-permute-done | bytes 1048608 | tf_op jit(solution)/shard_map/ppermute | solution.py:306
  38.2 3.7 fusion.27
  46.1 31.3 %all-gather.5.cloned.1.call-done = bf16[1664,1024]{1,0:T(8,128)(2,1)} async-done(((bf16[208,1024]{1,0:T(8,128)(2,1)}), bf16[1664,1024]{1,0:T(8,128)(2,1)}) %all-gather.5.cloned.1.call-update) | async-done | bytes 3407888 | tf_op jit(solution)/shard_map/all_gather | solution.py:358
  83.0 12.7 %fusion.19.qkv = f32[2048,1024]{1,0:T(8,128)} fusion(bf16[1024,1024]{1,0:T(8,128)(2,1)S(1)} %bitcast.66, f32[1024]{0:T(1024)S(1)} %get-tuple-element.63, f32[2048]{0:T(1024)S(1)} %add_rsqrt_fusion, bf16[512,1024]{1,0:T(8,128)(2,1)S(1)} %copy-done.21, bf16[512,1024]{1,0:T(8,128)(2,1)S(1)} %collective-permute-done.1, ...), kind=kOutput, calls=%fused_computation.54 | convolution fusion | flops 4318035968 | bytes 14692352 | tf_op jit(solution)/shard_map/dot_general | solution.py:59
  95.7 35.8 %attend.1 = (bf16[2048,512]{1,0:T(8,128)(2,1)}, f32[2,2,2048]{2,1,0:T(2,128)}) custom-call(s32[9]{0:T(128)} %pad_add_fusion.info, f32[2048,1024]{1,0:T(8,128)} %fusion.19.qkv, f32[2048,128]{1,0:T(8,128)} %get-tuple-element.74.cos, f32[2048,128]{1,0:T(8,128)} %get-tuple-element.75.sin, f32[1,128]{1,0:T(1,128)} %get-tuple-element.65.gain_q, ...), custom_call_target="tpu_custom_call" | custom-call | flops 8000000000 | bytes 14000000 | tf_op jit(solution)/shard_map/attend/pallas_call | solution.py:221
  131.5 3.9 convolution_convert_fusion
  140.8 24.0 %collective-permute-done.5 = bf16[512,1024]{1,0:T(8,128)(2,1)S(1)} collective-permute-done((bf16[512,1024]{1,0:T(8,128)(2,1)S(1)}, bf16[512,1024]{1,0:T(8,128)(2,1)S(1)}, u32[]{:S(2)}, u32[]{:S(2)}) %collective-permute-start.5) | collective-permute-done | bytes 1048608 | tf_op jit(solution)/shard_map/ppermute | solution.py:306
  168.2 19.1 %collective-permute-done.13 = bf16[512,1024]{1,0:T(8,128)(2,1)S(1)} collective-permute-done((bf16[512,1024]{1,0:T(8,128)(2,1)S(1)}, bf16[512,1024]{1,0:T(8,128)(2,1)S(1)}, u32[]{:S(2)}, u32[]{:S(2)}) %collective-permute-start.13) | collective-permute-done | bytes 1048608 | tf_op jit(solution)/shard_map/ppermute | solution.py:306
  187.8 21.3 %collective-permute-done.7 = bf16[512,1024]{1,0:T(8,128)(2,1)} collective-permute-done((bf16[512,1024]{1,0:T(8,128)(2,1)}, bf16[512,1024]{1,0:T(8,128)(2,1)}, u32[]{:S(2)}, u32[]{:S(2)}) %collective-permute-start.7) | collective-permute-done | bytes 1048608 | tf_op jit(solution)/shard_map/ppermute | solution.py:306
  213.3 3.7 slice.119
  219.8 5.3 copy.75
  228.7 11.8 %fusion.8 = f32[2048,1536]{0,1:T(8,128)} fusion(bf16[192,8,8,128]{3,2,1,0:T(8,128)(2,1)S(1)} %bitcast.75, bf16[512,1024]{1,0:T(8,128)(2,1)} %collective-permute-done.8, bf16[512,1024]{1,0:T(8,128)(2,1)} %collective-permute-done.7, bf16[512,1024]{1,0:T(8,128)(2,1)} %collective-permute-done.6, bf16[512,1024]{1,0:T(8,128)(2,1)} %multiply_convert_fusion.3), kind=kOutput, calls=%fused_computation.27 | convolution fusion | flops 6459228160 | bytes 19922944 | tf_op jit(solution)/shard_map/dot_general | solution.py:59
  240.5 11.3 %multiply_convert_fusion.1 = (bf16[2048,768]{0,1:T(8,128)(2,1)}, bf16[2048,768]{0,1:T(8,128)(2,1)}, bf16[2048,768]{0,1:T(8,128)(2,1)S(1)}) fusion(f32[2048,1536]{0,1:T(8,128)} %fusion.8, bf16[2048,1024]{1,0:T(8,128)(2,1)} %constant_dynamic-update-slice_fusion, bf16[768,1024]{1,0:T(8,128)(2,1)S(1)} %bitcast.80), kind=kOutput, calls=%fused_computation.7 | convolution fusion | flops 3244818432 | bytes 27787264 | tf_op jit(solution)/shard_map/dot_general | solution.py:55
  251.8 3.8 convolution_convert_fusion.1
  255.6 8.3 %convolution_convert_fusion.4 = bf16[768,1024]{1,0:T(8,128)(2,1)} fusion(bf16[2048,768]{0,1:T(8,128)(2,1)S(1)} %get-tuple-element.50, bf16[2048,1024]{1,0:T(8,128)(2,1)} %constant_dynamic-update-slice_fusion), kind=kOutput, calls=%fused_computation.49 | convolution fusion | flops 3222011904 | bytes 8912896 | tf_op jit(solution)/shard_map/dot_general | solution.py:441
  266.1 10.2 %fusion.5 = bf16[2048,1024]{1,0:T(8,128)(2,1)S(1)} fusion(bf16[2048,768]{0,1:T(8,128)(2,1)} %get-tuple-element.49, bf16[2048,768]{0,1:T(8,128)(2,1)} %get-tuple-element.48, bf16[192,8,8,128]{3,2,1,0:T(8,128)(2,1)} %bitcast.74), kind=kOutput, calls=%fused_computation.17 | convolution fusion | flops 6457131008 | bytes 13631488 | tf_op jit(solution)/shard_map/dot_general | solution.py:55
  280.9 10.6 %fusion.6 = bf16[1024,1536]{1,0:T(8,128)(2,1)} fusion(bf16[2048,768]{0,1:T(8,128)(2,1)S(1)} %copy-done.36, bf16[2048,768]{0,1:T(8,128)(2,1)S(1)} %copy-done.35, bf16[512,1024]{1,0:T(8,128)(2,1)} %collective-permute-done.8, bf16[512,1024]{1,0:T(8,128)(2,1)} %collective-permute-done.7, bf16[512,1024]{1,0:T(8,128)(2,1)} %collective-permute-done.6, ...), kind=kOutput, calls=%fused_computation.18 | convolution fusion | flops 6473383936 | bytes 13631488 | tf_op jit(solution)/shard_map/dot_general | solution.py:441
  298.2 21.6 %collective-permute-done.17 = bf16[512,1024]{1,0:T(8,128)(2,1)S(1)} collective-permute-done((bf16[512,1024]{1,0:T(8,128)(2,1)S(1)}, bf16[512,1024]{1,0:T(8,128)(2,1)S(1)}, u32[]{:S(2)}, u32[]{:S(2)}) %collective-permute-start.17) | collective-permute-done | bytes 1048608 | tf_op jit(solution)/shard_map/ppermute | solution.py:306
  320.8 21.2 %collective-permute-done.11 = bf16[512,1024]{1,0:T(8,128)(2,1)S(1)} collective-permute-done((bf16[512,1024]{1,0:T(8,128)(2,1)S(1)}, bf16[512,1024]{1,0:T(8,128)(2,1)S(1)}, u32[]{:S(2)}, u32[]{:S(2)}) %collective-permute-start.11) | collective-permute-done | bytes 1048608 | tf_op jit(solution)/shard_map/ppermute | solution.py:306
  342.0 3.9 fusion.45
  347.3 23.8 %collective-permute-done.19 = bf16[512,1024]{1,0:T(8,128)(2,1)} collective-permute-done((bf16[512,1024]{1,0:T(8,128)(2,1)}, bf16[512,1024]{1,0:T(8,128)(2,1)}, u32[]{:S(2)}, u32[]{:S(2)}) %collective-permute-start.19) | collective-permute-done | bytes 1048608 | tf_op jit(solution)/shard_map/ppermute | solution.py:306
  374.1 6.3 %convolution_convert_fusion.5 = bf16[512,1024]{1,0:T(8,128)(2,1)} fusion(bf16[2048,512]{1,0:T(8,128)(2,1)} %get-tuple-element.21.out, bf16[512,1024]{1,0:T(8,128)(2,1)} %collective-permute-done.20, bf16[512,1024]{1,0:T(8,128)(2,1)} %collective-permute-done.19, bf16[512,1024]{1,0:T(8,128)(2,1)} %collective-permute-done.18, ...), kind=kOutput, calls=%fused_computation.52 | convolution fusion | flops 2164785152 | bytes 7340032 | tf_op jit(solution)/shard_map/dot_general | solution.py:441
  380.7 6.3 %convolution_convert_fusion.3.grad_out = bf16[2048,512]{1,0:T(8,128)(2,1)} fusion(bf16[512,1024]{1,0:T(8,128)(2,1)} %bitcast.87, bf16[512,1024]{1,0:T(8,128)(2,1)} %collective-permute-done.20, bf16[512,1024]{1,0:T(8,128)(2,1)} %collective-permute-done.19, bf16[512,1024]{1,0:T(8,128)(2,1)} %collective-permute-done.18, bf16[512,1024]{1,0:T(8,128)(2,1)} %get-tuple-element.44), kind=kOutput, calls=%fused_computation.29 | convolution fusion | flops 2165309440 | bytes 7340032 | tf_op jit(solution)/shard_map/dot_general | solution.py:55
  387.1 50.2 %attend_back.1 = (bf16[2048,1024]{1,0:T(8,128)(2,1)}, f32[2,2,128]{2,1,0:T(2,128)}) custom-call(s32[9]{0:T(128)} %pad_add_fusion.info, f32[2048,1024]{1,0:T(8,128)} %fusion.19.qkv, f32[2048,128]{1,0:T(8,128)} %get-tuple-element.74.cos, f32[2048,128]{1,0:T(8,128)} %get-tuple-element.75.sin, f32[1,128]{1,0:T(1,128)} %get-tuple-element.65.gain_q, ...), custom_call_target="tpu_custom_call" | custom-call | flops 20000000000 | bytes 20000000 | tf_op jit(solution)/shard_map/attend_back/pallas_call | solution.py:262
  437.3 8.7 %multiply_reduce_fusion = (f32[1024]{0:T(1024)S(1)}, bf16[1024,1024]{0,1:T(8,128)(2,1)}) fusion(bf16[1024,1024]{0,1:T(8,128)(2,1)S(1)} %copy.82, bf16[2048,1024]{1,0:T(8,128)(2,1)} %get-tuple-element.23, f32[1024]{0:T(1024)S(1)} %copy-done.26, f32[2048]{0:T(1024)S(1)} %copy-done.30, bf16[512,1024]{1,0:T(8,128)(2,1)S(1)} %copy-done.22, ...), kind=kOutput, calls=%fused_computation.14 | convolution fusion | flops 4322229248 | bytes 12599296 | tf_op jit(solution)/shard_map/dot_general | solution.py:441
  446.0 4.2 copy.83
  450.2 7.3 %convolution_convert_fusion.2 = bf16[2048,1024]{1,0:T(8,128)(2,1)S(1)} fusion(bf16[2048,1024]{1,0:T(8,128)(2,1)} %get-tuple-element.23, bf16[1024,1024]{1,0:T(8,128)(2,1)S(1)} %bitcast.68), kind=kOutput, calls=%fused_computation.21 | convolution fusion | flops 4297064448 | bytes 10485760 | tf_op jit(solution)/shard_map/dot_general | solution.py:55
  471.1 14.0 %collective-permute-start.27 = (f32[2304]{0:T(1024)S(1)}, f32[2304]{0:T(1024)S(1)}, u32[]{:S(2)}, u32[]{:S(2)}) collective-permute-start(f32[2304]{0:T(1024)S(1)} %add.264), channel_id=1, source_target_pairs={{0,8},{4,12},{8,0},{12,4},{16,24},{20,28},{24,16},{28,20},{1,9},{5... | collective-permute-start | bytes 27656 | tf_op jit(solution)/shard_map/ppermute | solution.py:306
  498.7 5.2 multiply_subtract_fusion
  503.9 12.1 %collective-permute-done.23 = bf16[512,1024]{1,0:T(8,128)(2,1)S(1)} collective-permute-done((bf16[512,1024]{1,0:T(8,128)(2,1)}, bf16[512,1024]{1,0:T(8,128)(2,1)S(1)}, u32[]{:S(2)}, u32[]{:S(2)}) %collective-permute-start.23) | collective-permute-done | bytes 1048608 | tf_op jit(solution)/shard_map/ppermute | solution.py:306
  519.1 31.0 %reduce-scatter.13.cloned.1.call-done = bf16[128,1024]{1,0:T(8,128)(2,1)} async-done(((bf16[1024,1024]{1,0:T(8,128)(2,1)}), bf16[128,1024]{1,0:T(8,128)(2,1)}) %reduce-scatter.13.cloned.1.call-update) | async-done | bytes 262160
  551.4 4.2 multiply_subtract_fusion.1
  (211 shorter events, 91.0 us)
Async XLA Ops:
  7.2 70.2 %all-gather.5.cloned.1.call-start = ((), (), s32[]{:S(2)}) async-start(), calls=%async_computation.7 | async-start | bytes 3833856 | tf_op jit(solution)/shard_map/all_gather | solution.py:358
  11.0 202.3 %all-gather.7.cloned.1.call-start = ((), (), s32[]{:S(2)}) async-start(), calls=%async_computation.8 | async-start | bytes 5308416 | tf_op jit(solution)/shard_map/all_gather | solution.py:359
  11.1 26.4 %collective-permute-start.1 = (bf16[512,1024]{1,0:T(8,128)(2,1)}, bf16[512,1024]{1,0:T(8,128)(2,1)S(1)}, u32[]{:S(2)}, u32[]{:S(2)}) collective-permute-start(bf16[512,1024]{1,0:T(8,128)(2,1)} %param.18), channel_id=1, source_target_pairs={{0,2},{1,3},{2,0},{3,1},{4,6},{5,7},{6,4},{7,5},{8,10},{9,11},{10,... | collective-permute-start | bytes 3145736 | tf_op jit(solution)/shard_map/ppermute | solution.py:306
  14.1 29.8 %collective-permute-start = (bf16[512,1024]{1,0:T(8,128)(2,1)}, bf16[512,1024]{1,0:T(8,128)(2,1)S(1)}, u32[]{:S(2)}, u32[]{:S(2)}) collective-permute-start(bf16[512,1024]{1,0:T(8,128)(2,1)} %param.18), channel_id=1, source_target_pairs={{0,1},{1,0},{2,3},{3,2},{4,5},{5,4},{6,7},{7,6},{8,9},{9,8},{10,11... | collective-permute-start | bytes 3145736 | tf_op jit(solution)/shard_map/ppermute | solution.py:306
  16.7 468.3 %reduce-scatter.11.cloned.1.call-start = ((), (), s32[]{:S(2)}) async-start(), calls=%async_computation.6 | async-start | bytes 1769472 | tf_op jit(solution)/shard_map/reduce_scatter | solution.py:444
  37.5 6.4 %collective-permute-start.2 = (bf16[512,1024]{1,0:T(8,128)(2,1)S(1)}, bf16[512,1024]{1,0:T(8,128)(2,1)S(1)}, u32[]{:S(2)}, u32[]{:S(2)}) collective-permute-start(bf16[512,1024]{1,0:T(8,128)(2,1)S(1)} %collective-permute-done.1), channel_id=1, source_target_pairs={{0,1},{1,0},{2,3},{3,2},{4,5},{5,4},{6,7},{7,6},{8,9},{9,8},{10,11... | collective-permute-start | bytes 3145736 | tf_op jit(solution)/shard_map/ppermute | solution.py:306
  135.7 5.1 collective-permute-start.3
  138.7 26.1 %collective-permute-start.5 = (bf16[512,1024]{1,0:T(8,128)(2,1)S(1)}, bf16[512,1024]{1,0:T(8,128)(2,1)S(1)}, u32[]{:S(2)}, u32[]{:S(2)}) collective-permute-start(bf16[512,1024]{1,0:T(8,128)(2,1)S(1)} %add_convert_fusion.4), channel_id=1, source_target_pairs={{0,2},{1,3},{2,0},{3,1},{4,6},{5,7},{6,4},{7,5},{8,10},{9,11},{10,... | collective-permute-start | bytes 3145736 | tf_op jit(solution)/shard_map/ppermute | solution.py:306
  140.2 47.0 %collective-permute-start.13 = (bf16[512,1024]{1,0:T(8,128)(2,1)S(1)}, bf16[512,1024]{1,0:T(8,128)(2,1)S(1)}, u32[]{:S(2)}, u32[]{:S(2)}) collective-permute-start(bf16[512,1024]{1,0:T(8,128)(2,1)S(1)} %copy-done.9), channel_id=1, source_target_pairs={{0,2},{1,3},{2,0},{3,1},{4,6},{5,7},{6,4},{7,5},{8,10},{9,11},{10,... | collective-permute-start | bytes 3145736 | tf_op jit(solution)/shard_map/ppermute | solution.py:306
  166.7 42.3 %collective-permute-start.7 = (bf16[512,1024]{1,0:T(8,128)(2,1)}, bf16[512,1024]{1,0:T(8,128)(2,1)}, u32[]{:S(2)}, u32[]{:S(2)}) collective-permute-start(bf16[512,1024]{1,0:T(8,128)(2,1)} %multiply_convert_fusion.3), channel_id=1, source_target_pairs={{0,2},{1,3},{2,0},{3,1},{4,6},{5,7},{6,4},{7,5},{8,10},{9,11},{10,... | collective-permute-start | bytes 3145736 | tf_op jit(solution)/shard_map/ppermute | solution.py:306
  168.2 42.0 %collective-permute-start.12 = (bf16[512,1024]{1,0:T(8,128)(2,1)S(1)}, bf16[512,1024]{1,0:T(8,128)(2,1)S(1)}, u32[]{:S(2)}, u32[]{:S(2)}) collective-permute-start(bf16[512,1024]{1,0:T(8,128)(2,1)S(1)} %copy-done.9), channel_id=1, source_target_pairs={{0,1},{1,0},{2,3},{3,2},{4,5},{5,4},{6,7},{7,6},{8,9},{9,8},{10,11... | collective-permute-start | bytes 3145736 | tf_op jit(solution)/shard_map/ppermute | solution.py:306
  187.3 25.0 %collective-permute-start.14 = (bf16[512,1024]{1,0:T(8,128)(2,1)S(1)}, bf16[512,1024]{1,0:T(8,128)(2,1)S(1)}, u32[]{:S(2)}, u32[]{:S(2)}) collective-permute-start(bf16[512,1024]{1,0:T(8,128)(2,1)S(1)} %collective-permute-done.13), channel_id=1, source_target_pairs={{0,1},{1,0},{2,3},{3,2},{4,5},{5,4},{6,7},{7,6},{8,9},{9,8},{10,11... | collective-permute-start | bytes 3145736 | tf_op jit(solution)/shard_map/ppermute | solution.py:306
  187.3 41.4 %collective-permute-start.6 = (bf16[512,1024]{1,0:T(8,128)(2,1)}, bf16[512,1024]{1,0:T(8,128)(2,1)}, u32[]{:S(2)}, u32[]{:S(2)}) collective-permute-start(bf16[512,1024]{1,0:T(8,128)(2,1)} %multiply_convert_fusion.3), channel_id=1, source_target_pairs={{0,1},{1,0},{2,3},{3,2},{4,5},{5,4},{6,7},{7,6},{8,9},{9,8},{10,11... | collective-permute-start | bytes 3145736 | tf_op jit(solution)/shard_map/ppermute | solution.py:306
  209.0 19.7 %collective-permute-start.8 = (bf16[512,1024]{1,0:T(8,128)(2,1)}, bf16[512,1024]{1,0:T(8,128)(2,1)}, u32[]{:S(2)}, u32[]{:S(2)}) collective-permute-start(bf16[512,1024]{1,0:T(8,128)(2,1)} %collective-permute-done.7), channel_id=1, source_target_pairs={{0,1},{1,0},{2,3},{3,2},{4,5},{5,4},{6,7},{7,6},{8,9},{9,8},{10,11... | collective-permute-start | bytes 3145736 | tf_op jit(solution)/shard_map/ppermute | solution.py:306
  265.5 30.1 %collective-permute-start.10 = (bf16[512,1024]{1,0:T(8,128)(2,1)}, bf16[512,1024]{1,0:T(8,128)(2,1)}, u32[]{:S(2)}, u32[]{:S(2)}) collective-permute-start(bf16[512,1024]{1,0:T(8,128)(2,1)} %get-tuple-element.58), channel_id=1, source_target_pairs={{0,1},{1,0},{2,3},{3,2},{4,5},{5,4},{6,7},{7,6},{8,9},{9,8},{10,11... | collective-permute-start | bytes 3145736 | tf_op jit(solution)/shard_map/ppermute | solution.py:306
  266.0 228.1 %reduce-scatter.9.cloned.1.call-start = ((), (), s32[]{:S(2)}) async-start(), calls=%async_computation.5 | async-start | bytes 3538944 | tf_op jit(solution)/shard_map/reduce_scatter | solution.py:448
  279.8 11.8 %collective-permute-start.16 = (bf16[512,1024]{1,0:T(8,128)(2,1)}, bf16[512,1024]{1,0:T(8,128)(2,1)}, u32[]{:S(2)}, u32[]{:S(2)}) collective-permute-start(bf16[512,1024]{1,0:T(8,128)(2,1)} %get-tuple-element.56), channel_id=1, source_target_pairs={{0,1},{1,0},{2,3},{3,2},{4,5},{5,4},{6,7},{7,6},{8,9},{9,8},{10,11... | collective-permute-start | bytes 3145736 | tf_op jit(solution)/shard_map/ppermute | solution.py:306
  291.5 205.0 %reduce-scatter.7.cloned.1.call-start = ((), (), s32[]{:S(2)}) async-start(), calls=%async_computation.4 | async-start | bytes 1179648 | tf_op jit(solution)/shard_map/reduce_scatter | solution.py:456
  291.5 6.7 %collective-permute-start.15 = (bf16[512,1024]{1,0:T(8,128)(2,1)}, bf16[512,1024]{1,0:T(8,128)(2,1)S(1)}, u32[]{:S(2)}, u32[]{:S(2)}) collective-permute-start(bf16[512,1024]{1,0:T(8,128)(2,1)} %get-tuple-element.55), channel_id=1, source_target_pairs={{0,1},{1,0},{2,3},{3,2},{4,5},{5,4},{6,7},{7,6},{8,9},{9,8},{10,11... | collective-permute-start | bytes 3145736 | tf_op jit(solution)/shard_map/ppermute | solution.py:306
  293.8 26.0 %collective-permute-start.17 = (bf16[512,1024]{1,0:T(8,128)(2,1)S(1)}, bf16[512,1024]{1,0:T(8,128)(2,1)S(1)}, u32[]{:S(2)}, u32[]{:S(2)}) collective-permute-start(bf16[512,1024]{1,0:T(8,128)(2,1)S(1)} %add_convert_fusion.1), channel_id=1, source_target_pairs={{0,2},{1,3},{2,0},{3,1},{4,6},{5,7},{6,4},{7,5},{8,10},{9,11},{10,... | collective-permute-start | bytes 3145736 | tf_op jit(solution)/shard_map/ppermute | solution.py:306
  295.3 25.4 %collective-permute-start.9 = (bf16[512,1024]{1,0:T(8,128)(2,1)}, bf16[512,1024]{1,0:T(8,128)(2,1)S(1)}, u32[]{:S(2)}, u32[]{:S(2)}) collective-permute-start(bf16[512,1024]{1,0:T(8,128)(2,1)} %get-tuple-element.57), channel_id=1, source_target_pairs={{0,1},{1,0},{2,3},{3,2},{4,5},{5,4},{6,7},{7,6},{8,9},{9,8},{10,11... | collective-permute-start | bytes 3145736 | tf_op jit(solution)/shard_map/ppermute | solution.py:306
  297.6 44.4 %collective-permute-start.11 = (bf16[512,1024]{1,0:T(8,128)(2,1)S(1)}, bf16[512,1024]{1,0:T(8,128)(2,1)S(1)}, u32[]{:S(2)}, u32[]{:S(2)}) collective-permute-start(bf16[512,1024]{1,0:T(8,128)(2,1)S(1)} %add_convert_fusion.3), channel_id=1, source_target_pairs={{0,2},{1,3},{2,0},{3,1},{4,6},{5,7},{6,4},{7,5},{8,10},{9,11},{10,... | collective-permute-start | bytes 3145736 | tf_op jit(solution)/shard_map/ppermute | solution.py:306
  345.9 25.2 %collective-permute-start.19 = (bf16[512,1024]{1,0:T(8,128)(2,1)}, bf16[512,1024]{1,0:T(8,128)(2,1)}, u32[]{:S(2)}, u32[]{:S(2)}) collective-permute-start(bf16[512,1024]{1,0:T(8,128)(2,1)} %get-tuple-element.44), channel_id=1, source_target_pairs={{0,2},{1,3},{2,0},{3,1},{4,6},{5,7},{6,4},{7,5},{8,10},{9,11},{10,... | collective-permute-start | bytes 3145736 | tf_op jit(solution)/shard_map/ppermute | solution.py:306
  347.3 26.7 %collective-permute-start.18 = (bf16[512,1024]{1,0:T(8,128)(2,1)}, bf16[512,1024]{1,0:T(8,128)(2,1)}, u32[]{:S(2)}, u32[]{:S(2)}) collective-permute-start(bf16[512,1024]{1,0:T(8,128)(2,1)} %get-tuple-element.44), channel_id=1, source_target_pairs={{0,1},{1,0},{2,3},{3,2},{4,5},{5,4},{6,7},{7,6},{8,9},{9,8},{10,11... | collective-permute-start | bytes 3145736 | tf_op jit(solution)/shard_map/ppermute | solution.py:306
  380.5 169.6 %reduce-scatter.13.cloned.1.call-start = ((), (), s32[]{:S(2)}) async-start(), calls=%async_computation.9 | async-start | bytes 2359296
  461.0 28.2 %collective-permute-start.22 = (bf16[512,1024]{1,0:T(8,128)(2,1)}, bf16[512,1024]{1,0:T(8,128)(2,1)S(1)}, u32[]{:S(2)}, u32[]{:S(2)}) collective-permute-start(bf16[512,1024]{1,0:T(8,128)(2,1)} %get-tuple-element.54), channel_id=1, source_target_pairs={{0,1},{1,0},{2,3},{3,2},{4,5},{5,4},{6,7},{7,6},{8,9},{9,8},{10,11... | collective-permute-start | bytes 3145736 | tf_op jit(solution)/shard_map/ppermute | solution.py:306
  463.7 3.7 collective-permute-start.25
  467.4 3.7 collective-permute-start.26
  471.1 16.3 %collective-permute-start.27 = (f32[2304]{0:T(1024)S(1)}, f32[2304]{0:T(1024)S(1)}, u32[]{:S(2)}, u32[]{:S(2)}) collective-permute-start(f32[2304]{0:T(1024)S(1)} %add.264), channel_id=1, source_target_pairs={{0,8},{4,12},{8,0},{12,4},{16,24},{20,28},{24,16},{28,20},{1,9},{5... | collective-permute-start | bytes 27656 | tf_op jit(solution)/shard_map/ppermute | solution.py:306
  487.4 16.5 %collective-permute-start.21 = (bf16[512,1024]{1,0:T(8,128)(2,1)}, bf16[512,1024]{1,0:T(8,128)(2,1)S(1)}, u32[]{:S(2)}, u32[]{:S(2)}) collective-permute-start(bf16[512,1024]{1,0:T(8,128)(2,1)} %get-tuple-element.53), channel_id=1, source_target_pairs={{0,1},{1,0},{2,3},{3,2},{4,5},{5,4},{6,7},{7,6},{8,9},{9,8},{10,11... | collective-permute-start | bytes 3145736 | tf_op jit(solution)/shard_map/ppermute | solution.py:306
  487.4 6.0 %collective-permute-start.28 = (f32[2304]{0:T(1024)S(1)}, f32[2304]{0:T(1024)S(1)}, u32[]{:S(2)}, u32[]{:S(2)}) collective-permute-start(f32[2304]{0:T(1024)S(1)} %add.265), channel_id=1, source_target_pairs={{0,16},{4,20},{8,24},{12,28},{16,0},{20,4},{24,8},{28,12},{1,17},{... | collective-permute-start | bytes 27656 | tf_op jit(solution)/shard_map/ppermute | solution.py:306
  491.9 24.1 %collective-permute-start.23 = (bf16[512,1024]{1,0:T(8,128)(2,1)}, bf16[512,1024]{1,0:T(8,128)(2,1)S(1)}, u32[]{:S(2)}, u32[]{:S(2)}) collective-permute-start(bf16[512,1024]{1,0:T(8,128)(2,1)} %add_convert_fusion), channel_id=1, source_target_pairs={{0,2},{1,3},{2,0},{3,1},{4,6},{5,7},{6,4},{7,5},{8,10},{9,11},{10,... | collective-permute-start | bytes 3145736 | tf_op jit(solution)/shard_map/ppermute | solution.py:306
  (40 other events, 861.5 us)
Sparse Core Ops, SparseCore 0:
  11.2 66.2 all-gather.4
  80.2 78.3 all-gather.6
  266.1 70.1 reduce-scatter.10
  340.2 73.3 reduce-scatter.8
  417.2 62.7 reduce-scatter.6
  483.4 66.6 reduce-scatter.12

commit v2 on v1

v2 whole, which is shorter than its diff:
```python
import jax
import jax.numpy as jnp
from jax import lax
from jax.experimental import pallas as pl
from jax.experimental.pallas import tpu as pltpu
from jax.sharding import PartitionSpec as P

MODEL_WIDTH = 1024
QUERY_HEADS = 16
KEY_VALUE_HEADS = 8
HEAD_SIZE = 128
FF = 3072
STEP = 10

EPS = 1e-06
THETA = 1000000.0
BETA_ONE = 0.9
BETA_TWO = 0.95
ADAM_EPS = 1e-08
DECAY = 0.1

GROUP = QUERY_HEADS // KEY_VALUE_HEADS
SLOTS = GROUP + 2
SCALE = HEAD_SIZE ** (-0.5)
LOG2E = 1.4426950408889634
BLOCK = 256
VMEM_LIMIT = 48 * 1024 * 1024
RING = (0, 2, 4, 6, 7, 5, 3, 1)
F32 = jnp.float32
BF16 = jnp.bfloat16


def norm_rows(values, scales):
    return values * lax.rsqrt(jnp.mean(values * values, axis=-1, keepdims=True) + EPS) * scales


def norm_back(values, scales, grad):
    r = lax.rsqrt(jnp.mean(values * values, axis=-1, keepdims=True) + EPS)
    u = grad * scales
    back = r * u - values * (r * r * r) * jnp.mean(u * values, axis=-1, keepdims=True)
    return back, jnp.sum(grad * values * r, axis=0)


def adamw_update(master, moment_one, moment_two, gradient, step_rate, decay_rate):
    next_one = BETA_ONE * moment_one + (1.0 - BETA_ONE) * gradient
    next_two = BETA_TWO * moment_two + (1.0 - BETA_TWO) * gradient * gradient
    one_hat = next_one / (1.0 - BETA_ONE**STEP)
    two_hat = next_two / (1.0 - BETA_TWO**STEP)
    next_master = master - step_rate * (
        one_hat / (jnp.sqrt(two_hat) + ADAM_EPS) + decay_rate * master
    )
    return (next_one, next_two, next_master)


def nt(a, b):
    return lax.dot_general(a, b, (((1,), (1,)), ((), ())), preferred_element_type=F32)


def nn(a, b):
    return jnp.dot(a, b, preferred_element_type=F32)


def head_rotated(x, gain, cos, sin):
    r = lax.rsqrt(jnp.mean(x * x, axis=-1, keepdims=True) + EPS)
    y = x * r * gain
    return y * cos + pltpu.roll(y, HEAD_SIZE // 2, 1) * sin


def head_back(x, gain, cos, sin, grad):
    r = lax.rsqrt(jnp.mean(x * x, axis=-1, keepdims=True) + EPS)
    turned = grad * cos - pltpu.roll(grad, HEAD_SIZE // 2, 1) * sin
    u = turned * gain
    back = r * u - x * (r * r * r) * jnp.mean(u * x, axis=-1, keepdims=True)
    return back, jnp.sum(turned * x * r, axis=0, keepdims=True)


def at_block(index):
    return pl.ds(pl.multiple_of(index * BLOCK, BLOCK), BLOCK)


def allowed_block(key_block, query_block, start):
    keys = key_block * BLOCK + lax.broadcasted_iota(jnp.int32, (BLOCK, BLOCK), 0)
    queries = query_block * BLOCK + lax.broadcasted_iota(jnp.int32, (BLOCK, BLOCK), 1)
    return (keys >= start) & (keys <= queries)


def lanes_of(h):
    return slice(h * HEAD_SIZE, (h + 1) * HEAD_SIZE)


def project_kernel(
    x, gain, matrix, cos, sin, gain_q, gain_k, normed, raw_q, raw_k, q, k, v, k_turned, v_turned
):
    h = norm_rows(x[...].astype(F32), gain[...]).astype(BF16)
    normed[...] = h
    c, s = cos[...], sin[...]
    for j in range(matrix.shape[1] // (SLOTS * HEAD_SIZE)):
        base = j * SLOTS * HEAD_SIZE
        part = nn(h, matrix[:, base : base + SLOTS * HEAD_SIZE])
        for g in range(GROUP):
            value = part[:, lanes_of(g)]
            raw_q[:, lanes_of(j * GROUP + g)] = value
            q[:, lanes_of(j * GROUP + g)] = head_rotated(value, gain_q[...], c, s).astype(BF16)
        value = part[:, lanes_of(GROUP)]
        raw_k[:, lanes_of(j)] = value
        turned = head_rotated(value, gain_k[...], c, s)
        k[:, lanes_of(j)] = turned.astype(BF16)
        k_turned[lanes_of(j), :] = turned.T.astype(BF16)
        value = part[:, lanes_of(GROUP + 1)]
        v[:, lanes_of(j)] = value.astype(BF16)
        v_turned[lanes_of(j), :] = value.T.astype(BF16)


def attend_kernel(offset, info, q, k, v_turned, start, out, logs):
    blocks = k.shape[0] // BLOCK
    flip = info[blocks]

    def one_block(i, _):
        here = at_block(i)
        b = (i + offset) ^ flip
        first = start[:, here]
        queries = [q[here, lanes_of(h)] for h in range(GROUP)]

        def keys_step(kb, carry):
            there = at_block(kb ^ flip)
            key, value = k[there, :], v_turned[:, there]
            allowed = allowed_block(kb, b, first)
            after = []
            for h in range(GROUP):
                total, blend = carry[h]
                p = jnp.where(allowed, jnp.exp2(nt(key, queries[h]) * (SCALE * LOG2E)), 0.0)
                after.append(
                    (total + jnp.sum(p, axis=0, keepdims=True), blend + nn(value, p.astype(BF16)))
                )
            return tuple(after)

        zero = (jnp.zeros((1, BLOCK), F32), jnp.zeros((HEAD_SIZE, BLOCK), F32))
        done = lax.fori_loop(info[b], b + 1, keys_step, (zero,) * GROUP)
        for h in range(GROUP):
            total, blend = done[h]
            out[here, lanes_of(h)] = (blend / total).T.astype(BF16)
            logs[0, h : h + 1, here] = jnp.log2(total)
        return 0

    lax.fori_loop(0, q.shape[0] // BLOCK, one_block, 0)


def back_blocks(
    offset, info, q, k, v, k_turned, start, logs, out, grad_out, raw_q, cos, sin, gain_q,
    grad_k, grad_v, store,
):
    flip = info[k.shape[0] // BLOCK]

    def one_block(i, total_gain):
        here = at_block(i)
        b = (i + offset) ^ flip
        first = start[:, here]
        queries, gradients, across, log = [], [], [], []
        for h in range(GROUP):
            g = grad_out[here, lanes_of(h)]
            queries.append(q[here, lanes_of(h)])
            gradients.append(g)
            both = g.astype(F32) * out[here, lanes_of(h)].astype(F32)
            across.append(jnp.sum(both.T, axis=0, keepdims=True))
            log.append(logs[0, h : h + 1, here])

        def keys_step(kb, carry):
            there = at_block(kb ^ flip)
            key, value, key_turned = k[there, :], v[there, :], k_turned[:, there]
            allowed = allowed_block(kb, b, first)
            after, add_k, add_v = [], 0.0, 0.0
            for h in range(GROUP):
                s = nt(key, queries[h])
                p = jnp.where(allowed, jnp.exp2(s * (SCALE * LOG2E) - log[h]), 0.0)
                d = (p * (nt(value, gradients[h]) - across[h])).astype(BF16)
                add_v = add_v + nn(p.astype(BF16), gradients[h])
                add_k = add_k + nn(d, queries[h])
                after.append(carry[h] + nn(key_turned, d))
            grad_k[there, :] += add_k
            grad_v[there, :] += add_v
            return tuple(after)

        zero = jnp.zeros((HEAD_SIZE, BLOCK), F32)
        done = lax.fori_loop(info[b], b + 1, keys_step, (zero,) * GROUP)
        c, s = cos[here, :], sin[here, :]
        for h in range(GROUP):
            back, gain = head_back(raw_q[here, lanes_of(h)], gain_q[...], c, s, done[h].T * SCALE)
            store(i, h, back.astype(BF16))
            total_gain = total_gain + gain
        return total_gain

    return lax.fori_loop(0, q.shape[0] // BLOCK, one_block, jnp.zeros((1, HEAD_SIZE), F32))


def back_own_kernel(
    info, q, k, v, k_turned, start, logs, out, grad_out, raw_q, cos, sin, gain_q,
    grad_q, grad_k, grad_v, grad_gain,
):
    grad_k[...] = jnp.zeros(grad_k.shape, F32)
    grad_v[...] = jnp.zeros(grad_v.shape, F32)

    def store(i, h, value):
        grad_q[at_block(i), lanes_of(h)] = value

    grad_gain[0, :, :] = back_blocks(
        0, info, q, k, v, k_turned, start, logs, out, grad_out, raw_q, cos, sin, gain_q,
        grad_k, grad_v, store,
    )


def back_other_kernel(
    info, q, k, v, k_turned, start, logs, out, grad_out, raw_q, cos, sin, gain_q,
    cos_all, sin_all, raw_k, gain_k, grad_q_own, grad_k_own, grad_v_own,
    grad_qkv, grad_gains, grad_k, grad_v,
):
    half = q.shape[0] // BLOCK
    blocks = k.shape[0] // BLOCK
    queries = GROUP * HEAD_SIZE
    grad_k[...] = grad_k_own[...]
    grad_v[...] = grad_v_own[...]
    grad_qkv[: half * BLOCK, :queries] = grad_q_own[...]

    def store(i, h, value):
        grad_qkv[at_block(i + half), lanes_of(h)] = value

    grad_gains[0:1, :] = back_blocks(
        half, info, q, k, v, k_turned, start, logs, out, grad_out, raw_q, cos, sin, gain_q,
        grad_k, grad_v, store,
    )

    def finish(i, total_gain):
        rows = at_block(i)
        back, gain = head_back(
            raw_k[rows, :], gain_k[...], cos_all[rows, :], sin_all[rows, :], grad_k[rows, :] * SCALE
        )
        grad_qkv[rows, lanes_of(GROUP)] = back.astype(BF16)
        grad_qkv[rows, lanes_of(GROUP + 1)] = grad_v[rows, :].astype(BF16)
        return total_gain + gain

    grad_gains[1:2, :] = lax.fori_loop(0, blocks, finish, jnp.zeros((1, HEAD_SIZE), F32))


def feed_kernel(h, grad, gate_up, down, hidden, grad_gate_up, back_a, back_b, sum_a, sum_b):
    step = pl.program_id(0)
    width = down.shape[0]
    both = nn(h[...], gate_up[...])
    gate, up = both[:, :width], both[:, width:]
    sig = jax.nn.sigmoid(gate)
    gated = gate * sig
    value = (gated * up).astype(BF16)
    hidden[...] = value
    grad_hidden = nt(grad[...], down[...])
    grad_gate_up[:, :width] = (grad_hidden * up * (sig + gated * (1.0 - sig))).astype(BF16)
    grad_gate_up[:, width:] = (grad_hidden * gated).astype(BF16)
    back = nt(grad_gate_up[...], gate_up[...]).astype(BF16)
    total = nn(value, down[...]).astype(BF16)
    first = step < pl.num_programs(0) // 2

    @pl.when(first)
    def _():
        back_a[...] = back
        sum_a[...] = total

    @pl.when(jnp.logical_not(first))
    def _():
        back_b[...] = back
        sum_b[...] = total


def unproject_kernel(grad_zero, grad_one, matrix, out_a, out_b):
    width = grad_zero.shape[1]
    value = nt(grad_zero[...], matrix[:, :width]) + nt(grad_one[...], matrix[:, width:])
    value = value.astype(BF16)
    first = pl.program_id(0) < pl.num_programs(0) // 2

    @pl.when(first)
    def _():
        out_a[...] = value

    @pl.when(jnp.logical_not(first))
    def _():
        out_b[...] = value


def params(name, flops):
    return dict(
        compiler_params=pltpu.CompilerParams(
            dimension_semantics=("arbitrary",), vmem_limit_bytes=VMEM_LIMIT
        ),
        cost_estimate=pl.CostEstimate(flops=flops, bytes_accessed=8_000_000, transcendentals=0),
        name=name,
    )


def fixed(shape, index=None):
    index = (0,) * len(shape) if index is None else index
    return pl.BlockSpec(shape, lambda i, *_: index)


def shaped(shape, kind):
    return jax.ShapeDtypeStruct(shape, kind)


def project(x, gain, matrix, cos, sin, gain_q, gain_k):
    rows, width = x.shape
    heads = matrix.shape[1] // (SLOTS * HEAD_SIZE)
    by_rows = lambda n: pl.BlockSpec((BLOCK, n), lambda i: (i, 0))
    by_lanes = lambda n: pl.BlockSpec((n, BLOCK), lambda i: (0, i))
    q_width, k_width = heads * GROUP * HEAD_SIZE, heads * HEAD_SIZE
    return pl.pallas_call(
        project_kernel,
        grid=(rows // BLOCK,),
        in_specs=[
            by_rows(width), fixed((1, width)), fixed(matrix.shape), by_rows(HEAD_SIZE),
            by_rows(HEAD_SIZE), fixed((1, HEAD_SIZE)), fixed((1, HEAD_SIZE)),
        ],
        out_specs=[
            by_rows(width), by_rows(q_width), by_rows(k_width), by_rows(q_width),
            by_rows(k_width), by_rows(k_width), by_lanes(k_width), by_lanes(k_width),
        ],
        out_shape=[
            shaped((rows, width), BF16), shaped((rows, q_width), F32),
            shaped((rows, k_width), F32), shaped((rows, q_width), BF16),
            shaped((rows, k_width), BF16), shaped((rows, k_width), BF16),
            shaped((k_width, rows), BF16), shaped((k_width, rows), BF16),
        ],
        **params("project", 10_000_000_000),
    )(x, gain, matrix, cos, sin, gain_q, gain_k)


def head_specs(half, rows, head=None):
    at = (lambda j: j) if head is None else (lambda j: head)
    n = rows // 2
    return dict(
        q=pl.BlockSpec((n, GROUP * HEAD_SIZE), lambda j, info: (half, at(j))),
        k=pl.BlockSpec((rows, HEAD_SIZE), lambda j, info: (0, at(j))),
        turned=pl.BlockSpec((HEAD_SIZE, rows), lambda j, info: (at(j), 0)),
        start=pl.BlockSpec((1, n), lambda j, info: (0, half)),
        out=pl.BlockSpec((n, GROUP * HEAD_SIZE), lambda j, info: (0, at(j))),
        logs=pl.BlockSpec((1, GROUP, n), lambda j, info: (at(j), 0, 0)),
        angle=pl.BlockSpec((n, HEAD_SIZE), lambda j, info: (half, 0)),
    )


def attend(half, info, q, k, v_turned, start):
    rows = k.shape[0]
    n, heads = rows // 2, k.shape[1] // HEAD_SIZE
    s = head_specs(half, rows)
    return pl.pallas_call(
        lambda *refs: attend_kernel(half * n // BLOCK, *refs),
        grid_spec=pltpu.PrefetchScalarGridSpec(
            num_scalar_prefetch=1,
            grid=(heads,),
            in_specs=[s["q"], s["k"], s["turned"], s["start"]],
            out_specs=[s["out"], s["logs"]],
        ),
        out_shape=[shaped((n, q.shape[1]), BF16), shaped((heads, GROUP, n), F32)],
        **params("attend", 18_000_000_000),
    )(info, q, k, v_turned, start)


def attend_back_own(info, q, k, v, k_turned, start, logs, out, grad_out, raw_q, cos, sin, gain_q):
    rows = k.shape[0]
    n, heads = rows // 2, k.shape[1] // HEAD_SIZE
    s = head_specs(0, rows)
    return pl.pallas_call(
        back_own_kernel,
        grid_spec=pltpu.PrefetchScalarGridSpec(
            num_scalar_prefetch=1,
            grid=(heads,),
            in_specs=[
                s["q"], s["k"], s["k"], s["turned"], s["start"], s["logs"], s["out"], s["out"],
                s["q"], s["angle"], s["angle"], fixed((1, HEAD_SIZE)),
            ],
            out_specs=[
                s["out"], s["k"], s["k"],
                pl.BlockSpec((1, 1, HEAD_SIZE), lambda j, info: (j, 0, 0)),
            ],
        ),
        out_shape=[
            shaped((n, q.shape[1]), BF16), shaped(k.shape, F32), shaped(k.shape, F32),
            shaped((heads, 1, HEAD_SIZE), F32),
        ],
        **params("attend_back_own", 25_000_000_000),
    )(info, q, k, v, k_turned, start, logs, out, grad_out, raw_q, cos, sin, gain_q)


def attend_back_other(
    head, info, q, k, v, k_turned, start, logs, out, grad_out, raw_q, cos, sin, gain_q,
    raw_k, gain_k, grad_q, grad_k, grad_v,
):
    rows = k.shape[0]
    s = head_specs(1, rows, head)
    row = fixed((1, HEAD_SIZE))
    return pl.pallas_call(
        back_other_kernel,
        grid_spec=pltpu.PrefetchScalarGridSpec(
            num_scalar_prefetch=1,
            grid=(1,),
            in_specs=[
                s["q"], s["k"], s["k"], s["turned"], s["start"], s["logs"], s["out"], s["out"],
                s["q"], s["angle"], s["angle"], row,
                fixed((rows, HEAD_SIZE)), fixed((rows, HEAD_SIZE)), s["k"], row, s["out"], s["k"],
                s["k"],
            ],
            out_specs=[fixed((rows, SLOTS * HEAD_SIZE)), fixed((2, HEAD_SIZE))],
            scratch_shapes=[pltpu.VMEM((rows, HEAD_SIZE), F32)] * 2,
        ),
        out_shape=[shaped((rows, SLOTS * HEAD_SIZE), BF16), shaped((2, HEAD_SIZE), F32)],
        **params("attend_back_other", 14_000_000_000),
    )(
        info, q, k, v, k_turned, start, logs, out, grad_out, raw_q, cos, sin, gain_q,
        cos, sin, raw_k, gain_k, grad_q, grad_k, grad_v,
    )


def two_parts(rows, width):
    steps = rows // BLOCK // 2
    return (
        [
            pl.BlockSpec((BLOCK, width), lambda i: (jnp.minimum(i, steps - 1), 0)),
            pl.BlockSpec((BLOCK, width), lambda i: (jnp.maximum(i - steps, 0), 0)),
        ],
        [shaped((rows // 2, width), BF16)] * 2,
    )


def feed(h, grad, gate_up, down):
    rows, width = h.shape
    by_rows = lambda n: pl.BlockSpec((BLOCK, n), lambda i: (i, 0))
    specs, shapes = two_parts(rows, width)
    return pl.pallas_call(
        feed_kernel,
        grid=(rows // BLOCK,),
        in_specs=[by_rows(width), by_rows(width), fixed(gate_up.shape), fixed(down.shape)],
        out_specs=[by_rows(down.shape[0]), by_rows(gate_up.shape[1]), *specs, *specs],
        out_shape=[
            shaped((rows, down.shape[0]), BF16), shaped((rows, gate_up.shape[1]), BF16),
            *shapes, *shapes,
        ],
        **params("feed", 16_000_000_000),
    )(h, grad, gate_up, down)


def unproject(half, grad_zero, grad_one, matrix):
    rows, width = grad_zero.shape
    n = rows // 2
    steps = n // BLOCK
    by_rows = pl.BlockSpec((BLOCK, width), lambda i: (i + half * steps, 0))
    specs, shapes = two_parts(n, matrix.shape[0])
    return pl.pallas_call(
        unproject_kernel,
        grid=(steps,),
        in_specs=[by_rows, by_rows, fixed(matrix.shape)],
        out_specs=specs,
        out_shape=shapes,
        **params("unproject", 4_000_000_000),
    )(grad_zero, grad_one, matrix)


def flipped(value, axis, bit):
    return lax.ppermute(value, axis, [(i, i ^ bit) for i in range(lax.axis_size(axis))])


def together(*values):
    return lax.optimization_barrier(values)


def near_sum(part, beside):
    return part.astype(F32) + flipped(beside, "tensor", 1).astype(F32)


def ring_gather(value):
    n = lax.axis_size("dp")
    if n != len(RING):
        return lax.all_gather(value, "dp", axis=0, tiled=False)
    ring = jnp.array(RING, jnp.int32)
    at = jnp.argmax(ring == lax.axis_index("dp")).astype(jnp.int32)
    after = [(RING[i], RING[(i + 1) % n]) for i in range(n)]
    before = [(b, a) for a, b in after]
    pieces = {0: value}
    up = down = value
    for step in range(1, n // 2 + 1):
        up = lax.ppermute(up, "dp", after)
        pieces[-step] = up
        if step < n // 2:
            down = lax.ppermute(down, "dp", before)
            pieces[step] = down
    full = jnp.zeros((n,) + value.shape, value.dtype)
    for step, piece in pieces.items():
        full = lax.dynamic_update_index_in_dim(full, piece, ring[(at + step + n) % n], 0)
    return full


def exchanged_sum(parts, axis):
    n = lax.axis_size("dp")
    low = parts.astype(BF16)
    if n != len(RING):
        return jnp.squeeze(
            lax.psum_scatter(low, "dp", scatter_dimension=axis, tiled=True), axis
        ).astype(F32)
    me = lax.axis_index("dp")
    take = lambda a, i: lax.dynamic_index_in_dim(a, i, axis, keepdims=False)
    total = take(parts, me).astype(F32)
    for bit in range(1, n):
        total = total + flipped(take(low, me ^ bit), "dp", bit).astype(F32)
    return total


def per_device(
    tokens, cotangent, lengths,
    projection_weight, w_out, w_gate_up, w_down, gains,
    first_moment_projection, first_out, first_gate_up, first_down, first_gains,
    second_moment_projection, second_out, second_gate_up, second_down, second_gains,
):
    shards = lax.axis_size("tensor")
    spread = lax.axis_size("dp")
    me = lax.axis_index("tensor")
    local_rows = tokens.shape[0]
    rows = local_rows * shards
    blocks = rows // BLOCK
    kv_local = projection_weight.shape[1]
    hidden_local = w_gate_up.shape[2]
    out_heads, out_depth = w_out.shape[0], w_out.shape[1]
    down_blocks, down_depth = w_down.shape[0], w_down.shape[1]
    depth = projection_weight.shape[0]
    gain_count = gains.shape[0]

    full_one = ring_gather(
        jnp.concatenate(
            [
                projection_weight.astype(BF16).reshape(depth, -1),
                jnp.pad(gains.astype(BF16)[None, :], ((0, 15), (0, MODEL_WIDTH - gain_count))),
            ],
            axis=0,
        )
    )
    half = MODEL_WIDTH // 2
    pieces = 2 * hidden_local // half
    out_rows, gate_rows = 2 * out_heads * out_depth, pieces * depth
    fold = lambda value: value.reshape(-1, 2, half).swapaxes(0, 1).reshape(-1, half)
    full_two = lax.all_gather(
        jnp.concatenate(
            [
                fold(w_out.astype(BF16)),
                w_gate_up.astype(BF16).reshape(depth, pieces, half).swapaxes(0, 1).reshape(-1, half),
                fold(w_down.astype(BF16)),
            ],
            axis=0,
        ),
        "dp", axis=0, tiled=False,
    )
    unfold = lambda value, count, deep: (
        value.reshape(spread, 2, count, deep, half).transpose(2, 0, 3, 1, 4).reshape(-1, MODEL_WIDTH)
    )
    qkv_matrix = full_one[:, :depth].reshape(MODEL_WIDTH, -1)
    gains_all = full_one[:, depth, :gain_count].reshape(-1).astype(F32)
    out_matrix = unfold(full_two[:, :out_rows], out_heads, out_depth)
    gate_up_matrix = (
        full_two[:, out_rows : out_rows + gate_rows]
        .reshape(spread, pieces, depth, half)
        .swapaxes(1, 2)
        .reshape(MODEL_WIDTH, -1)
    )
    down_matrix = unfold(full_two[:, out_rows + gate_rows :], down_blocks, down_depth)
    gain_attn = gains_all[None, :MODEL_WIDTH]
    gain_mlp = gains_all[MODEL_WIDTH : 2 * MODEL_WIDTH]
    gain_query = gains_all[None, 2 * MODEL_WIDTH : 2 * MODEL_WIDTH + HEAD_SIZE]
    gain_key = gains_all[None, 2 * MODEL_WIDTH + HEAD_SIZE :]

    doc_ends = jnp.cumsum(lengths[0])
    doc_starts = doc_ends - lengths[0]

    def start_of(index):
        return jnp.max(
            jnp.where(index[:, None] >= doc_starts[None, :], doc_starts[None, :], 0), axis=1
        )

    order = me ^ jnp.arange(shards, dtype=jnp.int32)
    index_of_row = (
        order[:, None] * local_rows + jnp.arange(local_rows, dtype=jnp.int32)[None, :]
    ).reshape(-1)
    start_of_row = start_of(index_of_row)
    position = index_of_row - start_of_row
    inverse = THETA ** (-2.0 * jnp.arange(HEAD_SIZE // 2, dtype=F32) / HEAD_SIZE)
    turned = position.astype(F32)[:, None] * inverse[None, :]
    cosine, sine = jnp.cos(turned), jnp.sin(turned)
    cos = jnp.concatenate([cosine, cosine], axis=1)
    sin = jnp.concatenate([-sine, sine], axis=1)
    block_starts = start_of(jnp.arange(blocks, dtype=jnp.int32) * BLOCK) // BLOCK
    info = jnp.concatenate([block_starts, (me * (local_rows // BLOCK))[None]]).astype(jnp.int32)
    start = start_of_row[None, :]

    def over_rows(a, b):
        return lax.dot_general(a, b, (((0,), (0,)), ((), ())), preferred_element_type=F32)

    rows_float = tokens.astype(F32)
    tokens_across = flipped(tokens, "tensor", 2)
    tokens_all = jnp.concatenate(
        [tokens, flipped(tokens, "tensor", 1), tokens_across, flipped(tokens_across, "tensor", 1)],
        axis=0,
    )
    normed_one, raw_q, raw_k, q, k, v, k_turned, v_turned = project(
        tokens_all, gain_attn, qkv_matrix, cos, sin, gain_query, gain_key
    )
    heads_other, logs_other = attend(1, info, q, k, v_turned, start)
    beside = nn(heads_other[local_rows:], out_matrix).astype(BF16)
    near = near_sum(nn(heads_other[:local_rows], out_matrix), beside).astype(BF16)
    grad_across = flipped(cotangent, "tensor", 2)
    near, grad_across, q_own = together(near, grad_across, q)
    attn_across = flipped(near, "tensor", 2)
    heads_own, logs_own = attend(0, info, q_own, k, v_turned, start)
    beside = nn(heads_own[local_rows:], out_matrix).astype(BF16)
    attn_rows = near_sum(nn(heads_own[:local_rows], out_matrix), beside) + attn_across.astype(F32)
    middle = rows_float + attn_rows

    grad_own = jnp.concatenate([cotangent, flipped(cotangent, "tensor", 1)], axis=0)
    grad_other = jnp.concatenate([grad_across, flipped(grad_across, "tensor", 1)], axis=0)
    normed_two = norm_rows(middle, gain_mlp).astype(BF16)
    normed_across = flipped(normed_two, "tensor", 2)
    normed_own = jnp.concatenate([normed_two, flipped(normed_two, "tensor", 1)], axis=0)
    hidden_own, feed_grad_own, back_0, back_1, sum_0, sum_1 = feed(
        normed_own, grad_own, gate_up_matrix, down_matrix
    )
    normed_across, back_0, back_1, sum_0, sum_1 = together(
        normed_across, back_0, back_1, sum_0, sum_1
    )
    normed_other = jnp.concatenate([normed_across, flipped(normed_across, "tensor", 1)], axis=0)
    hidden_other, feed_grad_other, back_2, back_3, sum_2, sum_3 = feed(
        normed_other, grad_other, gate_up_matrix, down_matrix
    )
    near = near_sum(back_2, back_3).astype(BF16)
    back_across = flipped(near, "tensor", 2)
    back_near = near_sum(back_0, back_1)

    grad_gate_up_w = (
        over_rows(normed_own, feed_grad_own) + over_rows(normed_other, feed_grad_other)
    ).astype(BF16)
    grad_down = (over_rows(hidden_own, grad_own) + over_rows(hidden_other, grad_other)).astype(BF16)
    back_across, grad_gate_up_w, grad_down = together(back_across, grad_gate_up_w, grad_down)
    feed_sum = lax.psum_scatter(
        jnp.concatenate(
            [
                grad_gate_up_w.reshape(spread, depth, pieces, half)
                .swapaxes(1, 2)
                .reshape(spread, -1, half),
                grad_down.reshape(down_blocks, spread, down_depth, 2, half)
                .transpose(1, 3, 0, 2, 4)
                .reshape(spread, -1, half),
            ],
            axis=1,
        ),
        "dp", scatter_dimension=0, tiled=True,
    )[0].astype(F32)
    sum_gate_up = (
        feed_sum[:gate_rows].reshape(pieces, depth, half).swapaxes(0, 1).reshape(w_gate_up.shape)
    )
    sum_down = (
        feed_sum[gate_rows:].reshape(2, -1, half).swapaxes(0, 1).reshape(w_down.shape)
    )

    grad_middle_part, grad_gain_mlp = norm_back(
        middle, gain_mlp, back_near + back_across.astype(F32)
    )
    grad_middle = cotangent.astype(F32) + grad_middle_part
    grad_middle_low = grad_middle.astype(BF16)
    grad_middle_across = flipped(grad_middle_low, "tensor", 2)

    grad_middle_own = jnp.concatenate(
        [grad_middle_low, flipped(grad_middle_low, "tensor", 1)], axis=0
    )
    grad_heads_own = nt(grad_middle_own, out_matrix).astype(BF16)
    grad_q, grad_k, grad_v, gain_own = attend_back_own(
        info, q, k, v, k_turned, start, logs_own, heads_own, grad_heads_own, raw_q, cos, sin,
        gain_query,
    )
    grad_middle_across, grad_q, sum_2, sum_3 = together(grad_middle_across, grad_q, sum_2, sum_3)
    mlp_across = flipped(near_sum(sum_2, sum_3).astype(BF16), "tensor", 2)
    grad_middle_other = jnp.concatenate(
        [grad_middle_across, flipped(grad_middle_across, "tensor", 1)], axis=0
    )
    grad_heads_other = nt(grad_middle_other, out_matrix).astype(BF16)
    grad_out_w = over_rows(heads_own, grad_middle_own) + over_rows(heads_other, grad_middle_other)
    sum_out = exchanged_sum(grad_out_w.reshape(out_heads, spread, out_depth, MODEL_WIDTH), 1)

    grad_qkv, grad_qkv_w, sum_qkv, gain_other = [], [], [], []
    for head in range(kv_local):
        one, gain_parts = attend_back_other(
            head, info, q, k, v, k_turned, start, logs_other, heads_other, grad_heads_other,
            raw_q, cos, sin, gain_query, raw_k, gain_key, grad_q, grad_k, grad_v,
        )
        product = over_rows(normed_one, one)
        grad_qkv.append(one)
        grad_qkv_w.append(product)
        gain_other.append(gain_parts)
        sum_qkv.append(exchanged_sum(product.reshape(spread, depth, -1), 0))
        if head + 1 < kv_local:
            grad_heads_other, _ = together(grad_heads_other, product)
    back_2, back_3 = unproject(1, *grad_qkv, qkv_matrix)
    back_0, back_1 = unproject(0, *grad_qkv, qkv_matrix)
    near = near_sum(back_2, back_3).astype(BF16)
    back_across = flipped(near, "tensor", 2)
    grad_normed_one = near_sum(back_0, back_1) + back_across.astype(F32)
    grad_rows_part, _ = norm_back(rows_float, gain_attn, grad_normed_one)
    grad_tokens = grad_middle + grad_rows_part
    mlp_rows = near_sum(sum_0, sum_1) + mlp_across.astype(F32)
    block_out = (middle + mlp_rows).astype(BF16)

    width = SLOTS * HEAD_SIZE
    grad_gain_attn = sum(
        jnp.sum(qkv_matrix[:, i * width : (i + 1) * width].astype(F32) * product, axis=1)
        for i, product in enumerate(grad_qkv_w)
    ) / gain_attn[0]
    grad_gain_heads = sum(gain_other) + jnp.pad(jnp.sum(gain_own, axis=0), ((0, 1), (0, 0)))
    gain_sums = jnp.concatenate([grad_gain_attn, grad_gain_mlp, grad_gain_heads.reshape(-1)])
    gain_sums, _ = together(gain_sums, near)
    gain_sums = gain_sums + sum(flipped(gain_sums, "tensor", bit) for bit in range(1, shards))
    if spread == len(RING):
        me_dp = lax.axis_index("dp")
        parts = gain_sums.reshape(spread, gain_count)
        take = lambda i: lax.dynamic_index_in_dim(parts, i, 0, keepdims=False)
        sum_gains = take(me_dp) + sum(
            flipped(take(me_dp ^ bit), "dp", bit) for bit in range(1, spread)
        )
    else:
        sum_gains = lax.psum_scatter(gain_sums, "dp", scatter_dimension=0, tiled=True)

    upd_qkv = adamw_update(
        projection_weight, first_moment_projection, second_moment_projection,
        jnp.stack(sum_qkv, axis=1), 2.0 * MODEL_WIDTH ** (-0.5), DECAY,
    )
    upd_out = adamw_update(
        w_out, first_out, second_out, sum_out,
        2.0 * (QUERY_HEADS * HEAD_SIZE // 64) ** (-0.5), DECAY,
    )
    upd_gate_up = adamw_update(
        w_gate_up, first_gate_up, second_gate_up, sum_gate_up,
        2.0 * MODEL_WIDTH ** (-0.5), DECAY,
    )
    upd_down = adamw_update(w_down, first_down, second_down, sum_down, 2.0 * FF ** (-0.5), DECAY)
    upd_gains = adamw_update(gains, first_gains, second_gains, sum_gains, 0.5, 0.0)
    updates = (upd_qkv, upd_out, upd_gate_up, upd_down, upd_gains)
    return (
        block_out,
        grad_tokens,
        *(update[2] for update in updates),
        *(update[0] for update in updates),
        *(update[1] for update in updates),
    )


def solution(mesh):
    weights = (
        P("dp", "tensor", None),
        P("tensor", "dp", None),
        P("dp", None, "tensor"),
        P("tensor", "dp", None),
        P("dp"),
    )
    batch = P(("dp", "tensor"), None)
    return jax.shard_map(
        per_device,
        mesh=mesh,
        in_specs=(batch, batch, P("dp", None), *weights, *weights, *weights),
        out_specs=(batch, batch, *weights, *weights, *weights),
        check_vma=False,
    )
```

time: 568 us -> 594 us (1.046)
  waiting for transfers between devices: 235 us -> 155 us
  starting transfers between devices: 32.4 us -> 105 us
  matrix products: 101 us -> 34.2 us
  Pallas kernels: 86 us -> 137 us
  local copies, waits for them, and re-layouts: 47.6 us -> 75 us
  between operations: 15.2 us -> 36.5 us
    ppermute x29 -> x55, starting transfers between devices: 31.9 us -> 90.2 us  [flipped(): lax.ppermute(value, axis, [(i, i ^ bit) for i in range(lax.axis_size(axis...]
    ppermute x29 -> x55, waiting for transfers between devices: 172 us -> 121 us  [flipped(): lax.ppermute(value, axis, [(i, i ^ bit) for i in range(lax.axis_size(axis...]
    pallas_call x2 -> x10, Pallas kernels: 86 us -> 137 us  [the longest x2 32.2 us: feed(): pl.pallas_call(feed_kernel, grid=(rows // BLOCK,), in_specs=[by_rows(widt...]
    ppermute x0 -> x7, waiting for transfers between devices: none -> 33.8 us  [the longest x4 33.4 us: ring_gather(): up = lax.ppermute(up, 'dp', after)]
    dot_general x4 -> x2, matrix products: 35 us -> 3.58 us  [nt(): lax.dot_general(a, b, (((1,), (1,)), ((), ())), preferred_element_type=F32)]
    all_gather x2 -> x1, waiting for transfers between devices: 31.3 us -> 0.01 us  [per_device(): lax.all_gather(jnp.concatenate([fold(w_out.astype(BF16)), w_gate_up.astyp...]
    unnamed x7 -> x2, waiting for transfers between devices: 31.1 us -> 0.03 us
    dot_general x4, matrix products: 32.2 us -> 2.95 us  [nn(): return jnp.dot(a, b, preferred_element_type=F32)]
  transfers between devices with their start and end apart: 35 -> 64, of which waited for: 15 -> 20; matrix products, arithmetic and copies ran while one was open for 25% -> 20% of each run, Pallas kernels for 15% -> 21%
where the time goes in v2:
time: 594 us; the launch traced here: 587 us
  waiting for transfers between devices  155 us (26%)
  Pallas kernels  137 us (23%)
  starting transfers between devices  105 us (18%)
  local copies, waits for them, and re-layouts  75 us (13%)
  other arithmetic  44.8 us (8%)
  between operations  36.5 us (6%)
  matrix products  34.2 us (6%)
    ppermute x55, waiting for transfers between devices, flipped(): lax.ppermute(value, axis, [(i, i ^ bit) for i in range(lax.axis_size(axis...  121 us
    ppermute x55, starting transfers between devices, flipped(): lax.ppermute(value, axis, [(i, i ^ bit) for i in range(lax.axis_size(axis...  90.2 us
    unnamed x191, local copies, waits for them, and re-layouts  39.4 us
    ppermute x4, waiting for transfers between devices, ring_gather(): up = lax.ppermute(up, 'dp', after)  33.4 us
    pallas_call x2, Pallas kernels, feed(): pl.pallas_call(feed_kernel, grid=(rows // BLOCK,), in_specs=[by_rows(widt...  32.2 us
    pallas_call x2, Pallas kernels, attend_back_other(): pl.pallas_call(back_other_kernel, grid_spec=pltpu.PrefetchScalarGridSpec(...  31.1 us
    dot_general x8, matrix products, over_rows(): lax.dot_general(a, b, (((0,), (0,)), ((), ())), preferred_element_type=F32)  27.6 us
    pallas_call x2, Pallas kernels, attend(): pl.pallas_call(lambda *refs: attend_kernel(half * n // BLOCK, *refs), gri...  26.7 us
  transfers between devices with their start and end apart: 64, of which 20 were waited for; matrix products, arithmetic and copies ran while one was open for 20% of the time, Pallas kernels for 21%

profile of v2, /device:TPU:0, one launch (start us, length us, event | category | flops | bytes accessed | tf_op | source)
XLA Modules:
  0.0 587.1 jit_solution(5574496279705359691)
XLA Ops:
  48.4 5.6 collective-permute-done.5
  56.1 13.3 %collective-permute-done.7 = bf16[144,1024]{1,0:T(8,128)(2,1)S(1)} collective-permute-done((bf16[144,1024]{1,0:T(8,128)(2,1)S(1)}, bf16[144,1024]{1,0:T(8,128)(2,1)S(1)}, u32[]{:S(2)}, u32[]{:S(2)}) %collective-permute-start.7) | collective-permute-done | bytes 294944 | tf_op jit(solution)/shard_map/ppermute | solution.py:484
  69.4 7.7 %collective-permute-start.9 = (bf16[144,1024]{1,0:T(8,128)(2,1)S(1)}, bf16[144,1024]{1,0:T(8,128)(2,1)S(1)}, u32[]{:S(2)}, u32[]{:S(2)}) collective-permute-start(bf16[144,1024]{1,0:T(8,128)(2,1)S(1)} %collective-permute-done.7), channel_id=1, source_target_pairs={{0,8},{8,16},{16,24},{24,28},{28,20},{20,12},{12,4},{4,0},{1,9},{9... | collective-permute-start | bytes 884744 | tf_op jit(solution)/shard_map/ppermute | solution.py:484
  77.6 14.5 %collective-permute-done.9 = bf16[144,1024]{1,0:T(8,128)(2,1)S(1)} collective-permute-done((bf16[144,1024]{1,0:T(8,128)(2,1)S(1)}, bf16[144,1024]{1,0:T(8,128)(2,1)S(1)}, u32[]{:S(2)}, u32[]{:S(2)}) %collective-permute-start.9) | collective-permute-done | bytes 294944 | tf_op jit(solution)/shard_map/ppermute | solution.py:484
  97.3 13.9 %project.1 = (bf16[2048,1024]{1,0:T(8,128)(2,1)}, f32[2048,512]{1,0:T(8,128)}, f32[2048,256]{1,0:T(8,128)}, bf16[2048,512]{1,0:T(8,128)(2,1)}, bf16[2048,256]{1,...) custom-call(bf16[2048,1024]{1,0:T(8,128)(2,1)} %pad_maximum_fusion.1, ...), custom_call_target="tpu_custom_call" | custom-call | flops 10000000000 | bytes 8000000 | tf_op jit(solution)/shard_map/project/pallas_call | solution.py:310
  114.5 12.1 %attend.2 = (bf16[1024,512]{1,0:T(8,128)(2,1)S(1)}, f32[2,2,1024]{2,1,0:T(2,128)S(1)}) custom-call(s32[9]{0:T(128)S(1)} %pad_add_fusion.refs_0_.info, bf16[2048,512]{1,0:T(8,128)(2,1)S(1)} %copy-done.10, bf16[2048,256]{1,0:T(8,128)(2,1)S(1)} %get-tuple-element.73.refs_2_.k, bf16[256,2048]{1,0:T(8,128)(2,1)S(1)} %get-tuple-element.74.refs_3_, ...), custom_call_target="tpu_custom_call" | custom-call | flops 17999998976 | bytes 8000000 | tf_op jit(solution)/shard_map/attend/pallas_call | solution.py:349
  135.6 23.0 %collective-permute-done.11 = bf16[512,1024]{1,0:T(8,128)(2,1)} collective-permute-done((bf16[512,1024]{1,0:T(8,128)(2,1)S(1)}, bf16[512,1024]{1,0:T(8,128)(2,1)}, u32[]{:S(2)}, u32[]{:S(2)}) %collective-permute-start.11) | collective-permute-done | bytes 1048608 | tf_op jit(solution)/shard_map/ppermute | solution.py:462
  158.5 14.7 %attend.3 = (bf16[1024,512]{1,0:T(8,128)(2,1)S(1)}, f32[2,2,1024]{2,1,0:T(2,128)S(1)}) custom-call(s32[9]{0:T(128)S(1)} %pad_add_fusion.refs_0_.info, bf16[2048,512]{1,0:T(8,128)(2,1)S(1)} %copy-done.11, bf16[2048,256]{1,0:T(8,128)(2,1)S(1)} %get-tuple-element.73.refs_2_.k, bf16[256,2048]{1,0:T(8,128)(2,1)S(1)} %copy-done.22, s32[1,2048]{1,0:T(1,128)S(1)} %bitcast.204), custom_call_target="tpu_custom_call" | custom-call | flops 17999998976 | bytes 8000000 | tf_op jit(solution)/shard_map/attend/pallas_call | solution.py:349
  176.7 22.9 %collective-permute-done.13 = bf16[512,1024]{1,0:T(8,128)(2,1)S(1)} collective-permute-done((bf16[512,1024]{1,0:T(8,128)(2,1)S(1)}, bf16[512,1024]{1,0:T(8,128)(2,1)S(1)}, u32[]{:S(2)}, u32[]{:S(2)}) %collective-permute-start.13) | collective-permute-done | bytes 1048608 | tf_op jit(solution)/shard_map/ppermute | solution.py:462
  213.4 16.2 %feed.2 = (bf16[1024,768]{1,0:T(8,128)(2,1)S(1)}, bf16[1024,1536]{1,0:T(8,128)(2,1)}, bf16[512,1024]{1,0:T(8,128)(2,1)S(1)}, bf16[512,1024]{1,0:T(8,128)(2,1)S(1...) custom-call(bf16[1024,1024]{1,0:T(8,128)(2,1)} %pad_maximum_fusion.2.h, bf16[1024,1024]{1,0:T(8,128)(2,1)} %copy-done.61, ...), custom_call_target="tpu_custom_call" | custom-call | flops 16000000000 | bytes 8000000 | tf_op jit(solution)/shard_map/feed/pallas_call | solution.py:432
  229.6 7.2 %collective-permute-done.14 = bf16[512,1024]{1,0:T(8,128)(2,1)S(1)} collective-permute-done((bf16[512,1024]{1,0:T(8,128)(2,1)S(1)}, bf16[512,1024]{1,0:T(8,128)(2,1)S(1)}, u32[]{:S(2)}, u32[]{:S(2)}) %collective-permute-start.14) | collective-permute-done | bytes 1048608 | tf_op jit(solution)/shard_map/ppermute | solution.py:462
  241.1 16.0 %feed.3 = (bf16[1024,768]{1,0:T(8,128)(2,1)S(1)}, bf16[1024,1536]{1,0:T(8,128)(2,1)}, bf16[512,1024]{1,0:T(8,128)(2,1)S(1)}, bf16[512,1024]{1,0:T(8,128)(2,1)S(1...) custom-call(bf16[1024,1024]{1,0:T(8,128)(2,1)} %constant_dynamic-update-slice_fusion.2.h, ...), custom_call_target="tpu_custom_call" | custom-call | flops 16000000000 | bytes 8000000 | tf_op jit(solution)/shard_map/feed/pallas_call | solution.py:432
  261.2 5.2 fusion.62
  271.1 5.4 add_convert_fusion
  276.6 15.7 %collective-permute-done.22 = bf16[512,1024]{1,0:T(8,128)(2,1)S(1)} collective-permute-done((bf16[512,1024]{1,0:T(8,128)(2,1)S(1)}, bf16[512,1024]{1,0:T(8,128)(2,1)S(1)}, u32[]{:S(2)}, u32[]{:S(2)}) %collective-permute-start.22) | collective-permute-done | bytes 1048608 | tf_op jit(solution)/shard_map/ppermute | solution.py:462
  301.9 22.5 %attend_back_own.1 = (bf16[1024,512]{1,0:T(8,128)(2,1)S(1)}, f32[2048,256]{1,0:T(8,128)}, f32[2048,256]{1,0:T(8,128)}, f32[2,1,128]{2,1,0:T(1,128)S(1)}) custom-call(s32[9]{0:T(128)S(1)} %pad_add_fusion.refs_0_.info, bf16[2048,512]{1,0:T(8,128)(2,1)} %get-tuple-element.76.refs_1_.q, bf16[2048,256]{1,0:T(8,128)(2,1)S(1)} %copy-done.13, ...), custom_call_target="tpu_custom_call" | custom-call | flops 24999999488 | bytes 8000000 | tf_op jit(solution)/shard_map/attend_back_own/pallas_call | solution.py:366
  330.1 4.7 copy.103
  334.8 4.4 copy.124
  339.1 5.0 copy.104
  357.6 15.4 %attend_back_other.2 = (bf16[2048,512]{1,0:T(8,128)(2,1)}, f32[2,128]{1,0:T(2,128)S(1)}) custom-call(s32[9]{0:T(128)S(1)} %pad_add_fusion.refs_0_.info, bf16[2048,512]{1,0:T(8,128)(2,1)} %get-tuple-element.76.refs_1_.q, bf16[2048,256]{1,0:T(8,128)(2,1)S(1)} %copy-done.14, bf16[2048,256]{1,0:T(8,128)(2,1)S(1)} %copy-done.17, ...), custom_call_target="tpu_custom_call" | custom-call | flops 14000000000 | bytes 8000000 | tf_op jit(solution)/shard_map/attend_back_other/pallas_call | solution.py:395
  373.0 5.2 fusion.64
  378.3 15.7 %attend_back_other.3 = (bf16[2048,512]{1,0:T(8,128)(2,1)}, f32[2,128]{1,0:T(2,128)S(1)}) custom-call(s32[9]{0:T(128)S(1)} %pad_add_fusion.refs_0_.info, bf16[2048,512]{1,0:T(8,128)(2,1)} %get-tuple-element.76.refs_1_.q, bf16[2048,256]{1,0:T(8,128)(2,1)S(1)} %copy-done.14, bf16[2048,256]{1,0:T(8,128)(2,1)S(1)} %copy-done.17, ...), custom_call_target="tpu_custom_call" | custom-call | flops 14000000000 | bytes 8000000 | tf_op jit(solution)/shard_map/attend_back_other/pallas_call | solution.py:395
  394.0 5.1 unproject.3
  400.6 23.3 %collective-permute-start.31 = (bf16[128,512]{1,0:T(8,128)(2,1)}, bf16[128,512]{1,0:T(8,128)(2,1)}, u32[]{:S(2)}, u32[]{:S(2)}) collective-permute-start(bf16[128,512]{1,0:T(8,128)(2,1)} %get-tuple-element.216), channel_id=1, source_target_pairs={{0,4},{4,0},{8,12},{12,8},{16,20},{20,16},{24,28},{28,24},{1,5},{5... | collective-permute-start | bytes 393224 | tf_op jit(solution)/shard_map/ppermute | solution.py:462
  436.2 5.4 unproject.2
  450.2 16.1 %collective-permute-done.34 = bf16[128,512]{1,0:T(8,128)(2,1)S(1)} collective-permute-done((bf16[128,512]{1,0:T(8,128)(2,1)S(1)}, bf16[128,512]{1,0:T(8,128)(2,1)S(1)}, u32[]{:S(2)}, u32[]{:S(2)}) %collective-permute-start.34) | collective-permute-done | bytes 131104 | tf_op jit(solution)/shard_map/ppermute | solution.py:462
  468.6 8.0 %collective-permute-done.35 = bf16[128,512]{1,0:T(8,128)(2,1)S(1)} collective-permute-done((bf16[128,512]{1,0:T(8,128)(2,1)S(1)}, bf16[128,512]{1,0:T(8,128)(2,1)S(1)}, u32[]{:S(2)}, u32[]{:S(2)}) %collective-permute-start.35) | collective-permute-done | bytes 131104 | tf_op jit(solution)/shard_map/ppermute | solution.py:462
  476.6 7.0 %collective-permute-start.39 = (bf16[128,512]{1,0:T(8,128)(2,1)S(1)}, bf16[128,512]{1,0:T(8,128)(2,1)S(1)}, u32[]{:S(2)}, u32[]{:S(2)}) collective-permute-start(bf16[128,512]{1,0:T(8,128)(2,1)S(1)} %get-tuple-element.229), channel_id=1, source_target_pairs={{0,8},{4,12},{8,0},{12,4},{16,24},{20,28},{24,16},{28,20},{1,9},{5... | collective-permute-start | bytes 393224 | tf_op jit(solution)/shard_map/ppermute | solution.py:462
  483.6 4.7 collective-permute-start.40
  501.8 4.9 collective-permute-done.41
  512.9 6.0 %collective-permute-start.47 = (bf16[4,16,1024]{2,1,0:T(8,128)(2,1)}, bf16[4,16,1024]{2,1,0:T(8,128)(2,1)}, u32[]{:S(2)}, u32[]{:S(2)}) collective-permute-start(bf16[4,16,1024]{2,1,0:T(8,128)(2,1)} %get-tuple-element.214), channel_id=1, source_target_pairs={{0,12},{4,8},{8,4},{12,0},{16,28},{20,24},{24,20},{28,16},{1,13},{... | collective-permute-start | bytes 393224 | tf_op jit(solution)/shard_map/ppermute | solution.py:462
  528.0 9.0 %collective-permute-done.48 = bf16[4,16,1024]{2,1,0:T(8,128)(2,1)} collective-permute-done((bf16[4,16,1024]{2,1,0:T(8,128)(2,1)}, bf16[4,16,1024]{2,1,0:T(8,128)(2,1)}, u32[]{:S(2)}, u32[]{:S(2)}) %collective-permute-start.48) | collective-permute-done | bytes 131104 | tf_op jit(solution)/shard_map/ppermute | solution.py:462
  (412 shorter events, 195.0 us)
Async XLA Ops:
  7.2 120.4 %all-gather.3.cloned.1.call-start = ((), (), s32[]{:S(2)}) async-start(), calls=%async_computation.2 | async-start | bytes 6488064 | tf_op jit(solution)/shard_map/all_gather | solution.py:542
  10.5 557.8 %reduce-scatter.2.cloned.1.call-start = ((), (), s32[]{:S(2)}) async-start(), calls=%async_computation.1 | async-start | bytes 5308416 | tf_op jit(solution)/shard_map/reduce_scatter | solution.py:641
  10.8 33.6 %collective-permute-start.3 = (bf16[144,1024]{1,0:T(8,128)(2,1)S(1)}, bf16[144,1024]{1,0:T(8,128)(2,1)}, u32[]{:S(2)}, u32[]{:S(2)}) collective-permute-start(bf16[144,1024]{1,0:T(8,128)(2,1)S(1)} %fusion.19), channel_id=1, source_target_pairs={{0,8},{8,16},{16,24},{24,28},{28,20},{20,12},{12,4},{4,0},{1,9},{9... | collective-permute-start | bytes 884744 | tf_op jit(solution)/shard_map/ppermute | solution.py:484
  13.9 32.1 %collective-permute-start.4 = (bf16[144,1024]{1,0:T(8,128)(2,1)S(1)}, bf16[144,1024]{1,0:T(8,128)(2,1)}, u32[]{:S(2)}, u32[]{:S(2)}) collective-permute-start(bf16[144,1024]{1,0:T(8,128)(2,1)S(1)} %fusion.19), channel_id=1, source_target_pairs={{8,0},{16,8},{24,16},{28,24},{20,28},{12,20},{4,12},{0,4},{9,1},{1... | collective-permute-start | bytes 884744 | tf_op jit(solution)/shard_map/ppermute | solution.py:487
  13.9 63.1 %collective-permute-start.1 = (bf16[512,1024]{1,0:T(8,128)(2,1)S(1)}, bf16[512,1024]{1,0:T(8,128)(2,1)S(1)}, u32[]{:S(2)}, u32[]{:S(2)}) collective-permute-start(bf16[512,1024]{1,0:T(8,128)(2,1)S(1)} %copy-done.26), channel_id=1, source_target_pairs={{0,2},{1,3},{2,0},{3,1},{4,6},{5,7},{6,4},{7,5},{8,10},{9,11},{10,... | collective-permute-start | bytes 3145736 | tf_op jit(solution)/shard_map/ppermute | solution.py:462
  15.9 77.9 %collective-permute-start = (bf16[512,1024]{1,0:T(8,128)(2,1)S(1)}, bf16[512,1024]{1,0:T(8,128)(2,1)}, u32[]{:S(2)}, u32[]{:S(2)}) collective-permute-start(bf16[512,1024]{1,0:T(8,128)(2,1)S(1)} %copy-done.26), channel_id=1, source_target_pairs={{0,1},{1,0},{2,3},{3,2},{4,5},{5,4},{6,7},{7,6},{8,9},{9,8},{10,11... | collective-permute-start | bytes 3145736 | tf_op jit(solution)/shard_map/ppermute | solution.py:462
  55.6 21.9 %collective-permute-start.8 = (bf16[144,1024]{1,0:T(8,128)(2,1)S(1)}, bf16[144,1024]{1,0:T(8,128)(2,1)S(1)}, u32[]{:S(2)}, u32[]{:S(2)}) collective-permute-start(bf16[144,1024]{1,0:T(8,128)(2,1)S(1)} %collective-permute-done.6), channel_id=1, source_target_pairs={{8,0},{16,8},{24,16},{28,24},{20,28},{12,20},{4,12},{0,4},{9,1},{1... | collective-permute-start | bytes 884744 | tf_op jit(solution)/shard_map/ppermute | solution.py:487
  69.4 22.7 %collective-permute-start.9 = (bf16[144,1024]{1,0:T(8,128)(2,1)S(1)}, bf16[144,1024]{1,0:T(8,128)(2,1)S(1)}, u32[]{:S(2)}, u32[]{:S(2)}) collective-permute-start(bf16[144,1024]{1,0:T(8,128)(2,1)S(1)} %collective-permute-done.7), channel_id=1, source_target_pairs={{0,8},{8,16},{16,24},{24,28},{28,20},{20,12},{12,4},{4,0},{1,9},{9... | collective-permute-start | bytes 884744 | tf_op jit(solution)/shard_map/ppermute | solution.py:484
  131.3 27.2 %collective-permute-start.11 = (bf16[512,1024]{1,0:T(8,128)(2,1)S(1)}, bf16[512,1024]{1,0:T(8,128)(2,1)}, u32[]{:S(2)}, u32[]{:S(2)}) collective-permute-start(bf16[512,1024]{1,0:T(8,128)(2,1)S(1)} %copy-done.37), channel_id=1, source_target_pairs={{0,2},{1,3},{2,0},{3,1},{4,6},{5,7},{6,4},{7,5},{8,10},{9,11},{10,... | collective-permute-start | bytes 3145736 | tf_op jit(solution)/shard_map/ppermute | solution.py:462
  174.1 25.6 %collective-permute-start.13 = (bf16[512,1024]{1,0:T(8,128)(2,1)S(1)}, bf16[512,1024]{1,0:T(8,128)(2,1)S(1)}, u32[]{:S(2)}, u32[]{:S(2)}) collective-permute-start(bf16[512,1024]{1,0:T(8,128)(2,1)S(1)} %add_convert_fusion.6), channel_id=1, source_target_pairs={{0,2},{1,3},{2,0},{3,1},{4,6},{5,7},{6,4},{7,5},{8,10},{9,11},{10,... | collective-permute-start | bytes 3145736 | tf_op jit(solution)/shard_map/ppermute | solution.py:462
  174.2 26.6 %collective-permute-start.16 = (bf16[512,1024]{1,0:T(8,128)(2,1)S(1)}, bf16[512,1024]{1,0:T(8,128)(2,1)S(1)}, u32[]{:S(2)}, u32[]{:S(2)}) collective-permute-start(bf16[512,1024]{1,0:T(8,128)(2,1)S(1)} %copy-done.37), channel_id=1, source_target_pairs={{0,1},{1,0},{2,3},{3,2},{4,5},{5,4},{6,7},{7,6},{8,9},{9,8},{10,11... | collective-permute-start | bytes 3145736 | tf_op jit(solution)/shard_map/ppermute | solution.py:462
  211.3 26.9 %collective-permute-start.20 = (bf16[512,1024]{1,0:T(8,128)(2,1)}, bf16[512,1024]{1,0:T(8,128)(2,1)S(1)}, u32[]{:S(2)}, u32[]{:S(2)}) collective-permute-start(bf16[512,1024]{1,0:T(8,128)(2,1)} %collective-permute-done.11), channel_id=1, source_target_pairs={{0,1},{1,0},{2,3},{3,2},{4,5},{5,4},{6,7},{7,6},{8,9},{9,8},{10,11... | collective-permute-start | bytes 3145736 | tf_op jit(solution)/shard_map/ppermute | solution.py:462
  211.5 25.4 %collective-permute-start.14 = (bf16[512,1024]{1,0:T(8,128)(2,1)S(1)}, bf16[512,1024]{1,0:T(8,128)(2,1)S(1)}, u32[]{:S(2)}, u32[]{:S(2)}) collective-permute-start(bf16[512,1024]{1,0:T(8,128)(2,1)S(1)} %multiply_convert_fusion), channel_id=1, source_target_pairs={{0,2},{1,3},{2,0},{3,1},{4,6},{5,7},{6,4},{7,5},{8,10},{9,11},{10,... | collective-permute-start | bytes 3145736 | tf_op jit(solution)/shard_map/ppermute | solution.py:462
  238.3 53.9 %collective-permute-start.18 = (bf16[512,1024]{1,0:T(8,128)(2,1)S(1)}, bf16[512,1024]{1,0:T(8,128)(2,1)S(1)}, u32[]{:S(2)}, u32[]{:S(2)}) collective-permute-start(bf16[512,1024]{1,0:T(8,128)(2,1)S(1)} %get-tuple-element.86), channel_id=1, source_target_pairs={{0,1},{1,0},{2,3},{3,2},{4,5},{5,4},{6,7},{7,6},{8,9},{9,8},{10,11... | collective-permute-start | bytes 3145736 | tf_op jit(solution)/shard_map/ppermute | solution.py:462
  266.8 25.4 %collective-permute-start.22 = (bf16[512,1024]{1,0:T(8,128)(2,1)S(1)}, bf16[512,1024]{1,0:T(8,128)(2,1)S(1)}, u32[]{:S(2)}, u32[]{:S(2)}) collective-permute-start(bf16[512,1024]{1,0:T(8,128)(2,1)S(1)} %add_convert_fusion.5), channel_id=1, source_target_pairs={{0,2},{1,3},{2,0},{3,1},{4,6},{5,7},{6,4},{7,5},{8,10},{9,11},{10,... | collective-permute-start | bytes 3145736 | tf_op jit(solution)/shard_map/ppermute | solution.py:462
  297.0 28.4 %collective-permute-start.23 = (bf16[512,1024]{1,0:T(8,128)(2,1)S(1)}, bf16[512,1024]{1,0:T(8,128)(2,1)}, u32[]{:S(2)}, u32[]{:S(2)}) collective-permute-start(bf16[512,1024]{1,0:T(8,128)(2,1)S(1)} %get-tuple-element.205), channel_id=1, source_target_pairs={{0,2},{1,3},{2,0},{3,1},{4,6},{5,7},{6,4},{7,5},{8,10},{9,11},{10,... | collective-permute-start | bytes 3145736 | tf_op jit(solution)/shard_map/ppermute | solution.py:462
  325.4 29.1 %collective-permute-start.27 = (bf16[512,1024]{1,0:T(8,128)(2,1)}, bf16[512,1024]{1,0:T(8,128)(2,1)}, u32[]{:S(2)}, u32[]{:S(2)}) collective-permute-start(bf16[512,1024]{1,0:T(8,128)(2,1)} %collective-permute-done.23), channel_id=1, source_target_pairs={{0,1},{1,0},{2,3},{3,2},{4,5},{5,4},{6,7},{7,6},{8,9},{9,8},{10,11... | collective-permute-start | bytes 3145736 | tf_op jit(solution)/shard_map/ppermute | solution.py:462
  329.7 112.7 %collective-permute-start.17 = (bf16[512,1024]{1,0:T(8,128)(2,1)}, bf16[512,1024]{1,0:T(8,128)(2,1)}, u32[]{:S(2)}, u32[]{:S(2)}) collective-permute-start(bf16[512,1024]{1,0:T(8,128)(2,1)} %copy-done.8), channel_id=1, source_target_pairs={{0,1},{1,0},{2,3},{3,2},{4,5},{5,4},{6,7},{7,6},{8,9},{9,8},{10,11... | collective-permute-start | bytes 3145736 | tf_op jit(solution)/shard_map/ppermute | solution.py:462
  352.9 71.1 %collective-permute-start.25 = (bf16[512,1024]{1,0:T(8,128)(2,1)}, bf16[512,1024]{1,0:T(8,128)(2,1)}, u32[]{:S(2)}, u32[]{:S(2)}) collective-permute-start(bf16[512,1024]{1,0:T(8,128)(2,1)} %copy-done.9), channel_id=1, source_target_pairs={{0,1},{1,0},{2,3},{3,2},{4,5},{5,4},{6,7},{7,6},{8,9},{9,8},{10,11... | collective-permute-start | bytes 3145736 | tf_op jit(solution)/shard_map/ppermute | solution.py:462
  399.1 98.1 %collective-permute-start.29 = (bf16[512,1024]{1,0:T(8,128)(2,1)S(1)}, bf16[512,1024]{1,0:T(8,128)(2,1)}, u32[]{:S(2)}, u32[]{:S(2)}) collective-permute-start(bf16[512,1024]{1,0:T(8,128)(2,1)S(1)} %get-tuple-element.118), channel_id=1, source_target_pairs={{0,1},{1,0},{2,3},{3,2},{4,5},{5,4},{6,7},{7,6},{8,9},{9,8},{10,11... | collective-permute-start | bytes 3145736 | tf_op jit(solution)/shard_map/ppermute | solution.py:462
  400.6 41.9 %collective-permute-start.31 = (bf16[128,512]{1,0:T(8,128)(2,1)}, bf16[128,512]{1,0:T(8,128)(2,1)}, u32[]{:S(2)}, u32[]{:S(2)}) collective-permute-start(bf16[128,512]{1,0:T(8,128)(2,1)} %get-tuple-element.216), channel_id=1, source_target_pairs={{0,4},{4,0},{8,12},{12,8},{16,20},{20,16},{24,28},{28,24},{1,5},{5... | collective-permute-start | bytes 393224 | tf_op jit(solution)/shard_map/ppermute | solution.py:462
  423.9 22.9 %collective-permute-start.32 = (bf16[128,512]{1,0:T(8,128)(2,1)}, bf16[128,512]{1,0:T(8,128)(2,1)}, u32[]{:S(2)}, u32[]{:S(2)}) collective-permute-start(bf16[128,512]{1,0:T(8,128)(2,1)} %get-tuple-element.222), channel_id=1, source_target_pairs={{0,8},{4,12},{8,0},{12,4},{16,24},{20,28},{24,16},{28,20},{1,9},{5... | collective-permute-start | bytes 393224 | tf_op jit(solution)/shard_map/ppermute | solution.py:462
  423.9 22.9 %collective-permute-start.33 = (bf16[128,512]{1,0:T(8,128)(2,1)}, bf16[128,512]{1,0:T(8,128)(2,1)}, u32[]{:S(2)}, u32[]{:S(2)}) collective-permute-start(bf16[128,512]{1,0:T(8,128)(2,1)} %get-tuple-element.221), channel_id=1, source_target_pairs={{0,12},{4,8},{8,4},{12,0},{16,28},{20,24},{24,20},{28,16},{1,13},{... | collective-permute-start | bytes 393224 | tf_op jit(solution)/shard_map/ppermute | solution.py:462
  442.4 23.9 %collective-permute-start.34 = (bf16[128,512]{1,0:T(8,128)(2,1)S(1)}, bf16[128,512]{1,0:T(8,128)(2,1)S(1)}, u32[]{:S(2)}, u32[]{:S(2)}) collective-permute-start(bf16[128,512]{1,0:T(8,128)(2,1)S(1)} %copy-done.73), channel_id=1, source_target_pairs={{0,16},{4,20},{8,24},{12,28},{16,0},{20,4},{24,8},{28,12},{1,17},{... | collective-permute-start | bytes 393224 | tf_op jit(solution)/shard_map/ppermute | solution.py:462
  442.5 34.1 %collective-permute-start.35 = (bf16[128,512]{1,0:T(8,128)(2,1)S(1)}, bf16[128,512]{1,0:T(8,128)(2,1)S(1)}, u32[]{:S(2)}, u32[]{:S(2)}) collective-permute-start(bf16[128,512]{1,0:T(8,128)(2,1)S(1)} %copy-done.72), channel_id=1, source_target_pairs={{0,20},{4,16},{8,28},{12,24},{16,4},{20,0},{24,12},{28,8},{1,21},{... | collective-permute-start | bytes 393224 | tf_op jit(solution)/shard_map/ppermute | solution.py:462
  446.8 29.8 %collective-permute-start.36 = (bf16[128,512]{1,0:T(8,128)(2,1)S(1)}, bf16[128,512]{1,0:T(8,128)(2,1)S(1)}, u32[]{:S(2)}, u32[]{:S(2)}) collective-permute-start(bf16[128,512]{1,0:T(8,128)(2,1)S(1)} %copy-done.71), channel_id=1, source_target_pairs={{0,24},{4,28},{8,16},{12,20},{16,8},{20,12},{24,0},{28,4},{1,25},{... | collective-permute-start | bytes 393224 | tf_op jit(solution)/shard_map/ppermute | solution.py:462
  446.8 36.7 %collective-permute-start.37 = (bf16[128,512]{1,0:T(8,128)(2,1)S(1)}, bf16[128,512]{1,0:T(8,128)(2,1)S(1)}, u32[]{:S(2)}, u32[]{:S(2)}) collective-permute-start(bf16[128,512]{1,0:T(8,128)(2,1)S(1)} %get-tuple-element.217), channel_id=1, source_target_pairs={{0,28},{4,24},{8,20},{12,16},{16,12},{20,8},{24,4},{28,0},{1,29},{... | collective-permute-start | bytes 393224 | tf_op jit(solution)/shard_map/ppermute | solution.py:462
  466.3 23.1 %collective-permute-start.45 = (bf16[4,16,1024]{2,1,0:T(8,128)(2,1)S(1)}, bf16[4,16,1024]{2,1,0:T(8,128)(2,1)S(1)}, u32[]{:S(2)}, u32[]{:S(2)}) collective-permute-start(bf16[4,16,1024]{2,1,0:T(8,128)(2,1)S(1)} %get-tuple-element.209), channel_id=1, source_target_pairs={{0,4},{4,0},{8,12},{12,8},{16,20},{20,16},{24,28},{28,24},{1,5},{5... | collective-permute-start | bytes 393224 | tf_op jit(solution)/shard_map/ppermute | solution.py:462
  489.5 19.9 %collective-permute-start.42 = (bf16[128,512]{1,0:T(8,128)(2,1)S(1)}, bf16[128,512]{1,0:T(8,128)(2,1)S(1)}, u32[]{:S(2)}, u32[]{:S(2)}) collective-permute-start(bf16[128,512]{1,0:T(8,128)(2,1)S(1)} %get-tuple-element.226), channel_id=1, source_target_pairs={{0,20},{4,16},{8,28},{12,24},{16,4},{20,0},{24,12},{28,8},{1,21},{... | collective-permute-start | bytes 393224 | tf_op jit(solution)/shard_map/ppermute | solution.py:462
  497.2 48.9 %collective-permute-start.26 = (bf16[512,1024]{1,0:T(8,128)(2,1)}, bf16[512,1024]{1,0:T(8,128)(2,1)}, u32[]{:S(2)}, u32[]{:S(2)}) collective-permute-start(bf16[512,1024]{1,0:T(8,128)(2,1)} %add_convert_fusion.4), channel_id=1, source_target_pairs={{0,2},{1,3},{2,0},{3,1},{4,6},{5,7},{6,4},{7,5},{8,10},{9,11},{10,... | collective-permute-start | bytes 3145736 | tf_op jit(solution)/shard_map/ppermute | solution.py:462
  537.0 27.4 %collective-permute-start.28 = (bf16[512,1024]{1,0:T(8,128)(2,1)S(1)}, bf16[512,1024]{1,0:T(8,128)(2,1)S(1)}, u32[]{:S(2)}, u32[]{:S(2)}) collective-permute-start(bf16[512,1024]{1,0:T(8,128)(2,1)S(1)} %get-tuple-element.116), channel_id=1, source_target_pairs={{0,1},{1,0},{2,3},{3,2},{4,5},{5,4},{6,7},{7,6},{8,9},{9,8},{10,11... | collective-permute-start | bytes 3145736 | tf_op jit(solution)/shard_map/ppermute | solution.py:462
  540.4 24.0 %collective-permute-start.30 = (bf16[512,1024]{1,0:T(8,128)(2,1)}, bf16[512,1024]{1,0:T(8,128)(2,1)S(1)}, u32[]{:S(2)}, u32[]{:S(2)}) collective-permute-start(bf16[512,1024]{1,0:T(8,128)(2,1)} %add_convert_fusion.2), channel_id=1, source_target_pairs={{0,2},{1,3},{2,0},{3,1},{4,6},{5,7},{6,4},{7,5},{8,10},{9,11},{10,... | collective-permute-start | bytes 3145736 | tf_op jit(solution)/shard_map/ppermute | solution.py:462
  (118 other events, 1226.8 us)
Sparse Core Ops, SparseCore 0:
  10.8 105.9 all-gather.2
  353.0 133.2 reduce-scatter.1

commit v3 on v2

--- a/solution.py
+++ b/solution.py
@@ -89,10 +89,11 @@
 
 
 def project_kernel(
-    x, gain, matrix, cos, sin, gain_q, gain_k, normed, raw_q, raw_k, q, k, v, k_turned, v_turned
+    x, gain, matrix, cos, sin, gain_q, gain_k, normed_turned, raw_q, raw_k, q, k, v, k_turned, v_turned
 ):
-    h = norm_rows(x[...].astype(F32), gain[...]).astype(BF16)
-    normed[...] = h
+    normed = norm_rows(x[...].astype(F32), gain[...])
+    normed_turned[...] = normed.T.astype(BF16)
+    h = normed.astype(BF16)
     c, s = cos[...], sin[...]
     for j in range(matrix.shape[1] // (SLOTS * HEAD_SIZE)):
         base = j * SLOTS * HEAD_SIZE
@@ -111,7 +112,7 @@
         v_turned[lanes_of(j), :] = value.T.astype(BF16)
 
 
-def attend_kernel(offset, info, q, k, v_turned, start, out, logs):
+def attend_kernel(offset, info, q, k, v_turned, start, out, out_turned, logs):
     blocks = k.shape[0] // BLOCK
     flip = info[blocks]
 
@@ -138,7 +139,9 @@
         done = lax.fori_loop(info[b], b + 1, keys_step, (zero,) * GROUP)
         for h in range(GROUP):
             total, blend = done[h]
-            out[here, lanes_of(h)] = (blend / total).T.astype(BF16)
+            result = blend / total
+            out[here, lanes_of(h)] = result.T.astype(BF16)
+            out_turned[lanes_of(h), here] = result.astype(BF16)
             logs[0, h : h + 1, here] = jnp.log2(total)
         return 0
 
@@ -223,7 +226,7 @@
     def store(i, h, value):
         grad_qkv[at_block(i + half), lanes_of(h)] = value
 
-    grad_gains[0:1, :] = back_blocks(
+    grad_gains[0, 0:1, :] = back_blocks(
         half, info, q, k, v, k_turned, start, logs, out, grad_out, raw_q, cos, sin, gain_q,
         grad_k, grad_v, store,
     )
@@ -237,23 +240,53 @@
         grad_qkv[rows, lanes_of(GROUP + 1)] = grad_v[rows, :].astype(BF16)
         return total_gain + gain
 
-    grad_gains[1:2, :] = lax.fori_loop(0, blocks, finish, jnp.zeros((1, HEAD_SIZE), F32))
-
-
-def feed_kernel(h, grad, gate_up, down, hidden, grad_gate_up, back_a, back_b, sum_a, sum_b):
+    grad_gains[0, 1:2, :] = lax.fori_loop(0, blocks, finish, jnp.zeros((1, HEAD_SIZE), F32))
+
+
+def unpack(packed, gate_up, down):
+    n, _, half = packed.shape
+    depth = gate_up.shape[0] // n
+    pieces = gate_up.shape[1] // half
+    blocks = down.shape[0] // HEAD_SIZE
+    deep = HEAD_SIZE // n
+    for d in range(n):
+        for b in range(pieces):
+            gate_up[d * depth : (d + 1) * depth, b * half : (b + 1) * half] = packed[
+                d, b * depth : (b + 1) * depth, :
+            ]
+        for c in range(2):
+            for i in range(blocks):
+                at = pieces * depth + (c * blocks + i) * deep
+                to = i * HEAD_SIZE + d * deep
+                down[to : to + deep, c * half : (c + 1) * half] = packed[d, at : at + deep, :]
+
+
+def feed_kernel(packs, h, grad, *refs):
     step = pl.program_id(0)
+    if packs:
+        packed, *refs = refs
+        *refs, gate_up, down = refs
+
+        @pl.when(step == 0)
+        def _():
+            unpack(packed, gate_up, down)
+    else:
+        gate_up, down, *refs = refs
+    h_turned, hidden_turned, grad_gate_up, back_a, back_b, sum_a, sum_b = refs
     width = down.shape[0]
-    both = nn(h[...], gate_up[...])
+    rows = h[...]
+    both = nn(rows, gate_up[...])
     gate, up = both[:, :width], both[:, width:]
     sig = jax.nn.sigmoid(gate)
     gated = gate * sig
-    value = (gated * up).astype(BF16)
-    hidden[...] = value
+    value = gated * up
+    hidden_turned[...] = value.T.astype(BF16)
+    h_turned[...] = rows.astype(F32).T.astype(BF16)
     grad_hidden = nt(grad[...], down[...])
     grad_gate_up[:, :width] = (grad_hidden * up * (sig + gated * (1.0 - sig))).astype(BF16)
     grad_gate_up[:, width:] = (grad_hidden * gated).astype(BF16)
     back = nt(grad_gate_up[...], gate_up[...]).astype(BF16)
-    total = nn(value, down[...]).astype(BF16)
+    total = nn(value.astype(BF16), down[...]).astype(BF16)
     first = step < pl.num_programs(0) // 2
 
     @pl.when(first)
@@ -267,10 +300,46 @@
         sum_b[...] = total
 
 
-def unproject_kernel(grad_zero, grad_one, matrix, out_a, out_b):
-    width = grad_zero.shape[1]
-    value = nt(grad_zero[...], matrix[:, :width]) + nt(grad_one[...], matrix[:, width:])
-    value = value.astype(BF16)
+def feed_weights_kernel(
+    packs, pieces, h_own, h_other, grad_own, grad_other, hidden_own, hidden_other, dy_own, dy_other,
+    *out
+):
+    step = pl.program_id(0)
+    half = dy_own.shape[1]
+
+    for b in range(pieces):
+        @pl.when(step == b)
+        def _():
+            value = nn(h_own[...], grad_own[...]) + nn(h_other[...], grad_other[...])
+            value = value.astype(BF16)
+            if packs:
+                n = out[0].shape[0]
+                depth = value.shape[0] // n
+                for d in range(n):
+                    out[0][d, b * depth : (b + 1) * depth, :] = value[d * depth : (d + 1) * depth]
+            else:
+                out[0][:, b * half : (b + 1) * half] = value
+
+    for c in range(2):
+        @pl.when(step == pieces + c)
+        def _():
+            value = nn(hidden_own[...], dy_own[...]) + nn(hidden_other[...], dy_other[...])
+            value = value.astype(BF16)
+            if packs:
+                n = out[0].shape[0]
+                depth, deep = h_own.shape[0] // n, HEAD_SIZE // n
+                blocks = value.shape[0] // HEAD_SIZE
+                for d in range(n):
+                    for i in range(blocks):
+                        at = pieces * depth + (c * blocks + i) * deep
+                        of = i * HEAD_SIZE + d * deep
+                        out[0][d, at : at + deep, :] = value[of : of + deep]
+            else:
+                out[1][:, c * half : (c + 1) * half] = value
+
+
+def unproject_kernel(grad, matrix, out_a, out_b):
+    value = nt(grad[...], matrix[...]).astype(BF16)
     first = pl.program_id(0) < pl.num_programs(0) // 2
 
     @pl.when(first)
@@ -287,7 +356,7 @@
         compiler_params=pltpu.CompilerParams(
             dimension_semantics=("arbitrary",), vmem_limit_bytes=VMEM_LIMIT
         ),
-        cost_estimate=pl.CostEstimate(flops=flops, bytes_accessed=8_000_000, transcendentals=0),
+        cost_estimate=pl.CostEstimate(flops=flops // 64, bytes_accessed=1_000, transcendentals=0),
         name=name,
     )
 
@@ -315,11 +384,11 @@
             by_rows(HEAD_SIZE), fixed((1, HEAD_SIZE)), fixed((1, HEAD_SIZE)),
         ],
         out_specs=[
-            by_rows(width), by_rows(q_width), by_rows(k_width), by_rows(q_width),
+            by_lanes(width), by_rows(q_width), by_rows(k_width), by_rows(q_width),
             by_rows(k_width), by_rows(k_width), by_lanes(k_width), by_lanes(k_width),
         ],
         out_shape=[
-            shaped((rows, width), BF16), shaped((rows, q_width), F32),
+            shaped((width, rows), BF16), shaped((rows, q_width), F32),
             shaped((rows, k_width), F32), shaped((rows, q_width), BF16),
             shaped((rows, k_width), BF16), shaped((rows, k_width), BF16),
             shaped((k_width, rows), BF16), shaped((k_width, rows), BF16),
@@ -328,8 +397,8 @@
     )(x, gain, matrix, cos, sin, gain_q, gain_k)
 
 
-def head_specs(half, rows, head=None):
-    at = (lambda j: j) if head is None else (lambda j: head)
+def head_specs(half, rows):
+    at = lambda j: j
     n = rows // 2
     return dict(
         q=pl.BlockSpec((n, GROUP * HEAD_SIZE), lambda j, info: (half, at(j))),
@@ -352,9 +421,14 @@
             num_scalar_prefetch=1,
             grid=(heads,),
             in_specs=[s["q"], s["k"], s["turned"], s["start"]],
-            out_specs=[s["out"], s["logs"]],
+            out_specs=[
+                s["out"], pl.BlockSpec((GROUP * HEAD_SIZE, n), lambda j, info: (j, 0)), s["logs"],
+            ],
         ),
-        out_shape=[shaped((n, q.shape[1]), BF16), shaped((heads, GROUP, n), F32)],
+        out_shape=[
+            shaped((n, q.shape[1]), BF16), shaped((q.shape[1], n), BF16),
+            shaped((heads, GROUP, n), F32),
+        ],
         **params("attend", 18_000_000_000),
     )(info, q, k, v_turned, start)
 
@@ -386,28 +460,33 @@
 
 
 def attend_back_other(
-    head, info, q, k, v, k_turned, start, logs, out, grad_out, raw_q, cos, sin, gain_q,
+    info, q, k, v, k_turned, start, logs, out, grad_out, raw_q, cos, sin, gain_q,
     raw_k, gain_k, grad_q, grad_k, grad_v,
 ):
     rows = k.shape[0]
-    s = head_specs(1, rows, head)
+    heads = k.shape[1] // HEAD_SIZE
+    width = SLOTS * HEAD_SIZE
+    s = head_specs(1, rows)
     row = fixed((1, HEAD_SIZE))
     return pl.pallas_call(
         back_other_kernel,
         grid_spec=pltpu.PrefetchScalarGridSpec(
             num_scalar_prefetch=1,
-            grid=(1,),
+            grid=(heads,),
             in_specs=[
                 s["q"], s["k"], s["k"], s["turned"], s["start"], s["logs"], s["out"], s["out"],
                 s["q"], s["angle"], s["angle"], row,
                 fixed((rows, HEAD_SIZE)), fixed((rows, HEAD_SIZE)), s["k"], row, s["out"], s["k"],
                 s["k"],
             ],
-            out_specs=[fixed((rows, SLOTS * HEAD_SIZE)), fixed((2, HEAD_SIZE))],
+            out_specs=[
+                pl.BlockSpec((rows, width), lambda j, info: (0, j)),
+                pl.BlockSpec((1, 2, HEAD_SIZE), lambda j, info: (j, 0, 0)),
+            ],
             scratch_shapes=[pltpu.VMEM((rows, HEAD_SIZE), F32)] * 2,
         ),
-        out_shape=[shaped((rows, SLOTS * HEAD_SIZE), BF16), shaped((2, HEAD_SIZE), F32)],
-        **params("attend_back_other", 14_000_000_000),
+        out_shape=[shaped((rows, heads * width), BF16), shaped((heads, 2, HEAD_SIZE), F32)],
+        **params("attend_back_other", 28_000_000_000),
     )(
         info, q, k, v, k_turned, start, logs, out, grad_out, raw_q, cos, sin, gain_q,
         cos, sin, raw_k, gain_k, grad_q, grad_k, grad_v,
@@ -425,41 +504,106 @@
     )
 
 
-def feed(h, grad, gate_up, down):
+def feed(h, grad, weights, hidden_count):
     rows, width = h.shape
+    packs = len(weights) == 1
     by_rows = lambda n: pl.BlockSpec((BLOCK, n), lambda i: (i, 0))
+    by_lanes = lambda n: pl.BlockSpec((n, BLOCK), lambda i: (0, i))
     specs, shapes = two_parts(rows, width)
+    scratch = [
+        pltpu.VMEM((width, 2 * hidden_count), BF16), pltpu.VMEM((hidden_count, width), BF16)
+    ]
     return pl.pallas_call(
-        feed_kernel,
+        lambda *refs: feed_kernel(packs, *refs),
         grid=(rows // BLOCK,),
-        in_specs=[by_rows(width), by_rows(width), fixed(gate_up.shape), fixed(down.shape)],
-        out_specs=[by_rows(down.shape[0]), by_rows(gate_up.shape[1]), *specs, *specs],
+        in_specs=[by_rows(width), by_rows(width), *(fixed(w.shape) for w in weights)],
+        out_specs=[
+            by_lanes(width), by_lanes(hidden_count), by_rows(2 * hidden_count), *specs, *specs
+        ],
         out_shape=[
-            shaped((rows, down.shape[0]), BF16), shaped((rows, gate_up.shape[1]), BF16),
-            *shapes, *shapes,
-        ],
+            shaped((width, rows), BF16), shaped((hidden_count, rows), BF16),
+            shaped((rows, 2 * hidden_count), BF16), *shapes, *shapes,
+        ],
+        scratch_shapes=scratch if packs else [],
         **params("feed", 16_000_000_000),
-    )(h, grad, gate_up, down)
-
-
-def unproject(half, grad_zero, grad_one, matrix):
-    rows, width = grad_zero.shape
+    )(h, grad, *weights)
+
+
+def feed_weights(packed_shape, h, grads, hidden, dy):
+    width, n = h[0].shape
+    half = width // 2
+    pieces = grads[0].shape[1] // half
+    count = hidden[0].shape[0]
+    packs = packed_shape is not None
+    gate_block = pl.BlockSpec((n, half), lambda i: (0, jnp.minimum(i, pieces - 1)))
+    down_block = pl.BlockSpec((n, half), lambda i: (0, jnp.maximum(i - pieces, 0)))
+    shapes = [packed_shape] if packs else [(width, 2 * count), (count, width)]
+    return pl.pallas_call(
+        lambda *refs: feed_weights_kernel(packs, pieces, *refs),
+        grid=(pieces + 2,),
+        in_specs=[
+            fixed((width, n)), fixed((width, n)), gate_block, gate_block,
+            fixed((count, n)), fixed((count, n)), down_block, down_block,
+        ],
+        out_specs=[fixed(shape) for shape in shapes],
+        out_shape=[shaped(shape, BF16) for shape in shapes],
+        **params("feed_weights", 16_000_000_000),
+    )(*h, *grads, *hidden, *dy)
+
+
+def unproject(half, grad, matrix):
+    rows, width = grad.shape
     n = rows // 2
     steps = n // BLOCK
-    by_rows = pl.BlockSpec((BLOCK, width), lambda i: (i + half * steps, 0))
     specs, shapes = two_parts(n, matrix.shape[0])
     return pl.pallas_call(
         unproject_kernel,
         grid=(steps,),
-        in_specs=[by_rows, by_rows, fixed(matrix.shape)],
+        in_specs=[pl.BlockSpec((BLOCK, width), lambda i: (i + half * steps, 0)), fixed(matrix.shape)],
         out_specs=specs,
         out_shape=shapes,
         **params("unproject", 4_000_000_000),
-    )(grad_zero, grad_one, matrix)
-
-
-def flipped(value, axis, bit):
-    return lax.ppermute(value, axis, [(i, i ^ bit) for i in range(lax.axis_size(axis))])
+    )(grad, matrix)
+
+
+def times_turned_kernel(a, b, out):
+    out[...] = nt(a[...], b[...]).astype(BF16)
+
+
+def times_turned(a, b):
+    rows, width = a.shape
+    by_rows = lambda n: pl.BlockSpec((BLOCK, n), lambda i: (i, 0))
+    return pl.pallas_call(
+        times_turned_kernel,
+        grid=(rows // BLOCK,),
+        in_specs=[by_rows(width), fixed(b.shape)],
+        out_specs=by_rows(b.shape[0]),
+        out_shape=shaped((rows, b.shape[0]), BF16),
+        **params("times_turned", 2_000_000_000),
+    )(a, b)
+
+
+def two_products_kernel(a, b, c, d, out):
+    out[...] = nn(a[...], b[...]) + nn(c[...], d[...])
+
+
+def two_products(a, b, c, d):
+    rows, depth = a.shape
+    half = b.shape[1] // 2
+    columns = lambda n: pl.BlockSpec((n, half), lambda i: (0, i))
+    return pl.pallas_call(
+        two_products_kernel,
+        grid=(2,),
+        in_specs=[fixed(a.shape), columns(depth), fixed(c.shape), columns(depth)],
+        out_specs=columns(rows),
+        out_shape=shaped((rows, b.shape[1]), F32),
+        **params("two_products", 2_000_000_000),
+    )(a, b, c, d)
+
+
+def flipped(value, axis, bit, name="part"):
+    with jax.named_scope(name):
+        return lax.ppermute(value, axis, [(i, i ^ bit) for i in range(lax.axis_size(axis))])
 
 
 def together(*values):
@@ -470,10 +614,8 @@
     return part.astype(F32) + flipped(beside, "tensor", 1).astype(F32)
 
 
-def ring_gather(value):
-    n = lax.axis_size("dp")
-    if n != len(RING):
-        return lax.all_gather(value, "dp", axis=0, tiled=False)
+def ring_gather(value, place, later):
+    n = len(RING)
     ring = jnp.array(RING, jnp.int32)
     at = jnp.argmax(ring == lax.axis_index("dp")).astype(jnp.int32)
     after = [(RING[i], RING[(i + 1) % n]) for i in range(n)]
@@ -482,29 +624,24 @@
     up = down = value
     for step in range(1, n // 2 + 1):
         up = lax.ppermute(up, "dp", after)
+        if step < n // 2:
+            down = lax.ppermute(down, "dp", before)
+        if step == 1:
+            up, down, later = together(up, down, later)
         pieces[-step] = up
         if step < n // 2:
-            down = lax.ppermute(down, "dp", before)
             pieces[step] = down
-    full = jnp.zeros((n,) + value.shape, value.dtype)
+    full = None
     for step, piece in pieces.items():
-        full = lax.dynamic_update_index_in_dim(full, piece, ring[(at + step + n) % n], 0)
-    return full
-
-
-def exchanged_sum(parts, axis):
-    n = lax.axis_size("dp")
-    low = parts.astype(BF16)
-    if n != len(RING):
-        return jnp.squeeze(
-            lax.psum_scatter(low, "dp", scatter_dimension=axis, tiled=True), axis
-        ).astype(F32)
-    me = lax.axis_index("dp")
-    take = lambda a, i: lax.dynamic_index_in_dim(a, i, axis, keepdims=False)
-    total = take(parts, me).astype(F32)
-    for bit in range(1, n):
-        total = total + flipped(take(low, me ^ bit), "dp", bit).astype(F32)
-    return total
+        full = place(full, piece, ring[(at + step + n) % n])
+    return full, later
+
+
+def halved(parts, axis, bit):
+    mine = (lax.axis_index("dp") // bit) % 2
+    send = lax.dynamic_index_in_dim(parts, 1 - mine, axis, keepdims=False).astype(BF16)
+    keep = lax.dynamic_index_in_dim(parts, mine, axis, keepdims=False)
+    return keep + flipped(send, "dp", bit).astype(F32)
 
 
 def per_device(
@@ -526,43 +663,60 @@
     depth = projection_weight.shape[0]
     gain_count = gains.shape[0]
 
-    full_one = ring_gather(
-        jnp.concatenate(
-            [
-                projection_weight.astype(BF16).reshape(depth, -1),
-                jnp.pad(gains.astype(BF16)[None, :], ((0, 15), (0, MODEL_WIDTH - gain_count))),
-            ],
-            axis=0,
-        )
-    )
     half = MODEL_WIDTH // 2
     pieces = 2 * hidden_local // half
-    out_rows, gate_rows = 2 * out_heads * out_depth, pieces * depth
-    fold = lambda value: value.reshape(-1, 2, half).swapaxes(0, 1).reshape(-1, half)
-    full_two = lax.all_gather(
-        jnp.concatenate(
-            [
-                fold(w_out.astype(BF16)),
-                w_gate_up.astype(BF16).reshape(depth, pieces, half).swapaxes(0, 1).reshape(-1, half),
-                fold(w_down.astype(BF16)),
-            ],
-            axis=0,
-        ),
-        "dp", axis=0, tiled=False,
-    )
-    unfold = lambda value, count, deep: (
-        value.reshape(spread, 2, count, deep, half).transpose(2, 0, 3, 1, 4).reshape(-1, MODEL_WIDTH)
-    )
-    qkv_matrix = full_one[:, :depth].reshape(MODEL_WIDTH, -1)
-    gains_all = full_one[:, depth, :gain_count].reshape(-1).astype(F32)
-    out_matrix = unfold(full_two[:, :out_rows], out_heads, out_depth)
-    gate_up_matrix = (
-        full_two[:, out_rows : out_rows + gate_rows]
-        .reshape(spread, pieces, depth, half)
-        .swapaxes(1, 2)
-        .reshape(MODEL_WIDTH, -1)
-    )
-    down_matrix = unfold(full_two[:, out_rows + gate_rows :], down_blocks, down_depth)
+    gate_rows = pieces * depth
+    out_rows = out_heads * out_depth
+    ringed = spread == len(RING)
+
+    pack_one = jnp.concatenate(
+        [
+            projection_weight.astype(BF16).reshape(depth, -1),
+            w_out.astype(BF16).reshape(-1, MODEL_WIDTH),
+            jnp.pad(gains.astype(BF16)[None, :], ((0, 15), (0, MODEL_WIDTH - gain_count))),
+        ],
+        axis=0,
+    )
+    pack_two = jnp.concatenate(
+        [
+            w_gate_up.astype(BF16).reshape(depth, pieces, half).swapaxes(0, 1).reshape(-1, half),
+            w_down.astype(BF16).reshape(-1, 2, half).swapaxes(0, 1).reshape(-1, half),
+        ],
+        axis=0,
+    )
+
+    def split_one(value):
+        return (
+            value[..., :depth, :],
+            value[..., depth : depth + out_rows, :],
+            value[..., depth + out_rows, :gain_count],
+        )
+
+    if ringed:
+        def place(full, piece, index):
+            if full is None:
+                full = (
+                    jnp.zeros((spread, depth, MODEL_WIDTH), BF16),
+                    jnp.zeros((out_heads, spread, out_depth, MODEL_WIDTH), BF16),
+                    jnp.zeros((spread, gain_count), BF16),
+                )
+            one, two, three = split_one(piece)
+            two = two.reshape(out_heads, out_depth, MODEL_WIDTH)
+            put = lax.dynamic_update_index_in_dim
+            return (
+                put(full[0], one, index, 0), put(full[1], two, index, 1), put(full[2], three, index, 0)
+            )
+
+        (full_qkv, full_out, full_gains), pack_two = ring_gather(pack_one, place, pack_two)
+    else:
+        full_qkv, full_out, full_gains = split_one(
+            lax.all_gather(pack_one, "dp", axis=0, tiled=False)
+        )
+        full_out = full_out.reshape(spread, out_heads, out_depth, MODEL_WIDTH).swapaxes(0, 1)
+    full_two = lax.all_gather(pack_two, "dp", axis=0, tiled=False)
+    qkv_matrix = full_qkv.reshape(MODEL_WIDTH, -1)
+    out_matrix = full_out.reshape(-1, MODEL_WIDTH)
+    gains_all = full_gains.reshape(-1).astype(F32)
     gain_attn = gains_all[None, :MODEL_WIDTH]
     gain_mlp = gains_all[MODEL_WIDTH : 2 * MODEL_WIDTH]
     gain_query = gains_all[None, 2 * MODEL_WIDTH : 2 * MODEL_WIDTH + HEAD_SIZE]
@@ -591,143 +745,170 @@
     info = jnp.concatenate([block_starts, (me * (local_rows // BLOCK))[None]]).astype(jnp.int32)
     start = start_of_row[None, :]
 
-    def over_rows(a, b):
-        return lax.dot_general(a, b, (((0,), (0,)), ((), ())), preferred_element_type=F32)
-
     rows_float = tokens.astype(F32)
-    tokens_across = flipped(tokens, "tensor", 2)
+    tokens_across = flipped(tokens, "tensor", 2, "tokens_across")
     tokens_all = jnp.concatenate(
         [tokens, flipped(tokens, "tensor", 1), tokens_across, flipped(tokens_across, "tensor", 1)],
         axis=0,
     )
-    normed_one, raw_q, raw_k, q, k, v, k_turned, v_turned = project(
+    normed_turned, raw_q, raw_k, q, k, v, k_turned, v_turned = project(
         tokens_all, gain_attn, qkv_matrix, cos, sin, gain_query, gain_key
     )
-    heads_other, logs_other = attend(1, info, q, k, v_turned, start)
+    grad_across = flipped(cotangent, "tensor", 2, "grad_across")
+    heads_other, heads_other_turned, logs_other = attend(1, info, q, k, v_turned, start)
+    heads_other, grad_across = together(heads_other, grad_across)
     beside = nn(heads_other[local_rows:], out_matrix).astype(BF16)
     near = near_sum(nn(heads_other[:local_rows], out_matrix), beside).astype(BF16)
-    grad_across = flipped(cotangent, "tensor", 2)
-    near, grad_across, q_own = together(near, grad_across, q)
-    attn_across = flipped(near, "tensor", 2)
-    heads_own, logs_own = attend(0, info, q_own, k, v_turned, start)
+    near, q_own = together(near, q)
+    attn_across = flipped(near, "tensor", 2, "attn_across")
+    heads_own, heads_own_turned, logs_own = attend(0, info, q_own, k, v_turned, start)
+    heads_own, attn_across, full_two = together(heads_own, attn_across, full_two)
     beside = nn(heads_own[local_rows:], out_matrix).astype(BF16)
     attn_rows = near_sum(nn(heads_own[:local_rows], out_matrix), beside) + attn_across.astype(F32)
     middle = rows_float + attn_rows
+    if ringed:
+        feed_matrices = (full_two,)
+    else:
+        feed_matrices = (
+            full_two[:, :gate_rows]
+            .reshape(spread, pieces, depth, half)
+            .swapaxes(1, 2)
+            .reshape(MODEL_WIDTH, -1),
+            full_two[:, gate_rows:]
+            .reshape(spread, 2, down_blocks, down_depth, half)
+            .transpose(2, 0, 3, 1, 4)
+            .reshape(-1, MODEL_WIDTH),
+        )
 
     grad_own = jnp.concatenate([cotangent, flipped(cotangent, "tensor", 1)], axis=0)
     grad_other = jnp.concatenate([grad_across, flipped(grad_across, "tensor", 1)], axis=0)
     normed_two = norm_rows(middle, gain_mlp).astype(BF16)
-    normed_across = flipped(normed_two, "tensor", 2)
+    normed_across = flipped(normed_two, "tensor", 2, "normed_across")
     normed_own = jnp.concatenate([normed_two, flipped(normed_two, "tensor", 1)], axis=0)
-    hidden_own, feed_grad_own, back_0, back_1, sum_0, sum_1 = feed(
-        normed_own, grad_own, gate_up_matrix, down_matrix
-    )
-    normed_across, back_0, back_1, sum_0, sum_1 = together(
-        normed_across, back_0, back_1, sum_0, sum_1
-    )
+    h_own, hidden_own, feed_grad_own, back_0, back_1, sum_0, sum_1 = feed(
+        normed_own, grad_own, feed_matrices, hidden_local
+    )
+    normed_across, back_0 = together(normed_across, back_0)
     normed_other = jnp.concatenate([normed_across, flipped(normed_across, "tensor", 1)], axis=0)
-    hidden_other, feed_grad_other, back_2, back_3, sum_2, sum_3 = feed(
-        normed_other, grad_other, gate_up_matrix, down_matrix
+    h_other, hidden_other, feed_grad_other, back_2, back_3, sum_2, sum_3 = feed(
+        normed_other, grad_other, feed_matrices, hidden_local
     )
     near = near_sum(back_2, back_3).astype(BF16)
-    back_across = flipped(near, "tensor", 2)
     back_near = near_sum(back_0, back_1)
-
-    grad_gate_up_w = (
-        over_rows(normed_own, feed_grad_own) + over_rows(normed_other, feed_grad_other)
-    ).astype(BF16)
-    grad_down = (over_rows(hidden_own, grad_own) + over_rows(hidden_other, grad_other)).astype(BF16)
-    back_across, grad_gate_up_w, grad_down = together(back_across, grad_gate_up_w, grad_down)
-    feed_sum = lax.psum_scatter(
-        jnp.concatenate(
+    near, h_own = together(near, h_own)
+    back_across = flipped(near, "tensor", 2, "back_across")
+
+    feed_grads = feed_weights(
+        full_two.shape if ringed else None, (h_own, h_other), (feed_grad_own, feed_grad_other),
+        (hidden_own, hidden_other), (grad_own, grad_other),
+    )
+    back_across, *feed_grads = together(back_across, *feed_grads)
+    if ringed:
+        feed_pack = feed_grads[0]
+    else:
+        feed_pack = jnp.concatenate(
             [
-                grad_gate_up_w.reshape(spread, depth, pieces, half)
+                feed_grads[0].reshape(spread, depth, pieces, half)
                 .swapaxes(1, 2)
                 .reshape(spread, -1, half),
-                grad_down.reshape(down_blocks, spread, down_depth, 2, half)
+                feed_grads[1].reshape(down_blocks, spread, down_depth, 2, half)
                 .transpose(1, 3, 0, 2, 4)
                 .reshape(spread, -1, half),
             ],
             axis=1,
-        ),
-        "dp", scatter_dimension=0, tiled=True,
-    )[0].astype(F32)
-    sum_gate_up = (
-        feed_sum[:gate_rows].reshape(pieces, depth, half).swapaxes(0, 1).reshape(w_gate_up.shape)
-    )
-    sum_down = (
-        feed_sum[gate_rows:].reshape(2, -1, half).swapaxes(0, 1).reshape(w_down.shape)
-    )
-
+        )
+    feed_sum = lax.psum_scatter(feed_pack, "dp", scatter_dimension=0, tiled=True)[0].astype(F32)
     grad_middle_part, grad_gain_mlp = norm_back(
         middle, gain_mlp, back_near + back_across.astype(F32)
     )
     grad_middle = cotangent.astype(F32) + grad_middle_part
     grad_middle_low = grad_middle.astype(BF16)
-    grad_middle_across = flipped(grad_middle_low, "tensor", 2)
+    grad_middle_across = flipped(grad_middle_low, "tensor", 2, "grad_middle_across")
 
     grad_middle_own = jnp.concatenate(
         [grad_middle_low, flipped(grad_middle_low, "tensor", 1)], axis=0
     )
-    grad_heads_own = nt(grad_middle_own, out_matrix).astype(BF16)
+    grad_heads_own = times_turned(grad_middle_own, out_matrix)
     grad_q, grad_k, grad_v, gain_own = attend_back_own(
         info, q, k, v, k_turned, start, logs_own, heads_own, grad_heads_own, raw_q, cos, sin,
         gain_query,
     )
     grad_middle_across, grad_q, sum_2, sum_3 = together(grad_middle_across, grad_q, sum_2, sum_3)
-    mlp_across = flipped(near_sum(sum_2, sum_3).astype(BF16), "tensor", 2)
+    near_mlp = near_sum(sum_2, sum_3).astype(BF16)
     grad_middle_other = jnp.concatenate(
         [grad_middle_across, flipped(grad_middle_across, "tensor", 1)], axis=0
     )
-    grad_heads_other = nt(grad_middle_other, out_matrix).astype(BF16)
-    grad_out_w = over_rows(heads_own, grad_middle_own) + over_rows(heads_other, grad_middle_other)
-    sum_out = exchanged_sum(grad_out_w.reshape(out_heads, spread, out_depth, MODEL_WIDTH), 1)
-
-    grad_qkv, grad_qkv_w, sum_qkv, gain_other = [], [], [], []
-    for head in range(kv_local):
-        one, gain_parts = attend_back_other(
-            head, info, q, k, v, k_turned, start, logs_other, heads_other, grad_heads_other,
-            raw_q, cos, sin, gain_query, raw_k, gain_key, grad_q, grad_k, grad_v,
+    grad_heads_other = times_turned(grad_middle_other, out_matrix)
+    grad_out_w = two_products(
+        heads_own_turned, grad_middle_own, heads_other_turned, grad_middle_other
+    )
+    near_mlp, grad_out_w, grad_heads_other = together(near_mlp, grad_out_w, grad_heads_other)
+    mlp_across = flipped(near_mlp, "tensor", 2, "mlp_across")
+    grad_qkv, gain_other = attend_back_other(
+        info, q, k, v, k_turned, start, logs_other, heads_other, grad_heads_other,
+        raw_q, cos, sin, gain_query, raw_k, gain_key, grad_q, grad_k, grad_v,
+    )
+    grad_qkv, mlp_across = together(grad_qkv, mlp_across)
+    grad_qkv_w = nn(normed_turned, grad_qkv)
+    grad_qkv, grad_qkv_w = together(grad_qkv, grad_qkv_w)
+    grad_gain_attn = jnp.sum(qkv_matrix.astype(F32) * grad_qkv_w, axis=1) / gain_attn[0]
+    grad_gain_heads = jnp.sum(gain_other, axis=0) + jnp.pad(
+        jnp.sum(gain_own, axis=0), ((0, 1), (0, 0))
+    )
+    gain_sums = jnp.concatenate([grad_gain_attn, grad_gain_mlp, grad_gain_heads.reshape(-1)])
+    back_2, back_3 = unproject(1, grad_qkv, qkv_matrix)
+    back_0, back_1 = unproject(0, grad_qkv, qkv_matrix)
+    near = near_sum(back_2, back_3).astype(BF16)
+    back_across = flipped(near, "tensor", 2, "back_across")
+    if ringed:
+        cube = (2, 2, 2)
+        columns = grad_qkv_w.shape[1] // 2
+        gain_rows = jnp.pad(
+            gain_sums.reshape(cube + (1, gain_count)),
+            ((0, 0),) * 3 + ((0, 15), (0, columns - gain_count)),
         )
-        product = over_rows(normed_one, one)
-        grad_qkv.append(one)
-        grad_qkv_w.append(product)
-        gain_other.append(gain_parts)
-        sum_qkv.append(exchanged_sum(product.reshape(spread, depth, -1), 0))
-        if head + 1 < kv_local:
-            grad_heads_other, _ = together(grad_heads_other, product)
-    back_2, back_3 = unproject(1, *grad_qkv, qkv_matrix)
-    back_0, back_1 = unproject(0, *grad_qkv, qkv_matrix)
-    near = near_sum(back_2, back_3).astype(BF16)
-    back_across = flipped(near, "tensor", 2)
+        sum_one = jnp.concatenate(
+            [grad_qkv_w[:, :columns].reshape(cube + (depth, -1)), gain_rows], axis=3
+        )
+        sum_two = grad_qkv_w[:, columns:].reshape(cube + (depth, -1))
+        sum_one, sum_two = halved(sum_one, 1, 2), halved(sum_two, 2, 1)
+        sum_one, sum_two = halved(sum_one, 1, 1), halved(sum_two, 1, 2)
+        sum_one, sum_two, back_across, feed_sum = together(
+            sum_one, sum_two, back_across, feed_sum
+        )
+        sum_one, sum_two = halved(sum_one, 0, 4), halved(sum_two, 0, 4)
+        sum_qkv = jnp.concatenate([sum_one[:depth], sum_two], axis=1)
+        sum_qkv = sum_qkv.reshape(projection_weight.shape)
+        sum_gains = sum_one[depth, :gain_count]
+        sum_out = grad_out_w.reshape((out_heads,) + cube + (out_depth, MODEL_WIDTH))
+        sum_out = halved(halved(halved(sum_out, 2, 2), 2, 1), 1, 4)
+    else:
+        sum_qkv = (
+            lax.psum_scatter(grad_qkv_w.astype(BF16), "dp", scatter_dimension=0, tiled=True)
+            .astype(F32)
+            .reshape(projection_weight.shape)
+        )
+        sum_out = lax.psum_scatter(
+            grad_out_w.astype(BF16).reshape(out_heads, -1, MODEL_WIDTH), "dp",
+            scatter_dimension=1, tiled=True,
+        ).astype(F32)
+        sum_gains = lax.psum_scatter(gain_sums, "dp", scatter_dimension=0, tiled=True)
+    sum_gains = sum_gains + sum(flipped(sum_gains, "tensor", bit) for bit in range(1, shards))
+
     grad_normed_one = near_sum(back_0, back_1) + back_across.astype(F32)
     grad_rows_part, _ = norm_back(rows_float, gain_attn, grad_normed_one)
     grad_tokens = grad_middle + grad_rows_part
     mlp_rows = near_sum(sum_0, sum_1) + mlp_across.astype(F32)
     block_out = (middle + mlp_rows).astype(BF16)
 
-    width = SLOTS * HEAD_SIZE
-    grad_gain_attn = sum(
-        jnp.sum(qkv_matrix[:, i * width : (i + 1) * width].astype(F32) * product, axis=1)
-        for i, product in enumerate(grad_qkv_w)
-    ) / gain_attn[0]
-    grad_gain_heads = sum(gain_other) + jnp.pad(jnp.sum(gain_own, axis=0), ((0, 1), (0, 0)))
-    gain_sums = jnp.concatenate([grad_gain_attn, grad_gain_mlp, grad_gain_heads.reshape(-1)])
-    gain_sums, _ = together(gain_sums, near)
-    gain_sums = gain_sums + sum(flipped(gain_sums, "tensor", bit) for bit in range(1, shards))
-    if spread == len(RING):
-        me_dp = lax.axis_index("dp")
-        parts = gain_sums.reshape(spread, gain_count)
-        take = lambda i: lax.dynamic_index_in_dim(parts, i, 0, keepdims=False)
-        sum_gains = take(me_dp) + sum(
-            flipped(take(me_dp ^ bit), "dp", bit) for bit in range(1, spread)
-        )
-    else:
-        sum_gains = lax.psum_scatter(gain_sums, "dp", scatter_dimension=0, tiled=True)
+    sum_gate_up = (
+        feed_sum[:gate_rows].reshape(pieces, depth, half).swapaxes(0, 1).reshape(w_gate_up.shape)
+    )
+    sum_down = feed_sum[gate_rows:].reshape(2, -1, half).swapaxes(0, 1).reshape(w_down.shape)
 
     upd_qkv = adamw_update(
         projection_weight, first_moment_projection, second_moment_projection,
-        jnp.stack(sum_qkv, axis=1), 2.0 * MODEL_WIDTH ** (-0.5), DECAY,
+        sum_qkv, 2.0 * MODEL_WIDTH ** (-0.5), DECAY,
     )
     upd_out = adamw_update(
         w_out, first_out, second_out, sum_out,

time: 594 us -> 514 us (0.87)
  waiting for transfers between devices: 155 us -> 103 us
  starting transfers between devices: 105 us -> 56.4 us
  Pallas kernels: 137 us -> 172 us
  other arithmetic: 44.8 us -> 62.3 us
  matrix products: 34.2 us -> 16.9 us
  local copies, waits for them, and re-layouts: 75 us -> 61.4 us
    ppermute x55 -> x36, waiting for transfers between devices: 121 us -> 62.5 us  [flipped(): lax.ppermute(value, axis, [(i, i ^ bit) for i in range(lax.axis_size(axis...]
    ppermute x55 -> x36, starting transfers between devices: 90.2 us -> 42 us  [flipped(): lax.ppermute(value, axis, [(i, i ^ bit) for i in range(lax.axis_size(axis...]
    pallas_call x4 -> x8, Pallas kernels: 42.6 us -> 73.8 us  [the longest x2 33.8 us: feed(): pl.pallas_call(lambda *refs: feed_kernel(packs, *refs), grid=(rows // BLO...]
    dot_general x10 -> x0, matrix products: 31.2 us -> none  [the longest x8 27.6 us: over_rows(): lax.dot_general(a, b, (((0,), (0,)), ((), ())), preferred_element_type=F32)]
    unnamed x191 -> x158, local copies, waits for them, and re-layouts: 39.4 us -> 19.9 us
    dot_general x4 -> x5, matrix products: 2.95 us -> 16.9 us  [nn(): return jnp.dot(a, b, preferred_element_type=F32)]
    dynamic_update_slice x7 -> x23, local copies, waits for them, and re-layouts: 2.09 us -> 14.1 us  [the longest x8 6.97 us: place(): put(full[0], one, index, 0)]
    slice x4 -> x17, local copies, waits for them, and re-layouts: 3.13 us -> 13.7 us  [the longest x7 6.86 us: split_one(): value[..., depth:depth + out_rows, :]]
  transfers between devices with their start and end apart: 64 -> 45, of which waited for: 20 -> 21; matrix products, arithmetic and copies ran while one was open for 20% -> 23% of each run, Pallas kernels for 21% -> 30%
where the time goes in v3:
time: 514 us; the launch traced here: 508 us
  Pallas kernels  172 us (33%)
  waiting for transfers between devices  103 us (20%)
  other arithmetic  62.3 us (12%)
  local copies, waits for them, and re-layouts  61.4 us (12%)
  starting transfers between devices  56.4 us (11%)
  between operations  36.7 us (7%)
  matrix products  16.9 us (3%)
    ppermute x36, waiting for transfers between devices, flipped(): lax.ppermute(value, axis, [(i, i ^ bit) for i in range(lax.axis_size(axis...  62.5 us
    ppermute x36, starting transfers between devices, flipped(): lax.ppermute(value, axis, [(i, i ^ bit) for i in range(lax.axis_size(axis...  42 us
    ppermute x4, waiting for transfers between devices, ring_gather(): up = lax.ppermute(up, 'dp', after)  35.4 us
    pallas_call x2, Pallas kernels, feed(): pl.pallas_call(lambda *refs: feed_kernel(packs, *refs), grid=(rows // BLO...  33.8 us
    pallas_call x2, Pallas kernels, attend(): pl.pallas_call(lambda *refs: attend_kernel(half * n // BLOCK, *refs), gri...  31.8 us
    pallas_call x1, Pallas kernels, attend_back_other(): pl.pallas_call(back_other_kernel, grid_spec=pltpu.PrefetchScalarGridSpec(...  29.3 us
    pallas_call x1, Pallas kernels, attend_back_own(): pl.pallas_call(back_own_kernel, grid_spec=pltpu.PrefetchScalarGridSpec(nu...  22.7 us
    unnamed x158, local copies, waits for them, and re-layouts  19.9 us
  transfers between devices with their start and end apart: 45, of which 21 were waited for; matrix products, arithmetic and copies ran while one was open for 23% of the time, Pallas kernels for 30%

profile of v3, /device:TPU:0, one launch (start us, length us, event | category | flops | bytes accessed | tf_op | source)
XLA Modules:
  0.0 508.4 jit_solution(14328471669236454443)
XLA Ops:
  28.2 6.0 %collective-permute-done.3 = bf16[208,1024]{1,0:T(8,128)(2,1)} collective-permute-done((bf16[208,1024]{1,0:T(8,128)(2,1)S(1)}, bf16[208,1024]{1,0:T(8,128)(2,1)}, u32[]{:S(2)}, u32[]{:S(2)}) %collective-permute-start.3) | collective-permute-done | bytes 426016 | tf_op jit(solution)/shard_map/ppermute | solution.py:626
  50.6 3.7 fusion.17
  67.7 5.6 %collective-permute-done.5 = bf16[208,1024]{1,0:T(8,128)(2,1)} collective-permute-done((bf16[208,1024]{1,0:T(8,128)(2,1)}, bf16[208,1024]{1,0:T(8,128)(2,1)}, u32[]{:S(2)}, u32[]{:S(2)}) %collective-permute-start.5) | collective-permute-done | bytes 426016 | tf_op jit(solution)/shard_map/ppermute | solution.py:626
  83.7 11.3 %collective-permute-done.7 = bf16[208,1024]{1,0:T(8,128)(2,1)} collective-permute-done((bf16[208,1024]{1,0:T(8,128)(2,1)}, bf16[208,1024]{1,0:T(8,128)(2,1)}, u32[]{:S(2)}, u32[]{:S(2)}) %collective-permute-start.7) | collective-permute-done | bytes 426016 | tf_op jit(solution)/shard_map/ppermute | solution.py:626
  95.1 6.9 %collective-permute-start.9 = (bf16[208,1024]{1,0:T(8,128)(2,1)}, bf16[208,1024]{1,0:T(8,128)(2,1)}, u32[]{:S(2)}, u32[]{:S(2)}) collective-permute-start(bf16[208,1024]{1,0:T(8,128)(2,1)} %collective-permute-done.7), channel_id=1, source_target_pairs={{0,8},{8,16},{16,24},{24,28},{28,20},{20,12},{12,4},{4,0},{1,9},{9... | collective-permute-start | bytes 1277960 | tf_op jit(solution)/shard_map/ppermute | solution.py:626
  109.8 12.5 %collective-permute-done.9 = bf16[208,1024]{1,0:T(8,128)(2,1)} collective-permute-done((bf16[208,1024]{1,0:T(8,128)(2,1)}, bf16[208,1024]{1,0:T(8,128)(2,1)}, u32[]{:S(2)}, u32[]{:S(2)}) %collective-permute-start.9) | collective-permute-done | bytes 426016 | tf_op jit(solution)/shard_map/ppermute | solution.py:626
  126.2 4.5 pad_maximum_fusion.x
  130.7 14.0 %project.1 = (bf16[1024,2048]{1,0:T(8,128)(2,1)}, f32[2048,512]{1,0:T(8,128)}, f32[2048,256]{1,0:T(8,128)}, bf16[2048,512]{1,0:T(8,128)(2,1)}, bf16[2048,256]{1,...) custom-call(bf16[2048,1024]{1,0:T(8,128)(2,1)} %pad_maximum_fusion.x, ...), custom_call_target="tpu_custom_call" | custom-call | flops 156250000 | bytes 1000 | tf_op jit(solution)/shard_map/project/pallas_call | solution.py:379
  146.7 16.5 %attend.2 = (bf16[1024,512]{1,0:T(8,128)(2,1)S(1)}, bf16[512,1024]{1,0:T(8,128)(2,1)S(1)}, f32[2,2,1024]{2,1,0:T(2,128)S(1)}) custom-call(s32[9]{0:T(128)S(1)} %pad_add_fusion.refs_0_.info, bf16[2048,512]{1,0:T(8,128)(2,1)} %get-tuple-element.95.refs_1_.q, bf16[2048,256]{1,0:T(8,128)(2,1)S(1)} %get-tuple-element.91.refs_2_.k, ...), custom_call_target="tpu_custom_call" | custom-call | flops 281249984 | bytes 1000 | tf_op jit(solution)/shard_map/attend/pallas_call | solution.py:418
  170.8 15.3 %attend.3 = (bf16[1024,512]{1,0:T(8,128)(2,1)S(1)}, bf16[512,1024]{1,0:T(8,128)(2,1)S(1)}, f32[2,2,1024]{2,1,0:T(2,128)S(1)}) custom-call(s32[9]{0:T(128)S(1)} %pad_add_fusion.refs_0_.info, bf16[2048,512]{1,0:T(8,128)(2,1)} %get-tuple-element.95.refs_1_.q, bf16[2048,256]{1,0:T(8,128)(2,1)S(1)} %get-tuple-element.91.refs_2_.k, ...), custom_call_target="tpu_custom_call" | custom-call | flops 281249984 | bytes 1000 | tf_op jit(solution)/shard_map/attend/pallas_call | solution.py:418
  187.1 8.8 %collective-permute-done.12 = bf16[512,1024]{1,0:T(8,128)(2,1)S(1)} collective-permute-done((bf16[512,1024]{1,0:T(8,128)(2,1)S(1)}, bf16[512,1024]{1,0:T(8,128)(2,1)S(1)}, u32[]{:S(2)}, u32[]{:S(2)}) %collective-permute-start.12) | collective-permute-done | bytes 1048608 | tf_op jit(solution)/shard_map/attn_across/ppermute | solution.py:606
  208.5 16.7 %feed.2 = (bf16[1024,1024]{1,0:T(8,128)(2,1)}, bf16[768,1024]{1,0:T(8,128)(2,1)S(1)}, bf16[1024,1536]{1,0:T(8,128)(2,1)}, bf16[512,1024]{1,0:T(8,128)(2,1)S(1)},...) custom-call(bf16[1024,1024]{1,0:T(8,128)(2,1)} %pad_maximum_fusion.1.refs_0_, ...), custom_call_target="tpu_custom_call" | custom-call | flops 250000000 | bytes 1000 | tf_op jit(solution)/shard_map/feed/pallas_call | solution.py:516
  225.2 4.7 collective-permute-done.17
  234.1 17.1 %feed.3 = (bf16[1024,1024]{1,0:T(8,128)(2,1)}, bf16[768,1024]{1,0:T(8,128)(2,1)S(1)}, bf16[1024,1536]{1,0:T(8,128)(2,1)}, bf16[512,1024]{1,0:T(8,128)(2,1)S(1)},...) custom-call(bf16[1024,1024]{1,0:T(8,128)(2,1)} %pad_maximum_fusion.2.refs_0_, ...), custom_call_target="tpu_custom_call" | custom-call | flops 250000000 | bytes 1000 | tf_op jit(solution)/shard_map/feed/pallas_call | solution.py:516
  256.5 16.5 %feed_weights.1 = bf16[8,576,512]{2,1,0:T(8,128)(2,1)} custom-call(bf16[1024,1024]{1,0:T(8,128)(2,1)S(1)} %copy-done.18, bf16[1024,1024]{1,0:T(8,128)(2,1)} %get-tuple-element.117.refs_1_, bf16[1024,1536]{1,0:T(8,128)(2,1)} %get-tuple-element.118.refs_2_, bf16[1024,1536]{1,0:T(8,128)(2,1)} %get-tuple-element.119.refs_3_, ...), custom_call_target="tpu_custom_call" | custom-call | flops 250000000 | bytes 1000 | tf_op jit(solution)/shard_map/feed_weights/pallas_call | solution.py:541
  273.0 8.6 %collective-permute-done.22 = bf16[512,1024]{1,0:T(8,128)(2,1)S(1)} collective-permute-done((bf16[512,1024]{1,0:T(8,128)(2,1)}, bf16[512,1024]{1,0:T(8,128)(2,1)S(1)}, u32[]{:S(2)}, u32[]{:S(2)}) %collective-permute-start.22) | collective-permute-done | bytes 1048608 | tf_op jit(solution)/shard_map/back_across/ppermute | solution.py:606
  286.4 4.1 fusion.36
  293.4 3.9 times_turned.2.grad_out
  298.4 22.7 %attend_back_own.1 = (bf16[1024,512]{1,0:T(8,128)(2,1)S(1)}, f32[2048,256]{1,0:T(8,128)}, f32[2048,256]{1,0:T(8,128)}, f32[2,1,128]{2,1,0:T(1,128)S(1)}) custom-call(s32[9]{0:T(128)S(1)} %pad_add_fusion.refs_0_.info, bf16[2048,512]{1,0:T(8,128)(2,1)} %get-tuple-element.95.refs_1_.q, bf16[2048,256]{1,0:T(8,128)(2,1)S(1)} %copy-done.5, ...), custom_call_target="tpu_custom_call" | custom-call | flops 390624992 | bytes 1000 | tf_op jit(solution)/shard_map/attend_back_own/pallas_call | solution.py:440
  325.2 4.0 times_turned.3.grad_out
  329.2 4.6 two_products.1
  337.3 9.6 %collective-permute-start.37 = (bf16[4,2,2,16,1024]{4,3,0,1,2:T(8,128)(2,1)}, bf16[4,2,2,16,1024]{4,3,0,1,2:T(8,128)(2,1)}, u32[]{:S(2)}, u32[]{:S(2)}) collective-permute-start(bf16[4,2,2,16,1024]{4,3,0,1,2:T(8,128)(2,1)} %fusion.10), channel_id=1, source_target_pairs={{0,8},{4,12},{8,0},{12,4},{16,24},{20,28},{24,16},{28,20},{1,9},{5... | collective-permute-start | bytes 1572872 | tf_op jit(solution)/shard_map/part/ppermute | solution.py:606
  353.8 5.7 %collective-permute-done.37 = bf16[4,2,2,16,1024]{4,3,0,1,2:T(8,128)(2,1)} collective-permute-done((bf16[4,2,2,16,1024]{4,3,0,1,2:T(8,128)(2,1)}, bf16[4,2,2,16,1024]{4,3,0,1,2:T(8,128)(2,1)}, u32[]{:S(2)}, u32[]{:S(2)}) %collective-permute-start.37) | collective-permute-done | bytes 524320 | tf_op jit(solution)/shard_map/part/ppermute | solution.py:606
  360.7 5.2 %collective-permute-start.38 = (bf16[4,2,16,1024]{3,2,0,1:T(8,128)(2,1)S(1)}, bf16[4,2,16,1024]{3,2,0,1:T(8,128)(2,1)S(1)}, u32[]{:S(2)}, u32[]{:S(2)}) collective-permute-start(bf16[4,2,16,1024]{3,2,0,1:T(8,128)(2,1)S(1)} %fusion.21), channel_id=1, source_target_pairs={{0,4},{4,0},{8,12},{12,8},{16,20},{20,16},{24,28},{28,24},{1,5},{5... | collective-permute-start | bytes 786440 | tf_op jit(solution)/shard_map/part/ppermute | solution.py:606
  367.2 29.3 %attend_back_other.1 = (bf16[2048,1024]{1,0:T(8,128)(2,1)}, f32[2,2,128]{2,1,0:T(2,128)S(1)}) custom-call(s32[9]{0:T(128)S(1)} %pad_add_fusion.refs_0_.info, bf16[2048,512]{1,0:T(8,128)(2,1)} %get-tuple-element.95.refs_1_.q, bf16[2048,256]{1,0:T(8,128)(2,1)S(1)} %copy-done.5, bf16[2048,256]{1,0:T(8,128)(2,1)S(1)} %copy-done.9, ...), custom_call_target="tpu_custom_call" | custom-call | flops 437500000 | bytes 1000 | tf_op jit(solution)/shard_map/attend_back_other/pallas_call | solution.py:471
  397.3 4.7 collective-permute-start.39
  402.0 7.6 %fusion.40 = f32[1024,1024]{1,0:T(8,128)S(1)} fusion(bf16[1024,2048]{1,0:T(8,128)(2,1)} %get-tuple-element.142, bf16[2048,1024]{1,0:T(8,128)(2,1)} %get-tuple-element.143.grad), kind=kOutput, calls=%fused_computation.152 | convolution fusion | flops 4294967296 | bytes 12582912 | tf_op jit(solution)/shard_map/dot_general | solution.py:60
  409.7 5.4 %unproject.3 = (bf16[512,1024]{1,0:T(8,128)(2,1)S(1)}, bf16[512,1024]{1,0:T(8,128)(2,1)}) custom-call(bf16[2048,1024]{1,0:T(8,128)(2,1)} %get-tuple-element.143.grad, bf16[1024,1024]{1,0:T(8,128)(2,1)S(1)} %bitcast.148), custom_call_target="tpu_custom_call" | custom-call | flops 62500000 | bytes 1000 | tf_op jit(solution)/shard_map/unproject/pallas_call | solution.py:559
  425.9 5.7 %unproject.2 = (bf16[512,1024]{1,0:T(8,128)(2,1)S(1)}, bf16[512,1024]{1,0:T(8,128)(2,1)}) custom-call(bf16[2048,1024]{1,0:T(8,128)(2,1)} %get-tuple-element.143.grad, bf16[1024,1024]{1,0:T(8,128)(2,1)S(1)} %bitcast.149), custom_call_target="tpu_custom_call" | custom-call | flops 62500000 | bytes 1000 | tf_op jit(solution)/shard_map/unproject/pallas_call | solution.py:559
  451.2 17.1 %collective-permute-done.34 = bf16[512,1024]{1,0:T(8,128)(2,1)} collective-permute-done((bf16[512,1024]{1,0:T(8,128)(2,1)}, bf16[512,1024]{1,0:T(8,128)(2,1)}, u32[]{:S(2)}, u32[]{:S(2)}) %collective-permute-start.34) | collective-permute-done | bytes 1048608 | tf_op jit(solution)/shard_map/back_across/ppermute | solution.py:606
  484.0 4.1 fusion.3
  496.6 3.9 multiply_subtract_fusion.1
  (368 shorter events, 165.4 us)
Async XLA Ops:
  7.2 188.7 %all-gather.3.cloned.1.call-start = ((), (), s32[]{:S(2)}) async-start(), calls=%async_computation.2 | async-start | bytes 5308416 | tf_op jit(solution)/shard_map/all_gather | solution.py:716
  21.3 12.9 %collective-permute-start.3 = (bf16[208,1024]{1,0:T(8,128)(2,1)S(1)}, bf16[208,1024]{1,0:T(8,128)(2,1)}, u32[]{:S(2)}, u32[]{:S(2)}) collective-permute-start(bf16[208,1024]{1,0:T(8,128)(2,1)S(1)} %fusion.15), channel_id=1, source_target_pairs={{0,8},{8,16},{16,24},{24,28},{28,20},{20,12},{12,4},{4,0},{1,9},{9... | collective-permute-start | bytes 1277960 | tf_op jit(solution)/shard_map/ppermute | solution.py:626
  24.4 59.3 %collective-permute-start.1 = (bf16[512,1024]{1,0:T(8,128)(2,1)}, bf16[512,1024]{1,0:T(8,128)(2,1)}, u32[]{:S(2)}, u32[]{:S(2)}) collective-permute-start(bf16[512,1024]{1,0:T(8,128)(2,1)} %param.19), channel_id=1, source_target_pairs={{0,2},{1,3},{2,0},{3,1},{4,6},{5,7},{6,4},{7,5},{8,10},{9,11},{10,... | collective-permute-start | bytes 3145736 | tf_op jit(solution)/shard_map/tokens_across/ppermute | solution.py:606
  26.3 99.9 %collective-permute-start = (bf16[512,1024]{1,0:T(8,128)(2,1)}, bf16[512,1024]{1,0:T(8,128)(2,1)}, u32[]{:S(2)}, u32[]{:S(2)}) collective-permute-start(bf16[512,1024]{1,0:T(8,128)(2,1)} %param.19), channel_id=1, source_target_pairs={{0,1},{1,0},{2,3},{3,2},{4,5},{5,4},{6,7},{7,6},{8,9},{9,8},{10,11... | collective-permute-start | bytes 3145736 | tf_op jit(solution)/shard_map/part/ppermute | solution.py:606
  26.3 136.9 %collective-permute-start.10 = (bf16[512,1024]{1,0:T(8,128)(2,1)}, bf16[512,1024]{1,0:T(8,128)(2,1)}, u32[]{:S(2)}, u32[]{:S(2)}) collective-permute-start(bf16[512,1024]{1,0:T(8,128)(2,1)} %param.20), channel_id=1, source_target_pairs={{0,2},{1,3},{2,0},{3,1},{4,6},{5,7},{6,4},{7,5},{8,10},{9,11},{10,... | collective-permute-start | bytes 3145736 | tf_op jit(solution)/shard_map/grad_across/ppermute | solution.py:606
  35.8 414.3 %reduce-scatter.2.cloned.1.call-start = ((), (), s32[]{:S(2)}) async-start(), calls=%async_computation.1 | async-start | bytes 5308416 | tf_op jit(solution)/shard_map/reduce_scatter | solution.py:820
  55.9 17.4 %collective-permute-start.5 = (bf16[208,1024]{1,0:T(8,128)(2,1)}, bf16[208,1024]{1,0:T(8,128)(2,1)}, u32[]{:S(2)}, u32[]{:S(2)}) collective-permute-start(bf16[208,1024]{1,0:T(8,128)(2,1)} %collective-permute-done.3), channel_id=1, source_target_pairs={{0,8},{8,16},{16,24},{24,28},{28,20},{20,12},{12,4},{4,0},{1,9},{9... | collective-permute-start | bytes 1277960 | tf_op jit(solution)/shard_map/ppermute | solution.py:626
  58.2 17.2 %collective-permute-start.6 = (bf16[208,1024]{1,0:T(8,128)(2,1)}, bf16[208,1024]{1,0:T(8,128)(2,1)}, u32[]{:S(2)}, u32[]{:S(2)}) collective-permute-start(bf16[208,1024]{1,0:T(8,128)(2,1)} %collective-permute-done.4), channel_id=1, source_target_pairs={{8,0},{16,8},{24,16},{28,24},{20,28},{12,20},{4,12},{0,4},{9,1},{1... | collective-permute-start | bytes 1277960 | tf_op jit(solution)/shard_map/ppermute | solution.py:628
  76.2 18.9 %collective-permute-start.7 = (bf16[208,1024]{1,0:T(8,128)(2,1)}, bf16[208,1024]{1,0:T(8,128)(2,1)}, u32[]{:S(2)}, u32[]{:S(2)}) collective-permute-start(bf16[208,1024]{1,0:T(8,128)(2,1)} %collective-permute-done.5), channel_id=1, source_target_pairs={{0,8},{8,16},{16,24},{24,28},{28,20},{20,12},{12,4},{4,0},{1,9},{9... | collective-permute-start | bytes 1277960 | tf_op jit(solution)/shard_map/ppermute | solution.py:626
  77.9 27.0 %collective-permute-start.8 = (bf16[208,1024]{1,0:T(8,128)(2,1)}, bf16[208,1024]{1,0:T(8,128)(2,1)S(1)}, u32[]{:S(2)}, u32[]{:S(2)}) collective-permute-start(bf16[208,1024]{1,0:T(8,128)(2,1)} %collective-permute-done.6), channel_id=1, source_target_pairs={{8,0},{16,8},{24,16},{28,24},{20,28},{12,20},{4,12},{0,4},{9,1},{1... | collective-permute-start | bytes 1277960 | tf_op jit(solution)/shard_map/ppermute | solution.py:628
  83.6 42.6 %collective-permute-start.2 = (bf16[512,1024]{1,0:T(8,128)(2,1)}, bf16[512,1024]{1,0:T(8,128)(2,1)}, u32[]{:S(2)}, u32[]{:S(2)}) collective-permute-start(bf16[512,1024]{1,0:T(8,128)(2,1)} %collective-permute-done.1), channel_id=1, source_target_pairs={{0,1},{1,0},{2,3},{3,2},{4,5},{5,4},{6,7},{7,6},{8,9},{9,8},{10,11... | collective-permute-start | bytes 3145736 | tf_op jit(solution)/shard_map/part/ppermute | solution.py:606
  95.1 27.3 %collective-permute-start.9 = (bf16[208,1024]{1,0:T(8,128)(2,1)}, bf16[208,1024]{1,0:T(8,128)(2,1)}, u32[]{:S(2)}, u32[]{:S(2)}) collective-permute-start(bf16[208,1024]{1,0:T(8,128)(2,1)} %collective-permute-done.7), channel_id=1, source_target_pairs={{0,8},{8,16},{16,24},{24,28},{28,20},{20,12},{12,4},{4,0},{1,9},{9... | collective-permute-start | bytes 1277960 | tf_op jit(solution)/shard_map/ppermute | solution.py:626
  170.6 25.3 %collective-permute-start.12 = (bf16[512,1024]{1,0:T(8,128)(2,1)S(1)}, bf16[512,1024]{1,0:T(8,128)(2,1)S(1)}, u32[]{:S(2)}, u32[]{:S(2)}) collective-permute-start(bf16[512,1024]{1,0:T(8,128)(2,1)S(1)} %add_convert_fusion.4), channel_id=1, source_target_pairs={{0,2},{1,3},{2,0},{3,1},{4,6},{5,7},{6,4},{7,5},{8,10},{9,11},{10,... | collective-permute-start | bytes 3145736 | tf_op jit(solution)/shard_map/attn_across/ppermute | solution.py:606
  204.5 25.4 %collective-permute-start.17 = (bf16[512,1024]{1,0:T(8,128)(2,1)S(1)}, bf16[512,1024]{1,0:T(8,128)(2,1)S(1)}, u32[]{:S(2)}, u32[]{:S(2)}) collective-permute-start(bf16[512,1024]{1,0:T(8,128)(2,1)S(1)} %multiply_convert_fusion), channel_id=1, source_target_pairs={{0,2},{1,3},{2,0},{3,1},{4,6},{5,7},{6,4},{7,5},{8,10},{9,11},{10,... | collective-permute-start | bytes 3145736 | tf_op jit(solution)/shard_map/normed_across/ppermute | solution.py:606
  206.2 25.0 %collective-permute-start.20 = (bf16[512,1024]{1,0:T(8,128)(2,1)}, bf16[512,1024]{1,0:T(8,128)(2,1)S(1)}, u32[]{:S(2)}, u32[]{:S(2)}) collective-permute-start(bf16[512,1024]{1,0:T(8,128)(2,1)} %collective-permute-done.10), channel_id=1, source_target_pairs={{0,1},{1,0},{2,3},{3,2},{4,5},{5,4},{6,7},{7,6},{8,9},{9,8},{10,11... | collective-permute-start | bytes 3145736 | tf_op jit(solution)/shard_map/part/ppermute | solution.py:606
  256.2 25.4 %collective-permute-start.22 = (bf16[512,1024]{1,0:T(8,128)(2,1)}, bf16[512,1024]{1,0:T(8,128)(2,1)S(1)}, u32[]{:S(2)}, u32[]{:S(2)}) collective-permute-start(bf16[512,1024]{1,0:T(8,128)(2,1)} %add_convert_fusion.3), channel_id=1, source_target_pairs={{0,2},{1,3},{2,0},{3,1},{4,6},{5,7},{6,4},{7,5},{8,10},{9,11},{10,... | collective-permute-start | bytes 3145736 | tf_op jit(solution)/shard_map/back_across/ppermute | solution.py:606
  256.5 25.1 %collective-permute-start.18 = (bf16[512,1024]{1,0:T(8,128)(2,1)S(1)}, bf16[512,1024]{1,0:T(8,128)(2,1)}, u32[]{:S(2)}, u32[]{:S(2)}) collective-permute-start(bf16[512,1024]{1,0:T(8,128)(2,1)S(1)} %get-tuple-element.109), channel_id=1, source_target_pairs={{0,1},{1,0},{2,3},{3,2},{4,5},{5,4},{6,7},{7,6},{8,9},{9,8},{10,11... | collective-permute-start | bytes 3145736 | tf_op jit(solution)/shard_map/part/ppermute | solution.py:606
  290.5 31.6 %collective-permute-start.23 = (bf16[512,1024]{1,0:T(8,128)(2,1)S(1)}, bf16[512,1024]{1,0:T(8,128)(2,1)S(1)}, u32[]{:S(2)}, u32[]{:S(2)}) collective-permute-start(bf16[512,1024]{1,0:T(8,128)(2,1)S(1)} %get-tuple-element.227), channel_id=1, source_target_pairs={{0,2},{1,3},{2,0},{3,1},{4,6},{5,7},{6,4},{7,5},{8,10},{9,11},{10,... | collective-permute-start | bytes 3145736 | tf_op jit(solution)/shard_map/grad_middle_across/ppermute | solution.py:606
  322.2 11.6 %collective-permute-start.25 = (bf16[512,1024]{1,0:T(8,128)(2,1)}, bf16[512,1024]{1,0:T(8,128)(2,1)}, u32[]{:S(2)}, u32[]{:S(2)}) collective-permute-start(bf16[512,1024]{1,0:T(8,128)(2,1)} %get-tuple-element.129), channel_id=1, source_target_pairs={{0,1},{1,0},{2,3},{3,2},{4,5},{5,4},{6,7},{7,6},{8,9},{9,8},{10,11... | collective-permute-start | bytes 3145736 | tf_op jit(solution)/shard_map/part/ppermute | solution.py:606
  337.3 22.2 %collective-permute-start.37 = (bf16[4,2,2,16,1024]{4,3,0,1,2:T(8,128)(2,1)}, bf16[4,2,2,16,1024]{4,3,0,1,2:T(8,128)(2,1)}, u32[]{:S(2)}, u32[]{:S(2)}) collective-permute-start(bf16[4,2,2,16,1024]{4,3,0,1,2:T(8,128)(2,1)} %fusion.10), channel_id=1, source_target_pairs={{0,8},{4,12},{8,0},{12,4},{16,24},{20,28},{24,16},{28,20},{1,9},{5... | collective-permute-start | bytes 1572872 | tf_op jit(solution)/shard_map/part/ppermute | solution.py:606
  346.9 55.1 %collective-permute-start.27 = (bf16[512,1024]{1,0:T(8,128)(2,1)}, bf16[512,1024]{1,0:T(8,128)(2,1)}, u32[]{:S(2)}, u32[]{:S(2)}) collective-permute-start(bf16[512,1024]{1,0:T(8,128)(2,1)} %add_convert_fusion.2), channel_id=1, source_target_pairs={{0,2},{1,3},{2,0},{3,1},{4,6},{5,7},{6,4},{7,5},{8,10},{9,11},{10,... | collective-permute-start | bytes 3145736 | tf_op jit(solution)/shard_map/mlp_across/ppermute | solution.py:606
  353.8 91.8 %collective-permute-start.16 = (bf16[512,1024]{1,0:T(8,128)(2,1)}, bf16[512,1024]{1,0:T(8,128)(2,1)}, u32[]{:S(2)}, u32[]{:S(2)}) collective-permute-start(bf16[512,1024]{1,0:T(8,128)(2,1)} %copy-done.32), channel_id=1, source_target_pairs={{0,1},{1,0},{2,3},{3,2},{4,5},{5,4},{6,7},{7,6},{8,9},{9,8},{10,11... | collective-permute-start | bytes 3145736 | tf_op jit(solution)/shard_map/part/ppermute | solution.py:606
  360.7 35.8 %collective-permute-start.38 = (bf16[4,2,16,1024]{3,2,0,1:T(8,128)(2,1)S(1)}, bf16[4,2,16,1024]{3,2,0,1:T(8,128)(2,1)S(1)}, u32[]{:S(2)}, u32[]{:S(2)}) collective-permute-start(bf16[4,2,16,1024]{3,2,0,1:T(8,128)(2,1)S(1)} %fusion.21), channel_id=1, source_target_pairs={{0,4},{4,0},{8,12},{12,8},{16,20},{20,16},{24,28},{28,24},{1,5},{5... | collective-permute-start | bytes 786440 | tf_op jit(solution)/shard_map/part/ppermute | solution.py:606
  397.3 26.7 %collective-permute-start.39 = (bf16[4,16,1024]{2,1,0:T(8,128)(2,1)}, bf16[4,16,1024]{2,1,0:T(8,128)(2,1)}, u32[]{:S(2)}, u32[]{:S(2)}) collective-permute-start(bf16[4,16,1024]{2,1,0:T(8,128)(2,1)} %fusion.29), channel_id=1, source_target_pairs={{0,16},{4,20},{8,24},{12,28},{16,0},{20,4},{24,8},{28,12},{1,17},{... | collective-permute-start | bytes 393224 | tf_op jit(solution)/shard_map/part/ppermute | solution.py:606
  415.1 24.4 %collective-permute-start.33 = (bf16[512,1024]{1,0:T(8,128)(2,1)}, bf16[512,1024]{1,0:T(8,128)(2,1)}, u32[]{:S(2)}, u32[]{:S(2)}) collective-permute-start(bf16[512,1024]{1,0:T(8,128)(2,1)} %get-tuple-element.150), channel_id=1, source_target_pairs={{0,1},{1,0},{2,3},{3,2},{4,5},{5,4},{6,7},{7,6},{8,9},{9,8},{10,11... | collective-permute-start | bytes 3145736 | tf_op jit(solution)/shard_map/part/ppermute | solution.py:606
  418.1 14.4 %collective-permute-start.31 = (bf16[2,2,128,512]{3,2,1,0:T(8,128)(2,1)}, bf16[2,2,128,512]{3,2,1,0:T(8,128)(2,1)}, u32[]{:S(2)}, u32[]{:S(2)}) collective-permute-start(bf16[2,2,128,512]{3,2,1,0:T(8,128)(2,1)} %fusion.9), channel_id=1, source_target_pairs={{0,4},{4,0},{8,12},{12,8},{16,20},{20,16},{24,28},{28,24},{1,5},{5... | collective-permute-start | bytes 1572872 | tf_op jit(solution)/shard_map/part/ppermute | solution.py:606
  420.9 17.2 %collective-permute-start.29 = (bf16[2,2,144,512]{3,2,0,1:T(8,128)(2,1)S(1)}, bf16[2,2,144,512]{3,2,0,1:T(8,128)(2,1)S(1)}, u32[]{:S(2)}, u32[]{:S(2)}) collective-permute-start(bf16[2,2,144,512]{3,2,0,1:T(8,128)(2,1)S(1)} %fusion.7), channel_id=1, source_target_pairs={{0,8},{4,12},{8,0},{12,4},{16,24},{20,28},{24,16},{28,20},{1,9},{5... | collective-permute-start | bytes 1769480 | tf_op jit(solution)/shard_map/part/ppermute | solution.py:606
  431.7 43.1 %collective-permute-start.28 = (bf16[512,1024]{1,0:T(8,128)(2,1)}, bf16[512,1024]{1,0:T(8,128)(2,1)}, u32[]{:S(2)}, u32[]{:S(2)}) collective-permute-start(bf16[512,1024]{1,0:T(8,128)(2,1)} %get-tuple-element.145), channel_id=1, source_target_pairs={{0,1},{1,0},{2,3},{3,2},{4,5},{5,4},{6,7},{7,6},{8,9},{9,8},{10,11... | collective-permute-start | bytes 3145736 | tf_op jit(solution)/shard_map/part/ppermute | solution.py:606
  433.8 15.1 %collective-permute-start.32 = (bf16[2,128,512]{2,1,0:T(8,128)(2,1)S(1)}, bf16[2,128,512]{2,1,0:T(8,128)(2,1)S(1)}, u32[]{:S(2)}, u32[]{:S(2)}) collective-permute-start(bf16[2,128,512]{2,1,0:T(8,128)(2,1)S(1)} %fusion.20), channel_id=1, source_target_pairs={{0,8},{4,12},{8,0},{12,4},{16,24},{20,28},{24,16},{28,20},{1,9},{5... | collective-permute-start | bytes 786440 | tf_op jit(solution)/shard_map/part/ppermute | solution.py:606
  442.1 26.2 %collective-permute-start.34 = (bf16[512,1024]{1,0:T(8,128)(2,1)}, bf16[512,1024]{1,0:T(8,128)(2,1)}, u32[]{:S(2)}, u32[]{:S(2)}) collective-permute-start(bf16[512,1024]{1,0:T(8,128)(2,1)} %add_convert_fusion), channel_id=1, source_target_pairs={{0,2},{1,3},{2,0},{3,1},{4,6},{5,7},{6,4},{7,5},{8,10},{9,11},{10,... | collective-permute-start | bytes 3145736 | tf_op jit(solution)/shard_map/back_across/ppermute | solution.py:606
  470.0 23.0 %collective-permute-start.35 = (bf16[144,512]{1,0:T(8,128)(2,1)}, bf16[144,512]{1,0:T(8,128)(2,1)}, u32[]{:S(2)}, u32[]{:S(2)}) collective-permute-start(bf16[144,512]{1,0:T(8,128)(2,1)} %fusion.27), channel_id=1, source_target_pairs={{0,16},{4,20},{8,24},{12,28},{16,0},{20,4},{24,8},{28,12},{1,17},{... | collective-permute-start | bytes 442376 | tf_op jit(solution)/shard_map/part/ppermute | solution.py:606
  471.4 21.5 %collective-permute-start.36 = (bf16[128,512]{1,0:T(8,128)(2,1)}, bf16[128,512]{1,0:T(8,128)(2,1)S(1)}, u32[]{:S(2)}, u32[]{:S(2)}) collective-permute-start(bf16[128,512]{1,0:T(8,128)(2,1)} %fusion.28), channel_id=1, source_target_pairs={{0,16},{4,20},{8,24},{12,28},{16,0},{20,4},{24,8},{28,12},{1,17},{... | collective-permute-start | bytes 393224 | tf_op jit(solution)/shard_map/part/ppermute | solution.py:606
  (87 other events, 591.4 us)
Sparse Core Ops, SparseCore 0:
  35.9 100.6 all-gather.2
  285.0 109.3 reduce-scatter.1

commit v4 on v3

--- a/solution.py
+++ b/solution.py
@@ -2,6 +2,7 @@
 import jax.numpy as jnp
 from jax import lax
 from jax.experimental import pallas as pl
+from jax.experimental.layout import Layout, with_layout_constraint
 from jax.experimental.pallas import tpu as pltpu
 from jax.sharding import PartitionSpec as P
 
@@ -25,7 +26,6 @@
 LOG2E = 1.4426950408889634
 BLOCK = 256
 VMEM_LIMIT = 48 * 1024 * 1024
-RING = (0, 2, 4, 6, 7, 5, 3, 1)
 F32 = jnp.float32
 BF16 = jnp.bfloat16
 
@@ -39,6 +39,10 @@
     u = grad * scales
     back = r * u - values * (r * r * r) * jnp.mean(u * values, axis=-1, keepdims=True)
     return back, jnp.sum(grad * values * r, axis=0)
+
+
+def row_major(value):
+    return with_layout_constraint(value, Layout(major_to_minor=tuple(range(value.ndim))))
 
 
 def adamw_update(master, moment_one, moment_two, gradient, step_rate, decay_rate):
@@ -566,41 +570,6 @@
     )(grad, matrix)
 
 
-def times_turned_kernel(a, b, out):
-    out[...] = nt(a[...], b[...]).astype(BF16)
-
-
-def times_turned(a, b):
-    rows, width = a.shape
-    by_rows = lambda n: pl.BlockSpec((BLOCK, n), lambda i: (i, 0))
-    return pl.pallas_call(
-        times_turned_kernel,
-        grid=(rows // BLOCK,),
-        in_specs=[by_rows(width), fixed(b.shape)],
-        out_specs=by_rows(b.shape[0]),
-        out_shape=shaped((rows, b.shape[0]), BF16),
-        **params("times_turned", 2_000_000_000),
-    )(a, b)
-
-
-def two_products_kernel(a, b, c, d, out):
-    out[...] = nn(a[...], b[...]) + nn(c[...], d[...])
-
-
-def two_products(a, b, c, d):
-    rows, depth = a.shape
-    half = b.shape[1] // 2
-    columns = lambda n: pl.BlockSpec((n, half), lambda i: (0, i))
-    return pl.pallas_call(
-        two_products_kernel,
-        grid=(2,),
-        in_specs=[fixed(a.shape), columns(depth), fixed(c.shape), columns(depth)],
-        out_specs=columns(rows),
-        out_shape=shaped((rows, b.shape[1]), F32),
-        **params("two_products", 2_000_000_000),
-    )(a, b, c, d)
-
-
 def flipped(value, axis, bit, name="part"):
     with jax.named_scope(name):
         return lax.ppermute(value, axis, [(i, i ^ bit) for i in range(lax.axis_size(axis))])
@@ -612,29 +581,6 @@
 
 def near_sum(part, beside):
     return part.astype(F32) + flipped(beside, "tensor", 1).astype(F32)
-
-
-def ring_gather(value, place, later):
-    n = len(RING)
-    ring = jnp.array(RING, jnp.int32)
-    at = jnp.argmax(ring == lax.axis_index("dp")).astype(jnp.int32)
-    after = [(RING[i], RING[(i + 1) % n]) for i in range(n)]
-    before = [(b, a) for a, b in after]
-    pieces = {0: value}
-    up = down = value
-    for step in range(1, n // 2 + 1):
-        up = lax.ppermute(up, "dp", after)
-        if step < n // 2:
-            down = lax.ppermute(down, "dp", before)
-        if step == 1:
-            up, down, later = together(up, down, later)
-        pieces[-step] = up
-        if step < n // 2:
-            pieces[step] = down
-    full = None
-    for step, piece in pieces.items():
-        full = place(full, piece, ring[(at + step + n) % n])
-    return full, later
 
 
 def halved(parts, axis, bit):
@@ -667,7 +613,7 @@
     pieces = 2 * hidden_local // half
     gate_rows = pieces * depth
     out_rows = out_heads * out_depth
-    ringed = spread == len(RING)
+    cubic = spread == 8
 
     pack_one = jnp.concatenate(
         [
@@ -692,27 +638,8 @@
             value[..., depth + out_rows, :gain_count],
         )
 
-    if ringed:
-        def place(full, piece, index):
-            if full is None:
-                full = (
-                    jnp.zeros((spread, depth, MODEL_WIDTH), BF16),
-                    jnp.zeros((out_heads, spread, out_depth, MODEL_WIDTH), BF16),
-                    jnp.zeros((spread, gain_count), BF16),
-                )
-            one, two, three = split_one(piece)
-            two = two.reshape(out_heads, out_depth, MODEL_WIDTH)
-            put = lax.dynamic_update_index_in_dim
-            return (
-                put(full[0], one, index, 0), put(full[1], two, index, 1), put(full[2], three, index, 0)
-            )
-
-        (full_qkv, full_out, full_gains), pack_two = ring_gather(pack_one, place, pack_two)
-    else:
-        full_qkv, full_out, full_gains = split_one(
-            lax.all_gather(pack_one, "dp", axis=0, tiled=False)
-        )
-        full_out = full_out.reshape(spread, out_heads, out_depth, MODEL_WIDTH).swapaxes(0, 1)
+    full_qkv, full_out, full_gains = split_one(lax.all_gather(pack_one, "dp", axis=0, tiled=False))
+    full_out = full_out.reshape(spread, out_heads, out_depth, MODEL_WIDTH).swapaxes(0, 1)
     full_two = lax.all_gather(pack_two, "dp", axis=0, tiled=False)
     qkv_matrix = full_qkv.reshape(MODEL_WIDTH, -1)
     out_matrix = full_out.reshape(-1, MODEL_WIDTH)
@@ -766,7 +693,7 @@
     beside = nn(heads_own[local_rows:], out_matrix).astype(BF16)
     attn_rows = near_sum(nn(heads_own[:local_rows], out_matrix), beside) + attn_across.astype(F32)
     middle = rows_float + attn_rows
-    if ringed:
+    if cubic:
         feed_matrices = (full_two,)
     else:
         feed_matrices = (
@@ -799,11 +726,11 @@
     back_across = flipped(near, "tensor", 2, "back_across")
 
     feed_grads = feed_weights(
-        full_two.shape if ringed else None, (h_own, h_other), (feed_grad_own, feed_grad_other),
+        full_two.shape if cubic else None, (h_own, h_other), (feed_grad_own, feed_grad_other),
         (hidden_own, hidden_other), (grad_own, grad_other),
     )
     back_across, *feed_grads = together(back_across, *feed_grads)
-    if ringed:
+    if cubic:
         feed_pack = feed_grads[0]
     else:
         feed_pack = jnp.concatenate(
@@ -828,7 +755,7 @@
     grad_middle_own = jnp.concatenate(
         [grad_middle_low, flipped(grad_middle_low, "tensor", 1)], axis=0
     )
-    grad_heads_own = times_turned(grad_middle_own, out_matrix)
+    grad_heads_own = nt(grad_middle_own, out_matrix).astype(BF16)
     grad_q, grad_k, grad_v, gain_own = attend_back_own(
         info, q, k, v, k_turned, start, logs_own, heads_own, grad_heads_own, raw_q, cos, sin,
         gain_query,
@@ -838,10 +765,10 @@
     grad_middle_other = jnp.concatenate(
         [grad_middle_across, flipped(grad_middle_across, "tensor", 1)], axis=0
     )
-    grad_heads_other = times_turned(grad_middle_other, out_matrix)
-    grad_out_w = two_products(
-        heads_own_turned, grad_middle_own, heads_other_turned, grad_middle_other
-    )
+    grad_heads_other = nt(grad_middle_other, out_matrix).astype(BF16)
+    grad_out_w = (
+        nn(heads_own_turned, grad_middle_own) + nn(heads_other_turned, grad_middle_other)
+    ).astype(BF16)
     near_mlp, grad_out_w, grad_heads_other = together(near_mlp, grad_out_w, grad_heads_other)
     mlp_across = flipped(near_mlp, "tensor", 2, "mlp_across")
     grad_qkv, gain_other = attend_back_other(
@@ -849,18 +776,19 @@
         raw_q, cos, sin, gain_query, raw_k, gain_key, grad_q, grad_k, grad_v,
     )
     grad_qkv, mlp_across = together(grad_qkv, mlp_across)
+    back_2, back_3 = unproject(1, grad_qkv, qkv_matrix)
+    back_2, back_3, grad_qkv = together(back_2, back_3, grad_qkv)
     grad_qkv_w = nn(normed_turned, grad_qkv)
-    grad_qkv, grad_qkv_w = together(grad_qkv, grad_qkv_w)
+    near = near_sum(back_2, back_3).astype(BF16)
+    near, grad_qkv, grad_qkv_w, grad_out_w = together(near, grad_qkv, grad_qkv_w, grad_out_w)
+    back_across = flipped(near, "tensor", 2, "back_across")
     grad_gain_attn = jnp.sum(qkv_matrix.astype(F32) * grad_qkv_w, axis=1) / gain_attn[0]
     grad_gain_heads = jnp.sum(gain_other, axis=0) + jnp.pad(
         jnp.sum(gain_own, axis=0), ((0, 1), (0, 0))
     )
     gain_sums = jnp.concatenate([grad_gain_attn, grad_gain_mlp, grad_gain_heads.reshape(-1)])
-    back_2, back_3 = unproject(1, grad_qkv, qkv_matrix)
     back_0, back_1 = unproject(0, grad_qkv, qkv_matrix)
-    near = near_sum(back_2, back_3).astype(BF16)
-    back_across = flipped(near, "tensor", 2, "back_across")
-    if ringed:
+    if cubic:
         cube = (2, 2, 2)
         columns = grad_qkv_w.shape[1] // 2
         gain_rows = jnp.pad(
@@ -873,15 +801,16 @@
         sum_two = grad_qkv_w[:, columns:].reshape(cube + (depth, -1))
         sum_one, sum_two = halved(sum_one, 1, 2), halved(sum_two, 2, 1)
         sum_one, sum_two = halved(sum_one, 1, 1), halved(sum_two, 1, 2)
-        sum_one, sum_two, back_across, feed_sum = together(
-            sum_one, sum_two, back_across, feed_sum
+        sum_out = grad_out_w.reshape((out_heads,) + cube + (out_depth, MODEL_WIDTH))
+        sum_out = halved(halved(sum_out, 3, 1), 2, 2)
+        sum_one, sum_two, sum_out, back_across, feed_sum = together(
+            sum_one, sum_two, sum_out, back_across, feed_sum
         )
         sum_one, sum_two = halved(sum_one, 0, 4), halved(sum_two, 0, 4)
+        sum_out = halved(sum_out, 1, 4)
         sum_qkv = jnp.concatenate([sum_one[:depth], sum_two], axis=1)
         sum_qkv = sum_qkv.reshape(projection_weight.shape)
         sum_gains = sum_one[depth, :gain_count]
-        sum_out = grad_out_w.reshape((out_heads,) + cube + (out_depth, MODEL_WIDTH))
-        sum_out = halved(halved(halved(sum_out, 2, 2), 2, 1), 1, 4)
     else:
         sum_qkv = (
             lax.psum_scatter(grad_qkv_w.astype(BF16), "dp", scatter_dimension=0, tiled=True)
@@ -889,8 +818,7 @@
             .reshape(projection_weight.shape)
         )
         sum_out = lax.psum_scatter(
-            grad_out_w.astype(BF16).reshape(out_heads, -1, MODEL_WIDTH), "dp",
-            scatter_dimension=1, tiled=True,
+            grad_out_w.reshape(out_heads, -1, MODEL_WIDTH), "dp", scatter_dimension=1, tiled=True
         ).astype(F32)
         sum_gains = lax.psum_scatter(gain_sums, "dp", scatter_dimension=0, tiled=True)
     sum_gains = sum_gains + sum(flipped(sum_gains, "tensor", bit) for bit in range(1, shards))
@@ -908,14 +836,14 @@
 
     upd_qkv = adamw_update(
         projection_weight, first_moment_projection, second_moment_projection,
-        sum_qkv, 2.0 * MODEL_WIDTH ** (-0.5), DECAY,
+        row_major(sum_qkv), 2.0 * MODEL_WIDTH ** (-0.5), DECAY,
     )
     upd_out = adamw_update(
         w_out, first_out, second_out, sum_out,
         2.0 * (QUERY_HEADS * HEAD_SIZE // 64) ** (-0.5), DECAY,
     )
     upd_gate_up = adamw_update(
-        w_gate_up, first_gate_up, second_gate_up, sum_gate_up,
+        w_gate_up, first_gate_up, second_gate_up, row_major(sum_gate_up),
         2.0 * MODEL_WIDTH ** (-0.5), DECAY,
     )
     upd_down = adamw_update(w_down, first_down, second_down, sum_down, 2.0 * FF ** (-0.5), DECAY)

time: 514 us -> 446 us (0.87)
  starting transfers between devices: 56.4 us -> 29.7 us
  local copies, waits for them, and re-layouts: 61.4 us -> 36.6 us
  between operations: 36.7 us -> 15 us
  Pallas kernels: 172 us -> 160 us
  waiting for transfers between devices: 103 us -> 113 us
    ppermute x7 -> x0, waiting for transfers between devices: 40.4 us -> none  [the longest x4 35.4 us: ring_gather(): up = lax.ppermute(up, 'dp', after)]
    all_gather x0 -> x1, waiting for transfers between devices: none -> 27.9 us  [per_device(): lax.all_gather(pack_one, 'dp', axis=0, tiled=False)]
    ppermute x7 -> x0, starting transfers between devices: 14.4 us -> none  [the longest x4 13.3 us: ring_gather(): up = lax.ppermute(up, 'dp', after)]
    dynamic_update_slice x23 -> x0, local copies, waits for them, and re-layouts: 14.1 us -> none  [the longest x8 6.97 us: place(): put(full[0], one, index, 0)]
    pallas_call x3 -> x0, Pallas kernels: 12.5 us -> none  [the longest x2 7.91 us: times_turned(): pl.pallas_call(times_turned_kernel, grid=(rows // BLOCK,), in_specs=[by_r...]
    ppermute x36, starting transfers between devices: 42 us -> 29.6 us  [flipped(): lax.ppermute(value, axis, [(i, i ^ bit) for i in range(lax.axis_size(axis...]
    ppermute x36, waiting for transfers between devices: 62.5 us -> 74.8 us  [flipped(): lax.ppermute(value, axis, [(i, i ^ bit) for i in range(lax.axis_size(axis...]
    all_gather x1, waiting for transfers between devices: 0.01 us -> 10.7 us  [per_device(): full_two = lax.all_gather(pack_two, 'dp', axis=0, tiled=False)]
  transfers between devices with their start and end apart: 45 -> 39, of which waited for: 21 -> 18; matrix products, arithmetic and copies ran while one was open for 23% -> 21% of each run, Pallas kernels for 30% -> 33%
where the time goes in v4:
time: 446 us; the launch traced here: 440 us
  Pallas kernels  160 us (36%)
  waiting for transfers between devices  113 us (25%)
  other arithmetic  64.5 us (14%)
  local copies, waits for them, and re-layouts  36.6 us (8%)
  starting transfers between devices  29.7 us (7%)
  matrix products  20 us (4%)
  between operations  15 us (3%)
    ppermute x36, waiting for transfers between devices, flipped(): lax.ppermute(value, axis, [(i, i ^ bit) for i in range(lax.axis_size(axis...  74.8 us
    pallas_call x2, Pallas kernels, feed(): pl.pallas_call(lambda *refs: feed_kernel(packs, *refs), grid=(rows // BLO...  34 us
    pallas_call x2, Pallas kernels, attend(): pl.pallas_call(lambda *refs: attend_kernel(half * n // BLOCK, *refs), gri...  32.3 us
    pallas_call x1, Pallas kernels, attend_back_other(): pl.pallas_call(back_other_kernel, grid_spec=pltpu.PrefetchScalarGridSpec(...  32.2 us
    ppermute x36, starting transfers between devices, flipped(): lax.ppermute(value, axis, [(i, i ^ bit) for i in range(lax.axis_size(axis...  29.6 us
    all_gather x1, waiting for transfers between devices, per_device(): lax.all_gather(pack_one, 'dp', axis=0, tiled=False)  27.9 us
    pallas_call x1, Pallas kernels, attend_back_own(): pl.pallas_call(back_own_kernel, grid_spec=pltpu.PrefetchScalarGridSpec(nu...  20.2 us
    pallas_call x1, Pallas kernels, feed_weights(): pl.pallas_call(lambda *refs: feed_weights_kernel(packs, pieces, *refs), g...  16.6 us
  transfers between devices with their start and end apart: 39, of which 18 were waited for; matrix products, arithmetic and copies ran while one was open for 21% of the time, Pallas kernels for 33%

profile of v4, /device:TPU:0, one launch (start us, length us, event | category | flops | bytes accessed | tf_op | source)
XLA Modules:
  0.0 439.5 jit_solution(15071261173263886566)
XLA Ops:
  13.0 3.0 collective-permute-start.1
  16.8 23.4 %collective-permute-done.1 = bf16[512,1024]{1,0:T(8,128)(2,1)} collective-permute-done((bf16[512,1024]{1,0:T(8,128)(2,1)S(1)}, bf16[512,1024]{1,0:T(8,128)(2,1)}, u32[]{:S(2)}, u32[]{:S(2)}) %collective-permute-start.1) | collective-permute-done | bytes 1048608 | tf_op jit(solution)/shard_map/tokens_across/ppermute | solution.py:575
  40.1 3.7 fusion.17
  45.5 4.1 pad_maximum_fusion.x
  49.6 27.9 %all-gather.5.cloned.1.call-done = bf16[1664,1024]{1,0:T(8,128)(2,1)} async-done(((bf16[208,1024]{1,0:T(8,128)(2,1)}), bf16[1664,1024]{1,0:T(8,128)(2,1)}) %all-gather.5.cloned.1.call-update) | async-done | bytes 3407888 | tf_op jit(solution)/shard_map/all_gather | solution.py:641
  77.5 3.1 slice.70
  83.8 14.0 %project.1 = (bf16[1024,2048]{1,0:T(8,128)(2,1)}, f32[2048,512]{1,0:T(8,128)}, f32[2048,256]{1,0:T(8,128)}, bf16[2048,512]{1,0:T(8,128)(2,1)}, bf16[2048,256]{1,...) custom-call(bf16[2048,1024]{1,0:T(8,128)(2,1)} %pad_maximum_fusion.x, ...), custom_call_target="tpu_custom_call" | custom-call | flops 156250000 | bytes 1000 | tf_op jit(solution)/shard_map/project/pallas_call | solution.py:383
  98.8 19.5 %attend.2 = (bf16[1024,512]{1,0:T(8,128)(2,1)S(1)}, bf16[512,1024]{1,0:T(8,128)(2,1)S(1)}, f32[2,2,1024]{2,1,0:T(2,128)S(1)}) custom-call(s32[9]{0:T(128)S(1)} %pad_add_fusion.refs_0_.info, bf16[2048,512]{1,0:T(8,128)(2,1)} %get-tuple-element.94.refs_1_.q, bf16[2048,256]{1,0:T(8,128)(2,1)S(1)} %get-tuple-element.90.refs_2_.k, ...), custom_call_target="tpu_custom_call" | custom-call | flops 281249984 | bytes 1000 | tf_op jit(solution)/shard_map/attend/pallas_call | solution.py:422
  122.8 12.8 %attend.3 = (bf16[1024,512]{1,0:T(8,128)(2,1)S(1)}, bf16[512,1024]{1,0:T(8,128)(2,1)S(1)}, f32[2,2,1024]{2,1,0:T(2,128)S(1)}) custom-call(s32[9]{0:T(128)S(1)} %pad_add_fusion.refs_0_.info, bf16[2048,512]{1,0:T(8,128)(2,1)} %get-tuple-element.94.refs_1_.q, bf16[2048,256]{1,0:T(8,128)(2,1)S(1)} %get-tuple-element.90.refs_2_.k, ...), custom_call_target="tpu_custom_call" | custom-call | flops 281249984 | bytes 1000 | tf_op jit(solution)/shard_map/attend/pallas_call | solution.py:422
  136.6 11.4 %collective-permute-done.5 = bf16[512,1024]{1,0:T(8,128)(2,1)} collective-permute-done((bf16[512,1024]{1,0:T(8,128)(2,1)S(1)}, bf16[512,1024]{1,0:T(8,128)(2,1)}, u32[]{:S(2)}, u32[]{:S(2)}) %collective-permute-start.5) | collective-permute-done | bytes 1048608 | tf_op jit(solution)/shard_map/attn_across/ppermute | solution.py:575
  148.0 10.7 %all-gather.7.cloned.1.call-done = bf16[4608,512]{1,0:T(8,128)(2,1)} async-done(((bf16[576,512]{1,0:T(8,128)(2,1)}), bf16[4608,512]{1,0:T(8,128)(2,1)}) %all-gather.7.cloned.1.call-update) | async-done | bytes 4718608 | tf_op jit(solution)/shard_map/all_gather | solution.py:643
  171.5 17.1 %feed.2 = (bf16[1024,1024]{1,0:T(8,128)(2,1)}, bf16[768,1024]{1,0:T(8,128)(2,1)S(1)}, bf16[1024,1536]{1,0:T(8,128)(2,1)}, bf16[512,1024]{1,0:T(8,128)(2,1)S(1)},...) custom-call(bf16[1024,1024]{1,0:T(8,128)(2,1)} %pad_maximum_fusion.1.refs_0_, ...), custom_call_target="tpu_custom_call" | custom-call | flops 250000000 | bytes 1000 | tf_op jit(solution)/shard_map/feed/pallas_call | solution.py:520
  188.6 3.4 collective-permute-done.10
  196.2 16.9 %feed.3 = (bf16[1024,1024]{1,0:T(8,128)(2,1)}, bf16[768,1024]{1,0:T(8,128)(2,1)S(1)}, bf16[1024,1536]{1,0:T(8,128)(2,1)}, bf16[512,1024]{1,0:T(8,128)(2,1)S(1)},...) custom-call(bf16[1024,1024]{1,0:T(8,128)(2,1)} %pad_maximum_fusion.2.refs_0_, ...), custom_call_target="tpu_custom_call" | custom-call | flops 250000000 | bytes 1000 | tf_op jit(solution)/shard_map/feed/pallas_call | solution.py:520
  220.6 16.6 %feed_weights.1 = bf16[8,576,512]{2,1,0:T(8,128)(2,1)} custom-call(bf16[1024,1024]{1,0:T(8,128)(2,1)S(1)} %copy-done.11, bf16[1024,1024]{1,0:T(8,128)(2,1)} %get-tuple-element.115.refs_1_, bf16[1024,1536]{1,0:T(8,128)(2,1)} %get-tuple-element.116.refs_2_, bf16[1024,1536]{1,0:T(8,128)(2,1)} %get-tuple-element.117.refs_3_, ...), custom_call_target="tpu_custom_call" | custom-call | flops 250000000 | bytes 1000 | tf_op jit(solution)/shard_map/feed_weights/pallas_call | solution.py:545
  237.1 7.5 %collective-permute-done.15 = bf16[512,1024]{1,0:T(8,128)(2,1)} collective-permute-done((bf16[512,1024]{1,0:T(8,128)(2,1)}, bf16[512,1024]{1,0:T(8,128)(2,1)}, u32[]{:S(2)}, u32[]{:S(2)}) %collective-permute-start.15) | collective-permute-done | bytes 1048608 | tf_op jit(solution)/shard_map/back_across/ppermute | solution.py:575
  244.6 3.1 multiply_reduce_fusion.1
  247.8 4.5 %fusion.34 = (bf16[512,1024]{1,0:T(8,128)(2,1)}, f32[512,1024]{1,0:T(8,128)}) fusion(f32[512]{0:T(512)S(1)} %broadcast_multiply_fusion.1, f32[512,1024]{1,0:T(8,128)S(1)} %copy-done.27, f32[512]{0:T(512)S(1)} %get-tuple-element.197, f32[1024]{0:T(1024)S(1)} %get-tuple-element.188, bf16[512,1024]{1,0:T(8,128)(2,1)} %collective-permute-done.15, ...), kind=kLoop, calls=%fused_computation.136 | loop fusion | flops 6815744 | bytes 9447424 | tf_op jit(solution)/shard_map/convert_element_type | solution.py:752
  255.2 3.8 convolution_convert_fusion.1.grad_out
  259.1 20.2 %attend_back_own.1 = (bf16[1024,512]{1,0:T(8,128)(2,1)S(1)}, f32[2048,256]{1,0:T(8,128)}, f32[2048,256]{1,0:T(8,128)}, f32[2,1,128]{2,1,0:T(1,128)S(1)}) custom-call(s32[9]{0:T(128)S(1)} %pad_add_fusion.refs_0_.info, bf16[2048,512]{1,0:T(8,128)(2,1)} %get-tuple-element.94.refs_1_.q, bf16[2048,256]{1,0:T(8,128)(2,1)S(1)} %get-tuple-element.90.refs_2_.k, ...), custom_call_target="tpu_custom_call" | custom-call | flops 390624992 | bytes 1000 | tf_op jit(solution)/shard_map/attend_back_own/pallas_call | solution.py:444
  288.5 3.9 add_convert_fusion.2
  292.4 8.1 %collective-permute-start.20 = (bf16[512,1024]{1,0:T(8,128)(2,1)}, bf16[512,1024]{1,0:T(8,128)(2,1)}, u32[]{:S(2)}, u32[]{:S(2)}) collective-permute-start(bf16[512,1024]{1,0:T(8,128)(2,1)} %add_convert_fusion.3), channel_id=1, source_target_pairs={{0,2},{1,3},{2,0},{3,1},{4,6},{5,7},{6,4},{7,5},{8,10},{9,11},{10,... | collective-permute-start | bytes 3145736 | tf_op jit(solution)/shard_map/mlp_across/ppermute | solution.py:575
  305.4 32.2 %attend_back_other.1 = (bf16[2048,1024]{1,0:T(8,128)(2,1)}, f32[2,2,128]{2,1,0:T(2,128)S(1)}) custom-call(s32[9]{0:T(128)S(1)} %pad_add_fusion.refs_0_.info, bf16[2048,512]{1,0:T(8,128)(2,1)} %get-tuple-element.94.refs_1_.q, bf16[2048,256]{1,0:T(8,128)(2,1)S(1)} %copy-done.3, bf16[2048,256]{1,0:T(8,128)(2,1)S(1)} %copy-done.5, ...), custom_call_target="tpu_custom_call" | custom-call | flops 437500000 | bytes 1000 | tf_op jit(solution)/shard_map/attend_back_other/pallas_call | solution.py:475
  337.7 5.6 %unproject.2 = (bf16[512,1024]{1,0:T(8,128)(2,1)S(1)}, bf16[512,1024]{1,0:T(8,128)(2,1)S(1)}) custom-call(bf16[2048,1024]{1,0:T(8,128)(2,1)} %get-tuple-element.147.grad, bf16[1024,1024]{1,0:T(8,128)(2,1)S(1)} %bitcast.105), custom_call_target="tpu_custom_call" | custom-call | flops 62500000 | bytes 1000 | tf_op jit(solution)/shard_map/unproject/pallas_call | solution.py:563
  343.9 3.5 add_convert_fusion.1
  347.4 4.5 %fusion.38 = f32[1024,1024]{1,0:T(8,128)S(1)} fusion(bf16[1024,2048]{1,0:T(8,128)(2,1)S(1)} %copy-done.63, bf16[2048,1024]{1,0:T(8,128)(2,1)S(1)} %copy-done.29), kind=kOutput, calls=%fused_computation.140 | convolution fusion | flops 4294967296 | bytes 12582912 | tf_op jit(solution)/shard_map/dot_general | solution.py:64
  362.8 5.4 %unproject.3 = (bf16[512,1024]{1,0:T(8,128)(2,1)S(1)}, bf16[512,1024]{1,0:T(8,128)(2,1)}) custom-call(bf16[2048,1024]{1,0:T(8,128)(2,1)} %get-tuple-element.147.grad, bf16[1024,1024]{1,0:T(8,128)(2,1)S(1)} %bitcast.106), custom_call_target="tpu_custom_call" | custom-call | flops 62500000 | bytes 1000 | tf_op jit(solution)/shard_map/unproject/pallas_call | solution.py:563
  371.5 8.9 %collective-permute-done.25 = bf16[2,2,128,512]{3,2,0,1:T(8,128)(2,1)} collective-permute-done((bf16[2,2,128,512]{3,2,0,1:T(8,128)(2,1)}, bf16[2,2,128,512]{3,2,0,1:T(8,128)(2,1)}, u32[]{:S(2)}, u32[]{:S(2)}) %collective-permute-start.25) | collective-permute-done | bytes 524320 | tf_op jit(solution)/shard_map/part/ppermute | solution.py:575
  383.9 5.3 %collective-permute-done.26 = bf16[2,128,512]{2,1,0:T(8,128)(2,1)S(1)} collective-permute-done((bf16[2,128,512]{2,1,0:T(8,128)(2,1)S(1)}, bf16[2,128,512]{2,1,0:T(8,128)(2,1)S(1)}, u32[]{:S(2)}, u32[]{:S(2)}) %collective-permute-start.26) | collective-permute-done | bytes 262176 | tf_op jit(solution)/shard_map/part/ppermute | solution.py:575
  395.1 4.0 collective-permute-start.30
  412.8 5.3 %multiply_subtract_fusion = (f32[128,2,768]{2,1,0:T(2,128)}, f32[128,2,768]{2,1,0:T(2,128)}, f32[128,2,768]{2,1,0:T(2,128)}) fusion(f32[128,2,768]{2,1,0:T(2,128)S(1)} %copy-done.44, f32[128,2,768]{2,1,0:T(2,128)} %copy.94, f32[128,2,768]{2,1,0:T(2,128)} %param.28, f32[128,2,768]{2,1,0:T(2,128)} %param.33), kind=kLoop, calls=%fused_computation.46 | loop fusion | flops 2949120 | bytes 5505024 | tf_op jit(solution)/shard_map/sub | solution.py:53
  418.1 3.9 fusion.3
  (299 shorter events, 107.4 us)
Async XLA Ops:
  7.2 70.3 %all-gather.5.cloned.1.call-start = ((), (), s32[]{:S(2)}) async-start(), calls=%async_computation.2 | async-start | bytes 3833856 | tf_op jit(solution)/shard_map/all_gather | solution.py:641
  11.1 147.6 %all-gather.7.cloned.1.call-start = ((), (), s32[]{:S(2)}) async-start(), calls=%async_computation.3 | async-start | bytes 5308416 | tf_op jit(solution)/shard_map/all_gather | solution.py:643
  12.9 378.2 %reduce-scatter.2.cloned.1.call-start = ((), (), s32[]{:S(2)}) async-start(), calls=%async_computation.1 | async-start | bytes 5308416 | tf_op jit(solution)/shard_map/reduce_scatter | solution.py:747
  13.0 27.1 %collective-permute-start.1 = (bf16[512,1024]{1,0:T(8,128)(2,1)S(1)}, bf16[512,1024]{1,0:T(8,128)(2,1)}, u32[]{:S(2)}, u32[]{:S(2)}) collective-permute-start(bf16[512,1024]{1,0:T(8,128)(2,1)S(1)} %copy-done.30), channel_id=1, source_target_pairs={{0,2},{1,3},{2,0},{3,1},{4,6},{5,7},{6,4},{7,5},{8,10},{9,11},{10,... | collective-permute-start | bytes 3145736 | tf_op jit(solution)/shard_map/tokens_across/ppermute | solution.py:575
  16.0 29.5 %collective-permute-start = (bf16[512,1024]{1,0:T(8,128)(2,1)S(1)}, bf16[512,1024]{1,0:T(8,128)(2,1)}, u32[]{:S(2)}, u32[]{:S(2)}) collective-permute-start(bf16[512,1024]{1,0:T(8,128)(2,1)S(1)} %copy-done.30), channel_id=1, source_target_pairs={{0,1},{1,0},{2,3},{3,2},{4,5},{5,4},{6,7},{7,6},{8,9},{9,8},{10,11... | collective-permute-start | bytes 3145736 | tf_op jit(solution)/shard_map/part/ppermute | solution.py:575
  16.0 102.3 %collective-permute-start.3 = (bf16[512,1024]{1,0:T(8,128)(2,1)}, bf16[512,1024]{1,0:T(8,128)(2,1)}, u32[]{:S(2)}, u32[]{:S(2)}) collective-permute-start(bf16[512,1024]{1,0:T(8,128)(2,1)} %param.19), channel_id=1, source_target_pairs={{0,2},{1,3},{2,0},{3,1},{4,6},{5,7},{6,4},{7,5},{8,10},{9,11},{10,... | collective-permute-start | bytes 3145736 | tf_op jit(solution)/shard_map/grad_across/ppermute | solution.py:575
  40.1 5.4 %collective-permute-start.2 = (bf16[512,1024]{1,0:T(8,128)(2,1)}, bf16[512,1024]{1,0:T(8,128)(2,1)}, u32[]{:S(2)}, u32[]{:S(2)}) collective-permute-start(bf16[512,1024]{1,0:T(8,128)(2,1)} %collective-permute-done.1), channel_id=1, source_target_pairs={{0,1},{1,0},{2,3},{3,2},{4,5},{5,4},{6,7},{7,6},{8,9},{9,8},{10,11... | collective-permute-start | bytes 3145736 | tf_op jit(solution)/shard_map/part/ppermute | solution.py:575
  122.7 25.4 %collective-permute-start.5 = (bf16[512,1024]{1,0:T(8,128)(2,1)S(1)}, bf16[512,1024]{1,0:T(8,128)(2,1)}, u32[]{:S(2)}, u32[]{:S(2)}) collective-permute-start(bf16[512,1024]{1,0:T(8,128)(2,1)S(1)} %add_convert_fusion.5), channel_id=1, source_target_pairs={{0,2},{1,3},{2,0},{3,1},{4,6},{5,7},{6,4},{7,5},{8,10},{9,11},{10,... | collective-permute-start | bytes 3145736 | tf_op jit(solution)/shard_map/attn_across/ppermute | solution.py:575
  160.8 8.5 %collective-permute-start.8 = (bf16[512,1024]{1,0:T(8,128)(2,1)}, bf16[512,1024]{1,0:T(8,128)(2,1)S(1)}, u32[]{:S(2)}, u32[]{:S(2)}) collective-permute-start(bf16[512,1024]{1,0:T(8,128)(2,1)} %param.19), channel_id=1, source_target_pairs={{0,1},{1,0},{2,3},{3,2},{4,5},{5,4},{6,7},{7,6},{8,9},{9,8},{10,11... | collective-permute-start | bytes 3145736 | tf_op jit(solution)/shard_map/part/ppermute | solution.py:575
  166.5 25.4 %collective-permute-start.10 = (bf16[512,1024]{1,0:T(8,128)(2,1)S(1)}, bf16[512,1024]{1,0:T(8,128)(2,1)S(1)}, u32[]{:S(2)}, u32[]{:S(2)}) collective-permute-start(bf16[512,1024]{1,0:T(8,128)(2,1)S(1)} %multiply_convert_fusion), channel_id=1, source_target_pairs={{0,2},{1,3},{2,0},{3,1},{4,6},{5,7},{6,4},{7,5},{8,10},{9,11},{10,... | collective-permute-start | bytes 3145736 | tf_op jit(solution)/shard_map/normed_across/ppermute | solution.py:575
  169.5 23.8 %collective-permute-start.13 = (bf16[512,1024]{1,0:T(8,128)(2,1)}, bf16[512,1024]{1,0:T(8,128)(2,1)S(1)}, u32[]{:S(2)}, u32[]{:S(2)}) collective-permute-start(bf16[512,1024]{1,0:T(8,128)(2,1)} %collective-permute-done.3), channel_id=1, source_target_pairs={{0,1},{1,0},{2,3},{3,2},{4,5},{5,4},{6,7},{7,6},{8,9},{9,8},{10,11... | collective-permute-start | bytes 3145736 | tf_op jit(solution)/shard_map/part/ppermute | solution.py:575
  219.1 25.5 %collective-permute-start.15 = (bf16[512,1024]{1,0:T(8,128)(2,1)}, bf16[512,1024]{1,0:T(8,128)(2,1)}, u32[]{:S(2)}, u32[]{:S(2)}) collective-permute-start(bf16[512,1024]{1,0:T(8,128)(2,1)} %add_convert_fusion.4), channel_id=1, source_target_pairs={{0,2},{1,3},{2,0},{3,1},{4,6},{5,7},{6,4},{7,5},{8,10},{9,11},{10,... | collective-permute-start | bytes 3145736 | tf_op jit(solution)/shard_map/back_across/ppermute | solution.py:575
  220.6 24.1 %collective-permute-start.11 = (bf16[512,1024]{1,0:T(8,128)(2,1)}, bf16[512,1024]{1,0:T(8,128)(2,1)}, u32[]{:S(2)}, u32[]{:S(2)}) collective-permute-start(bf16[512,1024]{1,0:T(8,128)(2,1)} %get-tuple-element.107), channel_id=1, source_target_pairs={{0,1},{1,0},{2,3},{3,2},{4,5},{5,4},{6,7},{7,6},{8,9},{9,8},{10,11... | collective-permute-start | bytes 3145736 | tf_op jit(solution)/shard_map/part/ppermute | solution.py:575
  252.2 27.0 %collective-permute-start.16 = (bf16[512,1024]{1,0:T(8,128)(2,1)}, bf16[512,1024]{1,0:T(8,128)(2,1)}, u32[]{:S(2)}, u32[]{:S(2)}) collective-permute-start(bf16[512,1024]{1,0:T(8,128)(2,1)} %get-tuple-element.180), channel_id=1, source_target_pairs={{0,2},{1,3},{2,0},{3,1},{4,6},{5,7},{6,4},{7,5},{8,10},{9,11},{10,... | collective-permute-start | bytes 3145736 | tf_op jit(solution)/shard_map/grad_middle_across/ppermute | solution.py:575
  279.5 4.0 collective-permute-start.18
  292.4 45.3 %collective-permute-start.20 = (bf16[512,1024]{1,0:T(8,128)(2,1)}, bf16[512,1024]{1,0:T(8,128)(2,1)}, u32[]{:S(2)}, u32[]{:S(2)}) collective-permute-start(bf16[512,1024]{1,0:T(8,128)(2,1)} %add_convert_fusion.3), channel_id=1, source_target_pairs={{0,2},{1,3},{2,0},{3,1},{4,6},{5,7},{6,4},{7,5},{8,10},{9,11},{10,... | collective-permute-start | bytes 3145736 | tf_op jit(solution)/shard_map/mlp_across/ppermute | solution.py:575
  300.5 43.4 %collective-permute-start.9 = (bf16[512,1024]{1,0:T(8,128)(2,1)}, bf16[512,1024]{1,0:T(8,128)(2,1)}, u32[]{:S(2)}, u32[]{:S(2)}) collective-permute-start(bf16[512,1024]{1,0:T(8,128)(2,1)} %get-tuple-element.101), channel_id=1, source_target_pairs={{0,1},{1,0},{2,3},{3,2},{4,5},{5,4},{6,7},{7,6},{8,9},{9,8},{10,11... | collective-permute-start | bytes 3145736 | tf_op jit(solution)/shard_map/part/ppermute | solution.py:575
  343.3 8.6 %collective-permute-start.21 = (bf16[512,1024]{1,0:T(8,128)(2,1)S(1)}, bf16[512,1024]{1,0:T(8,128)(2,1)S(1)}, u32[]{:S(2)}, u32[]{:S(2)}) collective-permute-start(bf16[512,1024]{1,0:T(8,128)(2,1)S(1)} %get-tuple-element.143), channel_id=1, source_target_pairs={{0,1},{1,0},{2,3},{3,2},{4,5},{5,4},{6,7},{7,6},{8,9},{9,8},{10,11... | collective-permute-start | bytes 3145736 | tf_op jit(solution)/shard_map/part/ppermute | solution.py:575
  355.0 15.1 %collective-permute-start.27 = (bf16[4,2,2,16,1024]{4,3,0,1,2:T(8,128)(2,1)}, bf16[4,2,2,16,1024]{4,3,0,1,2:T(8,128)(2,1)}, u32[]{:S(2)}, u32[]{:S(2)}) collective-permute-start(bf16[4,2,2,16,1024]{4,3,0,1,2:T(8,128)(2,1)} %bitcast.103), channel_id=1, source_target_pairs={{0,4},{4,0},{8,12},{12,8},{16,20},{20,16},{24,28},{28,24},{1,5},{5... | collective-permute-start | bytes 1572872 | tf_op jit(solution)/shard_map/part/ppermute | solution.py:575
  357.8 22.6 %collective-permute-start.25 = (bf16[2,2,128,512]{3,2,0,1:T(8,128)(2,1)}, bf16[2,2,128,512]{3,2,0,1:T(8,128)(2,1)}, u32[]{:S(2)}, u32[]{:S(2)}) collective-permute-start(bf16[2,2,128,512]{3,2,0,1:T(8,128)(2,1)} %fusion.9), channel_id=1, source_target_pairs={{0,4},{4,0},{8,12},{12,8},{16,20},{20,16},{24,28},{28,24},{1,5},{5... | collective-permute-start | bytes 1572872 | tf_op jit(solution)/shard_map/part/ppermute | solution.py:575
  362.6 19.2 %collective-permute-start.23 = (bf16[2,2,144,512]{3,2,0,1:T(8,128)(2,1)S(1)}, bf16[2,2,144,512]{3,2,0,1:T(8,128)(2,1)S(1)}, u32[]{:S(2)}, u32[]{:S(2)}) collective-permute-start(bf16[2,2,144,512]{3,2,0,1:T(8,128)(2,1)S(1)} %fusion.7), channel_id=1, source_target_pairs={{0,8},{4,12},{8,0},{12,4},{16,24},{20,28},{24,16},{28,20},{1,9},{5... | collective-permute-start | bytes 1769480 | tf_op jit(solution)/shard_map/part/ppermute | solution.py:575
  362.7 29.8 %collective-permute-start.29 = (bf16[512,1024]{1,0:T(8,128)(2,1)}, bf16[512,1024]{1,0:T(8,128)(2,1)}, u32[]{:S(2)}, u32[]{:S(2)}) collective-permute-start(bf16[512,1024]{1,0:T(8,128)(2,1)} %add_convert_fusion), channel_id=1, source_target_pairs={{0,2},{1,3},{2,0},{3,1},{4,6},{5,7},{6,4},{7,5},{8,10},{9,11},{10,... | collective-permute-start | bytes 3145736 | tf_op jit(solution)/shard_map/back_across/ppermute | solution.py:575
  368.1 37.2 %collective-permute-start.22 = (bf16[512,1024]{1,0:T(8,128)(2,1)}, bf16[512,1024]{1,0:T(8,128)(2,1)}, u32[]{:S(2)}, u32[]{:S(2)}) collective-permute-start(bf16[512,1024]{1,0:T(8,128)(2,1)} %get-tuple-element.149), channel_id=1, source_target_pairs={{0,1},{1,0},{2,3},{3,2},{4,5},{5,4},{6,7},{7,6},{8,9},{9,8},{10,11... | collective-permute-start | bytes 3145736 | tf_op jit(solution)/shard_map/part/ppermute | solution.py:575
  371.4 11.6 %collective-permute-start.28 = (bf16[4,2,16,1024]{3,2,0,1:T(8,128)(2,1)S(1)}, bf16[4,2,16,1024]{3,2,0,1:T(8,128)(2,1)S(1)}, u32[]{:S(2)}, u32[]{:S(2)}) collective-permute-start(bf16[4,2,16,1024]{3,2,0,1:T(8,128)(2,1)S(1)} %fusion.21), channel_id=1, source_target_pairs={{0,8},{4,12},{8,0},{12,4},{16,24},{20,28},{24,16},{28,20},{1,9},{5... | collective-permute-start | bytes 786440 | tf_op jit(solution)/shard_map/part/ppermute | solution.py:575
  381.7 7.5 %collective-permute-start.26 = (bf16[2,128,512]{2,1,0:T(8,128)(2,1)S(1)}, bf16[2,128,512]{2,1,0:T(8,128)(2,1)S(1)}, u32[]{:S(2)}, u32[]{:S(2)}) collective-permute-start(bf16[2,128,512]{2,1,0:T(8,128)(2,1)S(1)} %fusion.20), channel_id=1, source_target_pairs={{0,8},{4,12},{8,0},{12,4},{16,24},{20,28},{24,16},{28,20},{1,9},{5... | collective-permute-start | bytes 786440 | tf_op jit(solution)/shard_map/part/ppermute | solution.py:575
  382.0 8.2 %collective-permute-start.24 = (bf16[2,144,512]{2,1,0:T(8,128)(2,1)S(1)}, bf16[2,144,512]{2,1,0:T(8,128)(2,1)S(1)}, u32[]{:S(2)}, u32[]{:S(2)}) collective-permute-start(bf16[2,144,512]{2,1,0:T(8,128)(2,1)S(1)} %fusion.18), channel_id=1, source_target_pairs={{0,4},{4,0},{8,12},{12,8},{16,20},{20,16},{24,28},{28,24},{1,5},{5... | collective-permute-start | bytes 884744 | tf_op jit(solution)/shard_map/part/ppermute | solution.py:575
  395.1 31.6 %collective-permute-start.30 = (bf16[144,512]{1,0:T(8,128)(2,1)}, bf16[144,512]{1,0:T(8,128)(2,1)S(1)}, u32[]{:S(2)}, u32[]{:S(2)}) collective-permute-start(bf16[144,512]{1,0:T(8,128)(2,1)} %fusion.22), channel_id=1, source_target_pairs={{0,16},{4,20},{8,24},{12,28},{16,0},{20,4},{24,8},{28,12},{1,17},{... | collective-permute-start | bytes 442376 | tf_op jit(solution)/shard_map/part/ppermute | solution.py:575
  400.8 22.5 %collective-permute-start.32 = (bf16[4,16,1024]{2,1,0:T(8,128)(2,1)}, bf16[4,16,1024]{2,1,0:T(8,128)(2,1)}, u32[]{:S(2)}, u32[]{:S(2)}) collective-permute-start(bf16[4,16,1024]{2,1,0:T(8,128)(2,1)} %fusion.24), channel_id=1, source_target_pairs={{0,16},{4,20},{8,24},{12,28},{16,0},{20,4},{24,8},{28,12},{1,17},{... | collective-permute-start | bytes 393224 | tf_op jit(solution)/shard_map/part/ppermute | solution.py:575
  402.4 23.2 %collective-permute-start.31 = (bf16[128,512]{1,0:T(8,128)(2,1)}, bf16[128,512]{1,0:T(8,128)(2,1)}, u32[]{:S(2)}, u32[]{:S(2)}) collective-permute-start(bf16[128,512]{1,0:T(8,128)(2,1)} %fusion.23), channel_id=1, source_target_pairs={{0,16},{4,20},{8,24},{12,28},{16,0},{20,4},{24,8},{28,12},{1,17},{... | collective-permute-start | bytes 393224 | tf_op jit(solution)/shard_map/part/ppermute | solution.py:575
  426.8 5.4 %collective-permute-start.33 = (f32[288]{0:T(512)S(1)}, f32[288]{0:T(512)S(1)}, u32[]{:S(2)}, u32[]{:S(2)}) collective-permute-start(f32[288]{0:T(512)S(1)} %slice_reduce_fusion), channel_id=1, source_target_pairs={{0,1},{1,0},{2,3},{3,2},{4,5},{5,4},{6,7},{7,6},{8,9},{9,8},{10,11... | collective-permute-start | bytes 3464 | tf_op jit(solution)/shard_map/part/ppermute | solution.py:575
  426.8 5.3 %collective-permute-start.34 = (f32[288]{0:T(512)S(1)}, f32[288]{0:T(512)S(1)}, u32[]{:S(2)}, u32[]{:S(2)}) collective-permute-start(f32[288]{0:T(512)S(1)} %slice_reduce_fusion), channel_id=1, source_target_pairs={{0,2},{1,3},{2,0},{3,1},{4,6},{5,7},{6,4},{7,5},{8,10},{9,11},{10,... | collective-permute-start | bytes 3464 | tf_op jit(solution)/shard_map/part/ppermute | solution.py:575
  426.9 5.3 %collective-permute-start.35 = (f32[288]{0:T(512)S(1)}, f32[288]{0:T(512)S(1)}, u32[]{:S(2)}, u32[]{:S(2)}) collective-permute-start(f32[288]{0:T(512)S(1)} %slice_reduce_fusion), channel_id=1, source_target_pairs={{0,3},{1,2},{2,1},{3,0},{4,7},{5,6},{6,5},{7,4},{8,11},{9,10},{10,... | collective-permute-start | bytes 3464 | tf_op jit(solution)/shard_map/part/ppermute | solution.py:575
  (73 other events, 715.4 us)
Sparse Core Ops, SparseCore 0:
  11.2 66.2 all-gather.4
  80.2 78.4 all-gather.6
  253.9 92.5 reduce-scatter.1

commit v5 on v4

--- a/solution.py
+++ b/solution.py
@@ -25,7 +25,8 @@
 SCALE = HEAD_SIZE ** (-0.5)
 LOG2E = 1.4426950408889634
 BLOCK = 256
-VMEM_LIMIT = 48 * 1024 * 1024
+WIDE_BLOCK = 512
+VMEM_LIMIT = 56 * 1024 * 1024
 F32 = jnp.float32
 BF16 = jnp.bfloat16
 
@@ -116,37 +117,45 @@
         v_turned[lanes_of(j), :] = value.T.astype(BF16)
 
 
+def heads_of(k):
+    return [(j, j * GROUP + g) for j in range(k.shape[1] // HEAD_SIZE) for g in range(GROUP)]
+
+
 def attend_kernel(offset, info, q, k, v_turned, start, out, out_turned, logs):
     blocks = k.shape[0] // BLOCK
     flip = info[blocks]
+    pairs = heads_of(k)
 
     def one_block(i, _):
         here = at_block(i)
         b = (i + offset) ^ flip
         first = start[:, here]
-        queries = [q[here, lanes_of(h)] for h in range(GROUP)]
+        queries = [q[here, lanes_of(h)] for _, h in pairs]
 
         def keys_step(kb, carry):
             there = at_block(kb ^ flip)
-            key, value = k[there, :], v_turned[:, there]
             allowed = allowed_block(kb, b, first)
             after = []
-            for h in range(GROUP):
+            for j, h in pairs:
                 total, blend = carry[h]
-                p = jnp.where(allowed, jnp.exp2(nt(key, queries[h]) * (SCALE * LOG2E)), 0.0)
+                score = nt(k[there, lanes_of(j)], queries[h])
+                p = jnp.where(allowed, jnp.exp2(score * (SCALE * LOG2E)), 0.0)
                 after.append(
-                    (total + jnp.sum(p, axis=0, keepdims=True), blend + nn(value, p.astype(BF16)))
+                    (
+                        total + jnp.sum(p, axis=0, keepdims=True),
+                        blend + nn(v_turned[lanes_of(j), there], p.astype(BF16)),
+                    )
                 )
             return tuple(after)
 
         zero = (jnp.zeros((1, BLOCK), F32), jnp.zeros((HEAD_SIZE, BLOCK), F32))
-        done = lax.fori_loop(info[b], b + 1, keys_step, (zero,) * GROUP)
-        for h in range(GROUP):
+        done = lax.fori_loop(info[b], b + 1, keys_step, (zero,) * len(pairs))
+        for _, h in pairs:
             total, blend = done[h]
             result = blend / total
             out[here, lanes_of(h)] = result.T.astype(BF16)
             out_turned[lanes_of(h), here] = result.astype(BF16)
-            logs[0, h : h + 1, here] = jnp.log2(total)
+            logs[h : h + 1, here] = jnp.log2(total)
         return 0
 
     lax.fori_loop(0, q.shape[0] // BLOCK, one_block, 0)
@@ -157,40 +166,39 @@
     grad_k, grad_v, store,
 ):
     flip = info[k.shape[0] // BLOCK]
+    pairs = heads_of(k)
 
     def one_block(i, total_gain):
         here = at_block(i)
         b = (i + offset) ^ flip
         first = start[:, here]
-        queries, gradients, across, log = [], [], [], []
-        for h in range(GROUP):
-            g = grad_out[here, lanes_of(h)]
-            queries.append(q[here, lanes_of(h)])
-            gradients.append(g)
-            both = g.astype(F32) * out[here, lanes_of(h)].astype(F32)
+        across = []
+        for _, h in pairs:
+            both = grad_out[here, lanes_of(h)].astype(F32) * out[here, lanes_of(h)].astype(F32)
             across.append(jnp.sum(both.T, axis=0, keepdims=True))
-            log.append(logs[0, h : h + 1, here])
 
         def keys_step(kb, carry):
             there = at_block(kb ^ flip)
-            key, value, key_turned = k[there, :], v[there, :], k_turned[:, there]
             allowed = allowed_block(kb, b, first)
-            after, add_k, add_v = [], 0.0, 0.0
-            for h in range(GROUP):
-                s = nt(key, queries[h])
-                p = jnp.where(allowed, jnp.exp2(s * (SCALE * LOG2E) - log[h]), 0.0)
-                d = (p * (nt(value, gradients[h]) - across[h])).astype(BF16)
-                add_v = add_v + nn(p.astype(BF16), gradients[h])
-                add_k = add_k + nn(d, queries[h])
-                after.append(carry[h] + nn(key_turned, d))
-            grad_k[there, :] += add_k
-            grad_v[there, :] += add_v
+            after = []
+            add_k, add_v = [0.0] * (len(pairs) // GROUP), [0.0] * (len(pairs) // GROUP)
+            for j, h in pairs:
+                query, gradient = q[here, lanes_of(h)], grad_out[here, lanes_of(h)]
+                s = nt(k[there, lanes_of(j)], query)
+                p = jnp.where(allowed, jnp.exp2(s * (SCALE * LOG2E) - logs[h : h + 1, here]), 0.0)
+                d = (p * (nt(v[there, lanes_of(j)], gradient) - across[h])).astype(BF16)
+                add_v[j] = add_v[j] + nn(p.astype(BF16), gradient)
+                add_k[j] = add_k[j] + nn(d, query)
+                after.append(carry[h] + nn(k_turned[lanes_of(j), there], d))
+            for j in range(len(add_k)):
+                grad_k[there, lanes_of(j)] += add_k[j]
+                grad_v[there, lanes_of(j)] += add_v[j]
             return tuple(after)
 
         zero = jnp.zeros((HEAD_SIZE, BLOCK), F32)
-        done = lax.fori_loop(info[b], b + 1, keys_step, (zero,) * GROUP)
+        done = lax.fori_loop(info[b], b + 1, keys_step, (zero,) * len(pairs))
         c, s = cos[here, :], sin[here, :]
-        for h in range(GROUP):
+        for _, h in pairs:
             back, gain = head_back(raw_q[here, lanes_of(h)], gain_q[...], c, s, done[h].T * SCALE)
             store(i, h, back.astype(BF16))
             total_gain = total_gain + gain
@@ -209,10 +217,14 @@
     def store(i, h, value):
         grad_q[at_block(i), lanes_of(h)] = value
 
-    grad_gain[0, :, :] = back_blocks(
+    grad_gain[...] = back_blocks(
         0, info, q, k, v, k_turned, start, logs, out, grad_out, raw_q, cos, sin, gain_q,
         grad_k, grad_v, store,
     )
+
+
+def slot_lanes(j, slot):
+    return lanes_of(j * SLOTS + slot)
 
 
 def back_other_kernel(
@@ -222,29 +234,33 @@
 ):
     half = q.shape[0] // BLOCK
     blocks = k.shape[0] // BLOCK
-    queries = GROUP * HEAD_SIZE
+    heads = k.shape[1] // HEAD_SIZE
     grad_k[...] = grad_k_own[...]
     grad_v[...] = grad_v_own[...]
-    grad_qkv[: half * BLOCK, :queries] = grad_q_own[...]
+    for h in range(heads * GROUP):
+        grad_qkv[: half * BLOCK, slot_lanes(h // GROUP, h % GROUP)] = grad_q_own[:, lanes_of(h)]
 
     def store(i, h, value):
-        grad_qkv[at_block(i + half), lanes_of(h)] = value
-
-    grad_gains[0, 0:1, :] = back_blocks(
+        grad_qkv[at_block(i + half), slot_lanes(h // GROUP, h % GROUP)] = value
+
+    grad_gains[0:1, :] = back_blocks(
         half, info, q, k, v, k_turned, start, logs, out, grad_out, raw_q, cos, sin, gain_q,
         grad_k, grad_v, store,
     )
 
     def finish(i, total_gain):
         rows = at_block(i)
-        back, gain = head_back(
-            raw_k[rows, :], gain_k[...], cos_all[rows, :], sin_all[rows, :], grad_k[rows, :] * SCALE
-        )
-        grad_qkv[rows, lanes_of(GROUP)] = back.astype(BF16)
-        grad_qkv[rows, lanes_of(GROUP + 1)] = grad_v[rows, :].astype(BF16)
-        return total_gain + gain
-
-    grad_gains[0, 1:2, :] = lax.fori_loop(0, blocks, finish, jnp.zeros((1, HEAD_SIZE), F32))
+        for j in range(heads):
+            back, gain = head_back(
+                raw_k[rows, lanes_of(j)], gain_k[...], cos_all[rows, :], sin_all[rows, :],
+                grad_k[rows, lanes_of(j)] * SCALE,
+            )
+            grad_qkv[rows, slot_lanes(j, GROUP)] = back.astype(BF16)
+            grad_qkv[rows, slot_lanes(j, GROUP + 1)] = grad_v[rows, lanes_of(j)].astype(BF16)
+            total_gain = total_gain + gain
+        return total_gain
+
+    grad_gains[1:2, :] = lax.fori_loop(0, blocks, finish, jnp.zeros((1, HEAD_SIZE), F32))
 
 
 def unpack(packed, gate_up, down):
@@ -377,12 +393,12 @@
 def project(x, gain, matrix, cos, sin, gain_q, gain_k):
     rows, width = x.shape
     heads = matrix.shape[1] // (SLOTS * HEAD_SIZE)
-    by_rows = lambda n: pl.BlockSpec((BLOCK, n), lambda i: (i, 0))
-    by_lanes = lambda n: pl.BlockSpec((n, BLOCK), lambda i: (0, i))
+    by_rows = lambda n: pl.BlockSpec((WIDE_BLOCK, n), lambda i: (i, 0))
+    by_lanes = lambda n: pl.BlockSpec((n, WIDE_BLOCK), lambda i: (0, i))
     q_width, k_width = heads * GROUP * HEAD_SIZE, heads * HEAD_SIZE
     return pl.pallas_call(
         project_kernel,
-        grid=(rows // BLOCK,),
+        grid=(rows // WIDE_BLOCK,),
         in_specs=[
             by_rows(width), fixed((1, width)), fixed(matrix.shape), by_rows(HEAD_SIZE),
             by_rows(HEAD_SIZE), fixed((1, HEAD_SIZE)), fixed((1, HEAD_SIZE)),
@@ -401,63 +417,57 @@
     )(x, gain, matrix, cos, sin, gain_q, gain_k)
 
 
-def head_specs(half, rows):
-    at = lambda j: j
-    n = rows // 2
+def head_specs(half, q, k):
+    rows, n = k.shape[0], q.shape[0] // 2
     return dict(
-        q=pl.BlockSpec((n, GROUP * HEAD_SIZE), lambda j, info: (half, at(j))),
-        k=pl.BlockSpec((rows, HEAD_SIZE), lambda j, info: (0, at(j))),
-        turned=pl.BlockSpec((HEAD_SIZE, rows), lambda j, info: (at(j), 0)),
-        start=pl.BlockSpec((1, n), lambda j, info: (0, half)),
-        out=pl.BlockSpec((n, GROUP * HEAD_SIZE), lambda j, info: (0, at(j))),
-        logs=pl.BlockSpec((1, GROUP, n), lambda j, info: (at(j), 0, 0)),
-        angle=pl.BlockSpec((n, HEAD_SIZE), lambda j, info: (half, 0)),
+        q=fixed((n, q.shape[1]), (half, 0)),
+        k=fixed(k.shape),
+        turned=fixed((k.shape[1], rows)),
+        start=fixed((1, n), (0, half)),
+        out=fixed((n, q.shape[1])),
+        out_turned=fixed((q.shape[1], n)),
+        logs=fixed((q.shape[1] // HEAD_SIZE, n)),
+        angle=fixed((n, HEAD_SIZE), (half, 0)),
+        row=fixed((1, HEAD_SIZE)),
     )
 
 
 def attend(half, info, q, k, v_turned, start):
-    rows = k.shape[0]
-    n, heads = rows // 2, k.shape[1] // HEAD_SIZE
-    s = head_specs(half, rows)
+    n = q.shape[0] // 2
+    s = head_specs(half, q, k)
     return pl.pallas_call(
         lambda *refs: attend_kernel(half * n // BLOCK, *refs),
         grid_spec=pltpu.PrefetchScalarGridSpec(
             num_scalar_prefetch=1,
-            grid=(heads,),
+            grid=(1,),
             in_specs=[s["q"], s["k"], s["turned"], s["start"]],
-            out_specs=[
-                s["out"], pl.BlockSpec((GROUP * HEAD_SIZE, n), lambda j, info: (j, 0)), s["logs"],
-            ],
+            out_specs=[s["out"], s["out_turned"], s["logs"]],
         ),
         out_shape=[
             shaped((n, q.shape[1]), BF16), shaped((q.shape[1], n), BF16),
-            shaped((heads, GROUP, n), F32),
+            shaped((q.shape[1] // HEAD_SIZE, n), F32),
         ],
         **params("attend", 18_000_000_000),
     )(info, q, k, v_turned, start)
 
 
 def attend_back_own(info, q, k, v, k_turned, start, logs, out, grad_out, raw_q, cos, sin, gain_q):
-    rows = k.shape[0]
-    n, heads = rows // 2, k.shape[1] // HEAD_SIZE
-    s = head_specs(0, rows)
+    n = q.shape[0] // 2
+    s = head_specs(0, q, k)
     return pl.pallas_call(
         back_own_kernel,
         grid_spec=pltpu.PrefetchScalarGridSpec(
             num_scalar_prefetch=1,
-            grid=(heads,),
+            grid=(1,),
             in_specs=[
                 s["q"], s["k"], s["k"], s["turned"], s["start"], s["logs"], s["out"], s["out"],
-                s["q"], s["angle"], s["angle"], fixed((1, HEAD_SIZE)),
+                s["q"], s["angle"], s["angle"], s["row"],
             ],
-            out_specs=[
-                s["out"], s["k"], s["k"],
-                pl.BlockSpec((1, 1, HEAD_SIZE), lambda j, info: (j, 0, 0)),
-            ],
+            out_specs=[s["out"], s["k"], s["k"], s["row"]],
         ),
         out_shape=[
             shaped((n, q.shape[1]), BF16), shaped(k.shape, F32), shaped(k.shape, F32),
-            shaped((heads, 1, HEAD_SIZE), F32),
+            shaped((1, HEAD_SIZE), F32),
         ],
         **params("attend_back_own", 25_000_000_000),
     )(info, q, k, v, k_turned, start, logs, out, grad_out, raw_q, cos, sin, gain_q)
@@ -468,28 +478,23 @@
     raw_k, gain_k, grad_q, grad_k, grad_v,
 ):
     rows = k.shape[0]
-    heads = k.shape[1] // HEAD_SIZE
-    width = SLOTS * HEAD_SIZE
-    s = head_specs(1, rows)
-    row = fixed((1, HEAD_SIZE))
+    width = k.shape[1] * SLOTS
+    s = head_specs(1, q, k)
+    whole = fixed((rows, HEAD_SIZE))
     return pl.pallas_call(
         back_other_kernel,
         grid_spec=pltpu.PrefetchScalarGridSpec(
             num_scalar_prefetch=1,
-            grid=(heads,),
+            grid=(1,),
             in_specs=[
                 s["q"], s["k"], s["k"], s["turned"], s["start"], s["logs"], s["out"], s["out"],
-                s["q"], s["angle"], s["angle"], row,
-                fixed((rows, HEAD_SIZE)), fixed((rows, HEAD_SIZE)), s["k"], row, s["out"], s["k"],
-                s["k"],
+                s["q"], s["angle"], s["angle"], s["row"],
+                whole, whole, s["k"], s["row"], s["out"], s["k"], s["k"],
             ],
-            out_specs=[
-                pl.BlockSpec((rows, width), lambda j, info: (0, j)),
-                pl.BlockSpec((1, 2, HEAD_SIZE), lambda j, info: (j, 0, 0)),
-            ],
-            scratch_shapes=[pltpu.VMEM((rows, HEAD_SIZE), F32)] * 2,
+            out_specs=[fixed((rows, width)), fixed((2, HEAD_SIZE))],
+            scratch_shapes=[pltpu.VMEM(k.shape, F32)] * 2,
         ),
-        out_shape=[shaped((rows, heads * width), BF16), shaped((heads, 2, HEAD_SIZE), F32)],
+        out_shape=[shaped((rows, width), BF16), shaped((2, HEAD_SIZE), F32)],
         **params("attend_back_other", 28_000_000_000),
     )(
         info, q, k, v, k_turned, start, logs, out, grad_out, raw_q, cos, sin, gain_q,
@@ -498,11 +503,11 @@
 
 
 def two_parts(rows, width):
-    steps = rows // BLOCK // 2
+    steps = rows // WIDE_BLOCK // 2
     return (
         [
-            pl.BlockSpec((BLOCK, width), lambda i: (jnp.minimum(i, steps - 1), 0)),
-            pl.BlockSpec((BLOCK, width), lambda i: (jnp.maximum(i - steps, 0), 0)),
+            pl.BlockSpec((WIDE_BLOCK, width), lambda i: (jnp.minimum(i, steps - 1), 0)),
+            pl.BlockSpec((WIDE_BLOCK, width), lambda i: (jnp.maximum(i - steps, 0), 0)),
         ],
         [shaped((rows // 2, width), BF16)] * 2,
     )
@@ -511,15 +516,15 @@
 def feed(h, grad, weights, hidden_count):
     rows, width = h.shape
     packs = len(weights) == 1
-    by_rows = lambda n: pl.BlockSpec((BLOCK, n), lambda i: (i, 0))
-    by_lanes = lambda n: pl.BlockSpec((n, BLOCK), lambda i: (0, i))
+    by_rows = lambda n: pl.BlockSpec((WIDE_BLOCK, n), lambda i: (i, 0))
+    by_lanes = lambda n: pl.BlockSpec((n, WIDE_BLOCK), lambda i: (0, i))
     specs, shapes = two_parts(rows, width)
     scratch = [
         pltpu.VMEM((width, 2 * hidden_count), BF16), pltpu.VMEM((hidden_count, width), BF16)
     ]
     return pl.pallas_call(
         lambda *refs: feed_kernel(packs, *refs),
-        grid=(rows // BLOCK,),
+        grid=(rows // WIDE_BLOCK,),
         in_specs=[by_rows(width), by_rows(width), *(fixed(w.shape) for w in weights)],
         out_specs=[
             by_lanes(width), by_lanes(hidden_count), by_rows(2 * hidden_count), *specs, *specs
@@ -558,18 +563,113 @@
 def unproject(half, grad, matrix):
     rows, width = grad.shape
     n = rows // 2
-    steps = n // BLOCK
+    steps = n // WIDE_BLOCK
     specs, shapes = two_parts(n, matrix.shape[0])
     return pl.pallas_call(
         unproject_kernel,
         grid=(steps,),
-        in_specs=[pl.BlockSpec((BLOCK, width), lambda i: (i + half * steps, 0)), fixed(matrix.shape)],
+        in_specs=[pl.BlockSpec((WIDE_BLOCK, width), lambda i: (i + half * steps, 0)), fixed(matrix.shape)],
         out_specs=specs,
         out_shape=shapes,
         **params("unproject", 4_000_000_000),
     )(grad, matrix)
 
 
+def bit_of(p, bit):
+    return (p // bit) % 2
+
+
+def place(p, order):
+    return sum(bit_of(p, bit) * 4 // 2**i for i, bit in enumerate(order))
+
+
+ORDERS = ((2, 1, 4), (1, 2, 4))
+
+
+def project_weights_kernel(me, h_turned, grad, matrix, keep_a, send_a, keep_b, send_b, gains):
+    p = pl.program_id(0)
+    value = nn(h_turned[...], grad[...])
+    rows, width = value.shape
+    lanes = width // 2
+    both = value * matrix[...].astype(F32)
+    folded = sum(both[:, i : i + 128] for i in range(0, width, 128))
+    gains[p, :, :] = jnp.sum(folded.T, axis=0, keepdims=True)
+    for order, keep, send, part in (
+        (ORDERS[0], keep_a, send_a, value[:, :lanes]), (ORDERS[1], keep_b, send_b, value[:, lanes:])
+    ):
+        at = place(p, order)
+
+        @pl.when(at < 4)
+        def _():
+            keep[at, :rows, :] = part.astype(BF16)
+
+        @pl.when(at >= 4)
+        def _():
+            send[at - 4, :rows, :] = part.astype(BF16)
+
+    @pl.when(p == 0)
+    def _():
+        zero = jnp.zeros((4, keep_a.shape[1] - rows, lanes), BF16)
+        keep_a[:, rows:, :] = zero
+        send_a[:, rows:, :] = zero
+
+
+def project_weights(me, h_turned, grad, matrix, extra):
+    width, rows = h_turned.shape
+    depth, lanes = width // 8, grad.shape[1] // 2
+    part = (4, depth, lanes)
+    longer = (4, depth + extra, lanes)
+    return pl.pallas_call(
+        project_weights_kernel,
+        grid_spec=pltpu.PrefetchScalarGridSpec(
+            num_scalar_prefetch=1,
+            grid=(8,),
+            in_specs=[
+                pl.BlockSpec((depth, rows), lambda p, me: (p ^ me[0], 0)),
+                fixed(grad.shape),
+                pl.BlockSpec((depth, grad.shape[1]), lambda p, me: (p ^ me[0], 0)),
+            ],
+            out_specs=[fixed(longer), fixed(longer), fixed(part), fixed(part), fixed((8, 1, depth))],
+        ),
+        out_shape=[
+            shaped(longer, BF16), shaped(longer, BF16), shaped(part, BF16), shaped(part, BF16),
+            shaped((8, 1, depth), F32),
+        ],
+        **params("project_weights", 8_000_000_000),
+    )(me, h_turned, grad, matrix)
+
+
+def out_weights_kernel(me, h_own, grad_own, h_other, grad_other, keep, send, value):
+    value[...] = nn(h_own[...], grad_own[...]) + nn(h_other[...], grad_other[...])
+    deep = HEAD_SIZE // 8
+    for p in range(8):
+        at = place(p, ORDERS[1])
+        to = (keep if at < 4 else send).at[at % 4]
+        for h in range(value.shape[0] // HEAD_SIZE):
+            of = pl.multiple_of(h * HEAD_SIZE + (p ^ me[0]) * deep, deep)
+            to[h * deep : (h + 1) * deep, :] = value[pl.ds(of, deep), :].astype(BF16)
+
+
+def out_weights(me, h_own, grad_own, h_other, grad_other):
+    count, rows = h_own.shape
+    width = grad_own.shape[1]
+    half = width // 2
+    columns = pl.BlockSpec((rows, half), lambda i, me: (0, i))
+    part = pl.BlockSpec((4, count // 8, half), lambda i, me: (0, 0, i))
+    return pl.pallas_call(
+        out_weights_kernel,
+        grid_spec=pltpu.PrefetchScalarGridSpec(
+            num_scalar_prefetch=1,
+            grid=(2,),
+            in_specs=[fixed((count, rows)), columns, fixed((count, rows)), columns],
+            out_specs=[part, part],
+            scratch_shapes=[pltpu.VMEM((count, half), F32)],
+        ),
+        out_shape=[shaped((4, count // 8, width), BF16)] * 2,
+        **params("out_weights", 4_000_000_000),
+    )(me, h_own, grad_own, h_other, grad_other)
+
+
 def flipped(value, axis, bit, name="part"):
     with jax.named_scope(name):
         return lax.ppermute(value, axis, [(i, i ^ bit) for i in range(lax.axis_size(axis))])
@@ -583,11 +683,13 @@
     return part.astype(F32) + flipped(beside, "tensor", 1).astype(F32)
 
 
-def halved(parts, axis, bit):
-    mine = (lax.axis_index("dp") // bit) % 2
-    send = lax.dynamic_index_in_dim(parts, 1 - mine, axis, keepdims=False).astype(BF16)
-    keep = lax.dynamic_index_in_dim(parts, mine, axis, keepdims=False)
-    return keep + flipped(send, "dp", bit).astype(F32)
+def added(keep, send, bit):
+    return keep.astype(F32) + flipped(send.astype(BF16), "dp", bit).astype(F32)
+
+
+def halved(value, bit):
+    half = value.shape[0] // 2
+    return added(value[:half], value[half:], bit)
 
 
 def per_device(
@@ -766,10 +868,7 @@
         [grad_middle_across, flipped(grad_middle_across, "tensor", 1)], axis=0
     )
     grad_heads_other = nt(grad_middle_other, out_matrix).astype(BF16)
-    grad_out_w = (
-        nn(heads_own_turned, grad_middle_own) + nn(heads_other_turned, grad_middle_other)
-    ).astype(BF16)
-    near_mlp, grad_out_w, grad_heads_other = together(near_mlp, grad_out_w, grad_heads_other)
+    near_mlp, grad_heads_other = together(near_mlp, grad_heads_other)
     mlp_across = flipped(near_mlp, "tensor", 2, "mlp_across")
     grad_qkv, gain_other = attend_back_other(
         info, q, k, v, k_turned, start, logs_other, heads_other, grad_heads_other,
@@ -778,48 +877,63 @@
     grad_qkv, mlp_across = together(grad_qkv, mlp_across)
     back_2, back_3 = unproject(1, grad_qkv, qkv_matrix)
     back_2, back_3, grad_qkv = together(back_2, back_3, grad_qkv)
-    grad_qkv_w = nn(normed_turned, grad_qkv)
-    near = near_sum(back_2, back_3).astype(BF16)
-    near, grad_qkv, grad_qkv_w, grad_out_w = together(near, grad_qkv, grad_qkv_w, grad_out_w)
-    back_across = flipped(near, "tensor", 2, "back_across")
-    grad_gain_attn = jnp.sum(qkv_matrix.astype(F32) * grad_qkv_w, axis=1) / gain_attn[0]
-    grad_gain_heads = jnp.sum(gain_other, axis=0) + jnp.pad(
-        jnp.sum(gain_own, axis=0), ((0, 1), (0, 0))
-    )
-    gain_sums = jnp.concatenate([grad_gain_attn, grad_gain_mlp, grad_gain_heads.reshape(-1)])
-    back_0, back_1 = unproject(0, grad_qkv, qkv_matrix)
+    grad_gain_heads = gain_other + jnp.pad(gain_own, ((0, 1), (0, 0)))
     if cubic:
-        cube = (2, 2, 2)
-        columns = grad_qkv_w.shape[1] // 2
-        gain_rows = jnp.pad(
-            gain_sums.reshape(cube + (1, gain_count)),
-            ((0, 0),) * 3 + ((0, 15), (0, columns - gain_count)),
+        extra = 16
+        me_dp = lax.axis_index("dp")
+        relative = jnp.arange(8, dtype=jnp.int32) ^ me_dp
+        where = me_dp.astype(jnp.int32)[None]
+        keep_a, send_a, keep_b, send_b, gain_blocks = project_weights(
+            where, normed_turned, grad_qkv, qkv_matrix, extra
         )
-        sum_one = jnp.concatenate(
-            [grad_qkv_w[:, :columns].reshape(cube + (depth, -1)), gain_rows], axis=3
+        near = near_sum(back_2, back_3).astype(BF16)
+        near, grad_qkv, send_a, send_b, heads_own_turned = together(
+            near, grad_qkv, send_a, send_b, heads_own_turned
         )
-        sum_two = grad_qkv_w[:, columns:].reshape(cube + (depth, -1))
-        sum_one, sum_two = halved(sum_one, 1, 2), halved(sum_two, 2, 1)
-        sum_one, sum_two = halved(sum_one, 1, 1), halved(sum_two, 1, 2)
-        sum_out = grad_out_w.reshape((out_heads,) + cube + (out_depth, MODEL_WIDTH))
-        sum_out = halved(halved(sum_out, 3, 1), 2, 2)
+        back_across = flipped(near, "tensor", 2, "back_across")
+        back_0, back_1 = unproject(0, grad_qkv, qkv_matrix)
+        sum_two = added(keep_b, send_b, ORDERS[1][0])
+        keep_out, send_out = out_weights(
+            where, heads_own_turned, grad_middle_own, heads_other_turned, grad_middle_other
+        )
+        grad_gain_attn = jnp.take(gain_blocks[:, 0], relative, axis=0).reshape(-1) / gain_attn[0]
+        gain_sums = jnp.concatenate([grad_gain_attn, grad_gain_mlp, grad_gain_heads.reshape(-1)])
+        gain_rows = jnp.take(gain_sums.reshape(8, 1, gain_count), relative, axis=0).astype(BF16)
+        slots = sorted(range(8), key=lambda p: place(p, ORDERS[0]))
+        gain_rows = jnp.stack([gain_rows[p] for p in slots])
+        put = lambda value, rows: lax.dynamic_update_slice(value, rows, (0, depth, 0))
+        keep_a, send_a = put(keep_a, gain_rows[:4]), put(send_a, gain_rows[4:])
+        sum_one = added(keep_a, send_a, ORDERS[0][0])
+        sum_out = added(keep_out, send_out, ORDERS[1][0])
+        sum_one, sum_two = halved(sum_one, ORDERS[0][1]), halved(sum_two, ORDERS[1][1])
+        sum_out = halved(sum_out, ORDERS[1][1])
         sum_one, sum_two, sum_out, back_across, feed_sum = together(
             sum_one, sum_two, sum_out, back_across, feed_sum
         )
-        sum_one, sum_two = halved(sum_one, 0, 4), halved(sum_two, 0, 4)
-        sum_out = halved(sum_out, 1, 4)
+        sum_one, sum_two, sum_out = (halved(value, 4)[0] for value in (sum_one, sum_two, sum_out))
         sum_qkv = jnp.concatenate([sum_one[:depth], sum_two], axis=1)
         sum_qkv = sum_qkv.reshape(projection_weight.shape)
         sum_gains = sum_one[depth, :gain_count]
+        sum_out = sum_out.reshape(w_out.shape)
     else:
+        grad_qkv_w = nn(normed_turned, grad_qkv)
+        near = near_sum(back_2, back_3).astype(BF16)
+        back_across = flipped(near, "tensor", 2, "back_across")
+        back_0, back_1 = unproject(0, grad_qkv, qkv_matrix)
         sum_qkv = (
             lax.psum_scatter(grad_qkv_w.astype(BF16), "dp", scatter_dimension=0, tiled=True)
             .astype(F32)
             .reshape(projection_weight.shape)
         )
+        grad_out_w = nn(heads_own_turned, grad_middle_own) + nn(
+            heads_other_turned, grad_middle_other
+        )
         sum_out = lax.psum_scatter(
-            grad_out_w.reshape(out_heads, -1, MODEL_WIDTH), "dp", scatter_dimension=1, tiled=True
+            grad_out_w.astype(BF16).reshape(out_heads, -1, MODEL_WIDTH), "dp",
+            scatter_dimension=1, tiled=True,
         ).astype(F32)
+        grad_gain_attn = jnp.sum(qkv_matrix.astype(F32) * grad_qkv_w, axis=1) / gain_attn[0]
+        gain_sums = jnp.concatenate([grad_gain_attn, grad_gain_mlp, grad_gain_heads.reshape(-1)])
         sum_gains = lax.psum_scatter(gain_sums, "dp", scatter_dimension=0, tiled=True)
     sum_gains = sum_gains + sum(flipped(sum_gains, "tensor", bit) for bit in range(1, shards))
 

time: 446 us -> 456 us (1.022)
  Pallas kernels: 160 us -> 178 us
  matrix products: 20 us -> 8.48 us
  local copies, waits for them, and re-layouts: 36.6 us -> 25.6 us
  starting transfers between devices: 29.7 us -> 35.7 us
  other arithmetic: 64.5 us -> 69.7 us
  waiting for transfers between devices: 113 us -> 118 us
    pallas_call x5 -> x7, Pallas kernels: 58.9 us -> 83.4 us  [the longest x2 36.8 us: feed(): pl.pallas_call(lambda *refs: feed_kernel(packs, *refs), grid=(rows // WID...]
    dot_general x7 -> x4, matrix products: 13.9 us -> 3.94 us  [nn(): return jnp.dot(a, b, preferred_element_type=F32)]
    unnamed x137 -> x107, local copies, waits for them, and re-layouts: 14.3 us -> 5.36 us
    convert_element_type x8 -> x0, local copies, waits for them, and re-layouts: 6.04 us -> none  [halved(): lax.dynamic_index_in_dim(parts, 1 - mine, axis, keepdims=False).astype(BF16)]
    ppermute x36, starting transfers between devices: 29.6 us -> 35.6 us  [flipped(): lax.ppermute(value, axis, [(i, i ^ bit) for i in range(lax.axis_size(axis...]
  transfers between devices with their start and end apart: 39 -> 39, of which waited for: 18 -> 19; matrix products, arithmetic and copies ran while one was open for 21% -> 20% of each run, Pallas kernels for 33% -> 35%
where the time goes in v5:
time: 456 us; the launch traced here: 450 us
  Pallas kernels  178 us (39%)
  waiting for transfers between devices  118 us (26%)
  other arithmetic  69.7 us (15%)
  starting transfers between devices  35.7 us (8%)
  local copies, waits for them, and re-layouts  25.6 us (6%)
  between operations  15.2 us (3%)
  matrix products  8.48 us (2%)
    ppermute x36, waiting for transfers between devices, flipped(): lax.ppermute(value, axis, [(i, i ^ bit) for i in range(lax.axis_size(axis...  79.2 us
    pallas_call x2, Pallas kernels, feed(): pl.pallas_call(lambda *refs: feed_kernel(packs, *refs), grid=(rows // WID...  36.8 us
    ppermute x36, starting transfers between devices, flipped(): lax.ppermute(value, axis, [(i, i ^ bit) for i in range(lax.axis_size(axis...  35.6 us
    pallas_call x1, Pallas kernels, attend_back_other(): pl.pallas_call(back_other_kernel, grid_spec=pltpu.PrefetchScalarGridSpec(...  28.9 us
    pallas_call x2, Pallas kernels, attend(): pl.pallas_call(lambda *refs: attend_kernel(half * n // BLOCK, *refs), gri...  28.6 us
    all_gather x1, waiting for transfers between devices, per_device(): lax.all_gather(pack_one, 'dp', axis=0, tiled=False)  27.7 us
    pallas_call x1, Pallas kernels, attend_back_own(): pl.pallas_call(back_own_kernel, grid_spec=pltpu.PrefetchScalarGridSpec(nu...  18.7 us
    pallas_call x1, Pallas kernels, feed_weights(): pl.pallas_call(lambda *refs: feed_weights_kernel(packs, pieces, *refs), g...  18 us
  transfers between devices with their start and end apart: 39, of which 19 were waited for; matrix products, arithmetic and copies ran while one was open for 20% of the time, Pallas kernels for 35%

profile of v5, /device:TPU:0, one launch (start us, length us, event | category | flops | bytes accessed | tf_op | source)
XLA Modules:
  0.0 450.1 jit_solution(2293373355552124497)
XLA Ops:
  16.8 23.2 %collective-permute-done.1 = bf16[512,1024]{1,0:T(8,128)(2,1)S(1)} collective-permute-done((bf16[512,1024]{1,0:T(8,128)(2,1)S(1)}, bf16[512,1024]{1,0:T(8,128)(2,1)S(1)}, u32[]{:S(2)}, u32[]{:S(2)}) %collective-permute-start.1) | collective-permute-done | bytes 1048608 | tf_op jit(solution)/shard_map/tokens_across/ppermute | solution.py:675
  40.0 3.7 fusion.15
  46.3 3.5 pad_maximum_fusion.x
  49.8 27.7 %all-gather.5.cloned.1.call-done = bf16[1664,1024]{1,0:T(8,128)(2,1)} async-done(((bf16[208,1024]{1,0:T(8,128)(2,1)}), bf16[1664,1024]{1,0:T(8,128)(2,1)}) %all-gather.5.cloned.1.call-update) | async-done | bytes 3407888 | tf_op jit(solution)/shard_map/all_gather | solution.py:743
  77.5 3.1 slice.157
  83.9 16.7 %project.1 = (bf16[1024,2048]{1,0:T(8,128)(2,1)}, f32[2048,512]{1,0:T(8,128)}, f32[2048,256]{1,0:T(8,128)}, bf16[2048,512]{1,0:T(8,128)(2,1)}, bf16[2048,256]{1,...) custom-call(bf16[2048,1024]{1,0:T(8,128)(2,1)} %pad_maximum_fusion.x, ...), custom_call_target="tpu_custom_call" | custom-call | flops 156250000 | bytes 1000 | tf_op jit(solution)/shard_map/project/pallas_call | solution.py:399
  100.6 16.0 %attend.2 = (bf16[1024,512]{1,0:T(8,128)(2,1)}, bf16[512,1024]{1,0:T(8,128)(2,1)}, f32[4,1024]{1,0:T(4,128)}) custom-call(s32[9]{0:T(128)} %pad_add_fusion.refs_0_.info, bf16[2048,512]{1,0:T(8,128)(2,1)} %get-tuple-element.101.refs_1_.q, bf16[2048,256]{1,0:T(8,128)(2,1)} %get-tuple-element.97.refs_2_.k, bf16[256,2048]{1,0:T(8,128)(2,1)} %get-tuple-element.98.refs_3_, ...), custom_call_target="tpu_custom_call" | custom-call | flops 281249984 | bytes 1000 | tf_op jit(solution)/shard_map/attend/pallas_call | solution.py:438
  122.5 12.6 %attend.3 = (bf16[1024,512]{1,0:T(8,128)(2,1)}, bf16[512,1024]{1,0:T(8,128)(2,1)}, f32[4,1024]{1,0:T(4,128)}) custom-call(s32[9]{0:T(128)} %pad_add_fusion.refs_0_.info, bf16[2048,512]{1,0:T(8,128)(2,1)} %get-tuple-element.101.refs_1_.q, bf16[2048,256]{1,0:T(8,128)(2,1)} %get-tuple-element.97.refs_2_.k, bf16[256,2048]{1,0:T(8,128)(2,1)} %get-tuple-element.98.refs_3_, ...), custom_call_target="tpu_custom_call" | custom-call | flops 281249984 | bytes 1000 | tf_op jit(solution)/shard_map/attend/pallas_call | solution.py:438
  135.1 12.6 %collective-permute-done.5 = bf16[512,1024]{1,0:T(8,128)(2,1)} collective-permute-done((bf16[512,1024]{1,0:T(8,128)(2,1)S(1)}, bf16[512,1024]{1,0:T(8,128)(2,1)}, u32[]{:S(2)}, u32[]{:S(2)}) %collective-permute-start.5) | collective-permute-done | bytes 1048608 | tf_op jit(solution)/shard_map/attn_across/ppermute | solution.py:675
  147.8 11.0 %all-gather.7.cloned.1.call-done = bf16[4608,512]{1,0:T(8,128)(2,1)} async-done(((bf16[576,512]{1,0:T(8,128)(2,1)}), bf16[4608,512]{1,0:T(8,128)(2,1)}) %all-gather.7.cloned.1.call-update) | async-done | bytes 4718608 | tf_op jit(solution)/shard_map/all_gather | solution.py:745
  171.1 18.6 %feed.2 = (bf16[1024,1024]{1,0:T(8,128)(2,1)}, bf16[768,1024]{1,0:T(8,128)(2,1)}, bf16[1024,1536]{1,0:T(8,128)(2,1)}, bf16[512,1024]{1,0:T(8,128)(2,1)}, bf16[51...) custom-call(bf16[1024,1024]{1,0:T(8,128)(2,1)} %pad_maximum_fusion.1.refs_0_, ...), custom_call_target="tpu_custom_call" | custom-call | flops 250000000 | bytes 1000 | tf_op jit(solution)/shard_map/feed/pallas_call | solution.py:525
  194.7 3.2 pad_maximum_fusion.2.refs_0_
  197.9 18.2 %feed.3 = (bf16[1024,1024]{1,0:T(8,128)(2,1)}, bf16[768,1024]{1,0:T(8,128)(2,1)}, bf16[1024,1536]{1,0:T(8,128)(2,1)}, bf16[512,1024]{1,0:T(8,128)(2,1)}, bf16[51...) custom-call(bf16[1024,1024]{1,0:T(8,128)(2,1)} %pad_maximum_fusion.2.refs_0_, ...), custom_call_target="tpu_custom_call" | custom-call | flops 250000000 | bytes 1000 | tf_op jit(solution)/shard_map/feed/pallas_call | solution.py:525
  223.3 18.0 %feed_weights.1 = bf16[8,576,512]{2,1,0:T(8,128)(2,1)} custom-call(bf16[1024,1024]{1,0:T(8,128)(2,1)} %get-tuple-element.121.refs_0_, bf16[1024,1024]{1,0:T(8,128)(2,1)} %get-tuple-element.122.refs_1_, bf16[1024,1536]{1,0:T(8,128)(2,1)} %get-tuple-element.123.refs_2_, bf16[1024,1536]{1,0:T(8,128)(2,1)} %get-tuple-element.124.refs_3_, ...), custom_call_target="tpu_custom_call" | custom-call | flops 250000000 | bytes 1000 | tf_op jit(solution)/shard_map/feed_weights/pallas_call | solution.py:550
  241.3 6.2 %collective-permute-done.15 = bf16[512,1024]{1,0:T(8,128)(2,1)} collective-permute-done((bf16[512,1024]{1,0:T(8,128)(2,1)}, bf16[512,1024]{1,0:T(8,128)(2,1)}, u32[]{:S(2)}, u32[]{:S(2)}) %collective-permute-start.15) | collective-permute-done | bytes 1048608 | tf_op jit(solution)/shard_map/back_across/ppermute | solution.py:675
  250.4 4.1 fusion.26
  259.5 18.7 %attend_back_own.1 = (bf16[1024,512]{1,0:T(8,128)(2,1)}, f32[2048,256]{1,0:T(8,128)}, f32[2048,256]{1,0:T(8,128)}, f32[1,128]{1,0:T(1,128)}) custom-call(s32[9]{0:T(128)} %pad_add_fusion.refs_0_.info, bf16[2048,512]{1,0:T(8,128)(2,1)} %get-tuple-element.101.refs_1_.q, bf16[2048,256]{1,0:T(8,128)(2,1)} %get-tuple-element.97.refs_2_.k, ...), custom_call_target="tpu_custom_call" | custom-call | flops 390624992 | bytes 1000 | tf_op jit(solution)/shard_map/attend_back_own/pallas_call | solution.py:457
  280.7 3.5 collective-permute-done.19
  291.3 28.9 %attend_back_other.1 = (bf16[2048,1024]{1,0:T(8,128)(2,1)}, f32[2,128]{1,0:T(2,128)}) custom-call(s32[9]{0:T(128)} %pad_add_fusion.refs_0_.info, bf16[2048,512]{1,0:T(8,128)(2,1)} %get-tuple-element.101.refs_1_.q, bf16[2048,256]{1,0:T(8,128)(2,1)} %get-tuple-element.97.refs_2_.k, bf16[2048,256]{1,0:T(8,128)(2,1)} %get-tuple-element.109.v, ...), custom_call_target="tpu_custom_call" | custom-call | flops 437500000 | bytes 1000 | tf_op jit(solution)/shard_map/attend_back_other/pallas_call | solution.py:484
  320.2 6.2 %unproject.2 = (bf16[512,1024]{1,0:T(8,128)(2,1)}, bf16[512,1024]{1,0:T(8,128)(2,1)}) custom-call(bf16[2048,1024]{1,0:T(8,128)(2,1)} %get-tuple-element.154.grad, bf16[1024,1024]{1,0:T(8,128)(2,1)} %bitcast.70), custom_call_target="tpu_custom_call" | custom-call | flops 62500000 | bytes 1000 | tf_op jit(solution)/shard_map/unproject/pallas_call | solution.py:568
  328.4 11.7 %project_weights.1 = (bf16[4,144,512]{2,1,0:T(8,128)(2,1)}, bf16[4,144,512]{2,1,0:T(8,128)(2,1)}, bf16[4,128,512]{2,1,0:T(8,128)(2,1)}, bf16[4,128,512]{2,1,0:T(8,128)(2,1)}, f32[8,1,128]{2,1,0:T(1,128)}) custom-call(s32[1]{0:T(128)} %bitcast.18.me, bf16[1024,2048]{1,0:T(8,128)(2,1)} %get-tuple-element.150.h_turned, ...), custom_call_target="tpu_custom_call" | custom-call | flops 125000000 | bytes 1000 | tf_op jit(solution)/shard_map/project_weights/pallas_call | solution.py:622
  342.1 3.7 add_convert_fusion.1
  348.4 5.7 %out_weights.1 = (bf16[4,64,1024]{2,1,0:T(8,128)(2,1)}, bf16[4,64,1024]{2,1,0:T(8,128)(2,1)}) custom-call(s32[1]{0:T(128)} %bitcast.18.me, bf16[512,1024]{1,0:T(8,128)(2,1)} %get-tuple-element.164.h_own, bf16[1024,1024]{1,0:T(8,128)(2,1)} %pad_maximum_fusion.3.grad_own, bf16[512,1024]{1,0:T(8,128)(2,1)} %get-tuple-element.165.h_other, ...), custom_call_target="tpu_custom_call" | custom-call | flops 62500000 | bytes 1000 | tf_op jit(solution)/shard_map/out_weights/pallas_call | solution.py:659
  354.1 9.9 %collective-permute-start.27 = (bf16[4,64,1024]{2,1,0:T(8,128)(2,1)}, bf16[4,64,1024]{2,1,0:T(8,128)(2,1)}, u32[]{:S(2)}, u32[]{:S(2)}) collective-permute-start(bf16[4,64,1024]{2,1,0:T(8,128)(2,1)} %get-tuple-element.167), channel_id=1, source_target_pairs={{0,4},{4,0},{8,12},{12,8},{16,20},{20,16},{24,28},{28,24},{1,5},{5... | collective-permute-start | bytes 1572872 | tf_op jit(solution)/shard_map/part/ppermute | solution.py:675
  370.6 6.4 %unproject.3 = (bf16[512,1024]{1,0:T(8,128)(2,1)}, bf16[512,1024]{1,0:T(8,128)(2,1)}) custom-call(bf16[2048,1024]{1,0:T(8,128)(2,1)} %get-tuple-element.154.grad, bf16[1024,1024]{1,0:T(8,128)(2,1)} %bitcast.72), custom_call_target="tpu_custom_call" | custom-call | flops 62500000 | bytes 1000 | tf_op jit(solution)/shard_map/unproject/pallas_call | solution.py:568
  380.4 7.3 %collective-permute-done.25 = bf16[4,128,512]{2,0,1:T(4,128)(2,1)} collective-permute-done((bf16[4,128,512]{2,0,1:T(4,128)(2,1)}, bf16[4,128,512]{2,0,1:T(4,128)(2,1)}, u32[]{:S(2)}, u32[]{:S(2)}) %collective-permute-start.25) | collective-permute-done | bytes 524320 | tf_op jit(solution)/shard_map/part/ppermute | solution.py:675
  393.0 4.3 collective-permute-done.26
  415.2 5.2 %multiply_subtract_fusion = (f32[128,2,768]{2,1,0:T(2,128)}, f32[128,2,768]{2,1,0:T(2,128)}, f32[128,2,768]{2,1,0:T(2,128)}) fusion(f32[128,2,768]{2,1,0:T(2,128)S(1)} %copy-done.14, f32[128,2,768]{2,1,0:T(2,128)S(1)} %copy-done.15, f32[128,2,768]{2,1,0:T(2,128)} %param.28, f32[128,2,768]{2,1,0:T(2,128)} %param.33), kind=kLoop, calls=%fused_computation.42 | loop fusion | flops 2949120 | bytes 5505024 | tf_op jit(solution)/shard_map/sub | solution.py:54
  420.5 3.8 fusion.3
  425.5 3.8 collective-permute-done.32
  430.4 4.1 collective-permute-done.31
  439.3 3.2 multiply_subtract_fusion.1
  (273 shorter events, 110.2 us)
Async XLA Ops:
  7.2 70.3 %all-gather.5.cloned.1.call-start = ((), (), s32[]{:S(2)}) async-start(), calls=%async_computation.2 | async-start | bytes 3833856 | tf_op jit(solution)/shard_map/all_gather | solution.py:743
  11.1 147.6 %all-gather.7.cloned.1.call-start = ((), (), s32[]{:S(2)}) async-start(), calls=%async_computation.3 | async-start | bytes 5308416 | tf_op jit(solution)/shard_map/all_gather | solution.py:745
  12.9 387.8 %reduce-scatter.2.cloned.1.call-start = ((), (), s32[]{:S(2)}) async-start(), calls=%async_computation.1 | async-start | bytes 5308416 | tf_op jit(solution)/shard_map/reduce_scatter | solution.py:849
  13.0 27.0 %collective-permute-start.1 = (bf16[512,1024]{1,0:T(8,128)(2,1)S(1)}, bf16[512,1024]{1,0:T(8,128)(2,1)S(1)}, u32[]{:S(2)}, u32[]{:S(2)}) collective-permute-start(bf16[512,1024]{1,0:T(8,128)(2,1)S(1)} %copy-done), channel_id=1, source_target_pairs={{0,2},{1,3},{2,0},{3,1},{4,6},{5,7},{6,4},{7,5},{8,10},{9,11},{10,... | collective-permute-start | bytes 3145736 | tf_op jit(solution)/shard_map/tokens_across/ppermute | solution.py:675
  16.0 30.3 %collective-permute-start = (bf16[512,1024]{1,0:T(8,128)(2,1)S(1)}, bf16[512,1024]{1,0:T(8,128)(2,1)S(1)}, u32[]{:S(2)}, u32[]{:S(2)}) collective-permute-start(bf16[512,1024]{1,0:T(8,128)(2,1)S(1)} %copy-done), channel_id=1, source_target_pairs={{0,1},{1,0},{2,3},{3,2},{4,5},{5,4},{6,7},{7,6},{8,9},{9,8},{10,11... | collective-permute-start | bytes 3145736 | tf_op jit(solution)/shard_map/part/ppermute | solution.py:675
  16.0 100.5 %collective-permute-start.3 = (bf16[512,1024]{1,0:T(8,128)(2,1)}, bf16[512,1024]{1,0:T(8,128)(2,1)}, u32[]{:S(2)}, u32[]{:S(2)}) collective-permute-start(bf16[512,1024]{1,0:T(8,128)(2,1)} %param.19), channel_id=1, source_target_pairs={{0,2},{1,3},{2,0},{3,1},{4,6},{5,7},{6,4},{7,5},{8,10},{9,11},{10,... | collective-permute-start | bytes 3145736 | tf_op jit(solution)/shard_map/grad_across/ppermute | solution.py:675
  40.0 6.3 %collective-permute-start.2 = (bf16[512,1024]{1,0:T(8,128)(2,1)S(1)}, bf16[512,1024]{1,0:T(8,128)(2,1)}, u32[]{:S(2)}, u32[]{:S(2)}) collective-permute-start(bf16[512,1024]{1,0:T(8,128)(2,1)S(1)} %collective-permute-done.1), channel_id=1, source_target_pairs={{0,1},{1,0},{2,3},{3,2},{4,5},{5,4},{6,7},{7,6},{8,9},{9,8},{10,11... | collective-permute-start | bytes 3145736 | tf_op jit(solution)/shard_map/part/ppermute | solution.py:675
  122.4 25.4 %collective-permute-start.5 = (bf16[512,1024]{1,0:T(8,128)(2,1)S(1)}, bf16[512,1024]{1,0:T(8,128)(2,1)}, u32[]{:S(2)}, u32[]{:S(2)}) collective-permute-start(bf16[512,1024]{1,0:T(8,128)(2,1)S(1)} %add_convert_fusion.4), channel_id=1, source_target_pairs={{0,2},{1,3},{2,0},{3,1},{4,6},{5,7},{6,4},{7,5},{8,10},{9,11},{10,... | collective-permute-start | bytes 3145736 | tf_op jit(solution)/shard_map/attn_across/ppermute | solution.py:675
  160.6 8.5 %collective-permute-start.8 = (bf16[512,1024]{1,0:T(8,128)(2,1)}, bf16[512,1024]{1,0:T(8,128)(2,1)S(1)}, u32[]{:S(2)}, u32[]{:S(2)}) collective-permute-start(bf16[512,1024]{1,0:T(8,128)(2,1)} %param.19), channel_id=1, source_target_pairs={{0,1},{1,0},{2,3},{3,2},{4,5},{5,4},{6,7},{7,6},{8,9},{9,8},{10,11... | collective-permute-start | bytes 3145736 | tf_op jit(solution)/shard_map/part/ppermute | solution.py:675
  166.3 25.5 %collective-permute-start.10 = (bf16[512,1024]{1,0:T(8,128)(2,1)S(1)}, bf16[512,1024]{1,0:T(8,128)(2,1)}, u32[]{:S(2)}, u32[]{:S(2)}) collective-permute-start(bf16[512,1024]{1,0:T(8,128)(2,1)S(1)} %multiply_convert_fusion), channel_id=1, source_target_pairs={{0,2},{1,3},{2,0},{3,1},{4,6},{5,7},{6,4},{7,5},{8,10},{9,11},{10,... | collective-permute-start | bytes 3145736 | tf_op jit(solution)/shard_map/normed_across/ppermute | solution.py:675
  169.1 24.0 %collective-permute-start.13 = (bf16[512,1024]{1,0:T(8,128)(2,1)}, bf16[512,1024]{1,0:T(8,128)(2,1)}, u32[]{:S(2)}, u32[]{:S(2)}) collective-permute-start(bf16[512,1024]{1,0:T(8,128)(2,1)} %collective-permute-done.3), channel_id=1, source_target_pairs={{0,1},{1,0},{2,3},{3,2},{4,5},{5,4},{6,7},{7,6},{8,9},{9,8},{10,11... | collective-permute-start | bytes 3145736 | tf_op jit(solution)/shard_map/part/ppermute | solution.py:675
  221.8 25.8 %collective-permute-start.15 = (bf16[512,1024]{1,0:T(8,128)(2,1)}, bf16[512,1024]{1,0:T(8,128)(2,1)}, u32[]{:S(2)}, u32[]{:S(2)}) collective-permute-start(bf16[512,1024]{1,0:T(8,128)(2,1)} %add_convert_fusion.3), channel_id=1, source_target_pairs={{0,2},{1,3},{2,0},{3,1},{4,6},{5,7},{6,4},{7,5},{8,10},{9,11},{10,... | collective-permute-start | bytes 3145736 | tf_op jit(solution)/shard_map/back_across/ppermute | solution.py:675
  223.2 24.3 %collective-permute-start.11 = (bf16[512,1024]{1,0:T(8,128)(2,1)}, bf16[512,1024]{1,0:T(8,128)(2,1)}, u32[]{:S(2)}, u32[]{:S(2)}) collective-permute-start(bf16[512,1024]{1,0:T(8,128)(2,1)} %get-tuple-element.114), channel_id=1, source_target_pairs={{0,1},{1,0},{2,3},{3,2},{4,5},{5,4},{6,7},{7,6},{8,9},{9,8},{10,11... | collective-permute-start | bytes 3145736 | tf_op jit(solution)/shard_map/part/ppermute | solution.py:675
  254.5 25.6 %collective-permute-start.16 = (bf16[512,1024]{1,0:T(8,128)(2,1)S(1)}, bf16[512,1024]{1,0:T(8,128)(2,1)S(1)}, u32[]{:S(2)}, u32[]{:S(2)}) collective-permute-start(bf16[512,1024]{1,0:T(8,128)(2,1)S(1)} %get-tuple-element.194), channel_id=1, source_target_pairs={{0,2},{1,3},{2,0},{3,1},{4,6},{5,7},{6,4},{7,5},{8,10},{9,11},{10,... | collective-permute-start | bytes 3145736 | tf_op jit(solution)/shard_map/grad_middle_across/ppermute | solution.py:675
  280.1 4.4 collective-permute-start.18
  288.3 31.9 %collective-permute-start.20 = (bf16[512,1024]{1,0:T(8,128)(2,1)}, bf16[512,1024]{1,0:T(8,128)(2,1)}, u32[]{:S(2)}, u32[]{:S(2)}) collective-permute-start(bf16[512,1024]{1,0:T(8,128)(2,1)} %add_convert_fusion.2), channel_id=1, source_target_pairs={{0,2},{1,3},{2,0},{3,1},{4,6},{5,7},{6,4},{7,5},{8,10},{9,11},{10,... | collective-permute-start | bytes 3145736 | tf_op jit(solution)/shard_map/mlp_across/ppermute | solution.py:675
  291.3 50.8 %collective-permute-start.9 = (bf16[512,1024]{1,0:T(8,128)(2,1)}, bf16[512,1024]{1,0:T(8,128)(2,1)}, u32[]{:S(2)}, u32[]{:S(2)}) collective-permute-start(bf16[512,1024]{1,0:T(8,128)(2,1)} %get-tuple-element.108), channel_id=1, source_target_pairs={{0,1},{1,0},{2,3},{3,2},{4,5},{5,4},{6,7},{7,6},{8,9},{9,8},{10,11... | collective-permute-start | bytes 3145736 | tf_op jit(solution)/shard_map/part/ppermute | solution.py:675
  326.4 19.4 %collective-permute-start.21 = (bf16[512,1024]{1,0:T(8,128)(2,1)}, bf16[512,1024]{1,0:T(8,128)(2,1)}, u32[]{:S(2)}, u32[]{:S(2)}) collective-permute-start(bf16[512,1024]{1,0:T(8,128)(2,1)} %get-tuple-element.148), channel_id=1, source_target_pairs={{0,1},{1,0},{2,3},{3,2},{4,5},{5,4},{6,7},{7,6},{8,9},{9,8},{10,11... | collective-permute-start | bytes 3145736 | tf_op jit(solution)/shard_map/part/ppermute | solution.py:675
  354.1 22.9 %collective-permute-start.27 = (bf16[4,64,1024]{2,1,0:T(8,128)(2,1)}, bf16[4,64,1024]{2,1,0:T(8,128)(2,1)}, u32[]{:S(2)}, u32[]{:S(2)}) collective-permute-start(bf16[4,64,1024]{2,1,0:T(8,128)(2,1)} %get-tuple-element.167), channel_id=1, source_target_pairs={{0,4},{4,0},{8,12},{12,8},{16,20},{20,16},{24,28},{28,24},{1,5},{5... | collective-permute-start | bytes 1572872 | tf_op jit(solution)/shard_map/part/ppermute | solution.py:675
  365.3 22.4 %collective-permute-start.25 = (bf16[4,128,512]{2,0,1:T(4,128)(2,1)}, bf16[4,128,512]{2,0,1:T(4,128)(2,1)}, u32[]{:S(2)}, u32[]{:S(2)}) collective-permute-start(bf16[4,128,512]{2,0,1:T(4,128)(2,1)} %copy.81), channel_id=1, source_target_pairs={{0,4},{4,0},{8,12},{12,8},{16,20},{20,16},{24,28},{28,24},{1,5},{5... | collective-permute-start | bytes 1572872 | tf_op jit(solution)/shard_map/part/ppermute | solution.py:675
  367.9 23.4 %collective-permute-start.23 = (bf16[4,144,512]{2,0,1:T(4,128)(2,1)}, bf16[4,144,512]{2,0,1:T(4,128)(2,1)S(1)}, u32[]{:S(2)}, u32[]{:S(2)}) collective-permute-start(bf16[4,144,512]{2,0,1:T(4,128)(2,1)} %dynamic_update_slice.7), channel_id=1, source_target_pairs={{0,8},{4,12},{8,0},{12,4},{16,24},{20,28},{24,16},{28,20},{1,9},{5... | collective-permute-start | bytes 1769480 | tf_op jit(solution)/shard_map/part/ppermute | solution.py:675
  370.6 31.5 %collective-permute-start.29 = (bf16[512,1024]{1,0:T(8,128)(2,1)}, bf16[512,1024]{1,0:T(8,128)(2,1)}, u32[]{:S(2)}, u32[]{:S(2)}) collective-permute-start(bf16[512,1024]{1,0:T(8,128)(2,1)} %add_convert_fusion), channel_id=1, source_target_pairs={{0,2},{1,3},{2,0},{3,1},{4,6},{5,7},{6,4},{7,5},{8,10},{9,11},{10,... | collective-permute-start | bytes 3145736 | tf_op jit(solution)/shard_map/back_across/ppermute | solution.py:675
  377.0 33.1 %collective-permute-start.22 = (bf16[512,1024]{1,0:T(8,128)(2,1)}, bf16[512,1024]{1,0:T(8,128)(2,1)}, u32[]{:S(2)}, u32[]{:S(2)}) collective-permute-start(bf16[512,1024]{1,0:T(8,128)(2,1)} %get-tuple-element.156), channel_id=1, source_target_pairs={{0,1},{1,0},{2,3},{3,2},{4,5},{5,4},{6,7},{7,6},{8,9},{9,8},{10,11... | collective-permute-start | bytes 3145736 | tf_op jit(solution)/shard_map/part/ppermute | solution.py:675
  378.3 13.8 %collective-permute-start.28 = (bf16[2,64,1024]{2,1,0:T(8,128)(2,1)S(1)}, bf16[2,64,1024]{2,1,0:T(8,128)(2,1)S(1)}, u32[]{:S(2)}, u32[]{:S(2)}) collective-permute-start(bf16[2,64,1024]{2,1,0:T(8,128)(2,1)S(1)} %slice.210), channel_id=1, source_target_pairs={{0,8},{4,12},{8,0},{12,4},{16,24},{20,28},{24,16},{28,20},{1,9},{5... | collective-permute-start | bytes 786440 | tf_op jit(solution)/shard_map/part/ppermute | solution.py:675
  389.5 7.8 %collective-permute-start.26 = (bf16[2,128,512]{2,0,1:T(2,128)(2,1)S(1)}, bf16[2,128,512]{2,0,1:T(2,128)(2,1)S(1)}, u32[]{:S(2)}, u32[]{:S(2)}) collective-permute-start(bf16[2,128,512]{2,0,1:T(2,128)(2,1)S(1)} %slice.211), channel_id=1, source_target_pairs={{0,8},{4,12},{8,0},{12,4},{16,24},{20,28},{24,16},{28,20},{1,9},{5... | collective-permute-start | bytes 786440 | tf_op jit(solution)/shard_map/part/ppermute | solution.py:675
  391.8 7.9 %collective-permute-start.24 = (bf16[2,144,512]{2,0,1:T(2,128)(2,1)S(1)}, bf16[2,144,512]{2,0,1:T(2,128)(2,1)S(1)}, u32[]{:S(2)}, u32[]{:S(2)}) collective-permute-start(bf16[2,144,512]{2,0,1:T(2,128)(2,1)S(1)} %slice.209), channel_id=1, source_target_pairs={{0,4},{4,0},{8,12},{12,8},{16,20},{20,16},{24,28},{28,24},{1,5},{5... | collective-permute-start | bytes 884744 | tf_op jit(solution)/shard_map/part/ppermute | solution.py:675
  403.2 32.6 %collective-permute-start.30 = (bf16[1,144,512]{2,0,1:T(2,128)(2,1)}, bf16[1,144,512]{2,0,1:T(2,128)(2,1)}, u32[]{:S(2)}, u32[]{:S(2)}) collective-permute-start(bf16[1,144,512]{2,0,1:T(2,128)(2,1)} %slice.212), channel_id=1, source_target_pairs={{0,16},{4,20},{8,24},{12,28},{16,0},{20,4},{24,8},{28,12},{1,17},{... | collective-permute-start | bytes 442376 | tf_op jit(solution)/shard_map/part/ppermute | solution.py:675
  406.2 23.1 %collective-permute-start.32 = (bf16[1,64,1024]{2,1,0:T(8,128)(2,1)}, bf16[1,64,1024]{2,1,0:T(8,128)(2,1)S(1)}, u32[]{:S(2)}, u32[]{:S(2)}) collective-permute-start(bf16[1,64,1024]{2,1,0:T(8,128)(2,1)} %slice.213), channel_id=1, source_target_pairs={{0,16},{4,20},{8,24},{12,28},{16,0},{20,4},{24,8},{28,12},{1,17},{... | collective-permute-start | bytes 393224 | tf_op jit(solution)/shard_map/part/ppermute | solution.py:675
  408.7 25.7 %collective-permute-start.31 = (bf16[1,128,512]{2,0,1:T(2,128)(2,1)}, bf16[1,128,512]{2,0,1:T(2,128)(2,1)}, u32[]{:S(2)}, u32[]{:S(2)}) collective-permute-start(bf16[1,128,512]{2,0,1:T(2,128)(2,1)} %slice.214), channel_id=1, source_target_pairs={{0,16},{4,20},{8,24},{12,28},{16,0},{20,4},{24,8},{28,12},{1,17},{... | collective-permute-start | bytes 393224 | tf_op jit(solution)/shard_map/part/ppermute | solution.py:675
  437.3 5.2 %collective-permute-start.33 = (f32[288]{0:T(512)S(1)}, f32[288]{0:T(512)S(1)}, u32[]{:S(2)}, u32[]{:S(2)}) collective-permute-start(f32[288]{0:T(512)S(1)} %slice_reduce_fusion), channel_id=1, source_target_pairs={{0,1},{1,0},{2,3},{3,2},{4,5},{5,4},{6,7},{7,6},{8,9},{9,8},{10,11... | collective-permute-start | bytes 3464 | tf_op jit(solution)/shard_map/part/ppermute | solution.py:675
  437.3 5.1 %collective-permute-start.34 = (f32[288]{0:T(512)S(1)}, f32[288]{0:T(512)S(1)}, u32[]{:S(2)}, u32[]{:S(2)}) collective-permute-start(f32[288]{0:T(512)S(1)} %slice_reduce_fusion), channel_id=1, source_target_pairs={{0,2},{1,3},{2,0},{3,1},{4,6},{5,7},{6,4},{7,5},{8,10},{9,11},{10,... | collective-permute-start | bytes 3464 | tf_op jit(solution)/shard_map/part/ppermute | solution.py:675
  437.4 5.0 %collective-permute-start.35 = (f32[288]{0:T(512)S(1)}, f32[288]{0:T(512)S(1)}, u32[]{:S(2)}, u32[]{:S(2)}) collective-permute-start(f32[288]{0:T(512)S(1)} %slice_reduce_fusion), channel_id=1, source_target_pairs={{0,3},{1,2},{2,1},{3,0},{4,7},{5,6},{6,5},{7,4},{8,11},{9,10},{10,... | collective-permute-start | bytes 3464 | tf_op jit(solution)/shard_map/part/ppermute | solution.py:675
  (58 other events, 400.8 us)
Sparse Core Ops, SparseCore 0:
  11.2 66.2 all-gather.4
  80.2 78.4 all-gather.6
  247.7 93.4 reduce-scatter.1

commit v6 on v4

--- a/solution.py
+++ b/solution.py
@@ -25,7 +25,7 @@
 SCALE = HEAD_SIZE ** (-0.5)
 LOG2E = 1.4426950408889634
 BLOCK = 256
-VMEM_LIMIT = 48 * 1024 * 1024
+VMEM_LIMIT = 56 * 1024 * 1024
 F32 = jnp.float32
 BF16 = jnp.bfloat16
 
@@ -93,7 +93,7 @@
 
 
 def project_kernel(
-    x, gain, matrix, cos, sin, gain_q, gain_k, normed_turned, raw_q, raw_k, q, k, v, k_turned, v_turned
+    x, gain, matrix, cos, sin, gain_q, gain_k, normed_turned, raw_q, raw_k, q, k, v, k_turned
 ):
     normed = norm_rows(x[...].astype(F32), gain[...])
     normed_turned[...] = normed.T.astype(BF16)
@@ -111,42 +111,56 @@
         turned = head_rotated(value, gain_k[...], c, s)
         k[:, lanes_of(j)] = turned.astype(BF16)
         k_turned[lanes_of(j), :] = turned.T.astype(BF16)
-        value = part[:, lanes_of(GROUP + 1)]
-        v[:, lanes_of(j)] = value.astype(BF16)
-        v_turned[lanes_of(j), :] = value.T.astype(BF16)
-
-
-def attend_kernel(offset, info, q, k, v_turned, start, out, out_turned, logs):
-    blocks = k.shape[0] // BLOCK
+        v[:, lanes_of(j)] = part[:, lanes_of(GROUP + 1)].astype(BF16)
+
+
+def stacked(value):
+    return jnp.concatenate([value[:, lanes_of(h)] for h in range(GROUP)], axis=0)
+
+
+def stacked_turned(value):
+    return jnp.concatenate(
+        [value[:, lanes_of(h)].astype(F32).T.astype(BF16) for h in range(GROUP)], axis=1
+    )
+
+
+def attend_kernel(offset, info, q, k_turned, v, out, out_turned, logs):
+    blocks = v.shape[0] // BLOCK
     flip = info[blocks]
+    documents = info.shape[0] - blocks - 1
 
     def one_block(i, _):
         here = at_block(i)
         b = (i + offset) ^ flip
-        first = start[:, here]
-        queries = [q[here, lanes_of(h)] for h in range(GROUP)]
+        index = b * BLOCK + lax.broadcasted_iota(jnp.int32, (BLOCK, 1), 0)
+        first = jnp.zeros((BLOCK, 1), jnp.int32)
+        for d in range(documents):
+            begin = info[blocks + 1 + d]
+            first = jnp.maximum(first, jnp.where(index >= begin, begin, 0))
+        query = stacked(q[here, :])
 
         def keys_step(kb, carry):
+            total, blend = carry
             there = at_block(kb ^ flip)
-            key, value = k[there, :], v_turned[:, there]
-            allowed = allowed_block(kb, b, first)
-            after = []
-            for h in range(GROUP):
-                total, blend = carry[h]
-                p = jnp.where(allowed, jnp.exp2(nt(key, queries[h]) * (SCALE * LOG2E)), 0.0)
-                after.append(
-                    (total + jnp.sum(p, axis=0, keepdims=True), blend + nn(value, p.astype(BF16)))
-                )
-            return tuple(after)
-
-        zero = (jnp.zeros((1, BLOCK), F32), jnp.zeros((HEAD_SIZE, BLOCK), F32))
-        done = lax.fori_loop(info[b], b + 1, keys_step, (zero,) * GROUP)
+            keys = kb * BLOCK + lax.broadcasted_iota(jnp.int32, (BLOCK, BLOCK), 1)
+            allowed = (keys >= first) & (keys <= index)
+            score = nn(query, k_turned[:, there]).reshape(GROUP, BLOCK, BLOCK)
+            p = jnp.where(allowed[None], jnp.exp2(score * (SCALE * LOG2E)), 0.0)
+            p = p.reshape(GROUP * BLOCK, BLOCK)
+            for lane in range(0, BLOCK, HEAD_SIZE):
+                total = total + p[:, lane : lane + HEAD_SIZE]
+            return total, blend + nn(p.astype(BF16), v[there, :])
+
+        zero = jnp.zeros((GROUP * BLOCK, HEAD_SIZE), F32)
+        total, blend = lax.fori_loop(info[b], b + 1, keys_step, (zero, zero))
+        total = jnp.sum(total, axis=1, keepdims=True)
+        result = blend / total
+        log = jnp.broadcast_to(jnp.log2(total), result.shape)
         for h in range(GROUP):
-            total, blend = done[h]
-            result = blend / total
-            out[here, lanes_of(h)] = result.T.astype(BF16)
-            out_turned[lanes_of(h), here] = result.astype(BF16)
-            logs[0, h : h + 1, here] = jnp.log2(total)
+            rows = slice(h * BLOCK, (h + 1) * BLOCK)
+            out[here, lanes_of(h)] = result[rows].astype(BF16)
+            out_turned[lanes_of(h), here] = result[rows].T.astype(BF16)
+            logs[0, h : h + 1, here] = log[rows].T[0:1, :]
         return 0
 
     lax.fori_loop(0, q.shape[0] // BLOCK, one_block, 0)
@@ -158,40 +172,40 @@
 ):
     flip = info[k.shape[0] // BLOCK]
 
+    def twice(row):
+        return jnp.concatenate([row] * GROUP, axis=1)
+
     def one_block(i, total_gain):
         here = at_block(i)
         b = (i + offset) ^ flip
         first = start[:, here]
-        queries, gradients, across, log = [], [], [], []
+        gradients = grad_out[here, :]
+        both = gradients.astype(F32) * out[here, :].astype(F32)
+        query, gradient = stacked(q[here, :]), stacked(gradients)
+        query_turned, gradient_turned = stacked_turned(q[here, :]), stacked_turned(gradients)
+        across, log = [], []
         for h in range(GROUP):
-            g = grad_out[here, lanes_of(h)]
-            queries.append(q[here, lanes_of(h)])
-            gradients.append(g)
-            both = g.astype(F32) * out[here, lanes_of(h)].astype(F32)
-            across.append(jnp.sum(both.T, axis=0, keepdims=True))
+            across.append(jnp.sum(both[:, lanes_of(h)].T, axis=0, keepdims=True))
             log.append(logs[0, h : h + 1, here])
-
-        def keys_step(kb, carry):
+        across, log = jnp.concatenate(across, axis=1), jnp.concatenate(log, axis=1)
+
+        def keys_step(kb, grad_query):
             there = at_block(kb ^ flip)
-            key, value, key_turned = k[there, :], v[there, :], k_turned[:, there]
-            allowed = allowed_block(kb, b, first)
-            after, add_k, add_v = [], 0.0, 0.0
-            for h in range(GROUP):
-                s = nt(key, queries[h])
-                p = jnp.where(allowed, jnp.exp2(s * (SCALE * LOG2E) - log[h]), 0.0)
-                d = (p * (nt(value, gradients[h]) - across[h])).astype(BF16)
-                add_v = add_v + nn(p.astype(BF16), gradients[h])
-                add_k = add_k + nn(d, queries[h])
-                after.append(carry[h] + nn(key_turned, d))
-            grad_k[there, :] += add_k
-            grad_v[there, :] += add_v
-            return tuple(after)
-
-        zero = jnp.zeros((HEAD_SIZE, BLOCK), F32)
-        done = lax.fori_loop(info[b], b + 1, keys_step, (zero,) * GROUP)
+            allowed = twice(allowed_block(kb, b, first).astype(jnp.int32)) > 0
+            s = nn(k[there, :], query_turned)
+            p = jnp.where(allowed, jnp.exp2(s * (SCALE * LOG2E) - log), 0.0)
+            d = (p * (nn(v[there, :], gradient_turned) - across)).astype(BF16)
+            grad_v[there, :] += nn(p.astype(BF16), gradient)
+            grad_k[there, :] += nn(d, query)
+            return grad_query + nn(k_turned[:, there], d)
+
+        done = lax.fori_loop(
+            info[b], b + 1, keys_step, jnp.zeros((HEAD_SIZE, GROUP * BLOCK), F32)
+        )
         c, s = cos[here, :], sin[here, :]
         for h in range(GROUP):
-            back, gain = head_back(raw_q[here, lanes_of(h)], gain_q[...], c, s, done[h].T * SCALE)
+            grad = done[:, h * BLOCK : (h + 1) * BLOCK].T * SCALE
+            back, gain = head_back(raw_q[here, lanes_of(h)], gain_q[...], c, s, grad)
             store(i, h, back.astype(BF16))
             total_gain = total_gain + gain
         return total_gain
@@ -389,52 +403,52 @@
         ],
         out_specs=[
             by_lanes(width), by_rows(q_width), by_rows(k_width), by_rows(q_width),
-            by_rows(k_width), by_rows(k_width), by_lanes(k_width), by_lanes(k_width),
+            by_rows(k_width), by_rows(k_width), by_lanes(k_width),
         ],
         out_shape=[
             shaped((width, rows), BF16), shaped((rows, q_width), F32),
             shaped((rows, k_width), F32), shaped((rows, q_width), BF16),
             shaped((rows, k_width), BF16), shaped((rows, k_width), BF16),
-            shaped((k_width, rows), BF16), shaped((k_width, rows), BF16),
+            shaped((k_width, rows), BF16),
         ],
         **params("project", 10_000_000_000),
     )(x, gain, matrix, cos, sin, gain_q, gain_k)
 
 
 def head_specs(half, rows):
-    at = lambda j: j
     n = rows // 2
+    queries = GROUP * HEAD_SIZE
     return dict(
-        q=pl.BlockSpec((n, GROUP * HEAD_SIZE), lambda j, info: (half, at(j))),
-        k=pl.BlockSpec((rows, HEAD_SIZE), lambda j, info: (0, at(j))),
-        turned=pl.BlockSpec((HEAD_SIZE, rows), lambda j, info: (at(j), 0)),
+        q=pl.BlockSpec((n, queries), lambda j, info: (half, j)),
+        k=pl.BlockSpec((rows, HEAD_SIZE), lambda j, info: (0, j)),
+        turned=pl.BlockSpec((HEAD_SIZE, rows), lambda j, info: (j, 0)),
         start=pl.BlockSpec((1, n), lambda j, info: (0, half)),
-        out=pl.BlockSpec((n, GROUP * HEAD_SIZE), lambda j, info: (0, at(j))),
-        logs=pl.BlockSpec((1, GROUP, n), lambda j, info: (at(j), 0, 0)),
+        out=pl.BlockSpec((n, queries), lambda j, info: (0, j)),
+        out_turned=pl.BlockSpec((queries, n), lambda j, info: (j, 0)),
+        logs=pl.BlockSpec((1, GROUP, n), lambda j, info: (j, 0, 0)),
         angle=pl.BlockSpec((n, HEAD_SIZE), lambda j, info: (half, 0)),
-    )
-
-
-def attend(half, info, q, k, v_turned, start):
-    rows = k.shape[0]
-    n, heads = rows // 2, k.shape[1] // HEAD_SIZE
+        row=fixed((1, HEAD_SIZE)),
+    )
+
+
+def attend(half, info, q, k_turned, v):
+    rows = v.shape[0]
+    n, heads = rows // 2, v.shape[1] // HEAD_SIZE
     s = head_specs(half, rows)
     return pl.pallas_call(
         lambda *refs: attend_kernel(half * n // BLOCK, *refs),
         grid_spec=pltpu.PrefetchScalarGridSpec(
             num_scalar_prefetch=1,
             grid=(heads,),
-            in_specs=[s["q"], s["k"], s["turned"], s["start"]],
-            out_specs=[
-                s["out"], pl.BlockSpec((GROUP * HEAD_SIZE, n), lambda j, info: (j, 0)), s["logs"],
-            ],
+            in_specs=[s["q"], s["turned"], s["k"]],
+            out_specs=[s["out"], s["out_turned"], s["logs"]],
         ),
         out_shape=[
             shaped((n, q.shape[1]), BF16), shaped((q.shape[1], n), BF16),
             shaped((heads, GROUP, n), F32),
         ],
         **params("attend", 18_000_000_000),
-    )(info, q, k, v_turned, start)
+    )(info, q, k_turned, v)
 
 
 def attend_back_own(info, q, k, v, k_turned, start, logs, out, grad_out, raw_q, cos, sin, gain_q):
@@ -448,7 +462,7 @@
             grid=(heads,),
             in_specs=[
                 s["q"], s["k"], s["k"], s["turned"], s["start"], s["logs"], s["out"], s["out"],
-                s["q"], s["angle"], s["angle"], fixed((1, HEAD_SIZE)),
+                s["q"], s["angle"], s["angle"], s["row"],
             ],
             out_specs=[
                 s["out"], s["k"], s["k"],
@@ -471,7 +485,7 @@
     heads = k.shape[1] // HEAD_SIZE
     width = SLOTS * HEAD_SIZE
     s = head_specs(1, rows)
-    row = fixed((1, HEAD_SIZE))
+    whole = fixed((rows, HEAD_SIZE))
     return pl.pallas_call(
         back_other_kernel,
         grid_spec=pltpu.PrefetchScalarGridSpec(
@@ -479,9 +493,8 @@
             grid=(heads,),
             in_specs=[
                 s["q"], s["k"], s["k"], s["turned"], s["start"], s["logs"], s["out"], s["out"],
-                s["q"], s["angle"], s["angle"], row,
-                fixed((rows, HEAD_SIZE)), fixed((rows, HEAD_SIZE)), s["k"], row, s["out"], s["k"],
-                s["k"],
+                s["q"], s["angle"], s["angle"], s["row"],
+                whole, whole, s["k"], s["row"], s["out"], s["k"], s["k"],
             ],
             out_specs=[
                 pl.BlockSpec((rows, width), lambda j, info: (0, j)),
@@ -539,6 +552,7 @@
     pieces = grads[0].shape[1] // half
     count = hidden[0].shape[0]
     packs = packed_shape is not None
+    written = pieces * width // 8 + 2 * count // 8
     gate_block = pl.BlockSpec((n, half), lambda i: (0, jnp.minimum(i, pieces - 1)))
     down_block = pl.BlockSpec((n, half), lambda i: (0, jnp.maximum(i - pieces, 0)))
     shapes = [packed_shape] if packs else [(width, 2 * count), (count, width)]
@@ -549,7 +563,7 @@
             fixed((width, n)), fixed((width, n)), gate_block, gate_block,
             fixed((count, n)), fixed((count, n)), down_block, down_block,
         ],
-        out_specs=[fixed(shape) for shape in shapes],
+        out_specs=[fixed((8, written) + shapes[0][2:])] if packs else [fixed(x) for x in shapes],
         out_shape=[shaped(shape, BF16) for shape in shapes],
         **params("feed_weights", 16_000_000_000),
     )(*h, *grads, *hidden, *dy)
@@ -570,6 +584,103 @@
     )(grad, matrix)
 
 
+def bit_of(p, bit):
+    return (p // bit) % 2
+
+
+def place(p, order):
+    return sum(bit_of(p, bit) * 4 // 2**i for i, bit in enumerate(order))
+
+
+ORDERS = ((2, 1, 4), (1, 2, 4))
+
+
+def project_weights_kernel(me, h_turned, grad, matrix, keep_a, send_a, keep_b, send_b, gains):
+    step = pl.program_id(0)
+    value = nn(h_turned[...], grad[...])
+    rows = value.shape[0] // 8
+    both = value * matrix[...].astype(F32)
+    folded = sum(both[:, i : i + 128] for i in range(0, both.shape[1], 128))
+    gains[0, :, :] = jnp.sum(folded.T, axis=0, keepdims=True)
+    for of, (order, keep, send) in enumerate(
+        ((ORDERS[0], keep_a, send_a), (ORDERS[1], keep_b, send_b))
+    ):
+        for d in range(8):
+            at = place(d ^ me[0], order)
+            part = value[d * rows : (d + 1) * rows].astype(BF16)
+
+            @pl.when((step == of) & (at < 4))
+            def _():
+                keep[at, :rows, :] = part
+
+            @pl.when((step == of) & (at >= 4))
+            def _():
+                send[at - 4, :rows, :] = part
+
+    @pl.when(step == 0)
+    def _():
+        zero = jnp.zeros((4, keep_a.shape[1] - rows, value.shape[1]), BF16)
+        keep_a[:, rows:, :] = zero
+        send_a[:, rows:, :] = zero
+
+
+def project_weights(me, h_turned, grad, matrix, extra):
+    width, rows = h_turned.shape
+    depth, lanes = width // 8, grad.shape[1] // 2
+    part = (4, depth, lanes)
+    longer = (4, depth + extra, lanes)
+    columns = lambda n: pl.BlockSpec((n, lanes), lambda i, me: (0, i))
+    return pl.pallas_call(
+        project_weights_kernel,
+        grid_spec=pltpu.PrefetchScalarGridSpec(
+            num_scalar_prefetch=1,
+            grid=(2,),
+            in_specs=[fixed((width, rows)), columns(rows), columns(width)],
+            out_specs=[
+                fixed(longer), fixed(longer), fixed(part), fixed(part),
+                pl.BlockSpec((1, 1, width), lambda i, me: (i, 0, 0)),
+            ],
+        ),
+        out_shape=[
+            shaped(longer, BF16), shaped(longer, BF16), shaped(part, BF16), shaped(part, BF16),
+            shaped((2, 1, width), F32),
+        ],
+        **params("project_weights", 8_000_000_000),
+    )(me, h_turned, grad, matrix)
+
+
+def out_weights_kernel(h_own, grad_own, h_other, grad_other, packed_in, packed):
+    value = (nn(h_own[...], grad_own[...]) + nn(h_other[...], grad_other[...])).astype(BF16)
+    n = packed.shape[0]
+    deep = HEAD_SIZE // n
+    heads = value.shape[0] // HEAD_SIZE
+    for d in range(n):
+        for h in range(heads):
+            of = h * HEAD_SIZE + d * deep
+            packed[d, h * deep : (h + 1) * deep, :] = value[of : of + deep]
+
+
+def out_weights(h_own, grad_own, h_other, grad_other, packed):
+    count, rows = h_own.shape
+    n, total, half = packed.shape
+    steps = grad_own.shape[1] // half
+    block = (n, count // n, half)
+    last = total // block[1] - steps
+    columns = pl.BlockSpec((rows, half), lambda i: (0, i))
+    return pl.pallas_call(
+        out_weights_kernel,
+        grid=(steps,),
+        in_specs=[
+            fixed((count, rows)), columns, fixed((count, rows)), columns,
+            pl.BlockSpec(memory_space=pl.ANY),
+        ],
+        out_specs=pl.BlockSpec(block, lambda i: (0, last + i, 0)),
+        out_shape=shaped(packed.shape, BF16),
+        input_output_aliases={4: 0},
+        **params("out_weights", 4_000_000_000),
+    )(h_own, grad_own, h_other, grad_other, packed)
+
+
 def flipped(value, axis, bit, name="part"):
     with jax.named_scope(name):
         return lax.ppermute(value, axis, [(i, i ^ bit) for i in range(lax.axis_size(axis))])
@@ -583,11 +694,13 @@
     return part.astype(F32) + flipped(beside, "tensor", 1).astype(F32)
 
 
-def halved(parts, axis, bit):
-    mine = (lax.axis_index("dp") // bit) % 2
-    send = lax.dynamic_index_in_dim(parts, 1 - mine, axis, keepdims=False).astype(BF16)
-    keep = lax.dynamic_index_in_dim(parts, mine, axis, keepdims=False)
-    return keep + flipped(send, "dp", bit).astype(F32)
+def added(keep, send, bit):
+    return keep.astype(F32) + flipped(send.astype(BF16), "dp", bit).astype(F32)
+
+
+def halved(value, bit):
+    half = value.shape[0] // 2
+    return added(value[:half], value[half:], bit)
 
 
 def per_device(
@@ -618,7 +731,7 @@
     pack_one = jnp.concatenate(
         [
             projection_weight.astype(BF16).reshape(depth, -1),
-            w_out.astype(BF16).reshape(-1, MODEL_WIDTH),
+            *([] if cubic else [w_out.astype(BF16).reshape(-1, MODEL_WIDTH)]),
             jnp.pad(gains.astype(BF16)[None, :], ((0, 15), (0, MODEL_WIDTH - gain_count))),
         ],
         axis=0,
@@ -631,15 +744,18 @@
         axis=0,
     )
 
-    def split_one(value):
-        return (
-            value[..., :depth, :],
-            value[..., depth : depth + out_rows, :],
-            value[..., depth + out_rows, :gain_count],
-        )
-
-    full_qkv, full_out, full_gains = split_one(lax.all_gather(pack_one, "dp", axis=0, tiled=False))
-    full_out = full_out.reshape(spread, out_heads, out_depth, MODEL_WIDTH).swapaxes(0, 1)
+    full_one = lax.all_gather(pack_one, "dp", axis=0, tiled=False)
+    full_qkv, full_gains = full_one[:, :depth], full_one[:, -16, :gain_count]
+    if cubic:
+        me_dp = lax.axis_index("dp")
+        own = w_out.astype(BF16)
+        full_out = jnp.zeros((out_heads, spread, out_depth, MODEL_WIDTH), BF16)
+        for bit in range(spread):
+            piece = flipped(own, "dp", bit, "w_out") if bit else own
+            full_out = lax.dynamic_update_index_in_dim(full_out, piece, me_dp ^ bit, 1)
+    else:
+        full_out = full_one[:, depth : depth + out_rows]
+        full_out = full_out.reshape(spread, out_heads, out_depth, MODEL_WIDTH).swapaxes(0, 1)
     full_two = lax.all_gather(pack_two, "dp", axis=0, tiled=False)
     qkv_matrix = full_qkv.reshape(MODEL_WIDTH, -1)
     out_matrix = full_out.reshape(-1, MODEL_WIDTH)
@@ -669,7 +785,9 @@
     cos = jnp.concatenate([cosine, cosine], axis=1)
     sin = jnp.concatenate([-sine, sine], axis=1)
     block_starts = start_of(jnp.arange(blocks, dtype=jnp.int32) * BLOCK) // BLOCK
-    info = jnp.concatenate([block_starts, (me * (local_rows // BLOCK))[None]]).astype(jnp.int32)
+    info = jnp.concatenate(
+        [block_starts, (me * (local_rows // BLOCK))[None], doc_starts]
+    ).astype(jnp.int32)
     start = start_of_row[None, :]
 
     rows_float = tokens.astype(F32)
@@ -678,17 +796,17 @@
         [tokens, flipped(tokens, "tensor", 1), tokens_across, flipped(tokens_across, "tensor", 1)],
         axis=0,
     )
-    normed_turned, raw_q, raw_k, q, k, v, k_turned, v_turned = project(
+    normed_turned, raw_q, raw_k, q, k, v, k_turned = project(
         tokens_all, gain_attn, qkv_matrix, cos, sin, gain_query, gain_key
     )
     grad_across = flipped(cotangent, "tensor", 2, "grad_across")
-    heads_other, heads_other_turned, logs_other = attend(1, info, q, k, v_turned, start)
+    heads_other, heads_other_turned, logs_other = attend(1, info, q, k_turned, v)
     heads_other, grad_across = together(heads_other, grad_across)
     beside = nn(heads_other[local_rows:], out_matrix).astype(BF16)
     near = near_sum(nn(heads_other[:local_rows], out_matrix), beside).astype(BF16)
     near, q_own = together(near, q)
     attn_across = flipped(near, "tensor", 2, "attn_across")
-    heads_own, heads_own_turned, logs_own = attend(0, info, q_own, k, v_turned, start)
+    heads_own, heads_own_turned, logs_own = attend(0, info, q_own, k_turned, v)
     heads_own, attn_across, full_two = together(heads_own, attn_across, full_two)
     beside = nn(heads_own[local_rows:], out_matrix).astype(BF16)
     attn_rows = near_sum(nn(heads_own[:local_rows], out_matrix), beside) + attn_across.astype(F32)
@@ -726,12 +844,36 @@
     back_across = flipped(near, "tensor", 2, "back_across")
 
     feed_grads = feed_weights(
-        full_two.shape if cubic else None, (h_own, h_other), (feed_grad_own, feed_grad_other),
+        (spread, full_two.shape[1] + 2 * out_rows, half) if cubic else None, (h_own, h_other), (feed_grad_own, feed_grad_other),
         (hidden_own, hidden_other), (grad_own, grad_other),
     )
     back_across, *feed_grads = together(back_across, *feed_grads)
+    grad_middle_part, grad_gain_mlp = norm_back(
+        middle, gain_mlp, back_near + back_across.astype(F32)
+    )
+    grad_middle = cotangent.astype(F32) + grad_middle_part
+    grad_middle_low = grad_middle.astype(BF16)
+    grad_middle_across = flipped(grad_middle_low, "tensor", 2, "grad_middle_across")
+
+    grad_middle_own = jnp.concatenate(
+        [grad_middle_low, flipped(grad_middle_low, "tensor", 1)], axis=0
+    )
+    grad_heads_own = nt(grad_middle_own, out_matrix).astype(BF16)
+    grad_q, grad_k, grad_v, gain_own = attend_back_own(
+        info, q, k, v, k_turned, start, logs_own, heads_own, grad_heads_own, raw_q, cos, sin,
+        gain_query,
+    )
+    grad_middle_across, grad_q, sum_2, sum_3 = together(grad_middle_across, grad_q, sum_2, sum_3)
+    near_mlp = near_sum(sum_2, sum_3).astype(BF16)
+    grad_middle_other = jnp.concatenate(
+        [grad_middle_across, flipped(grad_middle_across, "tensor", 1)], axis=0
+    )
+    grad_heads_other = nt(grad_middle_other, out_matrix).astype(BF16)
     if cubic:
-        feed_pack = feed_grads[0]
+        feed_pack = out_weights(
+            heads_own_turned, grad_middle_own, heads_other_turned, grad_middle_other, *feed_grads
+        )
+        feed_pack, near_mlp, grad_heads_other = together(feed_pack, near_mlp, grad_heads_other)
     else:
         feed_pack = jnp.concatenate(
             [
@@ -745,31 +887,6 @@
             axis=1,
         )
     feed_sum = lax.psum_scatter(feed_pack, "dp", scatter_dimension=0, tiled=True)[0].astype(F32)
-    grad_middle_part, grad_gain_mlp = norm_back(
-        middle, gain_mlp, back_near + back_across.astype(F32)
-    )
-    grad_middle = cotangent.astype(F32) + grad_middle_part
-    grad_middle_low = grad_middle.astype(BF16)
-    grad_middle_across = flipped(grad_middle_low, "tensor", 2, "grad_middle_across")
-
-    grad_middle_own = jnp.concatenate(
-        [grad_middle_low, flipped(grad_middle_low, "tensor", 1)], axis=0
-    )
-    grad_heads_own = nt(grad_middle_own, out_matrix).astype(BF16)
-    grad_q, grad_k, grad_v, gain_own = attend_back_own(
-        info, q, k, v, k_turned, start, logs_own, heads_own, grad_heads_own, raw_q, cos, sin,
-        gain_query,
-    )
-    grad_middle_across, grad_q, sum_2, sum_3 = together(grad_middle_across, grad_q, sum_2, sum_3)
-    near_mlp = near_sum(sum_2, sum_3).astype(BF16)
-    grad_middle_other = jnp.concatenate(
-        [grad_middle_across, flipped(grad_middle_across, "tensor", 1)], axis=0
-    )
-    grad_heads_other = nt(grad_middle_other, out_matrix).astype(BF16)
-    grad_out_w = (
-        nn(heads_own_turned, grad_middle_own) + nn(heads_other_turned, grad_middle_other)
-    ).astype(BF16)
-    near_mlp, grad_out_w, grad_heads_other = together(near_mlp, grad_out_w, grad_heads_other)
     mlp_across = flipped(near_mlp, "tensor", 2, "mlp_across")
     grad_qkv, gain_other = attend_back_other(
         info, q, k, v, k_turned, start, logs_other, heads_other, grad_heads_other,
@@ -778,48 +895,58 @@
     grad_qkv, mlp_across = together(grad_qkv, mlp_across)
     back_2, back_3 = unproject(1, grad_qkv, qkv_matrix)
     back_2, back_3, grad_qkv = together(back_2, back_3, grad_qkv)
-    grad_qkv_w = nn(normed_turned, grad_qkv)
-    near = near_sum(back_2, back_3).astype(BF16)
-    near, grad_qkv, grad_qkv_w, grad_out_w = together(near, grad_qkv, grad_qkv_w, grad_out_w)
-    back_across = flipped(near, "tensor", 2, "back_across")
-    grad_gain_attn = jnp.sum(qkv_matrix.astype(F32) * grad_qkv_w, axis=1) / gain_attn[0]
     grad_gain_heads = jnp.sum(gain_other, axis=0) + jnp.pad(
         jnp.sum(gain_own, axis=0), ((0, 1), (0, 0))
     )
-    gain_sums = jnp.concatenate([grad_gain_attn, grad_gain_mlp, grad_gain_heads.reshape(-1)])
-    back_0, back_1 = unproject(0, grad_qkv, qkv_matrix)
     if cubic:
-        cube = (2, 2, 2)
-        columns = grad_qkv_w.shape[1] // 2
-        gain_rows = jnp.pad(
-            gain_sums.reshape(cube + (1, gain_count)),
-            ((0, 0),) * 3 + ((0, 15), (0, columns - gain_count)),
+        extra = 16
+        relative = jnp.arange(8, dtype=jnp.int32) ^ me_dp
+        keep_a, send_a, keep_b, send_b, gain_halves = project_weights(
+            me_dp.astype(jnp.int32)[None], normed_turned, grad_qkv, qkv_matrix, extra
         )
-        sum_one = jnp.concatenate(
-            [grad_qkv_w[:, :columns].reshape(cube + (depth, -1)), gain_rows], axis=3
+        near = near_sum(back_2, back_3).astype(BF16)
+        near, grad_qkv, send_a, send_b, sum_0, sum_1 = together(
+            near, grad_qkv, send_a, send_b, sum_0, sum_1
         )
-        sum_two = grad_qkv_w[:, columns:].reshape(cube + (depth, -1))
-        sum_one, sum_two = halved(sum_one, 1, 2), halved(sum_two, 2, 1)
-        sum_one, sum_two = halved(sum_one, 1, 1), halved(sum_two, 1, 2)
-        sum_out = grad_out_w.reshape((out_heads,) + cube + (out_depth, MODEL_WIDTH))
-        sum_out = halved(halved(sum_out, 3, 1), 2, 2)
-        sum_one, sum_two, sum_out, back_across, feed_sum = together(
-            sum_one, sum_two, sum_out, back_across, feed_sum
-        )
-        sum_one, sum_two = halved(sum_one, 0, 4), halved(sum_two, 0, 4)
-        sum_out = halved(sum_out, 1, 4)
+        back_across = flipped(near, "tensor", 2, "back_across")
+        back_0, back_1 = unproject(0, grad_qkv, qkv_matrix)
+        sum_two = added(keep_b, send_b, ORDERS[1][0])
+        grad_gain_attn = jnp.sum(gain_halves, axis=(0, 1)) / gain_attn[0]
+        gain_sums = jnp.concatenate([grad_gain_attn, grad_gain_mlp, grad_gain_heads.reshape(-1)])
+        gain_rows = jnp.take(gain_sums.reshape(8, 1, gain_count), relative, axis=0).astype(BF16)
+        slots = sorted(range(8), key=lambda p: place(p, ORDERS[0]))
+        gain_rows = jnp.stack([gain_rows[p] for p in slots])
+        put = lambda value, rows: lax.dynamic_update_slice(value, rows, (0, depth, 0))
+        keep_a, send_a = put(keep_a, gain_rows[:4]), put(send_a, gain_rows[4:])
+        sum_one = added(keep_a, send_a, ORDERS[0][0])
+        sum_one, sum_two, back_across = together(sum_one, sum_two, back_across)
+        sum_one, sum_two = halved(sum_one, ORDERS[0][1]), halved(sum_two, ORDERS[1][1])
+        sum_one, sum_two, feed_sum = together(sum_one, sum_two, feed_sum)
+        sum_one, sum_two = halved(sum_one, 4)[0], halved(sum_two, 4)[0]
         sum_qkv = jnp.concatenate([sum_one[:depth], sum_two], axis=1)
         sum_qkv = sum_qkv.reshape(projection_weight.shape)
         sum_gains = sum_one[depth, :gain_count]
+        sum_out = feed_sum[-2 * out_rows :].reshape(2, out_rows, half).swapaxes(0, 1)
+        sum_out = sum_out.reshape(w_out.shape)
     else:
+        grad_qkv_w = nn(normed_turned, grad_qkv)
+        near = near_sum(back_2, back_3).astype(BF16)
+        back_across = flipped(near, "tensor", 2, "back_across")
+        back_0, back_1 = unproject(0, grad_qkv, qkv_matrix)
         sum_qkv = (
             lax.psum_scatter(grad_qkv_w.astype(BF16), "dp", scatter_dimension=0, tiled=True)
             .astype(F32)
             .reshape(projection_weight.shape)
         )
+        grad_out_w = nn(heads_own_turned, grad_middle_own) + nn(
+            heads_other_turned, grad_middle_other
+        )
         sum_out = lax.psum_scatter(
-            grad_out_w.reshape(out_heads, -1, MODEL_WIDTH), "dp", scatter_dimension=1, tiled=True
+            grad_out_w.astype(BF16).reshape(out_heads, -1, MODEL_WIDTH), "dp",
+            scatter_dimension=1, tiled=True,
         ).astype(F32)
+        grad_gain_attn = jnp.sum(qkv_matrix.astype(F32) * grad_qkv_w, axis=1) / gain_attn[0]
+        gain_sums = jnp.concatenate([grad_gain_attn, grad_gain_mlp, grad_gain_heads.reshape(-1)])
         sum_gains = lax.psum_scatter(gain_sums, "dp", scatter_dimension=0, tiled=True)
     sum_gains = sum_gains + sum(flipped(sum_gains, "tensor", bit) for bit in range(1, shards))
 
@@ -832,7 +959,7 @@
     sum_gate_up = (
         feed_sum[:gate_rows].reshape(pieces, depth, half).swapaxes(0, 1).reshape(w_gate_up.shape)
     )
-    sum_down = feed_sum[gate_rows:].reshape(2, -1, half).swapaxes(0, 1).reshape(w_down.shape)
+    sum_down = feed_sum[gate_rows : gate_rows + 2 * down_blocks * down_depth].reshape(2, -1, half).swapaxes(0, 1).reshape(w_down.shape)
 
     upd_qkv = adamw_update(
         projection_weight, first_moment_projection, second_moment_projection,

time: 446 us -> 470 us (1.054)
  waiting for transfers between devices: 113 us -> 130 us
  starting transfers between devices: 29.7 us -> 45.7 us
  local copies, waits for them, and re-layouts: 36.6 us -> 24 us
  Pallas kernels: 160 us -> 170 us
  matrix products: 20 us -> 13.1 us
    reduce_scatter x1, waiting for transfers between devices: 0.01 us -> 22.3 us  [per_device(): lax.psum_scatter(feed_pack, 'dp', scatter_dimension=0, tiled=True)[0]]
    pallas_call x0 -> x2, Pallas kernels: none -> 16.5 us  [the longest x1 10.9 us: project_weights(): pl.pallas_call(project_weights_kernel, grid_spec=pltpu.PrefetchScalarGrid...]
    ppermute x36 -> x40, starting transfers between devices: 29.6 us -> 45.5 us  [flipped(): lax.ppermute(value, axis, [(i, i ^ bit) for i in range(lax.axis_size(axis...]
    unnamed x137 -> x95, local copies, waits for them, and re-layouts: 14.3 us -> 4.69 us
    dot_general x7 -> x4, matrix products: 13.9 us -> 5.02 us  [nn(): return jnp.dot(a, b, preferred_element_type=F32)]
    all_gather x1, waiting for transfers between devices: 27.9 us -> 19.6 us  [per_device(): full_one = lax.all_gather(pack_one, 'dp', axis=0, tiled=False)]
    convert_element_type x8 -> x0, local copies, waits for them, and re-layouts: 6.04 us -> none  [halved(): lax.dynamic_index_in_dim(parts, 1 - mine, axis, keepdims=False).astype(BF16)]
    all_gather x1, waiting for transfers between devices: 10.7 us -> 16.6 us  [per_device(): full_two = lax.all_gather(pack_two, 'dp', axis=0, tiled=False)]
  transfers between devices with their start and end apart: 39 -> 43, of which waited for: 18 -> 21; matrix products, arithmetic and copies ran while one was open for 21% -> 17% of each run, Pallas kernels for 33% -> 33%
where the time goes in v6:
time: 470 us; the launch traced here: 463 us
  Pallas kernels  170 us (36%)
  waiting for transfers between devices  130 us (28%)
  other arithmetic  65 us (14%)
  starting transfers between devices  45.7 us (10%)
  local copies, waits for them, and re-layouts  24 us (5%)
  between operations  15.1 us (3%)
  matrix products  13.1 us (3%)
    ppermute x40, waiting for transfers between devices, flipped(): lax.ppermute(value, axis, [(i, i ^ bit) for i in range(lax.axis_size(axis...  71.6 us
    ppermute x40, starting transfers between devices, flipped(): lax.ppermute(value, axis, [(i, i ^ bit) for i in range(lax.axis_size(axis...  45.5 us
    pallas_call x2, Pallas kernels, feed(): pl.pallas_call(lambda *refs: feed_kernel(packs, *refs), grid=(rows // BLO...  35.2 us
    pallas_call x2, Pallas kernels, attend(): pl.pallas_call(lambda *refs: attend_kernel(half * n // BLOCK, *refs), gri...  28.6 us
    pallas_call x1, Pallas kernels, attend_back_other(): pl.pallas_call(back_other_kernel, grid_spec=pltpu.PrefetchScalarGridSpec(...  26.9 us
    reduce_scatter x1, waiting for transfers between devices, per_device(): lax.psum_scatter(feed_pack, 'dp', scatter_dimension=0, tiled=True)[0]  22.3 us
    all_gather x1, waiting for transfers between devices, per_device(): full_one = lax.all_gather(pack_one, 'dp', axis=0, tiled=False)  19.6 us
    pallas_call x1, Pallas kernels, attend_back_own(): pl.pallas_call(back_own_kernel, grid_spec=pltpu.PrefetchScalarGridSpec(nu...  18.3 us
  transfers between devices with their start and end apart: 43, of which 21 were waited for; matrix products, arithmetic and copies ran while one was open for 17% of the time, Pallas kernels for 33%

profile of v6, /device:TPU:0, one launch (start us, length us, event | category | flops | bytes accessed | tf_op | source)
XLA Modules:
  0.0 463.1 jit_solution(13063456105857300367)
XLA Ops:
  19.3 3.7 fusion.14
  29.6 3.7 collective-permute-start.9
  33.3 5.0 %collective-permute-done.1 = bf16[512,1024]{1,0:T(8,128)(2,1)} collective-permute-done((bf16[512,1024]{1,0:T(8,128)(2,1)S(1)}, bf16[512,1024]{1,0:T(8,128)(2,1)}, u32[]{:S(2)}, u32[]{:S(2)}) %collective-permute-start.1) | collective-permute-done | bytes 1048608 | tf_op jit(solution)/shard_map/tokens_across/ppermute | solution.py:686
  38.3 8.9 %collective-permute-done.7 = bf16[4,16,1024]{2,1,0:T(8,128)(2,1)S(1)} collective-permute-done((bf16[4,16,1024]{2,1,0:T(8,128)(2,1)S(1)}, bf16[4,16,1024]{2,1,0:T(8,128)(2,1)S(1)}, u32[]{:S(2)}, u32[]{:S(2)}) %collective-permute-start.7) | collective-permute-done | bytes 131104 | tf_op jit(solution)/shard_map/w_out/ppermute | solution.py:686
  55.1 4.0 pad_maximum_fusion.x
  59.1 19.6 %all-gather.5.cloned.1.call-done = bf16[1152,1024]{1,0:T(8,128)(2,1)} async-done(((bf16[144,1024]{1,0:T(8,128)(2,1)}), bf16[1152,1024]{1,0:T(8,128)(2,1)}) %all-gather.5.cloned.1.call-update) | async-done | bytes 2359312 | tf_op jit(solution)/shard_map/all_gather | solution.py:747
  83.8 13.6 %project.1 = (bf16[1024,2048]{1,0:T(8,128)(2,1)}, f32[2048,512]{1,0:T(8,128)}, f32[2048,256]{1,0:T(8,128)}, bf16[2048,512]{1,0:T(8,128)(2,1)}, bf16[2048,256]{1,...) custom-call(bf16[2048,1024]{1,0:T(8,128)(2,1)} %pad_maximum_fusion.x, f32[1,1024]{1,0:T(1,128)} %bitcast.135, ...), custom_call_target="tpu_custom_call" | custom-call | flops 156250000 | bytes 1000 | tf_op jit(solution)/shard_map/project/pallas_call | solution.py:397
  97.3 15.6 %attend.2 = (bf16[1024,512]{1,0:T(8,128)(2,1)}, bf16[512,1024]{1,0:T(8,128)(2,1)}, f32[2,2,1024]{2,1,0:T(2,128)}) custom-call(s32[17]{0:T(128)} %pad_add_fusion.refs_0_.info, bf16[2048,512]{1,0:T(8,128)(2,1)} %get-tuple-element.101.refs_1_.q, bf16[256,2048]{1,0:T(8,128)(2,1)} %get-tuple-element.97.refs_2_.k_turned, bf16[2048,256]{1,0:T(8,128)(2,1)} %get-tuple-element.98.refs_3_.v), custom_call_target="tpu_custom_call" | custom-call | flops 281249984 | bytes 1000 | tf_op jit(solution)/shard_map/attend/pallas_call | solution.py:438
  118.4 13.0 %attend.3 = (bf16[1024,512]{1,0:T(8,128)(2,1)}, bf16[512,1024]{1,0:T(8,128)(2,1)}, f32[2,2,1024]{2,1,0:T(2,128)}) custom-call(s32[17]{0:T(128)} %pad_add_fusion.refs_0_.info, bf16[2048,512]{1,0:T(8,128)(2,1)} %get-tuple-element.101.refs_1_.q, bf16[256,2048]{1,0:T(8,128)(2,1)} %get-tuple-element.97.refs_2_.k_turned, bf16[2048,256]{1,0:T(8,128)(2,1)} %get-tuple-element.98.refs_3_.v), custom_call_target="tpu_custom_call" | custom-call | flops 281249984 | bytes 1000 | tf_op jit(solution)/shard_map/attend/pallas_call | solution.py:438
  131.4 12.3 %collective-permute-done.12 = bf16[512,1024]{1,0:T(8,128)(2,1)} collective-permute-done((bf16[512,1024]{1,0:T(8,128)(2,1)S(1)}, bf16[512,1024]{1,0:T(8,128)(2,1)}, u32[]{:S(2)}, u32[]{:S(2)}) %collective-permute-start.12) | collective-permute-done | bytes 1048608 | tf_op jit(solution)/shard_map/attn_across/ppermute | solution.py:686
  143.7 16.6 %all-gather.7.cloned.1.call-done = bf16[4608,512]{1,0:T(8,128)(2,1)} async-done(((bf16[576,512]{1,0:T(8,128)(2,1)}), bf16[4608,512]{1,0:T(8,128)(2,1)}) %all-gather.7.cloned.1.call-update) | async-done | bytes 4718608 | tf_op jit(solution)/shard_map/all_gather | solution.py:759
  172.7 17.5 %feed.2 = (bf16[1024,1024]{1,0:T(8,128)(2,1)}, bf16[768,1024]{1,0:T(8,128)(2,1)}, bf16[1024,1536]{1,0:T(8,128)(2,1)}, bf16[512,1024]{1,0:T(8,128)(2,1)}, bf16[51...) custom-call(bf16[1024,1024]{1,0:T(8,128)(2,1)} %pad_maximum_fusion.1.refs_0_, ...), custom_call_target="tpu_custom_call" | custom-call | flops 250000000 | bytes 1000 | tf_op jit(solution)/shard_map/feed/pallas_call | solution.py:533
  196.2 3.2 pad_maximum_fusion.2.refs_0_
  199.4 17.7 %feed.3 = (bf16[1024,1024]{1,0:T(8,128)(2,1)}, bf16[768,1024]{1,0:T(8,128)(2,1)}, bf16[1024,1536]{1,0:T(8,128)(2,1)}, bf16[512,1024]{1,0:T(8,128)(2,1)}, bf16[51...) custom-call(bf16[1024,1024]{1,0:T(8,128)(2,1)} %pad_maximum_fusion.2.refs_0_, ...), custom_call_target="tpu_custom_call" | custom-call | flops 250000000 | bytes 1000 | tf_op jit(solution)/shard_map/feed/pallas_call | solution.py:533
  223.5 17.9 %feed_weights.1.packed_in = bf16[8,704,512]{2,1,0:T(8,128)(2,1)} custom-call(bf16[1024,1024]{1,0:T(8,128)(2,1)} %get-tuple-element.119.refs_0_, bf16[1024,1024]{1,0:T(8,128)(2,1)} %get-tuple-element.120.refs_1_, bf16[1024,1536]{1,0:T(8,128)(2,1)} %get-tuple-element.121.refs_2_, bf16[1024,1536]{1,0:T(8,128)(2,1)} %get-tuple-element.122.refs_3_, ...), custom_call_target="tpu_custom_call" | custom-call | flops 250000000 | bytes 1000 | tf_op jit(solution)/shard_map/feed_weights/pallas_call | solution.py:559
  241.4 5.9 %collective-permute-done.21 = bf16[512,1024]{1,0:T(8,128)(2,1)S(1)} collective-permute-done((bf16[512,1024]{1,0:T(8,128)(2,1)S(1)}, bf16[512,1024]{1,0:T(8,128)(2,1)S(1)}, u32[]{:S(2)}, u32[]{:S(2)}) %collective-permute-start.21) | collective-permute-done | bytes 1048608 | tf_op jit(solution)/shard_map/back_across/ppermute | solution.py:686
  248.2 3.9 fusion.27
  255.0 3.9 convolution_convert_fusion.1.grad_out
  258.9 18.3 %attend_back_own.1 = (bf16[1024,512]{1,0:T(8,128)(2,1)}, f32[2048,256]{1,0:T(8,128)}, f32[2048,256]{1,0:T(8,128)}, f32[2,1,128]{2,1,0:T(1,128)}) custom-call(s32[17]{0:T(128)} %pad_add_fusion.refs_0_.info, bf16[2048,512]{1,0:T(8,128)(2,1)} %get-tuple-element.101.refs_1_.q, bf16[2048,256]{1,0:T(8,128)(2,1)} %get-tuple-element.106.k, ...), custom_call_target="tpu_custom_call" | custom-call | flops 390624992 | bytes 1000 | tf_op jit(solution)/shard_map/attend_back_own/pallas_call | solution.py:458
  283.4 5.5 %out_weights.1 = bf16[8,704,512]{2,1,0:T(8,128)(2,1)} custom-call(bf16[512,1024]{1,0:T(8,128)(2,1)} %get-tuple-element.108.h_own, bf16[1024,1024]{1,0:T(8,128)(2,1)} %pad_maximum_fusion.3.grad_own, bf16[512,1024]{1,0:T(8,128)(2,1)} %get-tuple-element.126.h_other, bf16[1024,1024]{1,0:T(8,128)(2,1)} %copy-done.5, ...), custom_call_target="tpu_custom_call", output_to_operand_aliasing={{}: (4, {})} | custom-call | flops 62500000 | bytes 1000 | tf_op jit(solution)/shard_map/out_weights/pallas_call | solution.py:670
  288.9 4.2 convolution_convert_fusion.grad_out
  295.8 3.8 collective-permute-start.26
  299.6 26.9 %attend_back_other.1 = (bf16[2048,1024]{1,0:T(8,128)(2,1)}, f32[2,2,128]{2,1,0:T(2,128)}) custom-call(s32[17]{0:T(128)} %pad_add_fusion.refs_0_.info, bf16[2048,512]{1,0:T(8,128)(2,1)} %get-tuple-element.101.refs_1_.q, bf16[2048,256]{1,0:T(8,128)(2,1)} %get-tuple-element.106.k, bf16[2048,256]{1,0:T(8,128)(2,1)} %get-tuple-element.98.refs_3_.v, ...), custom_call_target="tpu_custom_call" | custom-call | flops 437500000 | bytes 1000 | tf_op jit(solution)/shard_map/attend_back_other/pallas_call | solution.py:489
  326.6 6.8 %unproject.2 = (bf16[512,1024]{1,0:T(8,128)(2,1)}, bf16[512,1024]{1,0:T(8,128)(2,1)}) custom-call(bf16[2048,1024]{1,0:T(8,128)(2,1)} %get-tuple-element.157.grad, bf16[1024,1024]{1,0:T(8,128)(2,1)} %bitcast.105), custom_call_target="tpu_custom_call" | custom-call | flops 62500000 | bytes 1000 | tf_op jit(solution)/shard_map/unproject/pallas_call | solution.py:577
  333.5 10.9 %project_weights.1 = (bf16[4,144,512]{2,1,0:T(8,128)(2,1)}, bf16[4,144,512]{2,1,0:T(8,128)(2,1)}, bf16[4,128,512]{2,1,0:T(8,128)(2,1)}, bf16[4,128,512]{2,1,0:T(8,128)(2,1)}, f32[2,1,1024]{2,1,0:T(1,128)}) custom-call(s32[1]{0:T(128)} %bitcast.34.me, bf16[1024,2048]{1,0:T(8,128)(2,1)} %get-tuple-element.149.h_turned, ...), custom_call_target="tpu_custom_call" | custom-call | flops 125000000 | bytes 1000 | tf_op jit(solution)/shard_map/project_weights/pallas_call | solution.py:633
  352.6 6.4 %unproject.3 = (bf16[512,1024]{1,0:T(8,128)(2,1)}, bf16[512,1024]{1,0:T(8,128)(2,1)}) custom-call(bf16[2048,1024]{1,0:T(8,128)(2,1)} %get-tuple-element.157.grad, bf16[1024,1024]{1,0:T(8,128)(2,1)} %bitcast.107), custom_call_target="tpu_custom_call" | custom-call | flops 62500000 | bytes 1000 | tf_op jit(solution)/shard_map/unproject/pallas_call | solution.py:577
  361.8 6.5 %collective-permute-start.30 = (bf16[4,144,512]{2,0,1:T(4,128)(2,1)}, bf16[4,144,512]{2,0,1:T(4,128)(2,1)}, u32[]{:S(2)}, u32[]{:S(2)}) collective-permute-start(bf16[4,144,512]{2,0,1:T(4,128)(2,1)} %dynamic_update_slice.40), channel_id=1, source_target_pairs={{0,8},{4,12},{8,0},{12,4},{16,24},{20,28},{24,16},{28,20},{1,9},{5... | collective-permute-start | bytes 1769480 | tf_op jit(solution)/shard_map/part/ppermute | solution.py:686
  374.7 7.6 %collective-permute-done.30 = bf16[4,144,512]{2,0,1:T(4,128)(2,1)} collective-permute-done((bf16[4,144,512]{2,0,1:T(4,128)(2,1)}, bf16[4,144,512]{2,0,1:T(4,128)(2,1)}, u32[]{:S(2)}, u32[]{:S(2)}) %collective-permute-start.30) | collective-permute-done | bytes 589856 | tf_op jit(solution)/shard_map/part/ppermute | solution.py:686
  388.8 3.8 fusion.3
  395.6 22.3 %reduce-scatter.2.cloned.1.call-done = bf16[1,704,512]{2,1,0:T(8,128)(2,1)} async-done(((bf16[8,704,512]{2,1,0:T(8,128)(2,1)}), bf16[1,704,512]{2,1,0:T(8,128)(2,1)}) %reduce-scatter.2.cloned.1.call-update) | async-done | bytes 720912 | tf_op jit(solution)/shard_map/reduce_scatter | solution.py:889
  426.3 5.1 %multiply_subtract_fusion = (f32[128,2,768]{2,1,0:T(2,128)}, f32[128,2,768]{2,1,0:T(2,128)}, f32[128,2,768]{2,1,0:T(2,128)}) fusion(f32[128,2,768]{2,1,0:T(2,128)S(1)} %copy-done.11, f32[128,2,768]{2,1,0:T(2,128)S(1)} %copy.116, f32[128,2,768]{2,1,0:T(2,128)} %param.28, f32[128,2,768]{2,1,0:T(2,128)} %param.33), kind=kLoop, calls=%fused_computation.38 | loop fusion | flops 2949120 | bytes 5505024 | tf_op jit(solution)/shard_map/sub | solution.py:53
  433.7 14.1 %collective-permute-done.36 = bf16[1,128,512]{2,0,1:T(2,128)(2,1)} collective-permute-done((bf16[1,128,512]{2,0,1:T(2,128)(2,1)}, bf16[1,128,512]{2,0,1:T(2,128)(2,1)}, u32[]{:S(2)}, u32[]{:S(2)}) %collective-permute-start.36) | collective-permute-done | bytes 131104 | tf_op jit(solution)/shard_map/part/ppermute | solution.py:686
  (276 shorter events, 119.8 us)
Async XLA Ops:
  7.2 71.4 %all-gather.5.cloned.1.call-start = ((), (), s32[]{:S(2)}) async-start(), calls=%async_computation.2 | async-start | bytes 2654208 | tf_op jit(solution)/shard_map/all_gather | solution.py:747
  10.1 150.2 %all-gather.7.cloned.1.call-start = ((), (), s32[]{:S(2)}) async-start(), calls=%async_computation.3 | async-start | bytes 5308416 | tf_op jit(solution)/shard_map/all_gather | solution.py:759
  11.9 406.0 %reduce-scatter.2.cloned.1.call-start = ((), (), s32[]{:S(2)}) async-start(), calls=%async_computation.1 | async-start | bytes 6488064 | tf_op jit(solution)/shard_map/reduce_scatter | solution.py:889
  12.0 26.3 %collective-permute-start.1 = (bf16[512,1024]{1,0:T(8,128)(2,1)S(1)}, bf16[512,1024]{1,0:T(8,128)(2,1)}, u32[]{:S(2)}, u32[]{:S(2)}) collective-permute-start(bf16[512,1024]{1,0:T(8,128)(2,1)S(1)} %copy-done), channel_id=1, source_target_pairs={{0,2},{1,3},{2,0},{3,1},{4,6},{5,7},{6,4},{7,5},{8,10},{9,11},{10,... | collective-permute-start | bytes 3145736 | tf_op jit(solution)/shard_map/tokens_across/ppermute | solution.py:686
  15.0 40.0 %collective-permute-start = (bf16[512,1024]{1,0:T(8,128)(2,1)S(1)}, bf16[512,1024]{1,0:T(8,128)(2,1)}, u32[]{:S(2)}, u32[]{:S(2)}) collective-permute-start(bf16[512,1024]{1,0:T(8,128)(2,1)S(1)} %copy-done), channel_id=1, source_target_pairs={{0,1},{1,0},{2,3},{3,2},{4,5},{5,4},{6,7},{7,6},{8,9},{9,8},{10,11... | collective-permute-start | bytes 3145736 | tf_op jit(solution)/shard_map/part/ppermute | solution.py:686
  15.2 10.5 %collective-permute-start.4 = (bf16[4,16,1024]{2,1,0:T(8,128)(2,1)S(1)}, bf16[4,16,1024]{2,1,0:T(8,128)(2,1)S(1)}, u32[]{:S(2)}, u32[]{:S(2)}) collective-permute-start(bf16[4,16,1024]{2,1,0:T(8,128)(2,1)S(1)} %get-tuple-element.199), channel_id=1, source_target_pairs={{0,4},{4,0},{8,12},{12,8},{16,20},{20,16},{24,28},{28,24},{1,5},{5... | collective-permute-start | bytes 393224 | tf_op jit(solution)/shard_map/w_out/ppermute | solution.py:686
  16.7 11.5 %collective-permute-start.5 = (bf16[4,16,1024]{2,1,0:T(8,128)(2,1)S(1)}, bf16[4,16,1024]{2,1,0:T(8,128)(2,1)S(1)}, u32[]{:S(2)}, u32[]{:S(2)}) collective-permute-start(bf16[4,16,1024]{2,1,0:T(8,128)(2,1)S(1)} %get-tuple-element.199), channel_id=1, source_target_pairs={{0,8},{4,12},{8,0},{12,4},{16,24},{20,28},{24,16},{28,20},{1,9},{5... | collective-permute-start | bytes 393224 | tf_op jit(solution)/shard_map/w_out/ppermute | solution.py:686
  18.3 11.3 %collective-permute-start.6 = (bf16[4,16,1024]{2,1,0:T(8,128)(2,1)S(1)}, bf16[4,16,1024]{2,1,0:T(8,128)(2,1)S(1)}, u32[]{:S(2)}, u32[]{:S(2)}) collective-permute-start(bf16[4,16,1024]{2,1,0:T(8,128)(2,1)S(1)} %get-tuple-element.199), channel_id=1, source_target_pairs={{0,12},{4,8},{8,4},{12,0},{16,28},{20,24},{24,20},{28,16},{1,13},{... | collective-permute-start | bytes 393224 | tf_op jit(solution)/shard_map/w_out/ppermute | solution.py:686
  25.7 21.5 %collective-permute-start.7 = (bf16[4,16,1024]{2,1,0:T(8,128)(2,1)S(1)}, bf16[4,16,1024]{2,1,0:T(8,128)(2,1)S(1)}, u32[]{:S(2)}, u32[]{:S(2)}) collective-permute-start(bf16[4,16,1024]{2,1,0:T(8,128)(2,1)S(1)} %get-tuple-element.199), channel_id=1, source_target_pairs={{0,16},{4,20},{8,24},{12,28},{16,0},{20,4},{24,8},{28,12},{1,17},{... | collective-permute-start | bytes 393224 | tf_op jit(solution)/shard_map/w_out/ppermute | solution.py:686
  28.3 22.8 %collective-permute-start.8 = (bf16[4,16,1024]{2,1,0:T(8,128)(2,1)S(1)}, bf16[4,16,1024]{2,1,0:T(8,128)(2,1)S(1)}, u32[]{:S(2)}, u32[]{:S(2)}) collective-permute-start(bf16[4,16,1024]{2,1,0:T(8,128)(2,1)S(1)} %get-tuple-element.199), channel_id=1, source_target_pairs={{0,20},{4,16},{8,28},{12,24},{16,4},{20,0},{24,12},{28,8},{1,21},{... | collective-permute-start | bytes 393224 | tf_op jit(solution)/shard_map/w_out/ppermute | solution.py:686
  29.6 23.6 %collective-permute-start.9 = (bf16[4,16,1024]{2,1,0:T(8,128)(2,1)S(1)}, bf16[4,16,1024]{2,1,0:T(8,128)(2,1)S(1)}, u32[]{:S(2)}, u32[]{:S(2)}) collective-permute-start(bf16[4,16,1024]{2,1,0:T(8,128)(2,1)S(1)} %get-tuple-element.199), channel_id=1, source_target_pairs={{0,24},{4,28},{8,16},{12,20},{16,8},{20,12},{24,0},{28,4},{1,25},{... | collective-permute-start | bytes 393224 | tf_op jit(solution)/shard_map/w_out/ppermute | solution.py:686
  38.3 16.8 %collective-permute-start.2 = (bf16[512,1024]{1,0:T(8,128)(2,1)}, bf16[512,1024]{1,0:T(8,128)(2,1)S(1)}, u32[]{:S(2)}, u32[]{:S(2)}) collective-permute-start(bf16[512,1024]{1,0:T(8,128)(2,1)} %collective-permute-done.1), channel_id=1, source_target_pairs={{0,1},{1,0},{2,3},{3,2},{4,5},{5,4},{6,7},{7,6},{8,9},{9,8},{10,11... | collective-permute-start | bytes 3145736 | tf_op jit(solution)/shard_map/part/ppermute | solution.py:686
  51.0 61.9 %collective-permute-start.3 = (bf16[512,1024]{1,0:T(8,128)(2,1)}, bf16[512,1024]{1,0:T(8,128)(2,1)}, u32[]{:S(2)}, u32[]{:S(2)}) collective-permute-start(bf16[512,1024]{1,0:T(8,128)(2,1)} %param.19), channel_id=1, source_target_pairs={{0,2},{1,3},{2,0},{3,1},{4,6},{5,7},{6,4},{7,5},{8,10},{9,11},{10,... | collective-permute-start | bytes 3145736 | tf_op jit(solution)/shard_map/grad_across/ppermute | solution.py:686
  118.3 25.4 %collective-permute-start.12 = (bf16[512,1024]{1,0:T(8,128)(2,1)S(1)}, bf16[512,1024]{1,0:T(8,128)(2,1)}, u32[]{:S(2)}, u32[]{:S(2)}) collective-permute-start(bf16[512,1024]{1,0:T(8,128)(2,1)S(1)} %add_convert_fusion.4), channel_id=1, source_target_pairs={{0,2},{1,3},{2,0},{3,1},{4,6},{5,7},{6,4},{7,5},{8,10},{9,11},{10,... | collective-permute-start | bytes 3145736 | tf_op jit(solution)/shard_map/attn_across/ppermute | solution.py:686
  162.1 8.6 %collective-permute-start.16 = (bf16[512,1024]{1,0:T(8,128)(2,1)}, bf16[512,1024]{1,0:T(8,128)(2,1)S(1)}, u32[]{:S(2)}, u32[]{:S(2)}) collective-permute-start(bf16[512,1024]{1,0:T(8,128)(2,1)} %param.19), channel_id=1, source_target_pairs={{0,1},{1,0},{2,3},{3,2},{4,5},{5,4},{6,7},{7,6},{8,9},{9,8},{10,11... | collective-permute-start | bytes 3145736 | tf_op jit(solution)/shard_map/part/ppermute | solution.py:686
  167.8 25.5 %collective-permute-start.14 = (bf16[512,1024]{1,0:T(8,128)(2,1)S(1)}, bf16[512,1024]{1,0:T(8,128)(2,1)}, u32[]{:S(2)}, u32[]{:S(2)}) collective-permute-start(bf16[512,1024]{1,0:T(8,128)(2,1)S(1)} %multiply_convert_fusion), channel_id=1, source_target_pairs={{0,2},{1,3},{2,0},{3,1},{4,6},{5,7},{6,4},{7,5},{8,10},{9,11},{10,... | collective-permute-start | bytes 3145736 | tf_op jit(solution)/shard_map/normed_across/ppermute | solution.py:686
  170.8 23.9 %collective-permute-start.19 = (bf16[512,1024]{1,0:T(8,128)(2,1)}, bf16[512,1024]{1,0:T(8,128)(2,1)}, u32[]{:S(2)}, u32[]{:S(2)}) collective-permute-start(bf16[512,1024]{1,0:T(8,128)(2,1)} %collective-permute-done.3), channel_id=1, source_target_pairs={{0,1},{1,0},{2,3},{3,2},{4,5},{5,4},{6,7},{7,6},{8,9},{9,8},{10,11... | collective-permute-start | bytes 3145736 | tf_op jit(solution)/shard_map/part/ppermute | solution.py:686
  221.8 25.5 %collective-permute-start.21 = (bf16[512,1024]{1,0:T(8,128)(2,1)S(1)}, bf16[512,1024]{1,0:T(8,128)(2,1)S(1)}, u32[]{:S(2)}, u32[]{:S(2)}) collective-permute-start(bf16[512,1024]{1,0:T(8,128)(2,1)S(1)} %add_convert_fusion.3), channel_id=1, source_target_pairs={{0,2},{1,3},{2,0},{3,1},{4,6},{5,7},{6,4},{7,5},{8,10},{9,11},{10,... | collective-permute-start | bytes 3145736 | tf_op jit(solution)/shard_map/back_across/ppermute | solution.py:686
  223.4 23.9 %collective-permute-start.17 = (bf16[512,1024]{1,0:T(8,128)(2,1)}, bf16[512,1024]{1,0:T(8,128)(2,1)S(1)}, u32[]{:S(2)}, u32[]{:S(2)}) collective-permute-start(bf16[512,1024]{1,0:T(8,128)(2,1)} %get-tuple-element.112), channel_id=1, source_target_pairs={{0,1},{1,0},{2,3},{3,2},{4,5},{5,4},{6,7},{7,6},{8,9},{9,8},{10,11... | collective-permute-start | bytes 3145736 | tf_op jit(solution)/shard_map/part/ppermute | solution.py:686
  252.1 25.8 %collective-permute-start.23 = (bf16[512,1024]{1,0:T(8,128)(2,1)}, bf16[512,1024]{1,0:T(8,128)(2,1)S(1)}, u32[]{:S(2)}, u32[]{:S(2)}) collective-permute-start(bf16[512,1024]{1,0:T(8,128)(2,1)} %get-tuple-element.194), channel_id=1, source_target_pairs={{0,2},{1,3},{2,0},{3,1},{4,6},{5,7},{6,4},{7,5},{8,10},{9,11},{10,... | collective-permute-start | bytes 3145736 | tf_op jit(solution)/shard_map/grad_middle_across/ppermute | solution.py:686
  277.9 15.2 %collective-permute-start.25 = (bf16[512,1024]{1,0:T(8,128)(2,1)}, bf16[512,1024]{1,0:T(8,128)(2,1)}, u32[]{:S(2)}, u32[]{:S(2)}) collective-permute-start(bf16[512,1024]{1,0:T(8,128)(2,1)} %get-tuple-element.135), channel_id=1, source_target_pairs={{0,1},{1,0},{2,3},{3,2},{4,5},{5,4},{6,7},{7,6},{8,9},{9,8},{10,11... | collective-permute-start | bytes 3145736 | tf_op jit(solution)/shard_map/part/ppermute | solution.py:686
  295.8 30.7 %collective-permute-start.26 = (bf16[512,1024]{1,0:T(8,128)(2,1)}, bf16[512,1024]{1,0:T(8,128)(2,1)S(1)}, u32[]{:S(2)}, u32[]{:S(2)}) collective-permute-start(bf16[512,1024]{1,0:T(8,128)(2,1)} %add_convert_fusion.2), channel_id=1, source_target_pairs={{0,2},{1,3},{2,0},{3,1},{4,6},{5,7},{6,4},{7,5},{8,10},{9,11},{10,... | collective-permute-start | bytes 3145736 | tf_op jit(solution)/shard_map/mlp_across/ppermute | solution.py:686
  333.4 12.5 %collective-permute-start.27 = (bf16[512,1024]{1,0:T(8,128)(2,1)}, bf16[512,1024]{1,0:T(8,128)(2,1)}, u32[]{:S(2)}, u32[]{:S(2)}) collective-permute-start(bf16[512,1024]{1,0:T(8,128)(2,1)} %get-tuple-element.147), channel_id=1, source_target_pairs={{0,1},{1,0},{2,3},{3,2},{4,5},{5,4},{6,7},{7,6},{8,9},{9,8},{10,11... | collective-permute-start | bytes 3145736 | tf_op jit(solution)/shard_map/part/ppermute | solution.py:686
  350.1 22.8 %collective-permute-start.31 = (bf16[4,128,512]{2,0,1:T(4,128)(2,1)}, bf16[4,128,512]{2,0,1:T(4,128)(2,1)}, u32[]{:S(2)}, u32[]{:S(2)}) collective-permute-start(bf16[4,128,512]{2,0,1:T(4,128)(2,1)} %copy.111), channel_id=1, source_target_pairs={{0,4},{4,0},{8,12},{12,8},{16,20},{20,16},{24,28},{28,24},{1,5},{5... | collective-permute-start | bytes 1572872 | tf_op jit(solution)/shard_map/part/ppermute | solution.py:686
  352.6 31.0 %collective-permute-start.32 = (bf16[512,1024]{1,0:T(8,128)(2,1)}, bf16[512,1024]{1,0:T(8,128)(2,1)}, u32[]{:S(2)}, u32[]{:S(2)}) collective-permute-start(bf16[512,1024]{1,0:T(8,128)(2,1)} %add_convert_fusion.1), channel_id=1, source_target_pairs={{0,2},{1,3},{2,0},{3,1},{4,6},{5,7},{6,4},{7,5},{8,10},{9,11},{10,... | collective-permute-start | bytes 3145736 | tf_op jit(solution)/shard_map/back_across/ppermute | solution.py:686
  359.0 27.2 %collective-permute-start.29 = (bf16[512,1024]{1,0:T(8,128)(2,1)}, bf16[512,1024]{1,0:T(8,128)(2,1)}, u32[]{:S(2)}, u32[]{:S(2)}) collective-permute-start(bf16[512,1024]{1,0:T(8,128)(2,1)} %get-tuple-element.159), channel_id=1, source_target_pairs={{0,1},{1,0},{2,3},{3,2},{4,5},{5,4},{6,7},{7,6},{8,9},{9,8},{10,11... | collective-permute-start | bytes 3145736 | tf_op jit(solution)/shard_map/part/ppermute | solution.py:686
  361.8 20.5 %collective-permute-start.30 = (bf16[4,144,512]{2,0,1:T(4,128)(2,1)}, bf16[4,144,512]{2,0,1:T(4,128)(2,1)}, u32[]{:S(2)}, u32[]{:S(2)}) collective-permute-start(bf16[4,144,512]{2,0,1:T(4,128)(2,1)} %dynamic_update_slice.40), channel_id=1, source_target_pairs={{0,8},{4,12},{8,0},{12,4},{16,24},{20,28},{24,16},{28,20},{1,9},{5... | collective-permute-start | bytes 1769480 | tf_op jit(solution)/shard_map/part/ppermute | solution.py:686
  372.4 20.3 %collective-permute-start.28 = (bf16[512,1024]{1,0:T(8,128)(2,1)}, bf16[512,1024]{1,0:T(8,128)(2,1)S(1)}, u32[]{:S(2)}, u32[]{:S(2)}) collective-permute-start(bf16[512,1024]{1,0:T(8,128)(2,1)} %get-tuple-element.155), channel_id=1, source_target_pairs={{0,1},{1,0},{2,3},{3,2},{4,5},{5,4},{6,7},{7,6},{8,9},{9,8},{10,11... | collective-permute-start | bytes 3145736 | tf_op jit(solution)/shard_map/part/ppermute | solution.py:686
  383.9 10.5 %collective-permute-start.34 = (bf16[2,128,512]{2,0,1:T(2,128)(2,1)S(1)}, bf16[2,128,512]{2,0,1:T(2,128)(2,1)S(1)}, u32[]{:S(2)}, u32[]{:S(2)}) collective-permute-start(bf16[2,128,512]{2,0,1:T(2,128)(2,1)S(1)} %slice.180), channel_id=1, source_target_pairs={{0,8},{4,12},{8,0},{12,4},{16,24},{20,28},{24,16},{28,20},{1,9},{5... | collective-permute-start | bytes 786440 | tf_op jit(solution)/shard_map/part/ppermute | solution.py:686
  386.0 9.3 %collective-permute-start.33 = (bf16[2,144,512]{2,0,1:T(2,128)(2,1)S(1)}, bf16[2,144,512]{2,0,1:T(2,128)(2,1)S(1)}, u32[]{:S(2)}, u32[]{:S(2)}) collective-permute-start(bf16[2,144,512]{2,0,1:T(2,128)(2,1)S(1)} %slice.179), channel_id=1, source_target_pairs={{0,4},{4,0},{8,12},{12,8},{16,20},{20,16},{24,28},{28,24},{1,5},{5... | collective-permute-start | bytes 884744 | tf_op jit(solution)/shard_map/part/ppermute | solution.py:686
  420.4 28.7 %collective-permute-start.35 = (bf16[1,144,512]{2,0,1:T(2,128)(2,1)}, bf16[1,144,512]{2,0,1:T(2,128)(2,1)}, u32[]{:S(2)}, u32[]{:S(2)}) collective-permute-start(bf16[1,144,512]{2,0,1:T(2,128)(2,1)} %slice.181), channel_id=1, source_target_pairs={{0,16},{4,20},{8,24},{12,28},{16,0},{20,4},{24,8},{28,12},{1,17},{... | collective-permute-start | bytes 442376 | tf_op jit(solution)/shard_map/part/ppermute | solution.py:686
  424.4 23.4 %collective-permute-start.36 = (bf16[1,128,512]{2,0,1:T(2,128)(2,1)}, bf16[1,128,512]{2,0,1:T(2,128)(2,1)}, u32[]{:S(2)}, u32[]{:S(2)}) collective-permute-start(bf16[1,128,512]{2,0,1:T(2,128)(2,1)} %slice.182), channel_id=1, source_target_pairs={{0,16},{4,20},{8,24},{12,28},{16,0},{20,4},{24,8},{28,12},{1,17},{... | collective-permute-start | bytes 393224 | tf_op jit(solution)/shard_map/part/ppermute | solution.py:686
  (57 other events, 484.2 us)
Sparse Core Ops, SparseCore 0:
  10.8 67.8 all-gather.4
  81.4 78.8 all-gather.6
  295.9 121.9 reduce-scatter.1

commit v7 on v4

--- a/solution.py
+++ b/solution.py
@@ -93,7 +93,7 @@
 
 
 def project_kernel(
-    x, gain, matrix, cos, sin, gain_q, gain_k, normed_turned, raw_q, raw_k, q, k, v, k_turned, v_turned
+    x, gain, matrix, cos, sin, gain_q, gain_k, normed_turned, raw_q, raw_k, q, k, v, k_turned
 ):
     normed = norm_rows(x[...].astype(F32), gain[...])
     normed_turned[...] = normed.T.astype(BF16)
@@ -111,42 +111,56 @@
         turned = head_rotated(value, gain_k[...], c, s)
         k[:, lanes_of(j)] = turned.astype(BF16)
         k_turned[lanes_of(j), :] = turned.T.astype(BF16)
-        value = part[:, lanes_of(GROUP + 1)]
-        v[:, lanes_of(j)] = value.astype(BF16)
-        v_turned[lanes_of(j), :] = value.T.astype(BF16)
-
-
-def attend_kernel(offset, info, q, k, v_turned, start, out, out_turned, logs):
-    blocks = k.shape[0] // BLOCK
+        v[:, lanes_of(j)] = part[:, lanes_of(GROUP + 1)].astype(BF16)
+
+
+def stacked(value):
+    return jnp.concatenate([value[:, lanes_of(h)] for h in range(GROUP)], axis=0)
+
+
+def stacked_turned(value):
+    return jnp.concatenate(
+        [value[:, lanes_of(h)].astype(F32).T.astype(BF16) for h in range(GROUP)], axis=1
+    )
+
+
+def attend_kernel(offset, info, q, k_turned, v, out, out_turned, logs):
+    blocks = v.shape[0] // BLOCK
     flip = info[blocks]
+    documents = info.shape[0] - blocks - 1
 
     def one_block(i, _):
         here = at_block(i)
         b = (i + offset) ^ flip
-        first = start[:, here]
-        queries = [q[here, lanes_of(h)] for h in range(GROUP)]
+        index = b * BLOCK + lax.broadcasted_iota(jnp.int32, (BLOCK, 1), 0)
+        first = jnp.zeros((BLOCK, 1), jnp.int32)
+        for d in range(documents):
+            begin = info[blocks + 1 + d]
+            first = jnp.maximum(first, jnp.where(index >= begin, begin, 0))
+        query = stacked(q[here, :])
 
         def keys_step(kb, carry):
+            total, blend = carry
             there = at_block(kb ^ flip)
-            key, value = k[there, :], v_turned[:, there]
-            allowed = allowed_block(kb, b, first)
-            after = []
-            for h in range(GROUP):
-                total, blend = carry[h]
-                p = jnp.where(allowed, jnp.exp2(nt(key, queries[h]) * (SCALE * LOG2E)), 0.0)
-                after.append(
-                    (total + jnp.sum(p, axis=0, keepdims=True), blend + nn(value, p.astype(BF16)))
-                )
-            return tuple(after)
-
-        zero = (jnp.zeros((1, BLOCK), F32), jnp.zeros((HEAD_SIZE, BLOCK), F32))
-        done = lax.fori_loop(info[b], b + 1, keys_step, (zero,) * GROUP)
+            keys = kb * BLOCK + lax.broadcasted_iota(jnp.int32, (BLOCK, BLOCK), 1)
+            allowed = (keys >= first) & (keys <= index)
+            score = nn(query, k_turned[:, there]).reshape(GROUP, BLOCK, BLOCK)
+            p = jnp.where(allowed[None], jnp.exp2(score * (SCALE * LOG2E)), 0.0)
+            p = p.reshape(GROUP * BLOCK, BLOCK)
+            for lane in range(0, BLOCK, HEAD_SIZE):
+                total = total + p[:, lane : lane + HEAD_SIZE]
+            return total, blend + nn(p.astype(BF16), v[there, :])
+
+        zero = jnp.zeros((GROUP * BLOCK, HEAD_SIZE), F32)
+        total, blend = lax.fori_loop(info[b], b + 1, keys_step, (zero, zero))
+        total = jnp.sum(total, axis=1, keepdims=True)
+        result = blend / total
+        log = jnp.broadcast_to(jnp.log2(total), result.shape)
         for h in range(GROUP):
-            total, blend = done[h]
-            result = blend / total
-            out[here, lanes_of(h)] = result.T.astype(BF16)
-            out_turned[lanes_of(h), here] = result.astype(BF16)
-            logs[0, h : h + 1, here] = jnp.log2(total)
+            rows = slice(h * BLOCK, (h + 1) * BLOCK)
+            out[here, lanes_of(h)] = result[rows].astype(BF16)
+            out_turned[lanes_of(h), here] = result[rows].T.astype(BF16)
+            logs[0, h : h + 1, here] = log[rows].T[0:1, :]
         return 0
 
     lax.fori_loop(0, q.shape[0] // BLOCK, one_block, 0)
@@ -158,40 +172,40 @@
 ):
     flip = info[k.shape[0] // BLOCK]
 
+    def twice(row):
+        return jnp.concatenate([row] * GROUP, axis=1)
+
     def one_block(i, total_gain):
         here = at_block(i)
         b = (i + offset) ^ flip
         first = start[:, here]
-        queries, gradients, across, log = [], [], [], []
+        gradients = grad_out[here, :]
+        both = gradients.astype(F32) * out[here, :].astype(F32)
+        query, gradient = stacked(q[here, :]), stacked(gradients)
+        query_turned, gradient_turned = stacked_turned(q[here, :]), stacked_turned(gradients)
+        across, log = [], []
         for h in range(GROUP):
-            g = grad_out[here, lanes_of(h)]
-            queries.append(q[here, lanes_of(h)])
-            gradients.append(g)
-            both = g.astype(F32) * out[here, lanes_of(h)].astype(F32)
-            across.append(jnp.sum(both.T, axis=0, keepdims=True))
+            across.append(jnp.sum(both[:, lanes_of(h)].T, axis=0, keepdims=True))
             log.append(logs[0, h : h + 1, here])
-
-        def keys_step(kb, carry):
+        across, log = jnp.concatenate(across, axis=1), jnp.concatenate(log, axis=1)
+
+        def keys_step(kb, grad_query):
             there = at_block(kb ^ flip)
-            key, value, key_turned = k[there, :], v[there, :], k_turned[:, there]
-            allowed = allowed_block(kb, b, first)
-            after, add_k, add_v = [], 0.0, 0.0
-            for h in range(GROUP):
-                s = nt(key, queries[h])
-                p = jnp.where(allowed, jnp.exp2(s * (SCALE * LOG2E) - log[h]), 0.0)
-                d = (p * (nt(value, gradients[h]) - across[h])).astype(BF16)
-                add_v = add_v + nn(p.astype(BF16), gradients[h])
-                add_k = add_k + nn(d, queries[h])
-                after.append(carry[h] + nn(key_turned, d))
-            grad_k[there, :] += add_k
-            grad_v[there, :] += add_v
-            return tuple(after)
-
-        zero = jnp.zeros((HEAD_SIZE, BLOCK), F32)
-        done = lax.fori_loop(info[b], b + 1, keys_step, (zero,) * GROUP)
+            allowed = twice(allowed_block(kb, b, first).astype(jnp.int32)) > 0
+            s = nn(k[there, :], query_turned)
+            p = jnp.where(allowed, jnp.exp2(s * (SCALE * LOG2E) - log), 0.0)
+            d = (p * (nn(v[there, :], gradient_turned) - across)).astype(BF16)
+            grad_v[there, :] += nn(p.astype(BF16), gradient)
+            grad_k[there, :] += nn(d, query)
+            return grad_query + nn(k_turned[:, there], d)
+
+        done = lax.fori_loop(
+            info[b], b + 1, keys_step, jnp.zeros((HEAD_SIZE, GROUP * BLOCK), F32)
+        )
         c, s = cos[here, :], sin[here, :]
         for h in range(GROUP):
-            back, gain = head_back(raw_q[here, lanes_of(h)], gain_q[...], c, s, done[h].T * SCALE)
+            grad = done[:, h * BLOCK : (h + 1) * BLOCK].T * SCALE
+            back, gain = head_back(raw_q[here, lanes_of(h)], gain_q[...], c, s, grad)
             store(i, h, back.astype(BF16))
             total_gain = total_gain + gain
         return total_gain
@@ -389,52 +403,52 @@
         ],
         out_specs=[
             by_lanes(width), by_rows(q_width), by_rows(k_width), by_rows(q_width),
-            by_rows(k_width), by_rows(k_width), by_lanes(k_width), by_lanes(k_width),
+            by_rows(k_width), by_rows(k_width), by_lanes(k_width),
         ],
         out_shape=[
             shaped((width, rows), BF16), shaped((rows, q_width), F32),
             shaped((rows, k_width), F32), shaped((rows, q_width), BF16),
             shaped((rows, k_width), BF16), shaped((rows, k_width), BF16),
-            shaped((k_width, rows), BF16), shaped((k_width, rows), BF16),
+            shaped((k_width, rows), BF16),
         ],
         **params("project", 10_000_000_000),
     )(x, gain, matrix, cos, sin, gain_q, gain_k)
 
 
 def head_specs(half, rows):
-    at = lambda j: j
     n = rows // 2
+    queries = GROUP * HEAD_SIZE
     return dict(
-        q=pl.BlockSpec((n, GROUP * HEAD_SIZE), lambda j, info: (half, at(j))),
-        k=pl.BlockSpec((rows, HEAD_SIZE), lambda j, info: (0, at(j))),
-        turned=pl.BlockSpec((HEAD_SIZE, rows), lambda j, info: (at(j), 0)),
+        q=pl.BlockSpec((n, queries), lambda j, info: (half, j)),
+        k=pl.BlockSpec((rows, HEAD_SIZE), lambda j, info: (0, j)),
+        turned=pl.BlockSpec((HEAD_SIZE, rows), lambda j, info: (j, 0)),
         start=pl.BlockSpec((1, n), lambda j, info: (0, half)),
-        out=pl.BlockSpec((n, GROUP * HEAD_SIZE), lambda j, info: (0, at(j))),
-        logs=pl.BlockSpec((1, GROUP, n), lambda j, info: (at(j), 0, 0)),
+        out=pl.BlockSpec((n, queries), lambda j, info: (0, j)),
+        out_turned=pl.BlockSpec((queries, n), lambda j, info: (j, 0)),
+        logs=pl.BlockSpec((1, GROUP, n), lambda j, info: (j, 0, 0)),
         angle=pl.BlockSpec((n, HEAD_SIZE), lambda j, info: (half, 0)),
-    )
-
-
-def attend(half, info, q, k, v_turned, start):
-    rows = k.shape[0]
-    n, heads = rows // 2, k.shape[1] // HEAD_SIZE
+        row=fixed((1, HEAD_SIZE)),
+    )
+
+
+def attend(half, info, q, k_turned, v):
+    rows = v.shape[0]
+    n, heads = rows // 2, v.shape[1] // HEAD_SIZE
     s = head_specs(half, rows)
     return pl.pallas_call(
         lambda *refs: attend_kernel(half * n // BLOCK, *refs),
         grid_spec=pltpu.PrefetchScalarGridSpec(
             num_scalar_prefetch=1,
             grid=(heads,),
-            in_specs=[s["q"], s["k"], s["turned"], s["start"]],
-            out_specs=[
-                s["out"], pl.BlockSpec((GROUP * HEAD_SIZE, n), lambda j, info: (j, 0)), s["logs"],
-            ],
+            in_specs=[s["q"], s["turned"], s["k"]],
+            out_specs=[s["out"], s["out_turned"], s["logs"]],
         ),
         out_shape=[
             shaped((n, q.shape[1]), BF16), shaped((q.shape[1], n), BF16),
             shaped((heads, GROUP, n), F32),
         ],
         **params("attend", 18_000_000_000),
-    )(info, q, k, v_turned, start)
+    )(info, q, k_turned, v)
 
 
 def attend_back_own(info, q, k, v, k_turned, start, logs, out, grad_out, raw_q, cos, sin, gain_q):
@@ -448,7 +462,7 @@
             grid=(heads,),
             in_specs=[
                 s["q"], s["k"], s["k"], s["turned"], s["start"], s["logs"], s["out"], s["out"],
-                s["q"], s["angle"], s["angle"], fixed((1, HEAD_SIZE)),
+                s["q"], s["angle"], s["angle"], s["row"],
             ],
             out_specs=[
                 s["out"], s["k"], s["k"],
@@ -471,7 +485,7 @@
     heads = k.shape[1] // HEAD_SIZE
     width = SLOTS * HEAD_SIZE
     s = head_specs(1, rows)
-    row = fixed((1, HEAD_SIZE))
+    whole = fixed((rows, HEAD_SIZE))
     return pl.pallas_call(
         back_other_kernel,
         grid_spec=pltpu.PrefetchScalarGridSpec(
@@ -479,9 +493,8 @@
             grid=(heads,),
             in_specs=[
                 s["q"], s["k"], s["k"], s["turned"], s["start"], s["logs"], s["out"], s["out"],
-                s["q"], s["angle"], s["angle"], row,
-                fixed((rows, HEAD_SIZE)), fixed((rows, HEAD_SIZE)), s["k"], row, s["out"], s["k"],
-                s["k"],
+                s["q"], s["angle"], s["angle"], s["row"],
+                whole, whole, s["k"], s["row"], s["out"], s["k"], s["k"],
             ],
             out_specs=[
                 pl.BlockSpec((rows, width), lambda j, info: (0, j)),
@@ -669,7 +682,9 @@
     cos = jnp.concatenate([cosine, cosine], axis=1)
     sin = jnp.concatenate([-sine, sine], axis=1)
     block_starts = start_of(jnp.arange(blocks, dtype=jnp.int32) * BLOCK) // BLOCK
-    info = jnp.concatenate([block_starts, (me * (local_rows // BLOCK))[None]]).astype(jnp.int32)
+    info = jnp.concatenate(
+        [block_starts, (me * (local_rows // BLOCK))[None], doc_starts]
+    ).astype(jnp.int32)
     start = start_of_row[None, :]
 
     rows_float = tokens.astype(F32)
@@ -678,21 +693,27 @@
         [tokens, flipped(tokens, "tensor", 1), tokens_across, flipped(tokens_across, "tensor", 1)],
         axis=0,
     )
-    normed_turned, raw_q, raw_k, q, k, v, k_turned, v_turned = project(
+    normed_turned, raw_q, raw_k, q, k, v, k_turned = project(
         tokens_all, gain_attn, qkv_matrix, cos, sin, gain_query, gain_key
     )
     grad_across = flipped(cotangent, "tensor", 2, "grad_across")
-    heads_other, heads_other_turned, logs_other = attend(1, info, q, k, v_turned, start)
+    heads_other, heads_other_turned, logs_other = attend(1, info, q, k_turned, v)
     heads_other, grad_across = together(heads_other, grad_across)
     beside = nn(heads_other[local_rows:], out_matrix).astype(BF16)
     near = near_sum(nn(heads_other[:local_rows], out_matrix), beside).astype(BF16)
     near, q_own = together(near, q)
     attn_across = flipped(near, "tensor", 2, "attn_across")
-    heads_own, heads_own_turned, logs_own = attend(0, info, q_own, k, v_turned, start)
-    heads_own, attn_across, full_two = together(heads_own, attn_across, full_two)
+    heads_own, heads_own_turned, logs_own = attend(0, info, q_own, k_turned, v)
+    heads_own, attn_across = together(heads_own, attn_across)
     beside = nn(heads_own[local_rows:], out_matrix).astype(BF16)
-    attn_rows = near_sum(nn(heads_own[:local_rows], out_matrix), beside) + attn_across.astype(F32)
-    middle = rows_float + attn_rows
+    own_sum = near_sum(nn(heads_own[:local_rows], out_matrix), beside)
+    own_sum, full_two = together(own_sum, full_two)
+    middle = rows_float + own_sum + attn_across.astype(F32)
+    grad_own = jnp.concatenate([cotangent, flipped(cotangent, "tensor", 1)], axis=0)
+    grad_other = jnp.concatenate([grad_across, flipped(grad_across, "tensor", 1)], axis=0)
+    normed_two = norm_rows(middle, gain_mlp).astype(BF16)
+    normed_across = flipped(normed_two, "tensor", 2, "normed_across")
+    normed_own = jnp.concatenate([normed_two, flipped(normed_two, "tensor", 1)], axis=0)
     if cubic:
         feed_matrices = (full_two,)
     else:
@@ -706,12 +727,6 @@
             .transpose(2, 0, 3, 1, 4)
             .reshape(-1, MODEL_WIDTH),
         )
-
-    grad_own = jnp.concatenate([cotangent, flipped(cotangent, "tensor", 1)], axis=0)
-    grad_other = jnp.concatenate([grad_across, flipped(grad_across, "tensor", 1)], axis=0)
-    normed_two = norm_rows(middle, gain_mlp).astype(BF16)
-    normed_across = flipped(normed_two, "tensor", 2, "normed_across")
-    normed_own = jnp.concatenate([normed_two, flipped(normed_two, "tensor", 1)], axis=0)
     h_own, hidden_own, feed_grad_own, back_0, back_1, sum_0, sum_1 = feed(
         normed_own, grad_own, feed_matrices, hidden_local
     )
@@ -760,8 +775,7 @@
         info, q, k, v, k_turned, start, logs_own, heads_own, grad_heads_own, raw_q, cos, sin,
         gain_query,
     )
-    grad_middle_across, grad_q, sum_2, sum_3 = together(grad_middle_across, grad_q, sum_2, sum_3)
-    near_mlp = near_sum(sum_2, sum_3).astype(BF16)
+    grad_middle_across, grad_q = together(grad_middle_across, grad_q)
     grad_middle_other = jnp.concatenate(
         [grad_middle_across, flipped(grad_middle_across, "tensor", 1)], axis=0
     )
@@ -769,18 +783,19 @@
     grad_out_w = (
         nn(heads_own_turned, grad_middle_own) + nn(heads_other_turned, grad_middle_other)
     ).astype(BF16)
-    near_mlp, grad_out_w, grad_heads_other = together(near_mlp, grad_out_w, grad_heads_other)
-    mlp_across = flipped(near_mlp, "tensor", 2, "mlp_across")
+    grad_out_w, grad_heads_other = together(grad_out_w, grad_heads_other)
     grad_qkv, gain_other = attend_back_other(
         info, q, k, v, k_turned, start, logs_other, heads_other, grad_heads_other,
         raw_q, cos, sin, gain_query, raw_k, gain_key, grad_q, grad_k, grad_v,
     )
-    grad_qkv, mlp_across = together(grad_qkv, mlp_across)
     back_2, back_3 = unproject(1, grad_qkv, qkv_matrix)
     back_2, back_3, grad_qkv = together(back_2, back_3, grad_qkv)
     grad_qkv_w = nn(normed_turned, grad_qkv)
     near = near_sum(back_2, back_3).astype(BF16)
-    near, grad_qkv, grad_qkv_w, grad_out_w = together(near, grad_qkv, grad_qkv_w, grad_out_w)
+    near, grad_qkv, grad_qkv_w, grad_out_w, sum_2, sum_3 = together(
+        near, grad_qkv, grad_qkv_w, grad_out_w, sum_2, sum_3
+    )
+    near_mlp = near_sum(sum_2, sum_3).astype(BF16)
     back_across = flipped(near, "tensor", 2, "back_across")
     grad_gain_attn = jnp.sum(qkv_matrix.astype(F32) * grad_qkv_w, axis=1) / gain_attn[0]
     grad_gain_heads = jnp.sum(gain_other, axis=0) + jnp.pad(
@@ -800,18 +815,23 @@
         )
         sum_two = grad_qkv_w[:, columns:].reshape(cube + (depth, -1))
         sum_one, sum_two = halved(sum_one, 1, 2), halved(sum_two, 2, 1)
+        sum_out = grad_out_w.reshape((out_heads,) + cube + (out_depth, MODEL_WIDTH))
+        sum_out = halved(sum_out, 3, 1)
+        sum_one, sum_two, back_across, sum_0, sum_1, near_mlp = together(
+            sum_one, sum_two, back_across, sum_0, sum_1, near_mlp
+        )
+        mlp_across = flipped(near_mlp, "tensor", 2, "mlp_across")
         sum_one, sum_two = halved(sum_one, 1, 1), halved(sum_two, 1, 2)
-        sum_out = grad_out_w.reshape((out_heads,) + cube + (out_depth, MODEL_WIDTH))
-        sum_out = halved(halved(sum_out, 3, 1), 2, 2)
-        sum_one, sum_two, sum_out, back_across, feed_sum = together(
-            sum_one, sum_two, sum_out, back_across, feed_sum
-        )
+        sum_out = halved(sum_out, 2, 2)
+        sum_one, sum_two, sum_out, feed_sum = together(sum_one, sum_two, sum_out, feed_sum)
         sum_one, sum_two = halved(sum_one, 0, 4), halved(sum_two, 0, 4)
         sum_out = halved(sum_out, 1, 4)
+        sum_one, sum_two, sum_out, mlp_across = together(sum_one, sum_two, sum_out, mlp_across)
         sum_qkv = jnp.concatenate([sum_one[:depth], sum_two], axis=1)
         sum_qkv = sum_qkv.reshape(projection_weight.shape)
         sum_gains = sum_one[depth, :gain_count]
     else:
+        mlp_across = flipped(near_mlp, "tensor", 2, "mlp_across")
         sum_qkv = (
             lax.psum_scatter(grad_qkv_w.astype(BF16), "dp", scatter_dimension=0, tiled=True)
             .astype(F32)

time: 446 us -> 420 us (0.942)
  Pallas kernels: 160 us -> 149 us
  local copies, waits for them, and re-layouts: 36.6 us -> 27.4 us
    unnamed x137 -> x123, local copies, waits for them, and re-layouts: 14.3 us -> 9.3 us
  transfers between devices with their start and end apart: 39 -> 39, of which waited for: 18 -> 19; matrix products, arithmetic and copies ran while one was open for 21% -> 22% of each run, Pallas kernels for 33% -> 32%
where the time goes in v7:
time: 420 us; the launch traced here: 414 us
  Pallas kernels  149 us (35%)
  waiting for transfers between devices  113 us (27%)
  other arithmetic  62.6 us (15%)
  local copies, waits for them, and re-layouts  27.4 us (7%)
  starting transfers between devices  25.6 us (6%)
  matrix products  20.7 us (5%)
  between operations  15.3 us (4%)
    ppermute x36, waiting for transfers between devices, flipped(): lax.ppermute(value, axis, [(i, i ^ bit) for i in range(lax.axis_size(axis...  77.3 us
    pallas_call x2, Pallas kernels, feed(): pl.pallas_call(lambda *refs: feed_kernel(packs, *refs), grid=(rows // BLO...  33.5 us
    pallas_call x2, Pallas kernels, attend(): pl.pallas_call(lambda *refs: attend_kernel(half * n // BLOCK, *refs), gri...  30.2 us
    all_gather x1, waiting for transfers between devices, per_device(): lax.all_gather(pack_one, 'dp', axis=0, tiled=False)  28.6 us
    pallas_call x1, Pallas kernels, attend_back_other(): pl.pallas_call(back_other_kernel, grid_spec=pltpu.PrefetchScalarGridSpec(...  28.1 us
    ppermute x36, starting transfers between devices, flipped(): lax.ppermute(value, axis, [(i, i ^ bit) for i in range(lax.axis_size(axis...  25.4 us
    pallas_call x1, Pallas kernels, attend_back_own(): pl.pallas_call(back_own_kernel, grid_spec=pltpu.PrefetchScalarGridSpec(nu...  17.9 us
    pallas_call x1, Pallas kernels, feed_weights(): pl.pallas_call(lambda *refs: feed_weights_kernel(packs, pieces, *refs), g...  16.5 us
  transfers between devices with their start and end apart: 39, of which 19 were waited for; matrix products, arithmetic and copies ran while one was open for 22% of the time, Pallas kernels for 32%

profile of v7, /device:TPU:0, one launch (start us, length us, event | category | flops | bytes accessed | tf_op | source)
XLA Modules:
  0.0 413.8 jit_solution(1255402082658635732)
XLA Ops:
  13.0 3.0 collective-permute-start.1
  16.8 23.4 %collective-permute-done.1 = bf16[512,1024]{1,0:T(8,128)(2,1)} collective-permute-done((bf16[512,1024]{1,0:T(8,128)(2,1)S(1)}, bf16[512,1024]{1,0:T(8,128)(2,1)}, u32[]{:S(2)}, u32[]{:S(2)}) %collective-permute-start.1) | collective-permute-done | bytes 1048608 | tf_op jit(solution)/shard_map/tokens_across/ppermute | solution.py:588
  40.1 3.7 fusion.17
  44.6 4.3 %pad_maximum_fusion.x = bf16[2048,1024]{1,0:T(8,128)(2,1)} fusion(bf16[512,1024]{1,0:T(8,128)(2,1)} %collective-permute-done.2, bf16[512,1024]{1,0:T(8,128)(2,1)} %collective-permute-done.1, bf16[512,1024]{1,0:T(8,128)(2,1)} %collective-permute-done, bf16[512,1024]{1,0:T(8,128)(2,1)S(1)} %copy-done.32), kind=kLoop, calls=%fused_computation | loop fusion | flops 16777216 | bytes 8388608 | tf_op jit(solution)/shard_map/concatenate | solution.py:692
  48.9 28.6 %all-gather.5.cloned.1.call-done = bf16[1664,1024]{1,0:T(8,128)(2,1)} async-done(((bf16[208,1024]{1,0:T(8,128)(2,1)}), bf16[1664,1024]{1,0:T(8,128)(2,1)}) %all-gather.5.cloned.1.call-update) | async-done | bytes 3407888 | tf_op jit(solution)/shard_map/all_gather | solution.py:654
  78.8 3.1 slice.70
  83.8 13.5 %project.1 = (bf16[1024,2048]{1,0:T(8,128)(2,1)}, f32[2048,512]{1,0:T(8,128)}, f32[2048,256]{1,0:T(8,128)}, bf16[2048,512]{1,0:T(8,128)(2,1)}, bf16[2048,256]{1,...) custom-call(bf16[2048,1024]{1,0:T(8,128)(2,1)} %pad_maximum_fusion.x, ...), custom_call_target="tpu_custom_call" | custom-call | flops 156250000 | bytes 1000 | tf_op jit(solution)/shard_map/project/pallas_call | solution.py:397
  97.3 17.7 %attend.2 = (bf16[1024,512]{1,0:T(8,128)(2,1)S(1)}, bf16[512,1024]{1,0:T(8,128)(2,1)S(1)}, f32[2,2,1024]{2,1,0:T(2,128)S(1)}) custom-call(s32[17]{0:T(128)S(1)} %pad_add_fusion.refs_0_.info, bf16[2048,512]{1,0:T(8,128)(2,1)} %get-tuple-element.100.refs_1_.q, bf16[256,2048]{1,0:T(8,128)(2,1)S(1)} %get-tuple-element.96.refs_2_.k_turned, ...), custom_call_target="tpu_custom_call" | custom-call | flops 281249984 | bytes 1000 | tf_op jit(solution)/shard_map/attend/pallas_call | solution.py:438
  116.0 2.6 collective-permute-done.4
  119.4 12.5 %attend.3 = (bf16[1024,512]{1,0:T(8,128)(2,1)S(1)}, bf16[512,1024]{1,0:T(8,128)(2,1)S(1)}, f32[2,2,1024]{2,1,0:T(2,128)S(1)}) custom-call(s32[17]{0:T(128)S(1)} %pad_add_fusion.refs_0_.info, bf16[2048,512]{1,0:T(8,128)(2,1)} %get-tuple-element.100.refs_1_.q, bf16[256,2048]{1,0:T(8,128)(2,1)S(1)} %get-tuple-element.96.refs_2_.k_turned, ...), custom_call_target="tpu_custom_call" | custom-call | flops 281249984 | bytes 1000 | tf_op jit(solution)/shard_map/attend/pallas_call | solution.py:438
  131.9 12.7 %collective-permute-done.5 = bf16[512,1024]{1,0:T(8,128)(2,1)S(1)} collective-permute-done((bf16[512,1024]{1,0:T(8,128)(2,1)S(1)}, bf16[512,1024]{1,0:T(8,128)(2,1)S(1)}, u32[]{:S(2)}, u32[]{:S(2)}) %collective-permute-start.5) | collective-permute-done | bytes 1048608 | tf_op jit(solution)/shard_map/attn_across/ppermute | solution.py:588
  146.9 2.9 collective-permute-done.6
  151.8 6.9 %all-gather.7.cloned.1.call-done = bf16[4608,512]{1,0:T(8,128)(2,1)} async-done(((bf16[576,512]{1,0:T(8,128)(2,1)}), bf16[4608,512]{1,0:T(8,128)(2,1)}) %all-gather.7.cloned.1.call-update) | async-done | bytes 4718608 | tf_op jit(solution)/shard_map/all_gather | solution.py:656
  167.7 16.7 %feed.2 = (bf16[1024,1024]{1,0:T(8,128)(2,1)}, bf16[768,1024]{1,0:T(8,128)(2,1)S(1)}, bf16[1024,1536]{1,0:T(8,128)(2,1)}, bf16[512,1024]{1,0:T(8,128)(2,1)S(1)},...) custom-call(bf16[1024,1024]{1,0:T(8,128)(2,1)} %pad_maximum_fusion.1.refs_0_, ...), custom_call_target="tpu_custom_call" | custom-call | flops 250000000 | bytes 1000 | tf_op jit(solution)/shard_map/feed/pallas_call | solution.py:533
  184.4 2.7 collective-permute-done.7
  191.2 16.8 %feed.3 = (bf16[1024,1024]{1,0:T(8,128)(2,1)}, bf16[768,1024]{1,0:T(8,128)(2,1)S(1)}, bf16[1024,1536]{1,0:T(8,128)(2,1)}, bf16[512,1024]{1,0:T(8,128)(2,1)S(1)},...) custom-call(bf16[1024,1024]{1,0:T(8,128)(2,1)} %pad_maximum_fusion.2.refs_0_, ...), custom_call_target="tpu_custom_call" | custom-call | flops 250000000 | bytes 1000 | tf_op jit(solution)/shard_map/feed/pallas_call | solution.py:533
  215.6 16.5 %feed_weights.1 = bf16[8,576,512]{2,1,0:T(8,128)(2,1)} custom-call(bf16[1024,1024]{1,0:T(8,128)(2,1)S(1)} %copy-done.12, bf16[1024,1024]{1,0:T(8,128)(2,1)} %get-tuple-element.120.refs_1_, bf16[1024,1536]{1,0:T(8,128)(2,1)} %get-tuple-element.121.refs_2_, bf16[1024,1536]{1,0:T(8,128)(2,1)} %get-tuple-element.122.refs_3_, ...), custom_call_target="tpu_custom_call" | custom-call | flops 250000000 | bytes 1000 | tf_op jit(solution)/shard_map/feed_weights/pallas_call | solution.py:558
  232.1 7.5 %collective-permute-done.14 = bf16[512,1024]{1,0:T(8,128)(2,1)} collective-permute-done((bf16[512,1024]{1,0:T(8,128)(2,1)}, bf16[512,1024]{1,0:T(8,128)(2,1)}, u32[]{:S(2)}, u32[]{:S(2)}) %collective-permute-start.14) | collective-permute-done | bytes 1048608 | tf_op jit(solution)/shard_map/back_across/ppermute | solution.py:588
  239.6 3.1 multiply_reduce_fusion.1
  242.7 4.4 %fusion.35 = (bf16[512,1024]{1,0:T(8,128)(2,1)}, f32[512,1024]{1,0:T(8,128)}) fusion(f32[512]{0:T(512)S(1)} %broadcast_multiply_fusion.1, f32[512,1024]{1,0:T(8,128)S(1)} %copy-done.29, f32[512]{0:T(512)S(1)} %get-tuple-element.209, f32[1024]{0:T(1024)S(1)} %get-tuple-element.200, bf16[512,1024]{1,0:T(8,128)(2,1)} %collective-permute-done.14, ...), kind=kLoop, calls=%fused_computation.139 | loop fusion | flops 6815744 | bytes 9447424 | tf_op jit(solution)/shard_map/convert_element_type | solution.py:767
  250.1 3.8 convolution_convert_fusion.1.grad_out
  253.9 17.9 %attend_back_own.1 = (bf16[1024,512]{1,0:T(8,128)(2,1)S(1)}, f32[2048,256]{1,0:T(8,128)}, f32[2048,256]{1,0:T(8,128)}, f32[2,1,128]{2,1,0:T(1,128)S(1)}) custom-call(s32[17]{0:T(128)S(1)} %pad_add_fusion.refs_0_.info, bf16[2048,512]{1,0:T(8,128)(2,1)} %get-tuple-element.100.refs_1_.q, bf16[2048,256]{1,0:T(8,128)(2,1)S(1)} %copy-done.8, ...), custom_call_target="tpu_custom_call" | custom-call | flops 390624992 | bytes 1000 | tf_op jit(solution)/shard_map/attend_back_own/pallas_call | solution.py:458
  278.6 3.9 add_convert_fusion.3
  282.5 28.1 %attend_back_other.1 = (bf16[2048,1024]{1,0:T(8,128)(2,1)}, f32[2,2,128]{2,1,0:T(2,128)S(1)}) custom-call(s32[17]{0:T(128)S(1)} %pad_add_fusion.refs_0_.info, bf16[2048,512]{1,0:T(8,128)(2,1)} %get-tuple-element.100.refs_1_.q, bf16[2048,256]{1,0:T(8,128)(2,1)S(1)} %copy-done.9, bf16[2048,256]{1,0:T(8,128)(2,1)S(1)} %copy-done.4, ...), custom_call_target="tpu_custom_call" | custom-call | flops 437500000 | bytes 1000 | tf_op jit(solution)/shard_map/attend_back_other/pallas_call | solution.py:489
  310.7 4.7 %unproject.2 = (bf16[512,1024]{1,0:T(8,128)(2,1)S(1)}, bf16[512,1024]{1,0:T(8,128)(2,1)S(1)}) custom-call(bf16[2048,1024]{1,0:T(8,128)(2,1)} %get-tuple-element.165.grad, bf16[1024,1024]{1,0:T(8,128)(2,1)S(1)} %bitcast.108), custom_call_target="tpu_custom_call" | custom-call | flops 62500000 | bytes 1000 | tf_op jit(solution)/shard_map/unproject/pallas_call | solution.py:576
  315.6 6.3 %fusion.40 = f32[1024,1024]{1,0:T(8,128)S(1)} fusion(bf16[1024,2048]{1,0:T(8,128)(2,1)} %get-tuple-element.142, bf16[2048,1024]{1,0:T(8,128)(2,1)S(1)} %copy-done.31), kind=kOutput, calls=%fused_computation.143 | convolution fusion | flops 4294967296 | bytes 12582912 | tf_op jit(solution)/shard_map/dot_general | solution.py:64
  333.2 4.8 %unproject.3 = (bf16[512,1024]{1,0:T(8,128)(2,1)S(1)}, bf16[512,1024]{1,0:T(8,128)(2,1)S(1)}) custom-call(bf16[2048,1024]{1,0:T(8,128)(2,1)} %get-tuple-element.165.grad, bf16[1024,1024]{1,0:T(8,128)(2,1)S(1)} %bitcast.109), custom_call_target="tpu_custom_call" | custom-call | flops 62500000 | bytes 1000 | tf_op jit(solution)/shard_map/unproject/pallas_call | solution.py:576
  340.2 9.7 %collective-permute-done.20 = bf16[2,2,128,512]{3,2,0,1:T(8,128)(2,1)S(1)} collective-permute-done((bf16[2,2,128,512]{3,2,0,1:T(8,128)(2,1)}, bf16[2,2,128,512]{3,2,0,1:T(8,128)(2,1)S(1)}, u32[]{:S(2)}, u32[]{:S(2)}) %collective-permute-start.20) | collective-permute-done | bytes 524320 | tf_op jit(solution)/shard_map/part/ppermute | solution.py:588
  354.2 4.1 collective-permute-done.27
  383.4 5.1 %multiply_subtract_fusion = (f32[128,2,768]{2,1,0:T(2,128)}, f32[128,2,768]{2,1,0:T(2,128)}, f32[128,2,768]{2,1,0:T(2,128)}) fusion(f32[128,2,768]{2,1,0:T(2,128)} %param.23, f32[128,2,768]{2,1,0:T(2,128)} %copy.94, f32[128,2,768]{2,1,0:T(2,128)} %param.28, f32[128,2,768]{2,1,0:T(2,128)} %param.33), kind=kLoop, calls=%fused_computation.48 | loop fusion | flops 2949120 | bytes 5505024 | tf_op jit(solution)/shard_map/sub | solution.py:53
  397.6 4.2 %multiply_subtract_fusion.1 = (f32[128,2,512]{2,1,0:T(2,128)}, f32[128,2,512]{2,1,0:T(2,128)}, f32[128,2,512]{2,1,0:T(2,128)}) fusion(f32[128,2,512]{2,1,0:T(2,128)S(1)} %copy-done.43, f32[128,2,512]{2,1,0:T(2,128)S(1)} %reshape.213, f32[128,2,512]{2,1,0:T(2,128)} %param.26, f32[128,2,512]{2,1,0:T(2,128)} %param.31), kind=kLoop, calls=%fused_computation.64 | loop fusion | flops 1966080 | bytes 3670016 | tf_op jit(solution)/shard_map/sub | solution.py:53
  401.8 3.4 add_convert_fusion
  (285 shorter events, 100.0 us)
Async XLA Ops:
  7.2 70.3 %all-gather.5.cloned.1.call-start = ((), (), s32[]{:S(2)}) async-start(), calls=%async_computation.2 | async-start | bytes 3833856 | tf_op jit(solution)/shard_map/all_gather | solution.py:654
  11.1 147.6 %all-gather.7.cloned.1.call-start = ((), (), s32[]{:S(2)}) async-start(), calls=%async_computation.3 | async-start | bytes 5308416 | tf_op jit(solution)/shard_map/all_gather | solution.py:656
  12.9 357.5 %reduce-scatter.2.cloned.1.call-start = ((), (), s32[]{:S(2)}) async-start(), calls=%async_computation.1 | async-start | bytes 5308416 | tf_op jit(solution)/shard_map/reduce_scatter | solution.py:762
  13.0 27.1 %collective-permute-start.1 = (bf16[512,1024]{1,0:T(8,128)(2,1)S(1)}, bf16[512,1024]{1,0:T(8,128)(2,1)}, u32[]{:S(2)}, u32[]{:S(2)}) collective-permute-start(bf16[512,1024]{1,0:T(8,128)(2,1)S(1)} %copy-done.32), channel_id=1, source_target_pairs={{0,2},{1,3},{2,0},{3,1},{4,6},{5,7},{6,4},{7,5},{8,10},{9,11},{10,... | collective-permute-start | bytes 3145736 | tf_op jit(solution)/shard_map/tokens_across/ppermute | solution.py:588
  16.0 28.6 %collective-permute-start = (bf16[512,1024]{1,0:T(8,128)(2,1)S(1)}, bf16[512,1024]{1,0:T(8,128)(2,1)}, u32[]{:S(2)}, u32[]{:S(2)}) collective-permute-start(bf16[512,1024]{1,0:T(8,128)(2,1)S(1)} %copy-done.32), channel_id=1, source_target_pairs={{0,1},{1,0},{2,3},{3,2},{4,5},{5,4},{6,7},{7,6},{8,9},{9,8},{10,11... | collective-permute-start | bytes 3145736 | tf_op jit(solution)/shard_map/part/ppermute | solution.py:588
  16.0 99.1 %collective-permute-start.3 = (bf16[512,1024]{1,0:T(8,128)(2,1)}, bf16[512,1024]{1,0:T(8,128)(2,1)}, u32[]{:S(2)}, u32[]{:S(2)}) collective-permute-start(bf16[512,1024]{1,0:T(8,128)(2,1)} %param.19), channel_id=1, source_target_pairs={{0,2},{1,3},{2,0},{3,1},{4,6},{5,7},{6,4},{7,5},{8,10},{9,11},{10,... | collective-permute-start | bytes 3145736 | tf_op jit(solution)/shard_map/grad_across/ppermute | solution.py:588
  119.3 25.3 %collective-permute-start.5 = (bf16[512,1024]{1,0:T(8,128)(2,1)S(1)}, bf16[512,1024]{1,0:T(8,128)(2,1)S(1)}, u32[]{:S(2)}, u32[]{:S(2)}) collective-permute-start(bf16[512,1024]{1,0:T(8,128)(2,1)S(1)} %add_convert_fusion.5), channel_id=1, source_target_pairs={{0,2},{1,3},{2,0},{3,1},{4,6},{5,7},{6,4},{7,5},{8,10},{9,11},{10,... | collective-permute-start | bytes 3145736 | tf_op jit(solution)/shard_map/attn_across/ppermute | solution.py:588
  146.4 17.9 %collective-permute-start.9 = (bf16[512,1024]{1,0:T(8,128)(2,1)}, bf16[512,1024]{1,0:T(8,128)(2,1)}, u32[]{:S(2)}, u32[]{:S(2)}) collective-permute-start(bf16[512,1024]{1,0:T(8,128)(2,1)} %param.19), channel_id=1, source_target_pairs={{0,1},{1,0},{2,3},{3,2},{4,5},{5,4},{6,7},{7,6},{8,9},{9,8},{10,11... | collective-permute-start | bytes 3145736 | tf_op jit(solution)/shard_map/part/ppermute | solution.py:588
  161.4 4.5 %collective-permute-start.8 = (bf16[512,1024]{1,0:T(8,128)(2,1)S(1)}, bf16[512,1024]{1,0:T(8,128)(2,1)S(1)}, u32[]{:S(2)}, u32[]{:S(2)}) collective-permute-start(bf16[512,1024]{1,0:T(8,128)(2,1)S(1)} %multiply_convert_fusion), channel_id=1, source_target_pairs={{0,1},{1,0},{2,3},{3,2},{4,5},{5,4},{6,7},{7,6},{8,9},{9,8},{10,11... | collective-permute-start | bytes 3145736 | tf_op jit(solution)/shard_map/part/ppermute | solution.py:588
  161.5 25.6 %collective-permute-start.7 = (bf16[512,1024]{1,0:T(8,128)(2,1)S(1)}, bf16[512,1024]{1,0:T(8,128)(2,1)S(1)}, u32[]{:S(2)}, u32[]{:S(2)}) collective-permute-start(bf16[512,1024]{1,0:T(8,128)(2,1)S(1)} %multiply_convert_fusion), channel_id=1, source_target_pairs={{0,2},{1,3},{2,0},{3,1},{4,6},{5,7},{6,4},{7,5},{8,10},{9,11},{10,... | collective-permute-start | bytes 3145736 | tf_op jit(solution)/shard_map/normed_across/ppermute | solution.py:588
  165.6 22.7 %collective-permute-start.12 = (bf16[512,1024]{1,0:T(8,128)(2,1)}, bf16[512,1024]{1,0:T(8,128)(2,1)S(1)}, u32[]{:S(2)}, u32[]{:S(2)}) collective-permute-start(bf16[512,1024]{1,0:T(8,128)(2,1)} %collective-permute-done.3), channel_id=1, source_target_pairs={{0,1},{1,0},{2,3},{3,2},{4,5},{5,4},{6,7},{7,6},{8,9},{9,8},{10,11... | collective-permute-start | bytes 3145736 | tf_op jit(solution)/shard_map/part/ppermute | solution.py:588
  214.1 25.5 %collective-permute-start.14 = (bf16[512,1024]{1,0:T(8,128)(2,1)}, bf16[512,1024]{1,0:T(8,128)(2,1)}, u32[]{:S(2)}, u32[]{:S(2)}) collective-permute-start(bf16[512,1024]{1,0:T(8,128)(2,1)} %add_convert_fusion.4), channel_id=1, source_target_pairs={{0,2},{1,3},{2,0},{3,1},{4,6},{5,7},{6,4},{7,5},{8,10},{9,11},{10,... | collective-permute-start | bytes 3145736 | tf_op jit(solution)/shard_map/back_across/ppermute | solution.py:588
  215.6 24.0 %collective-permute-start.10 = (bf16[512,1024]{1,0:T(8,128)(2,1)S(1)}, bf16[512,1024]{1,0:T(8,128)(2,1)}, u32[]{:S(2)}, u32[]{:S(2)}) collective-permute-start(bf16[512,1024]{1,0:T(8,128)(2,1)S(1)} %get-tuple-element.112), channel_id=1, source_target_pairs={{0,1},{1,0},{2,3},{3,2},{4,5},{5,4},{6,7},{7,6},{8,9},{9,8},{10,11... | collective-permute-start | bytes 3145736 | tf_op jit(solution)/shard_map/part/ppermute | solution.py:588
  247.1 25.9 %collective-permute-start.16 = (bf16[512,1024]{1,0:T(8,128)(2,1)}, bf16[512,1024]{1,0:T(8,128)(2,1)}, u32[]{:S(2)}, u32[]{:S(2)}) collective-permute-start(bf16[512,1024]{1,0:T(8,128)(2,1)} %get-tuple-element.192), channel_id=1, source_target_pairs={{0,2},{1,3},{2,0},{3,1},{4,6},{5,7},{6,4},{7,5},{8,10},{9,11},{10,... | collective-permute-start | bytes 3145736 | tf_op jit(solution)/shard_map/grad_middle_across/ppermute | solution.py:588
  315.4 6.5 %collective-permute-start.18 = (bf16[512,1024]{1,0:T(8,128)(2,1)S(1)}, bf16[512,1024]{1,0:T(8,128)(2,1)S(1)}, u32[]{:S(2)}, u32[]{:S(2)}) collective-permute-start(bf16[512,1024]{1,0:T(8,128)(2,1)S(1)} %get-tuple-element.140), channel_id=1, source_target_pairs={{0,1},{1,0},{2,3},{3,2},{4,5},{5,4},{6,7},{7,6},{8,9},{9,8},{10,11... | collective-permute-start | bytes 3145736 | tf_op jit(solution)/shard_map/part/ppermute | solution.py:588
  323.4 15.6 %collective-permute-start.26 = (bf16[4,2,2,16,1024]{4,3,0,1,2:T(8,128)(2,1)S(1)}, bf16[4,2,2,16,1024]{4,3,0,1,2:T(8,128)(2,1)}, u32[]{:S(2)}, u32[]{:S(2)}) collective-permute-start(bf16[4,2,2,16,1024]{4,3,0,1,2:T(8,128)(2,1)S(1)} %bitcast.137), channel_id=1, source_target_pairs={{0,4},{4,0},{8,12},{12,8},{16,20},{20,16},{24,28},{28,24},{1,5},{5... | collective-permute-start | bytes 1572872 | tf_op jit(solution)/shard_map/part/ppermute | solution.py:588
  328.4 21.5 %collective-permute-start.20 = (bf16[2,2,128,512]{3,2,0,1:T(8,128)(2,1)}, bf16[2,2,128,512]{3,2,0,1:T(8,128)(2,1)S(1)}, u32[]{:S(2)}, u32[]{:S(2)}) collective-permute-start(bf16[2,2,128,512]{3,2,0,1:T(8,128)(2,1)} %fusion.10), channel_id=1, source_target_pairs={{0,4},{4,0},{8,12},{12,8},{16,20},{20,16},{24,28},{28,24},{1,5},{5... | collective-permute-start | bytes 1572872 | tf_op jit(solution)/shard_map/part/ppermute | solution.py:588
  331.2 21.7 %collective-permute-start.19 = (bf16[2,2,144,512]{3,2,0,1:T(8,128)(2,1)S(1)}, bf16[2,2,144,512]{3,2,0,1:T(8,128)(2,1)}, u32[]{:S(2)}, u32[]{:S(2)}) collective-permute-start(bf16[2,2,144,512]{3,2,0,1:T(8,128)(2,1)S(1)} %fusion.8), channel_id=1, source_target_pairs={{0,8},{4,12},{8,0},{12,4},{16,24},{20,28},{24,16},{28,20},{1,9},{5... | collective-permute-start | bytes 1769480 | tf_op jit(solution)/shard_map/part/ppermute | solution.py:588
  331.9 27.9 %collective-permute-start.21 = (bf16[512,1024]{1,0:T(8,128)(2,1)S(1)}, bf16[512,1024]{1,0:T(8,128)(2,1)S(1)}, u32[]{:S(2)}, u32[]{:S(2)}) collective-permute-start(bf16[512,1024]{1,0:T(8,128)(2,1)S(1)} %copy-done.48), channel_id=1, source_target_pairs={{0,2},{1,3},{2,0},{3,1},{4,6},{5,7},{6,4},{7,5},{8,10},{9,11},{10,... | collective-permute-start | bytes 3145736 | tf_op jit(solution)/shard_map/back_across/ppermute | solution.py:588
  333.2 25.2 %collective-permute-start.22 = (bf16[512,1024]{1,0:T(8,128)(2,1)S(1)}, bf16[512,1024]{1,0:T(8,128)(2,1)S(1)}, u32[]{:S(2)}, u32[]{:S(2)}) collective-permute-start(bf16[512,1024]{1,0:T(8,128)(2,1)S(1)} %copy-done.23), channel_id=1, source_target_pairs={{0,1},{1,0},{2,3},{3,2},{4,5},{5,4},{6,7},{7,6},{8,9},{9,8},{10,11... | collective-permute-start | bytes 3145736 | tf_op jit(solution)/shard_map/part/ppermute | solution.py:588
  338.9 24.6 %collective-permute-start.32 = (bf16[512,1024]{1,0:T(8,128)(2,1)S(1)}, bf16[512,1024]{1,0:T(8,128)(2,1)S(1)}, u32[]{:S(2)}, u32[]{:S(2)}) collective-permute-start(bf16[512,1024]{1,0:T(8,128)(2,1)S(1)} %get-tuple-element.167), channel_id=1, source_target_pairs={{0,1},{1,0},{2,3},{3,2},{4,5},{5,4},{6,7},{7,6},{8,9},{9,8},{10,11... | collective-permute-start | bytes 3145736 | tf_op jit(solution)/shard_map/part/ppermute | solution.py:588
  349.9 8.4 %collective-permute-start.27 = (bf16[4,2,16,1024]{3,2,0,1:T(8,128)(2,1)S(1)}, bf16[4,2,16,1024]{3,2,0,1:T(8,128)(2,1)S(1)}, u32[]{:S(2)}, u32[]{:S(2)}) collective-permute-start(bf16[4,2,16,1024]{3,2,0,1:T(8,128)(2,1)S(1)} %fusion.21), channel_id=1, source_target_pairs={{0,8},{4,12},{8,0},{12,4},{16,24},{20,28},{24,16},{28,20},{1,9},{5... | collective-permute-start | bytes 786440 | tf_op jit(solution)/shard_map/part/ppermute | solution.py:588
  359.9 10.5 %collective-permute-start.24 = (bf16[2,144,512]{2,1,0:T(8,128)(2,1)S(1)}, bf16[2,144,512]{2,1,0:T(8,128)(2,1)S(1)}, u32[]{:S(2)}, u32[]{:S(2)}) collective-permute-start(bf16[2,144,512]{2,1,0:T(8,128)(2,1)S(1)} %fusion.18), channel_id=1, source_target_pairs={{0,4},{4,0},{8,12},{12,8},{16,20},{20,16},{24,28},{28,24},{1,5},{5... | collective-permute-start | bytes 884744 | tf_op jit(solution)/shard_map/part/ppermute | solution.py:588
  361.4 8.0 %collective-permute-start.25 = (bf16[2,128,512]{2,1,0:T(8,128)(2,1)S(1)}, bf16[2,128,512]{2,1,0:T(8,128)(2,1)S(1)}, u32[]{:S(2)}, u32[]{:S(2)}) collective-permute-start(bf16[2,128,512]{2,1,0:T(8,128)(2,1)S(1)} %fusion.20), channel_id=1, source_target_pairs={{0,8},{4,12},{8,0},{12,4},{16,24},{20,28},{24,16},{28,20},{1,9},{5... | collective-permute-start | bytes 786440 | tf_op jit(solution)/shard_map/part/ppermute | solution.py:588
  362.0 32.8 %collective-permute-start.31 = (bf16[512,1024]{1,0:T(8,128)(2,1)}, bf16[512,1024]{1,0:T(8,128)(2,1)}, u32[]{:S(2)}, u32[]{:S(2)}) collective-permute-start(bf16[512,1024]{1,0:T(8,128)(2,1)} %add_convert_fusion.1), channel_id=1, source_target_pairs={{0,2},{1,3},{2,0},{3,1},{4,6},{5,7},{6,4},{7,5},{8,10},{9,11},{10,... | collective-permute-start | bytes 3145736 | tf_op jit(solution)/shard_map/mlp_across/ppermute | solution.py:588
  363.5 38.3 %collective-permute-start.23 = (bf16[512,1024]{1,0:T(8,128)(2,1)S(1)}, bf16[512,1024]{1,0:T(8,128)(2,1)}, u32[]{:S(2)}, u32[]{:S(2)}) collective-permute-start(bf16[512,1024]{1,0:T(8,128)(2,1)S(1)} %copy-done.21), channel_id=1, source_target_pairs={{0,1},{1,0},{2,3},{3,2},{4,5},{5,4},{6,7},{7,6},{8,9},{9,8},{10,11... | collective-permute-start | bytes 3145736 | tf_op jit(solution)/shard_map/part/ppermute | solution.py:588
  372.5 21.3 %collective-permute-start.28 = (bf16[144,512]{1,0:T(8,128)(2,1)}, bf16[144,512]{1,0:T(8,128)(2,1)}, u32[]{:S(2)}, u32[]{:S(2)}) collective-permute-start(bf16[144,512]{1,0:T(8,128)(2,1)} %fusion.22), channel_id=1, source_target_pairs={{0,16},{4,20},{8,24},{12,28},{16,0},{20,4},{24,8},{28,12},{1,17},{... | collective-permute-start | bytes 442376 | tf_op jit(solution)/shard_map/part/ppermute | solution.py:588
  376.3 15.4 %collective-permute-start.29 = (bf16[128,512]{1,0:T(8,128)(2,1)}, bf16[128,512]{1,0:T(8,128)(2,1)}, u32[]{:S(2)}, u32[]{:S(2)}) collective-permute-start(bf16[128,512]{1,0:T(8,128)(2,1)} %fusion.23), channel_id=1, source_target_pairs={{0,16},{4,20},{8,24},{12,28},{16,0},{20,4},{24,8},{28,12},{1,17},{... | collective-permute-start | bytes 393224 | tf_op jit(solution)/shard_map/part/ppermute | solution.py:588
  377.8 15.1 %collective-permute-start.30 = (bf16[4,16,1024]{2,1,0:T(8,128)(2,1)}, bf16[4,16,1024]{2,1,0:T(8,128)(2,1)}, u32[]{:S(2)}, u32[]{:S(2)}) collective-permute-start(bf16[4,16,1024]{2,1,0:T(8,128)(2,1)} %fusion.24), channel_id=1, source_target_pairs={{0,16},{4,20},{8,24},{12,28},{16,0},{20,4},{24,8},{28,12},{1,17},{... | collective-permute-start | bytes 393224 | tf_op jit(solution)/shard_map/part/ppermute | solution.py:588
  394.9 11.4 %collective-permute-start.35 = (f32[288]{0:T(512)S(1)}, f32[288]{0:T(512)S(1)}, u32[]{:S(2)}, u32[]{:S(2)}) collective-permute-start(f32[288]{0:T(512)S(1)} %slice_reduce_fusion), channel_id=1, source_target_pairs={{0,3},{1,2},{2,1},{3,0},{4,7},{5,6},{6,5},{7,4},{8,11},{9,10},{10,... | collective-permute-start | bytes 3464 | tf_op jit(solution)/shard_map/part/ppermute | solution.py:588
  394.9 11.3 %collective-permute-start.33 = (f32[288]{0:T(512)S(1)}, f32[288]{0:T(512)S(1)}, u32[]{:S(2)}, u32[]{:S(2)}) collective-permute-start(f32[288]{0:T(512)S(1)} %slice_reduce_fusion), channel_id=1, source_target_pairs={{0,1},{1,0},{2,3},{3,2},{4,5},{5,4},{6,7},{7,6},{8,9},{9,8},{10,11... | collective-permute-start | bytes 3464 | tf_op jit(solution)/shard_map/part/ppermute | solution.py:588
  396.3 9.9 %collective-permute-start.34 = (f32[288]{0:T(512)S(1)}, f32[288]{0:T(512)S(1)}, u32[]{:S(2)}, u32[]{:S(2)}) collective-permute-start(f32[288]{0:T(512)S(1)} %slice_reduce_fusion), channel_id=1, source_target_pairs={{0,2},{1,3},{2,0},{3,1},{4,6},{5,7},{6,4},{7,5},{8,10},{9,11},{10,... | collective-permute-start | bytes 3464 | tf_op jit(solution)/shard_map/part/ppermute | solution.py:588
  (65 other events, 587.2 us)
Sparse Core Ops, SparseCore 0:
  11.2 66.2 all-gather.4
  80.2 78.4 all-gather.6
  248.7 96.0 reduce-scatter.1

commit v8 on v7

--- a/solution.py
+++ b/solution.py
@@ -99,9 +99,10 @@
     normed_turned[...] = normed.T.astype(BF16)
     h = normed.astype(BF16)
     c, s = cos[...], sin[...]
-    for j in range(matrix.shape[1] // (SLOTS * HEAD_SIZE)):
+    for j in range(matrix.shape[2] // (SLOTS * HEAD_SIZE)):
         base = j * SLOTS * HEAD_SIZE
-        part = nn(h, matrix[:, base : base + SLOTS * HEAD_SIZE])
+        columns = matrix[:, :, base : base + SLOTS * HEAD_SIZE]
+        part = nn(h, columns.reshape(-1, SLOTS * HEAD_SIZE))
         for g in range(GROUP):
             value = part[:, lanes_of(g)]
             raw_q[:, lanes_of(j * GROUP + g)] = value
@@ -390,7 +391,7 @@
 
 def project(x, gain, matrix, cos, sin, gain_q, gain_k):
     rows, width = x.shape
-    heads = matrix.shape[1] // (SLOTS * HEAD_SIZE)
+    heads = matrix.shape[2] // (SLOTS * HEAD_SIZE)
     by_rows = lambda n: pl.BlockSpec((BLOCK, n), lambda i: (i, 0))
     by_lanes = lambda n: pl.BlockSpec((n, BLOCK), lambda i: (0, i))
     q_width, k_width = heads * GROUP * HEAD_SIZE, heads * HEAD_SIZE
@@ -398,7 +399,8 @@
         project_kernel,
         grid=(rows // BLOCK,),
         in_specs=[
-            by_rows(width), fixed((1, width)), fixed(matrix.shape), by_rows(HEAD_SIZE),
+            by_rows(width), fixed((1, width)),
+            fixed((matrix.shape[0], width // matrix.shape[0], matrix.shape[2])), by_rows(HEAD_SIZE),
             by_rows(HEAD_SIZE), fixed((1, HEAD_SIZE)), fixed((1, HEAD_SIZE)),
         ],
         out_specs=[
@@ -583,6 +585,40 @@
     )(grad, matrix)
 
 
+def middle_back_kernel(own, beside, across, value, grad, gain, out, out_low, grad_gain):
+    total = own[...].astype(F32) + beside[...].astype(F32) + across[...].astype(F32)
+    x = value[...]
+    r = lax.rsqrt(jnp.mean(x * x, axis=-1, keepdims=True) + EPS)
+    u = total * gain[...]
+    back = r * u - x * (r * r * r) * jnp.mean(u * x, axis=-1, keepdims=True)
+    result = grad[...].astype(F32) + back
+    out[...] = result
+    out_low[...] = result.astype(BF16)
+    part = jnp.sum(total * x * r, axis=0, keepdims=True)
+
+    @pl.when(pl.program_id(0) == 0)
+    def _():
+        grad_gain[...] = part
+
+    @pl.when(pl.program_id(0) > 0)
+    def _():
+        grad_gain[...] += part
+
+
+def middle_back(own, beside, across, value, grad, gain):
+    rows, width = value.shape
+    block = pl.BlockSpec((BLOCK // 2, width), lambda i: (i, 0))
+    row = fixed((1, width))
+    return pl.pallas_call(
+        middle_back_kernel,
+        grid=(rows // (BLOCK // 2),),
+        in_specs=[block] * 5 + [row],
+        out_specs=[block, block, row],
+        out_shape=[shaped((rows, width), F32), shaped((rows, width), BF16), shaped((1, width), F32)],
+        **params("middle_back", 2_000_000_000),
+    )(own, beside, across, value, grad, gain)
+
+
 def flipped(value, axis, bit, name="part"):
     with jax.named_scope(name):
         return lax.ppermute(value, axis, [(i, i ^ bit) for i in range(lax.axis_size(axis))])
@@ -651,7 +687,8 @@
             value[..., depth + out_rows, :gain_count],
         )
 
-    full_qkv, full_out, full_gains = split_one(lax.all_gather(pack_one, "dp", axis=0, tiled=False))
+    full_one = lax.all_gather(pack_one, "dp", axis=0, tiled=False)
+    full_qkv, full_out, full_gains = split_one(full_one)
     full_out = full_out.reshape(spread, out_heads, out_depth, MODEL_WIDTH).swapaxes(0, 1)
     full_two = lax.all_gather(pack_two, "dp", axis=0, tiled=False)
     qkv_matrix = full_qkv.reshape(MODEL_WIDTH, -1)
@@ -694,7 +731,7 @@
         axis=0,
     )
     normed_turned, raw_q, raw_k, q, k, v, k_turned = project(
-        tokens_all, gain_attn, qkv_matrix, cos, sin, gain_query, gain_key
+        tokens_all, gain_attn, full_one if cubic else qkv_matrix[None], cos, sin, gain_query, gain_key
     )
     grad_across = flipped(cotangent, "tensor", 2, "grad_across")
     heads_other, heads_other_turned, logs_other = attend(1, info, q, k_turned, v)
@@ -736,7 +773,7 @@
         normed_other, grad_other, feed_matrices, hidden_local
     )
     near = near_sum(back_2, back_3).astype(BF16)
-    back_near = near_sum(back_0, back_1)
+    back_beside = flipped(back_1, "tensor", 1)
     near, h_own = together(near, h_own)
     back_across = flipped(near, "tensor", 2, "back_across")
 
@@ -744,7 +781,7 @@
         full_two.shape if cubic else None, (h_own, h_other), (feed_grad_own, feed_grad_other),
         (hidden_own, hidden_other), (grad_own, grad_other),
     )
-    back_across, *feed_grads = together(back_across, *feed_grads)
+    back_across, _ = together(back_across, feed_grads[0])
     if cubic:
         feed_pack = feed_grads[0]
     else:
@@ -760,11 +797,10 @@
             axis=1,
         )
     feed_sum = lax.psum_scatter(feed_pack, "dp", scatter_dimension=0, tiled=True)[0].astype(F32)
-    grad_middle_part, grad_gain_mlp = norm_back(
-        middle, gain_mlp, back_near + back_across.astype(F32)
-    )
-    grad_middle = cotangent.astype(F32) + grad_middle_part
-    grad_middle_low = grad_middle.astype(BF16)
+    grad_middle, grad_middle_low, grad_gain_mlp = middle_back(
+        back_0, back_beside, back_across, middle, cotangent, gain_mlp[None, :]
+    )
+    grad_gain_mlp = grad_gain_mlp[0]
     grad_middle_across = flipped(grad_middle_low, "tensor", 2, "grad_middle_across")
 
     grad_middle_own = jnp.concatenate(
@@ -780,10 +816,6 @@
         [grad_middle_across, flipped(grad_middle_across, "tensor", 1)], axis=0
     )
     grad_heads_other = nt(grad_middle_other, out_matrix).astype(BF16)
-    grad_out_w = (
-        nn(heads_own_turned, grad_middle_own) + nn(heads_other_turned, grad_middle_other)
-    ).astype(BF16)
-    grad_out_w, grad_heads_other = together(grad_out_w, grad_heads_other)
     grad_qkv, gain_other = attend_back_other(
         info, q, k, v, k_turned, start, logs_other, heads_other, grad_heads_other,
         raw_q, cos, sin, gain_query, raw_k, gain_key, grad_q, grad_k, grad_v,
@@ -792,9 +824,7 @@
     back_2, back_3, grad_qkv = together(back_2, back_3, grad_qkv)
     grad_qkv_w = nn(normed_turned, grad_qkv)
     near = near_sum(back_2, back_3).astype(BF16)
-    near, grad_qkv, grad_qkv_w, grad_out_w, sum_2, sum_3 = together(
-        near, grad_qkv, grad_qkv_w, grad_out_w, sum_2, sum_3
-    )
+    near, grad_qkv, grad_qkv_w, sum_2, sum_3 = together(near, grad_qkv, grad_qkv_w, sum_2, sum_3)
     near_mlp = near_sum(sum_2, sum_3).astype(BF16)
     back_across = flipped(near, "tensor", 2, "back_across")
     grad_gain_attn = jnp.sum(qkv_matrix.astype(F32) * grad_qkv_w, axis=1) / gain_attn[0]
@@ -803,6 +833,10 @@
     )
     gain_sums = jnp.concatenate([grad_gain_attn, grad_gain_mlp, grad_gain_heads.reshape(-1)])
     back_0, back_1 = unproject(0, grad_qkv, qkv_matrix)
+
+    def out_gradient(own_turned, other_turned):
+        return (nn(own_turned, grad_middle_own) + nn(other_turned, grad_middle_other)).astype(BF16)
+
     if cubic:
         cube = (2, 2, 2)
         columns = grad_qkv_w.shape[1] // 2
@@ -815,30 +849,34 @@
         )
         sum_two = grad_qkv_w[:, columns:].reshape(cube + (depth, -1))
         sum_one, sum_two = halved(sum_one, 1, 2), halved(sum_two, 2, 1)
-        sum_out = grad_out_w.reshape((out_heads,) + cube + (out_depth, MODEL_WIDTH))
-        sum_out = halved(sum_out, 3, 1)
-        sum_one, sum_two, back_across, sum_0, sum_1, near_mlp = together(
-            sum_one, sum_two, back_across, sum_0, sum_1, near_mlp
+        sum_one, sum_two, back_across, sum_0, sum_1, near_mlp, *heads_turned = together(
+            sum_one, sum_two, back_across, sum_0, sum_1, near_mlp,
+            heads_own_turned, heads_other_turned,
         )
         mlp_across = flipped(near_mlp, "tensor", 2, "mlp_across")
         sum_one, sum_two = halved(sum_one, 1, 1), halved(sum_two, 1, 2)
-        sum_out = halved(sum_out, 2, 2)
-        sum_one, sum_two, sum_out, feed_sum = together(sum_one, sum_two, sum_out, feed_sum)
+        sum_one, sum_two, feed_sum = together(sum_one, sum_two, feed_sum)
+        grad_out_w = out_gradient(*heads_turned)
+        sum_out = grad_out_w.reshape((out_heads,) + cube + (out_depth, MODEL_WIDTH))
+        sum_out = halved(halved(sum_out, 3, 1), 2, 2)
         sum_one, sum_two = halved(sum_one, 0, 4), halved(sum_two, 0, 4)
         sum_out = halved(sum_out, 1, 4)
-        sum_one, sum_two, sum_out, mlp_across = together(sum_one, sum_two, sum_out, mlp_across)
+        block_out = (middle + near_sum(sum_0, sum_1) + mlp_across.astype(F32)).astype(BF16)
+        sum_one, sum_two, block_out = together(sum_one, sum_two, block_out)
         sum_qkv = jnp.concatenate([sum_one[:depth], sum_two], axis=1)
         sum_qkv = sum_qkv.reshape(projection_weight.shape)
         sum_gains = sum_one[depth, :gain_count]
     else:
         mlp_across = flipped(near_mlp, "tensor", 2, "mlp_across")
+        block_out = (middle + near_sum(sum_0, sum_1) + mlp_across.astype(F32)).astype(BF16)
         sum_qkv = (
             lax.psum_scatter(grad_qkv_w.astype(BF16), "dp", scatter_dimension=0, tiled=True)
             .astype(F32)
             .reshape(projection_weight.shape)
         )
         sum_out = lax.psum_scatter(
-            grad_out_w.reshape(out_heads, -1, MODEL_WIDTH), "dp", scatter_dimension=1, tiled=True
+            out_gradient(heads_own_turned, heads_other_turned).reshape(out_heads, -1, MODEL_WIDTH), "dp",
+            scatter_dimension=1, tiled=True,
         ).astype(F32)
         sum_gains = lax.psum_scatter(gain_sums, "dp", scatter_dimension=0, tiled=True)
     sum_gains = sum_gains + sum(flipped(sum_gains, "tensor", bit) for bit in range(1, shards))
@@ -846,8 +884,6 @@
     grad_normed_one = near_sum(back_0, back_1) + back_across.astype(F32)
     grad_rows_part, _ = norm_back(rows_float, gain_attn, grad_normed_one)
     grad_tokens = grad_middle + grad_rows_part
-    mlp_rows = near_sum(sum_0, sum_1) + mlp_across.astype(F32)
-    block_out = (middle + mlp_rows).astype(BF16)
 
     sum_gate_up = (
         feed_sum[:gate_rows].reshape(pieces, depth, half).swapaxes(0, 1).reshape(w_gate_up.shape)

time: 420 us -> 437 us (1.040)
  waiting for transfers between devices: 113 us -> 140 us
  other arithmetic: 62.6 us -> 51.8 us
  Pallas kernels: 149 us -> 155 us
    ppermute x36, waiting for transfers between devices: 77.3 us -> 101 us  [flipped(): lax.ppermute(value, axis, [(i, i ^ bit) for i in range(lax.axis_size(axis...]
    convert_element_type x2 -> x1, other arithmetic: 7.79 us -> 1.78 us  [per_device(): (middle + near_sum(sum_0, sum_1) + mlp_across.astype(F32)).astype(BF16)]
    pallas_call x0 -> x1, Pallas kernels: none -> 5 us  [middle_back(): pl.pallas_call(middle_back_kernel, grid=(rows // (BLOCK // 2),), in_specs...]
    unnamed x123 -> x128, local copies, waits for them, and re-layouts: 9.3 us -> 11.9 us
  transfers between devices with their start and end apart: 39 -> 39, of which waited for: 19 -> 18; matrix products, arithmetic and copies ran while one was open for 22% -> 18% of each run, Pallas kernels for 32% -> 31%
where the time goes in v8:
time: 437 us; the launch traced here: 431 us
  Pallas kernels  155 us (35%)
  waiting for transfers between devices  140 us (32%)
  other arithmetic  51.8 us (12%)
  local copies, waits for them, and re-layouts  28.4 us (6%)
  starting transfers between devices  23.3 us (5%)
  matrix products  16.6 us (4%)
  between operations  15.5 us (4%)
    ppermute x36, waiting for transfers between devices, flipped(): lax.ppermute(value, axis, [(i, i ^ bit) for i in range(lax.axis_size(axis...  101 us
    pallas_call x2, Pallas kernels, feed(): pl.pallas_call(lambda *refs: feed_kernel(packs, *refs), grid=(rows // BLO...  33.9 us
    pallas_call x2, Pallas kernels, attend(): pl.pallas_call(lambda *refs: attend_kernel(half * n // BLOCK, *refs), gri...  29.7 us
    pallas_call x1, Pallas kernels, attend_back_other(): pl.pallas_call(back_other_kernel, grid_spec=pltpu.PrefetchScalarGridSpec(...  29.4 us
    all_gather x1, waiting for transfers between devices, per_device(): full_one = lax.all_gather(pack_one, 'dp', axis=0, tiled=False)  28.6 us
    ppermute x36, starting transfers between devices, flipped(): lax.ppermute(value, axis, [(i, i ^ bit) for i in range(lax.axis_size(axis...  23.2 us
    pallas_call x1, Pallas kernels, attend_back_own(): pl.pallas_call(back_own_kernel, grid_spec=pltpu.PrefetchScalarGridSpec(nu...  16.9 us
    pallas_call x1, Pallas kernels, feed_weights(): pl.pallas_call(lambda *refs: feed_weights_kernel(packs, pieces, *refs), g...  16.5 us
  transfers between devices with their start and end apart: 39, of which 18 were waited for; matrix products, arithmetic and copies ran while one was open for 18% of the time, Pallas kernels for 31%

profile of v8, /device:TPU:0, one launch (start us, length us, event | category | flops | bytes accessed | tf_op | source)
XLA Modules:
  0.0 430.7 jit_solution(13873669525663396703)
XLA Ops:
  13.0 3.0 collective-permute-start.1
  16.8 23.4 %collective-permute-done.1 = bf16[512,1024]{1,0:T(8,128)(2,1)} collective-permute-done((bf16[512,1024]{1,0:T(8,128)(2,1)S(1)}, bf16[512,1024]{1,0:T(8,128)(2,1)}, u32[]{:S(2)}, u32[]{:S(2)}) %collective-permute-start.1) | collective-permute-done | bytes 1048608 | tf_op jit(solution)/shard_map/tokens_across/ppermute | solution.py:624
  40.1 3.7 fusion.17
  44.6 4.3 pad_maximum_fusion.x
  48.8 28.6 %all-gather.5.cloned.1.call-done = bf16[1664,1024]{1,0:T(8,128)(2,1)} async-done(((bf16[208,1024]{1,0:T(8,128)(2,1)}), bf16[1664,1024]{1,0:T(8,128)(2,1)}) %all-gather.5.cloned.1.call-update) | async-done | bytes 3407888 | tf_op jit(solution)/shard_map/all_gather | solution.py:690
  79.9 13.7 %project.1 = (bf16[1024,2048]{1,0:T(8,128)(2,1)}, f32[2048,512]{1,0:T(8,128)}, f32[2048,256]{1,0:T(8,128)}, bf16[2048,512]{1,0:T(8,128)(2,1)}, bf16[2048,256]{1,...) custom-call(bf16[2048,1024]{1,0:T(8,128)(2,1)} %pad_maximum_fusion.x, ...), custom_call_target="tpu_custom_call" | custom-call | flops 156250000 | bytes 1000 | tf_op jit(solution)/shard_map/project/pallas_call | solution.py:398
  93.6 18.1 %attend.2 = (bf16[1024,512]{1,0:T(8,128)(2,1)S(1)}, bf16[512,1024]{1,0:T(8,128)(2,1)S(1)}, f32[2,2,1024]{2,1,0:T(2,128)S(1)}) custom-call(s32[17]{0:T(128)S(1)} %pad_add_fusion.refs_0_.info, bf16[2048,512]{1,0:T(8,128)(2,1)} %get-tuple-element.101.refs_1_.q, bf16[256,2048]{1,0:T(8,128)(2,1)S(1)} %get-tuple-element.97.refs_2_.k_turned, ...), custom_call_target="tpu_custom_call" | custom-call | flops 281249984 | bytes 1000 | tf_op jit(solution)/shard_map/attend/pallas_call | solution.py:440
  116.0 11.6 %attend.3 = (bf16[1024,512]{1,0:T(8,128)(2,1)S(1)}, bf16[512,1024]{1,0:T(8,128)(2,1)S(1)}, f32[2,2,1024]{2,1,0:T(2,128)S(1)}) custom-call(s32[17]{0:T(128)S(1)} %pad_add_fusion.refs_0_.info, bf16[2048,512]{1,0:T(8,128)(2,1)} %get-tuple-element.101.refs_1_.q, bf16[256,2048]{1,0:T(8,128)(2,1)S(1)} %get-tuple-element.97.refs_2_.k_turned, ...), custom_call_target="tpu_custom_call" | custom-call | flops 281249984 | bytes 1000 | tf_op jit(solution)/shard_map/attend/pallas_call | solution.py:440
  127.6 13.7 %collective-permute-done.5 = bf16[512,1024]{1,0:T(8,128)(2,1)} collective-permute-done((bf16[512,1024]{1,0:T(8,128)(2,1)S(1)}, bf16[512,1024]{1,0:T(8,128)(2,1)}, u32[]{:S(2)}, u32[]{:S(2)}) %collective-permute-start.5) | collective-permute-done | bytes 1048608 | tf_op jit(solution)/shard_map/attn_across/ppermute | solution.py:624
  142.6 2.9 collective-permute-done.6
  147.5 11.1 %all-gather.7.cloned.1.call-done = bf16[4608,512]{1,0:T(8,128)(2,1)} async-done(((bf16[576,512]{1,0:T(8,128)(2,1)}), bf16[4608,512]{1,0:T(8,128)(2,1)}) %all-gather.7.cloned.1.call-update) | async-done | bytes 4718608 | tf_op jit(solution)/shard_map/all_gather | solution.py:693
  158.7 2.7 multiply_reduce_fusion.1
  167.9 16.9 %feed.2 = (bf16[1024,1024]{1,0:T(8,128)(2,1)}, bf16[768,1024]{1,0:T(8,128)(2,1)S(1)}, bf16[1024,1536]{1,0:T(8,128)(2,1)}, bf16[512,1024]{1,0:T(8,128)(2,1)S(1)},...) custom-call(bf16[1024,1024]{1,0:T(8,128)(2,1)} %pad_maximum_fusion.1.refs_0_, ...), custom_call_target="tpu_custom_call" | custom-call | flops 250000000 | bytes 1000 | tf_op jit(solution)/shard_map/feed/pallas_call | solution.py:535
  191.4 16.9 %feed.3 = (bf16[1024,1024]{1,0:T(8,128)(2,1)}, bf16[768,1024]{1,0:T(8,128)(2,1)S(1)}, bf16[1024,1536]{1,0:T(8,128)(2,1)}, bf16[512,1024]{1,0:T(8,128)(2,1)S(1)},...) custom-call(bf16[1024,1024]{1,0:T(8,128)(2,1)} %pad_maximum_fusion.2.refs_0_, ...), custom_call_target="tpu_custom_call" | custom-call | flops 250000000 | bytes 1000 | tf_op jit(solution)/shard_map/feed/pallas_call | solution.py:535
  215.8 16.5 %feed_weights.1 = bf16[8,576,512]{2,1,0:T(8,128)(2,1)} custom-call(bf16[1024,1024]{1,0:T(8,128)(2,1)S(1)} %copy-done.9, bf16[1024,1024]{1,0:T(8,128)(2,1)} %get-tuple-element.118.refs_1_, bf16[1024,1536]{1,0:T(8,128)(2,1)} %get-tuple-element.119.refs_2_, bf16[1024,1536]{1,0:T(8,128)(2,1)} %get-tuple-element.120.refs_3_, ...), custom_call_target="tpu_custom_call" | custom-call | flops 250000000 | bytes 1000 | tf_op jit(solution)/shard_map/feed_weights/pallas_call | solution.py:560
  232.3 7.5 %collective-permute-done.14.across = bf16[512,1024]{1,0:T(8,128)(2,1)} collective-permute-done((bf16[512,1024]{1,0:T(8,128)(2,1)}, bf16[512,1024]{1,0:T(8,128)(2,1)}, u32[]{:S(2)}, u32[]{:S(2)}) %collective-permute-start.14) | collective-permute-done | bytes 1048608 | tf_op jit(solution)/shard_map/back_across/ppermute | solution.py:624
  239.9 5.0 %middle_back.1 = (f32[512,1024]{1,0:T(8,128)}, bf16[512,1024]{1,0:T(8,128)(2,1)S(1)}, f32[1,1024]{1,0:T(1,128)S(1)}) custom-call(bf16[512,1024]{1,0:T(8,128)(2,1)S(1)} %get-tuple-element.109.own, bf16[512,1024]{1,0:T(8,128)(2,1)} %collective-permute-done.10.beside, bf16[512,1024]{1,0:T(8,128)(2,1)} %collective-permute-done.14.across, ...), custom_call_target="tpu_custom_call" | custom-call | flops 31250000 | bytes 1000 | tf_op jit(solution)/shard_map/middle_back/pallas_call | solution.py:612
  250.1 16.9 %attend_back_own.1 = (bf16[1024,512]{1,0:T(8,128)(2,1)S(1)}, f32[2048,256]{1,0:T(8,128)}, f32[2048,256]{1,0:T(8,128)}, f32[2,1,128]{2,1,0:T(1,128)S(1)}) custom-call(s32[17]{0:T(128)S(1)} %pad_add_fusion.refs_0_.info, bf16[2048,512]{1,0:T(8,128)(2,1)} %get-tuple-element.101.refs_1_.q, bf16[2048,256]{1,0:T(8,128)(2,1)S(1)} %copy-done.7, ...), custom_call_target="tpu_custom_call" | custom-call | flops 390624992 | bytes 1000 | tf_op jit(solution)/shard_map/attend_back_own/pallas_call | solution.py:460
  277.8 29.4 %attend_back_other.1 = (bf16[2048,1024]{1,0:T(8,128)(2,1)}, f32[2,2,128]{2,1,0:T(2,128)S(1)}) custom-call(s32[17]{0:T(128)S(1)} %pad_add_fusion.refs_0_.info, bf16[2048,512]{1,0:T(8,128)(2,1)} %get-tuple-element.101.refs_1_.q, bf16[2048,256]{1,0:T(8,128)(2,1)S(1)} %copy-done.8, bf16[2048,256]{1,0:T(8,128)(2,1)S(1)} %copy-done.3, ...), custom_call_target="tpu_custom_call" | custom-call | flops 437500000 | bytes 1000 | tf_op jit(solution)/shard_map/attend_back_other/pallas_call | solution.py:491
  307.2 4.7 %unproject.2 = (bf16[512,1024]{1,0:T(8,128)(2,1)S(1)}, bf16[512,1024]{1,0:T(8,128)(2,1)S(1)}) custom-call(bf16[2048,1024]{1,0:T(8,128)(2,1)} %get-tuple-element.162.grad, bf16[1024,1024]{1,0:T(8,128)(2,1)S(1)} %bitcast.117), custom_call_target="tpu_custom_call" | custom-call | flops 62500000 | bytes 1000 | tf_op jit(solution)/shard_map/unproject/pallas_call | solution.py:578
  312.5 6.3 %fusion.36 = f32[1024,1024]{1,0:T(8,128)S(1)} fusion(bf16[1024,2048]{1,0:T(8,128)(2,1)} %get-tuple-element.139, bf16[2048,1024]{1,0:T(8,128)(2,1)S(1)} %copy-done.27), kind=kOutput, calls=%fused_computation.134 | convolution fusion | flops 4294967296 | bytes 12582912 | tf_op jit(solution)/shard_map/dot_general | solution.py:64
  321.8 2.8 fusion.34
  328.8 5.0 %unproject.3 = (bf16[512,1024]{1,0:T(8,128)(2,1)S(1)}, bf16[512,1024]{1,0:T(8,128)(2,1)S(1)}) custom-call(bf16[2048,1024]{1,0:T(8,128)(2,1)} %get-tuple-element.162.grad, bf16[1024,1024]{1,0:T(8,128)(2,1)S(1)} %bitcast.118), custom_call_target="tpu_custom_call" | custom-call | flops 62500000 | bytes 1000 | tf_op jit(solution)/shard_map/unproject/pallas_call | solution.py:578
  334.1 12.0 %collective-permute-done.20 = bf16[2,2,128,512]{3,2,0,1:T(8,128)(2,1)} collective-permute-done((bf16[2,2,128,512]{3,2,0,1:T(8,128)(2,1)}, bf16[2,2,128,512]{3,2,0,1:T(8,128)(2,1)}, u32[]{:S(2)}, u32[]{:S(2)}) %collective-permute-start.20) | collective-permute-done | bytes 524320 | tf_op jit(solution)/shard_map/part/ppermute | solution.py:624
  350.6 3.8 collective-permute-done.21
  364.2 14.8 %collective-permute-done.30 = bf16[4,2,2,16,1024]{4,3,0,1,2:T(8,128)(2,1)S(1)} collective-permute-done((bf16[4,2,2,16,1024]{4,3,0,1,2:T(8,128)(2,1)S(1)}, bf16[4,2,2,16,1024]{4,3,0,1,2:T(8,128)(2,1)S(1)}, u32[]{:S(2)}, u32[]{:S(2)}) %collective-permute-start.30) | collective-permute-done | bytes 524320 | tf_op jit(solution)/shard_map/part/ppermute | solution.py:624
  380.9 3.4 fusion.4
  384.3 2.9 collective-permute-done.31
  389.6 5.7 %collective-permute-done.32 = bf16[4,16,1024]{2,1,0:T(8,128)(2,1)S(1)} collective-permute-done((bf16[4,16,1024]{2,1,0:T(8,128)(2,1)S(1)}, bf16[4,16,1024]{2,1,0:T(8,128)(2,1)S(1)}, u32[]{:S(2)}, u32[]{:S(2)}) %collective-permute-start.32) | collective-permute-done | bytes 131104 | tf_op jit(solution)/shard_map/part/ppermute | solution.py:624
  401.8 2.8 collective-permute-start.25
  407.0 5.2 %multiply_subtract_fusion = (f32[128,2,768]{2,1,0:T(2,128)}, f32[128,2,768]{2,1,0:T(2,128)}, f32[128,2,768]{2,1,0:T(2,128)}) fusion(f32[128,2,768]{2,1,0:T(2,128)S(1)} %copy-done.41, f32[128,2,768]{2,1,0:T(2,128)S(1)} %copy.95, f32[128,2,768]{2,1,0:T(2,128)} %param.28, f32[128,2,768]{2,1,0:T(2,128)} %param.33), kind=kLoop, calls=%fused_computation.43 | loop fusion | flops 2949120 | bytes 5505024 | tf_op jit(solution)/shard_map/sub | solution.py:53
  419.2 3.9 multiply_subtract_fusion.1
  (288 shorter events, 96.0 us)
Async XLA Ops:
  7.2 70.3 %all-gather.5.cloned.1.call-start = ((), (), s32[]{:S(2)}) async-start(), calls=%async_computation.2 | async-start | bytes 3833856 | tf_op jit(solution)/shard_map/all_gather | solution.py:690
  11.1 147.6 %all-gather.7.cloned.1.call-start = ((), (), s32[]{:S(2)}) async-start(), calls=%async_computation.3 | async-start | bytes 5308416 | tf_op jit(solution)/shard_map/all_gather | solution.py:693
  12.9 385.3 %reduce-scatter.2.cloned.1.call-start = ((), (), s32[]{:S(2)}) async-start(), calls=%async_computation.1 | async-start | bytes 5308416 | tf_op jit(solution)/shard_map/reduce_scatter | solution.py:799
  13.0 27.1 %collective-permute-start.1 = (bf16[512,1024]{1,0:T(8,128)(2,1)S(1)}, bf16[512,1024]{1,0:T(8,128)(2,1)}, u32[]{:S(2)}, u32[]{:S(2)}) collective-permute-start(bf16[512,1024]{1,0:T(8,128)(2,1)S(1)} %copy-done.29), channel_id=1, source_target_pairs={{0,2},{1,3},{2,0},{3,1},{4,6},{5,7},{6,4},{7,5},{8,10},{9,11},{10,... | collective-permute-start | bytes 3145736 | tf_op jit(solution)/shard_map/tokens_across/ppermute | solution.py:624
  16.0 28.6 %collective-permute-start = (bf16[512,1024]{1,0:T(8,128)(2,1)S(1)}, bf16[512,1024]{1,0:T(8,128)(2,1)}, u32[]{:S(2)}, u32[]{:S(2)}) collective-permute-start(bf16[512,1024]{1,0:T(8,128)(2,1)S(1)} %copy-done.29), channel_id=1, source_target_pairs={{0,1},{1,0},{2,3},{3,2},{4,5},{5,4},{6,7},{7,6},{8,9},{9,8},{10,11... | collective-permute-start | bytes 3145736 | tf_op jit(solution)/shard_map/part/ppermute | solution.py:624
  16.0 95.7 %collective-permute-start.3 = (bf16[512,1024]{1,0:T(8,128)(2,1)}, bf16[512,1024]{1,0:T(8,128)(2,1)}, u32[]{:S(2)}, u32[]{:S(2)}) collective-permute-start(bf16[512,1024]{1,0:T(8,128)(2,1)} %grad.1), channel_id=1, source_target_pairs={{0,2},{1,3},{2,0},{3,1},{4,6},{5,7},{6,4},{7,5},{8,10},{9,11},{10,... | collective-permute-start | bytes 3145736 | tf_op jit(solution)/shard_map/grad_across/ppermute | solution.py:624
  115.9 25.4 %collective-permute-start.5 = (bf16[512,1024]{1,0:T(8,128)(2,1)S(1)}, bf16[512,1024]{1,0:T(8,128)(2,1)}, u32[]{:S(2)}, u32[]{:S(2)}) collective-permute-start(bf16[512,1024]{1,0:T(8,128)(2,1)S(1)} %add_convert_fusion.5), channel_id=1, source_target_pairs={{0,2},{1,3},{2,0},{3,1},{4,6},{5,7},{6,4},{7,5},{8,10},{9,11},{10,... | collective-permute-start | bytes 3145736 | tf_op jit(solution)/shard_map/attn_across/ppermute | solution.py:624
  142.1 22.4 %collective-permute-start.9 = (bf16[512,1024]{1,0:T(8,128)(2,1)}, bf16[512,1024]{1,0:T(8,128)(2,1)}, u32[]{:S(2)}, u32[]{:S(2)}) collective-permute-start(bf16[512,1024]{1,0:T(8,128)(2,1)} %grad.1), channel_id=1, source_target_pairs={{0,1},{1,0},{2,3},{3,2},{4,5},{5,4},{6,7},{7,6},{8,9},{9,8},{10,11... | collective-permute-start | bytes 3145736 | tf_op jit(solution)/shard_map/part/ppermute | solution.py:624
  161.6 4.5 %collective-permute-start.8 = (bf16[512,1024]{1,0:T(8,128)(2,1)S(1)}, bf16[512,1024]{1,0:T(8,128)(2,1)S(1)}, u32[]{:S(2)}, u32[]{:S(2)}) collective-permute-start(bf16[512,1024]{1,0:T(8,128)(2,1)S(1)} %multiply_convert_fusion), channel_id=1, source_target_pairs={{0,1},{1,0},{2,3},{3,2},{4,5},{5,4},{6,7},{7,6},{8,9},{9,8},{10,11... | collective-permute-start | bytes 3145736 | tf_op jit(solution)/shard_map/part/ppermute | solution.py:624
  161.7 25.6 %collective-permute-start.7 = (bf16[512,1024]{1,0:T(8,128)(2,1)S(1)}, bf16[512,1024]{1,0:T(8,128)(2,1)S(1)}, u32[]{:S(2)}, u32[]{:S(2)}) collective-permute-start(bf16[512,1024]{1,0:T(8,128)(2,1)S(1)} %multiply_convert_fusion), channel_id=1, source_target_pairs={{0,2},{1,3},{2,0},{3,1},{4,6},{5,7},{6,4},{7,5},{8,10},{9,11},{10,... | collective-permute-start | bytes 3145736 | tf_op jit(solution)/shard_map/normed_across/ppermute | solution.py:624
  165.9 22.7 %collective-permute-start.12 = (bf16[512,1024]{1,0:T(8,128)(2,1)}, bf16[512,1024]{1,0:T(8,128)(2,1)S(1)}, u32[]{:S(2)}, u32[]{:S(2)}) collective-permute-start(bf16[512,1024]{1,0:T(8,128)(2,1)} %collective-permute-done.3), channel_id=1, source_target_pairs={{0,1},{1,0},{2,3},{3,2},{4,5},{5,4},{6,7},{7,6},{8,9},{9,8},{10,11... | collective-permute-start | bytes 3145736 | tf_op jit(solution)/shard_map/part/ppermute | solution.py:624
  214.3 25.5 %collective-permute-start.14 = (bf16[512,1024]{1,0:T(8,128)(2,1)}, bf16[512,1024]{1,0:T(8,128)(2,1)}, u32[]{:S(2)}, u32[]{:S(2)}) collective-permute-start(bf16[512,1024]{1,0:T(8,128)(2,1)} %add_convert_fusion.4), channel_id=1, source_target_pairs={{0,2},{1,3},{2,0},{3,1},{4,6},{5,7},{6,4},{7,5},{8,10},{9,11},{10,... | collective-permute-start | bytes 3145736 | tf_op jit(solution)/shard_map/back_across/ppermute | solution.py:624
  215.8 24.0 %collective-permute-start.10 = (bf16[512,1024]{1,0:T(8,128)(2,1)}, bf16[512,1024]{1,0:T(8,128)(2,1)}, u32[]{:S(2)}, u32[]{:S(2)}) collective-permute-start(bf16[512,1024]{1,0:T(8,128)(2,1)} %get-tuple-element.110), channel_id=1, source_target_pairs={{0,1},{1,0},{2,3},{3,2},{4,5},{5,4},{6,7},{7,6},{8,9},{9,8},{10,11... | collective-permute-start | bytes 3145736 | tf_op jit(solution)/shard_map/part/ppermute | solution.py:624
  244.9 25.7 %collective-permute-start.15 = (bf16[512,1024]{1,0:T(8,128)(2,1)S(1)}, bf16[512,1024]{1,0:T(8,128)(2,1)}, u32[]{:S(2)}, u32[]{:S(2)}) collective-permute-start(bf16[512,1024]{1,0:T(8,128)(2,1)S(1)} %get-tuple-element.124), channel_id=1, source_target_pairs={{0,2},{1,3},{2,0},{3,1},{4,6},{5,7},{6,4},{7,5},{8,10},{9,11},{10,... | collective-permute-start | bytes 3145736 | tf_op jit(solution)/shard_map/grad_middle_across/ppermute | solution.py:624
  311.9 6.9 %collective-permute-start.18 = (bf16[512,1024]{1,0:T(8,128)(2,1)S(1)}, bf16[512,1024]{1,0:T(8,128)(2,1)S(1)}, u32[]{:S(2)}, u32[]{:S(2)}) collective-permute-start(bf16[512,1024]{1,0:T(8,128)(2,1)S(1)} %get-tuple-element.137), channel_id=1, source_target_pairs={{0,1},{1,0},{2,3},{3,2},{4,5},{5,4},{6,7},{7,6},{8,9},{9,8},{10,11... | collective-permute-start | bytes 3145736 | tf_op jit(solution)/shard_map/part/ppermute | solution.py:624
  325.6 20.5 %collective-permute-start.20 = (bf16[2,2,128,512]{3,2,0,1:T(8,128)(2,1)}, bf16[2,2,128,512]{3,2,0,1:T(8,128)(2,1)}, u32[]{:S(2)}, u32[]{:S(2)}) collective-permute-start(bf16[2,2,128,512]{3,2,0,1:T(8,128)(2,1)} %fusion.10), channel_id=1, source_target_pairs={{0,4},{4,0},{8,12},{12,8},{16,20},{20,16},{24,28},{28,24},{1,5},{5... | collective-permute-start | bytes 1572872 | tf_op jit(solution)/shard_map/part/ppermute | solution.py:624
  325.6 23.2 %collective-permute-start.22 = (bf16[512,1024]{1,0:T(8,128)(2,1)S(1)}, bf16[512,1024]{1,0:T(8,128)(2,1)}, u32[]{:S(2)}, u32[]{:S(2)}) collective-permute-start(bf16[512,1024]{1,0:T(8,128)(2,1)S(1)} %copy-done.24), channel_id=1, source_target_pairs={{0,1},{1,0},{2,3},{3,2},{4,5},{5,4},{6,7},{7,6},{8,9},{9,8},{10,11... | collective-permute-start | bytes 3145736 | tf_op jit(solution)/shard_map/part/ppermute | solution.py:624
  328.4 18.9 %collective-permute-start.19 = (bf16[2,2,144,512]{3,2,0,1:T(8,128)(2,1)}, bf16[2,2,144,512]{3,2,0,1:T(8,128)(2,1)}, u32[]{:S(2)}, u32[]{:S(2)}) collective-permute-start(bf16[2,2,144,512]{3,2,0,1:T(8,128)(2,1)} %fusion.8), channel_id=1, source_target_pairs={{0,8},{4,12},{8,0},{12,4},{16,24},{20,28},{24,16},{28,20},{1,9},{5... | collective-permute-start | bytes 1769480 | tf_op jit(solution)/shard_map/part/ppermute | solution.py:624
  328.8 25.6 %collective-permute-start.21 = (bf16[512,1024]{1,0:T(8,128)(2,1)}, bf16[512,1024]{1,0:T(8,128)(2,1)}, u32[]{:S(2)}, u32[]{:S(2)}) collective-permute-start(bf16[512,1024]{1,0:T(8,128)(2,1)} %add_convert_fusion.3), channel_id=1, source_target_pairs={{0,2},{1,3},{2,0},{3,1},{4,6},{5,7},{6,4},{7,5},{8,10},{9,11},{10,... | collective-permute-start | bytes 3145736 | tf_op jit(solution)/shard_map/back_across/ppermute | solution.py:624
  333.8 28.1 %collective-permute-start.29 = (bf16[512,1024]{1,0:T(8,128)(2,1)S(1)}, bf16[512,1024]{1,0:T(8,128)(2,1)S(1)}, u32[]{:S(2)}, u32[]{:S(2)}) collective-permute-start(bf16[512,1024]{1,0:T(8,128)(2,1)S(1)} %get-tuple-element.164), channel_id=1, source_target_pairs={{0,1},{1,0},{2,3},{3,2},{4,5},{5,4},{6,7},{7,6},{8,9},{9,8},{10,11... | collective-permute-start | bytes 3145736 | tf_op jit(solution)/shard_map/part/ppermute | solution.py:624
  354.4 29.8 %collective-permute-start.24 = (bf16[2,128,512]{2,1,0:T(8,128)(2,1)S(1)}, bf16[2,128,512]{2,1,0:T(8,128)(2,1)S(1)}, u32[]{:S(2)}, u32[]{:S(2)}) collective-permute-start(bf16[2,128,512]{2,1,0:T(8,128)(2,1)S(1)} %fusion.20), channel_id=1, source_target_pairs={{0,8},{4,12},{8,0},{12,4},{16,24},{20,28},{24,16},{28,20},{1,9},{5... | collective-permute-start | bytes 786440 | tf_op jit(solution)/shard_map/part/ppermute | solution.py:624
  356.0 33.6 %collective-permute-start.23 = (bf16[2,144,512]{2,1,0:T(8,128)(2,1)S(1)}, bf16[2,144,512]{2,1,0:T(8,128)(2,1)S(1)}, u32[]{:S(2)}, u32[]{:S(2)}) collective-permute-start(bf16[2,144,512]{2,1,0:T(8,128)(2,1)S(1)} %fusion.18), channel_id=1, source_target_pairs={{0,4},{4,0},{8,12},{12,8},{16,20},{20,16},{24,28},{28,24},{1,5},{5... | collective-permute-start | bytes 884744 | tf_op jit(solution)/shard_map/part/ppermute | solution.py:624
  360.8 18.3 %collective-permute-start.30 = (bf16[4,2,2,16,1024]{4,3,0,1,2:T(8,128)(2,1)S(1)}, bf16[4,2,2,16,1024]{4,3,0,1,2:T(8,128)(2,1)S(1)}, u32[]{:S(2)}, u32[]{:S(2)}) collective-permute-start(bf16[4,2,2,16,1024]{4,3,0,1,2:T(8,128)(2,1)S(1)} %bitcast.149), channel_id=1, source_target_pairs={{0,4},{4,0},{8,12},{12,8},{16,20},{20,16},{24,28},{28,24},{1,5},{5... | collective-permute-start | bytes 1572872 | tf_op jit(solution)/shard_map/part/ppermute | solution.py:624
  361.8 34.6 %collective-permute-start.27 = (bf16[512,1024]{1,0:T(8,128)(2,1)S(1)}, bf16[512,1024]{1,0:T(8,128)(2,1)S(1)}, u32[]{:S(2)}, u32[]{:S(2)}) collective-permute-start(bf16[512,1024]{1,0:T(8,128)(2,1)S(1)} %copy-done.18), channel_id=1, source_target_pairs={{0,1},{1,0},{2,3},{3,2},{4,5},{5,4},{6,7},{7,6},{8,9},{9,8},{10,11... | collective-permute-start | bytes 3145736 | tf_op jit(solution)/shard_map/part/ppermute | solution.py:624
  361.8 34.6 %collective-permute-start.28 = (bf16[512,1024]{1,0:T(8,128)(2,1)S(1)}, bf16[512,1024]{1,0:T(8,128)(2,1)S(1)}, u32[]{:S(2)}, u32[]{:S(2)}) collective-permute-start(bf16[512,1024]{1,0:T(8,128)(2,1)S(1)} %add_convert_fusion.2), channel_id=1, source_target_pairs={{0,2},{1,3},{2,0},{3,1},{4,6},{5,7},{6,4},{7,5},{8,10},{9,11},{10,... | collective-permute-start | bytes 3145736 | tf_op jit(solution)/shard_map/mlp_across/ppermute | solution.py:624
  379.3 8.0 %collective-permute-start.31 = (bf16[4,2,16,1024]{3,2,0,1:T(8,128)(2,1)S(1)}, bf16[4,2,16,1024]{3,2,0,1:T(8,128)(2,1)S(1)}, u32[]{:S(2)}, u32[]{:S(2)}) collective-permute-start(bf16[4,2,16,1024]{3,2,0,1:T(8,128)(2,1)S(1)} %fusion.21), channel_id=1, source_target_pairs={{0,8},{4,12},{8,0},{12,4},{16,24},{20,28},{24,16},{28,20},{1,9},{5... | collective-permute-start | bytes 786440 | tf_op jit(solution)/shard_map/part/ppermute | solution.py:624
  387.4 8.0 %collective-permute-start.32 = (bf16[4,16,1024]{2,1,0:T(8,128)(2,1)S(1)}, bf16[4,16,1024]{2,1,0:T(8,128)(2,1)S(1)}, u32[]{:S(2)}, u32[]{:S(2)}) collective-permute-start(bf16[4,16,1024]{2,1,0:T(8,128)(2,1)S(1)} %fusion.24), channel_id=1, source_target_pairs={{0,16},{4,20},{8,24},{12,28},{16,0},{20,4},{24,8},{28,12},{1,17},{... | collective-permute-start | bytes 393224 | tf_op jit(solution)/shard_map/part/ppermute | solution.py:624
  400.9 12.5 %collective-permute-start.26 = (bf16[128,512]{1,0:T(8,128)(2,1)}, bf16[128,512]{1,0:T(8,128)(2,1)}, u32[]{:S(2)}, u32[]{:S(2)}) collective-permute-start(bf16[128,512]{1,0:T(8,128)(2,1)} %fusion.23), channel_id=1, source_target_pairs={{0,16},{4,20},{8,24},{12,28},{16,0},{20,4},{24,8},{28,12},{1,17},{... | collective-permute-start | bytes 393224 | tf_op jit(solution)/shard_map/part/ppermute | solution.py:624
  401.8 14.0 %collective-permute-start.25 = (bf16[144,512]{1,0:T(8,128)(2,1)}, bf16[144,512]{1,0:T(8,128)(2,1)}, u32[]{:S(2)}, u32[]{:S(2)}) collective-permute-start(bf16[144,512]{1,0:T(8,128)(2,1)} %fusion.22), channel_id=1, source_target_pairs={{0,16},{4,20},{8,24},{12,28},{16,0},{20,4},{24,8},{28,12},{1,17},{... | collective-permute-start | bytes 442376 | tf_op jit(solution)/shard_map/part/ppermute | solution.py:624
  416.7 6.3 %collective-permute-start.35 = (f32[288]{0:T(512)S(1)}, f32[288]{0:T(512)S(1)}, u32[]{:S(2)}, u32[]{:S(2)}) collective-permute-start(f32[288]{0:T(512)S(1)} %slice_reduce_fusion), channel_id=1, source_target_pairs={{0,3},{1,2},{2,1},{3,0},{4,7},{5,6},{6,5},{7,4},{8,11},{9,10},{10,... | collective-permute-start | bytes 3464 | tf_op jit(solution)/shard_map/part/ppermute | solution.py:624
  416.8 6.3 %collective-permute-start.34 = (f32[288]{0:T(512)S(1)}, f32[288]{0:T(512)S(1)}, u32[]{:S(2)}, u32[]{:S(2)}) collective-permute-start(f32[288]{0:T(512)S(1)} %slice_reduce_fusion), channel_id=1, source_target_pairs={{0,2},{1,3},{2,0},{3,1},{4,6},{5,7},{6,4},{7,5},{8,10},{9,11},{10,... | collective-permute-start | bytes 3464 | tf_op jit(solution)/shard_map/part/ppermute | solution.py:624
  418.3 4.7 %collective-permute-start.33 = (f32[288]{0:T(512)S(1)}, f32[288]{0:T(512)S(1)}, u32[]{:S(2)}, u32[]{:S(2)}) collective-permute-start(f32[288]{0:T(512)S(1)} %slice_reduce_fusion), channel_id=1, source_target_pairs={{0,1},{1,0},{2,3},{3,2},{4,5},{5,4},{6,7},{7,6},{8,9},{9,8},{10,11... | collective-permute-start | bytes 3464 | tf_op jit(solution)/shard_map/part/ppermute | solution.py:624
  (67 other events, 626.7 us)
Sparse Core Ops, SparseCore 0:
  11.2 66.2 all-gather.4
  80.2 78.4 all-gather.6
  272.6 108.2 reduce-scatter.1

commit v9 on v8

--- a/solution.py
+++ b/solution.py
@@ -636,7 +636,7 @@
     mine = (lax.axis_index("dp") // bit) % 2
     send = lax.dynamic_index_in_dim(parts, 1 - mine, axis, keepdims=False).astype(BF16)
     keep = lax.dynamic_index_in_dim(parts, mine, axis, keepdims=False)
-    return keep + flipped(send, "dp", bit).astype(F32)
+    return keep.astype(F32) + flipped(send, "dp", bit).astype(F32)
 
 
 def per_device(
@@ -781,7 +781,7 @@
         full_two.shape if cubic else None, (h_own, h_other), (feed_grad_own, feed_grad_other),
         (hidden_own, hidden_other), (grad_own, grad_other),
     )
-    back_across, _ = together(back_across, feed_grads[0])
+    back_across, *feed_grads = together(back_across, *feed_grads)
     if cubic:
         feed_pack = feed_grads[0]
     else:
@@ -816,32 +816,37 @@
         [grad_middle_across, flipped(grad_middle_across, "tensor", 1)], axis=0
     )
     grad_heads_other = nt(grad_middle_other, out_matrix).astype(BF16)
+    grad_out_w = (
+        nn(heads_own_turned, grad_middle_own) + nn(heads_other_turned, grad_middle_other)
+    ).astype(BF16)
+    grad_out_w, grad_heads_other = together(grad_out_w, grad_heads_other)
     grad_qkv, gain_other = attend_back_other(
         info, q, k, v, k_turned, start, logs_other, heads_other, grad_heads_other,
         raw_q, cos, sin, gain_query, raw_k, gain_key, grad_q, grad_k, grad_v,
     )
     back_2, back_3 = unproject(1, grad_qkv, qkv_matrix)
     back_2, back_3, grad_qkv = together(back_2, back_3, grad_qkv)
-    grad_qkv_w = nn(normed_turned, grad_qkv)
+    grad_qkv_w = nn(normed_turned, grad_qkv).astype(BF16)
     near = near_sum(back_2, back_3).astype(BF16)
-    near, grad_qkv, grad_qkv_w, sum_2, sum_3 = together(near, grad_qkv, grad_qkv_w, sum_2, sum_3)
+    near, grad_qkv, grad_qkv_w, grad_out_w, sum_2, sum_3 = together(
+        near, grad_qkv, grad_qkv_w, grad_out_w, sum_2, sum_3
+    )
     near_mlp = near_sum(sum_2, sum_3).astype(BF16)
     back_across = flipped(near, "tensor", 2, "back_across")
-    grad_gain_attn = jnp.sum(qkv_matrix.astype(F32) * grad_qkv_w, axis=1) / gain_attn[0]
+    grad_gain_attn = jnp.sum(
+        qkv_matrix.astype(F32) * grad_qkv_w.astype(F32), axis=1
+    ) / gain_attn[0]
     grad_gain_heads = jnp.sum(gain_other, axis=0) + jnp.pad(
         jnp.sum(gain_own, axis=0), ((0, 1), (0, 0))
     )
     gain_sums = jnp.concatenate([grad_gain_attn, grad_gain_mlp, grad_gain_heads.reshape(-1)])
     back_0, back_1 = unproject(0, grad_qkv, qkv_matrix)
-
-    def out_gradient(own_turned, other_turned):
-        return (nn(own_turned, grad_middle_own) + nn(other_turned, grad_middle_other)).astype(BF16)
 
     if cubic:
         cube = (2, 2, 2)
         columns = grad_qkv_w.shape[1] // 2
         gain_rows = jnp.pad(
-            gain_sums.reshape(cube + (1, gain_count)),
+            gain_sums.astype(BF16).reshape(cube + (1, gain_count)),
             ((0, 0),) * 3 + ((0, 15), (0, columns - gain_count)),
         )
         sum_one = jnp.concatenate(
@@ -849,20 +854,19 @@
         )
         sum_two = grad_qkv_w[:, columns:].reshape(cube + (depth, -1))
         sum_one, sum_two = halved(sum_one, 1, 2), halved(sum_two, 2, 1)
-        sum_one, sum_two, back_across, sum_0, sum_1, near_mlp, *heads_turned = together(
-            sum_one, sum_two, back_across, sum_0, sum_1, near_mlp,
-            heads_own_turned, heads_other_turned,
+        sum_out = grad_out_w.reshape((out_heads,) + cube + (out_depth, MODEL_WIDTH))
+        sum_out = halved(sum_out, 3, 1)
+        sum_one, sum_two, back_across, sum_0, sum_1, near_mlp = together(
+            sum_one, sum_two, back_across, sum_0, sum_1, near_mlp
         )
         mlp_across = flipped(near_mlp, "tensor", 2, "mlp_across")
         sum_one, sum_two = halved(sum_one, 1, 1), halved(sum_two, 1, 2)
-        sum_one, sum_two, feed_sum = together(sum_one, sum_two, feed_sum)
-        grad_out_w = out_gradient(*heads_turned)
-        sum_out = grad_out_w.reshape((out_heads,) + cube + (out_depth, MODEL_WIDTH))
-        sum_out = halved(halved(sum_out, 3, 1), 2, 2)
+        sum_out = halved(sum_out, 2, 2)
+        sum_one, sum_two, sum_out, feed_sum = together(sum_one, sum_two, sum_out, feed_sum)
         sum_one, sum_two = halved(sum_one, 0, 4), halved(sum_two, 0, 4)
         sum_out = halved(sum_out, 1, 4)
         block_out = (middle + near_sum(sum_0, sum_1) + mlp_across.astype(F32)).astype(BF16)
-        sum_one, sum_two, block_out = together(sum_one, sum_two, block_out)
+        sum_one, sum_two, sum_out, block_out = together(sum_one, sum_two, sum_out, block_out)
         sum_qkv = jnp.concatenate([sum_one[:depth], sum_two], axis=1)
         sum_qkv = sum_qkv.reshape(projection_weight.shape)
         sum_gains = sum_one[depth, :gain_count]
@@ -875,7 +879,7 @@
             .reshape(projection_weight.shape)
         )
         sum_out = lax.psum_scatter(
-            out_gradient(heads_own_turned, heads_other_turned).reshape(out_heads, -1, MODEL_WIDTH), "dp",
+            grad_out_w.reshape(out_heads, -1, MODEL_WIDTH), "dp",
             scatter_dimension=1, tiled=True,
         ).astype(F32)
         sum_gains = lax.psum_scatter(gain_sums, "dp", scatter_dimension=0, tiled=True)

time: 437 us -> 454 us (1.039)
  waiting for transfers between devices: 140 us -> 168 us
  other arithmetic: 51.8 us -> 45.8 us
    ppermute x36, waiting for transfers between devices: 101 us -> 128 us  [flipped(): lax.ppermute(value, axis, [(i, i ^ bit) for i in range(lax.axis_size(axis...]
    unnamed x128 -> x124, local copies, waits for them, and re-layouts: 11.9 us -> 9.97 us
  transfers between devices with their start and end apart: 39 -> 39, of which waited for: 18 -> 20; matrix products, arithmetic and copies ran while one was open for 18% -> 16% of each run, Pallas kernels for 31% -> 30%
where the time goes in v9:
time: 454 us; the launch traced here: 448 us
  waiting for transfers between devices  168 us (37%)
  Pallas kernels  156 us (34%)
  other arithmetic  45.8 us (10%)
  local copies, waits for them, and re-layouts  24.9 us (5%)
  starting transfers between devices  19.1 us (4%)
  matrix products  18.3 us (4%)
  between operations  15.5 us (3%)
    ppermute x36, waiting for transfers between devices, flipped(): lax.ppermute(value, axis, [(i, i ^ bit) for i in range(lax.axis_size(axis...  128 us
    pallas_call x2, Pallas kernels, feed(): pl.pallas_call(lambda *refs: feed_kernel(packs, *refs), grid=(rows // BLO...  33.9 us
    pallas_call x2, Pallas kernels, attend(): pl.pallas_call(lambda *refs: attend_kernel(half * n // BLOCK, *refs), gri...  30.6 us
    pallas_call x1, Pallas kernels, attend_back_other(): pl.pallas_call(back_other_kernel, grid_spec=pltpu.PrefetchScalarGridSpec(...  29.1 us
    all_gather x1, waiting for transfers between devices, per_device(): full_one = lax.all_gather(pack_one, 'dp', axis=0, tiled=False)  28.7 us
    ppermute x36, starting transfers between devices, flipped(): lax.ppermute(value, axis, [(i, i ^ bit) for i in range(lax.axis_size(axis...  19 us
    pallas_call x1, Pallas kernels, attend_back_own(): pl.pallas_call(back_own_kernel, grid_spec=pltpu.PrefetchScalarGridSpec(nu...  17.9 us
    pallas_call x1, Pallas kernels, feed_weights(): pl.pallas_call(lambda *refs: feed_weights_kernel(packs, pieces, *refs), g...  16.5 us
  transfers between devices with their start and end apart: 39, of which 20 were waited for; matrix products, arithmetic and copies ran while one was open for 16% of the time, Pallas kernels for 30%

profile of v9, /device:TPU:0, one launch (start us, length us, event | category | flops | bytes accessed | tf_op | source)
XLA Modules:
  0.0 447.7 jit_solution(8447917333828111039)
XLA Ops:
  13.0 3.0 collective-permute-start.1
  16.8 23.4 %collective-permute-done.1 = bf16[512,1024]{1,0:T(8,128)(2,1)} collective-permute-done((bf16[512,1024]{1,0:T(8,128)(2,1)S(1)}, bf16[512,1024]{1,0:T(8,128)(2,1)}, u32[]{:S(2)}, u32[]{:S(2)}) %collective-permute-start.1) | collective-permute-done | bytes 1048608 | tf_op jit(solution)/shard_map/tokens_across/ppermute | solution.py:624
  40.1 3.7 fusion.17
  44.6 4.2 pad_maximum_fusion.x
  48.8 28.7 %all-gather.5.cloned.1.call-done = bf16[1664,1024]{1,0:T(8,128)(2,1)} async-done(((bf16[208,1024]{1,0:T(8,128)(2,1)}), bf16[1664,1024]{1,0:T(8,128)(2,1)}) %all-gather.5.cloned.1.call-update) | async-done | bytes 3407888 | tf_op jit(solution)/shard_map/all_gather | solution.py:690
  79.9 13.7 %project.1 = (bf16[1024,2048]{1,0:T(8,128)(2,1)}, f32[2048,512]{1,0:T(8,128)}, f32[2048,256]{1,0:T(8,128)}, bf16[2048,512]{1,0:T(8,128)(2,1)}, bf16[2048,256]{1,...) custom-call(bf16[2048,1024]{1,0:T(8,128)(2,1)} %pad_maximum_fusion.x, ...), custom_call_target="tpu_custom_call" | custom-call | flops 156250000 | bytes 1000 | tf_op jit(solution)/shard_map/project/pallas_call | solution.py:398
  93.6 18.1 %attend.2 = (bf16[1024,512]{1,0:T(8,128)(2,1)S(1)}, bf16[512,1024]{1,0:T(8,128)(2,1)S(1)}, f32[2,2,1024]{2,1,0:T(2,128)S(1)}) custom-call(s32[17]{0:T(128)S(1)} %pad_add_fusion.refs_0_.info, bf16[2048,512]{1,0:T(8,128)(2,1)} %get-tuple-element.105.refs_1_.q, bf16[256,2048]{1,0:T(8,128)(2,1)S(1)} %get-tuple-element.101.refs_2_.k_turned, ...), custom_call_target="tpu_custom_call" | custom-call | flops 281249984 | bytes 1000 | tf_op jit(solution)/shard_map/attend/pallas_call | solution.py:440
  112.6 2.6 collective-permute-done.4
  116.1 12.5 %attend.3 = (bf16[1024,512]{1,0:T(8,128)(2,1)S(1)}, bf16[512,1024]{1,0:T(8,128)(2,1)S(1)}, f32[2,2,1024]{2,1,0:T(2,128)S(1)}) custom-call(s32[17]{0:T(128)S(1)} %pad_add_fusion.refs_0_.info, bf16[2048,512]{1,0:T(8,128)(2,1)} %get-tuple-element.105.refs_1_.q, bf16[256,2048]{1,0:T(8,128)(2,1)S(1)} %get-tuple-element.101.refs_2_.k_turned, ...), custom_call_target="tpu_custom_call" | custom-call | flops 281249984 | bytes 1000 | tf_op jit(solution)/shard_map/attend/pallas_call | solution.py:440
  128.6 12.8 %collective-permute-done.5 = bf16[512,1024]{1,0:T(8,128)(2,1)} collective-permute-done((bf16[512,1024]{1,0:T(8,128)(2,1)S(1)}, bf16[512,1024]{1,0:T(8,128)(2,1)}, u32[]{:S(2)}, u32[]{:S(2)}) %collective-permute-start.5) | collective-permute-done | bytes 1048608 | tf_op jit(solution)/shard_map/attn_across/ppermute | solution.py:624
  142.7 2.9 collective-permute-done.6
  147.7 11.1 %all-gather.7.cloned.1.call-done = bf16[4608,512]{1,0:T(8,128)(2,1)} async-done(((bf16[576,512]{1,0:T(8,128)(2,1)}), bf16[4608,512]{1,0:T(8,128)(2,1)}) %all-gather.7.cloned.1.call-update) | async-done | bytes 4718608 | tf_op jit(solution)/shard_map/all_gather | solution.py:693
  158.7 2.7 multiply_reduce_fusion.1
  167.8 17.0 %feed.2 = (bf16[1024,1024]{1,0:T(8,128)(2,1)}, bf16[768,1024]{1,0:T(8,128)(2,1)S(1)}, bf16[1024,1536]{1,0:T(8,128)(2,1)}, bf16[512,1024]{1,0:T(8,128)(2,1)S(1)},...) custom-call(bf16[1024,1024]{1,0:T(8,128)(2,1)} %pad_maximum_fusion.1.refs_0_, ...), custom_call_target="tpu_custom_call" | custom-call | flops 250000000 | bytes 1000 | tf_op jit(solution)/shard_map/feed/pallas_call | solution.py:535
  184.8 2.5 collective-permute-done.7
  191.4 16.9 %feed.3 = (bf16[1024,1024]{1,0:T(8,128)(2,1)}, bf16[768,1024]{1,0:T(8,128)(2,1)S(1)}, bf16[1024,1536]{1,0:T(8,128)(2,1)}, bf16[512,1024]{1,0:T(8,128)(2,1)S(1)},...) custom-call(bf16[1024,1024]{1,0:T(8,128)(2,1)} %pad_maximum_fusion.2.refs_0_, ...), custom_call_target="tpu_custom_call" | custom-call | flops 250000000 | bytes 1000 | tf_op jit(solution)/shard_map/feed/pallas_call | solution.py:535
  210.5 2.5 collective-permute-done.13
  215.8 16.5 %feed_weights.1 = bf16[8,576,512]{2,1,0:T(8,128)(2,1)} custom-call(bf16[1024,1024]{1,0:T(8,128)(2,1)S(1)} %copy-done.9, bf16[1024,1024]{1,0:T(8,128)(2,1)} %get-tuple-element.123.refs_1_, bf16[1024,1536]{1,0:T(8,128)(2,1)} %get-tuple-element.124.refs_2_, bf16[1024,1536]{1,0:T(8,128)(2,1)} %get-tuple-element.125.refs_3_, ...), custom_call_target="tpu_custom_call" | custom-call | flops 250000000 | bytes 1000 | tf_op jit(solution)/shard_map/feed_weights/pallas_call | solution.py:560
  232.4 7.5 %collective-permute-done.14.across = bf16[512,1024]{1,0:T(8,128)(2,1)} collective-permute-done((bf16[512,1024]{1,0:T(8,128)(2,1)}, bf16[512,1024]{1,0:T(8,128)(2,1)}, u32[]{:S(2)}, u32[]{:S(2)}) %collective-permute-start.14) | collective-permute-done | bytes 1048608 | tf_op jit(solution)/shard_map/back_across/ppermute | solution.py:624
  239.9 5.0 %middle_back.1 = (f32[512,1024]{1,0:T(8,128)}, bf16[512,1024]{1,0:T(8,128)(2,1)S(1)}, f32[1,1024]{1,0:T(1,128)S(1)}) custom-call(bf16[512,1024]{1,0:T(8,128)(2,1)S(1)} %get-tuple-element.114.own, bf16[512,1024]{1,0:T(8,128)(2,1)} %collective-permute-done.10.beside, bf16[512,1024]{1,0:T(8,128)(2,1)} %collective-permute-done.14.across, ...), custom_call_target="tpu_custom_call" | custom-call | flops 31250000 | bytes 1000 | tf_op jit(solution)/shard_map/middle_back/pallas_call | solution.py:612
  250.1 17.9 %attend_back_own.1 = (bf16[1024,512]{1,0:T(8,128)(2,1)S(1)}, f32[2048,256]{1,0:T(8,128)}, f32[2048,256]{1,0:T(8,128)}, f32[2,1,128]{2,1,0:T(1,128)S(1)}) custom-call(s32[17]{0:T(128)S(1)} %pad_add_fusion.refs_0_.info, bf16[2048,512]{1,0:T(8,128)(2,1)} %get-tuple-element.105.refs_1_.q, bf16[2048,256]{1,0:T(8,128)(2,1)S(1)} %copy-done.7, ...), custom_call_target="tpu_custom_call" | custom-call | flops 390624992 | bytes 1000 | tf_op jit(solution)/shard_map/attend_back_own/pallas_call | solution.py:460
  280.8 29.1 %attend_back_other.1 = (bf16[2048,1024]{1,0:T(8,128)(2,1)}, f32[2,2,128]{2,1,0:T(2,128)S(1)}) custom-call(s32[17]{0:T(128)S(1)} %pad_add_fusion.refs_0_.info, bf16[2048,512]{1,0:T(8,128)(2,1)} %get-tuple-element.105.refs_1_.q, bf16[2048,256]{1,0:T(8,128)(2,1)S(1)} %copy-done.8, bf16[2048,256]{1,0:T(8,128)(2,1)S(1)} %copy-done.3, ...), custom_call_target="tpu_custom_call" | custom-call | flops 437500000 | bytes 1000 | tf_op jit(solution)/shard_map/attend_back_other/pallas_call | solution.py:491
  309.9 4.7 %unproject.2 = (bf16[512,1024]{1,0:T(8,128)(2,1)S(1)}, bf16[512,1024]{1,0:T(8,128)(2,1)S(1)}) custom-call(bf16[2048,1024]{1,0:T(8,128)(2,1)} %get-tuple-element.171.grad, bf16[1024,1024]{1,0:T(8,128)(2,1)S(1)} %bitcast.115), custom_call_target="tpu_custom_call" | custom-call | flops 62500000 | bytes 1000 | tf_op jit(solution)/shard_map/unproject/pallas_call | solution.py:578
  315.2 6.9 %convolution_convert_fusion = bf16[1024,1024]{1,0:T(8,128)(2,1)S(1)} fusion(bf16[1024,2048]{1,0:T(8,128)(2,1)} %get-tuple-element.146, bf16[2048,1024]{1,0:T(8,128)(2,1)S(1)} %copy-done.27), kind=kOutput, calls=%fused_computation.26 | convolution fusion | flops 4296015872 | bytes 10485760 | tf_op jit(solution)/shard_map/dot_general | solution.py:64
  328.0 4.8 %unproject.3 = (bf16[512,1024]{1,0:T(8,128)(2,1)S(1)}, bf16[512,1024]{1,0:T(8,128)(2,1)S(1)}) custom-call(bf16[2048,1024]{1,0:T(8,128)(2,1)} %get-tuple-element.171.grad, bf16[1024,1024]{1,0:T(8,128)(2,1)S(1)} %bitcast.116), custom_call_target="tpu_custom_call" | custom-call | flops 62500000 | bytes 1000 | tf_op jit(solution)/shard_map/unproject/pallas_call | solution.py:578
  332.8 13.4 %collective-permute-done.25 = bf16[4,2,2,16,1024]{4,3,0,1,2:T(8,128)(2,1)S(1)} collective-permute-done((bf16[4,2,2,16,1024]{4,3,0,1,2:T(8,128)(2,1)S(1)}, bf16[4,2,2,16,1024]{4,3,0,1,2:T(8,128)(2,1)S(1)}, u32[]{:S(2)}, u32[]{:S(2)}) %collective-permute-start.25) | collective-permute-done | bytes 524320 | tf_op jit(solution)/shard_map/part/ppermute | solution.py:624
  346.5 10.1 %collective-permute-done.20 = bf16[2,2,128,512]{3,2,0,1:T(8,128)(2,1)S(1)} collective-permute-done((bf16[2,2,128,512]{3,2,0,1:T(8,128)(2,1)S(1)}, bf16[2,2,128,512]{3,2,0,1:T(8,128)(2,1)S(1)}, u32[]{:S(2)}, u32[]{:S(2)}) %collective-permute-start.20) | collective-permute-done | bytes 524320 | tf_op jit(solution)/shard_map/part/ppermute | solution.py:624
  357.0 21.2 %collective-permute-done.26 = bf16[4,2,16,1024]{3,2,0,1:T(8,128)(2,1)S(1)} collective-permute-done((bf16[4,2,16,1024]{3,2,0,1:T(8,128)(2,1)S(1)}, bf16[4,2,16,1024]{3,2,0,1:T(8,128)(2,1)S(1)}, u32[]{:S(2)}, u32[]{:S(2)}) %collective-permute-start.26) | collective-permute-done | bytes 262176 | tf_op jit(solution)/shard_map/part/ppermute | solution.py:624
  383.6 4.4 collective-permute-done.24
  388.3 16.9 %collective-permute-done.31 = bf16[512,1024]{1,0:T(8,128)(2,1)S(1)} collective-permute-done((bf16[512,1024]{1,0:T(8,128)(2,1)S(1)}, bf16[512,1024]{1,0:T(8,128)(2,1)S(1)}, u32[]{:S(2)}, u32[]{:S(2)}) %collective-permute-start.31) | collective-permute-done | bytes 1048608 | tf_op jit(solution)/shard_map/mlp_across/ppermute | solution.py:624
  419.0 5.3 %multiply_subtract_fusion = (f32[128,2,768]{2,1,0:T(2,128)}, f32[128,2,768]{2,1,0:T(2,128)}, f32[128,2,768]{2,1,0:T(2,128)}) fusion(f32[128,2,768]{2,1,0:T(2,128)S(1)} %copy-done.38, f32[128,2,768]{2,1,0:T(2,128)S(1)} %copy.95, f32[128,2,768]{2,1,0:T(2,128)} %param.28, f32[128,2,768]{2,1,0:T(2,128)} %param.33), kind=kLoop, calls=%fused_computation.43 | loop fusion | flops 2949120 | bytes 5505024 | tf_op jit(solution)/shard_map/sub | solution.py:53
  434.9 4.2 multiply_subtract_fusion.1
  (287 shorter events, 85.9 us)
Async XLA Ops:
  7.2 70.3 %all-gather.5.cloned.1.call-start = ((), (), s32[]{:S(2)}) async-start(), calls=%async_computation.2 | async-start | bytes 3833856 | tf_op jit(solution)/shard_map/all_gather | solution.py:690
  11.1 147.6 %all-gather.7.cloned.1.call-start = ((), (), s32[]{:S(2)}) async-start(), calls=%async_computation.3 | async-start | bytes 5308416 | tf_op jit(solution)/shard_map/all_gather | solution.py:693
  12.9 393.9 %reduce-scatter.2.cloned.1.call-start = ((), (), s32[]{:S(2)}) async-start(), calls=%async_computation.1 | async-start | bytes 5308416 | tf_op jit(solution)/shard_map/reduce_scatter | solution.py:799
  13.0 27.1 %collective-permute-start.1 = (bf16[512,1024]{1,0:T(8,128)(2,1)S(1)}, bf16[512,1024]{1,0:T(8,128)(2,1)}, u32[]{:S(2)}, u32[]{:S(2)}) collective-permute-start(bf16[512,1024]{1,0:T(8,128)(2,1)S(1)} %copy-done.28), channel_id=1, source_target_pairs={{0,2},{1,3},{2,0},{3,1},{4,6},{5,7},{6,4},{7,5},{8,10},{9,11},{10,... | collective-permute-start | bytes 3145736 | tf_op jit(solution)/shard_map/tokens_across/ppermute | solution.py:624
  16.0 28.6 %collective-permute-start = (bf16[512,1024]{1,0:T(8,128)(2,1)S(1)}, bf16[512,1024]{1,0:T(8,128)(2,1)}, u32[]{:S(2)}, u32[]{:S(2)}) collective-permute-start(bf16[512,1024]{1,0:T(8,128)(2,1)S(1)} %copy-done.28), channel_id=1, source_target_pairs={{0,1},{1,0},{2,3},{3,2},{4,5},{5,4},{6,7},{7,6},{8,9},{9,8},{10,11... | collective-permute-start | bytes 3145736 | tf_op jit(solution)/shard_map/part/ppermute | solution.py:624
  16.0 95.8 %collective-permute-start.3 = (bf16[512,1024]{1,0:T(8,128)(2,1)}, bf16[512,1024]{1,0:T(8,128)(2,1)}, u32[]{:S(2)}, u32[]{:S(2)}) collective-permute-start(bf16[512,1024]{1,0:T(8,128)(2,1)} %grad.1), channel_id=1, source_target_pairs={{0,2},{1,3},{2,0},{3,1},{4,6},{5,7},{6,4},{7,5},{8,10},{9,11},{10,... | collective-permute-start | bytes 3145736 | tf_op jit(solution)/shard_map/grad_across/ppermute | solution.py:624
  40.1 4.5 %collective-permute-start.2 = (bf16[512,1024]{1,0:T(8,128)(2,1)}, bf16[512,1024]{1,0:T(8,128)(2,1)}, u32[]{:S(2)}, u32[]{:S(2)}) collective-permute-start(bf16[512,1024]{1,0:T(8,128)(2,1)} %collective-permute-done.1), channel_id=1, source_target_pairs={{0,1},{1,0},{2,3},{3,2},{4,5},{5,4},{6,7},{7,6},{8,9},{9,8},{10,11... | collective-permute-start | bytes 3145736 | tf_op jit(solution)/shard_map/part/ppermute | solution.py:624
  116.0 25.4 %collective-permute-start.5 = (bf16[512,1024]{1,0:T(8,128)(2,1)S(1)}, bf16[512,1024]{1,0:T(8,128)(2,1)}, u32[]{:S(2)}, u32[]{:S(2)}) collective-permute-start(bf16[512,1024]{1,0:T(8,128)(2,1)S(1)} %add_convert_fusion.5), channel_id=1, source_target_pairs={{0,2},{1,3},{2,0},{3,1},{4,6},{5,7},{6,4},{7,5},{8,10},{9,11},{10,... | collective-permute-start | bytes 3145736 | tf_op jit(solution)/shard_map/attn_across/ppermute | solution.py:624
  142.2 22.3 %collective-permute-start.9 = (bf16[512,1024]{1,0:T(8,128)(2,1)}, bf16[512,1024]{1,0:T(8,128)(2,1)}, u32[]{:S(2)}, u32[]{:S(2)}) collective-permute-start(bf16[512,1024]{1,0:T(8,128)(2,1)} %grad.1), channel_id=1, source_target_pairs={{0,1},{1,0},{2,3},{3,2},{4,5},{5,4},{6,7},{7,6},{8,9},{9,8},{10,11... | collective-permute-start | bytes 3145736 | tf_op jit(solution)/shard_map/part/ppermute | solution.py:624
  161.7 25.6 %collective-permute-start.7 = (bf16[512,1024]{1,0:T(8,128)(2,1)S(1)}, bf16[512,1024]{1,0:T(8,128)(2,1)S(1)}, u32[]{:S(2)}, u32[]{:S(2)}) collective-permute-start(bf16[512,1024]{1,0:T(8,128)(2,1)S(1)} %multiply_convert_fusion), channel_id=1, source_target_pairs={{0,2},{1,3},{2,0},{3,1},{4,6},{5,7},{6,4},{7,5},{8,10},{9,11},{10,... | collective-permute-start | bytes 3145736 | tf_op jit(solution)/shard_map/normed_across/ppermute | solution.py:624
  165.9 22.7 %collective-permute-start.12 = (bf16[512,1024]{1,0:T(8,128)(2,1)}, bf16[512,1024]{1,0:T(8,128)(2,1)S(1)}, u32[]{:S(2)}, u32[]{:S(2)}) collective-permute-start(bf16[512,1024]{1,0:T(8,128)(2,1)} %collective-permute-done.3), channel_id=1, source_target_pairs={{0,1},{1,0},{2,3},{3,2},{4,5},{5,4},{6,7},{7,6},{8,9},{9,8},{10,11... | collective-permute-start | bytes 3145736 | tf_op jit(solution)/shard_map/part/ppermute | solution.py:624
  214.4 25.5 %collective-permute-start.14 = (bf16[512,1024]{1,0:T(8,128)(2,1)}, bf16[512,1024]{1,0:T(8,128)(2,1)}, u32[]{:S(2)}, u32[]{:S(2)}) collective-permute-start(bf16[512,1024]{1,0:T(8,128)(2,1)} %add_convert_fusion.4), channel_id=1, source_target_pairs={{0,2},{1,3},{2,0},{3,1},{4,6},{5,7},{6,4},{7,5},{8,10},{9,11},{10,... | collective-permute-start | bytes 3145736 | tf_op jit(solution)/shard_map/back_across/ppermute | solution.py:624
  215.8 24.1 %collective-permute-start.10 = (bf16[512,1024]{1,0:T(8,128)(2,1)}, bf16[512,1024]{1,0:T(8,128)(2,1)}, u32[]{:S(2)}, u32[]{:S(2)}) collective-permute-start(bf16[512,1024]{1,0:T(8,128)(2,1)} %get-tuple-element.115), channel_id=1, source_target_pairs={{0,1},{1,0},{2,3},{3,2},{4,5},{5,4},{6,7},{7,6},{8,9},{9,8},{10,11... | collective-permute-start | bytes 3145736 | tf_op jit(solution)/shard_map/part/ppermute | solution.py:624
  244.9 25.7 %collective-permute-start.16 = (bf16[512,1024]{1,0:T(8,128)(2,1)S(1)}, bf16[512,1024]{1,0:T(8,128)(2,1)}, u32[]{:S(2)}, u32[]{:S(2)}) collective-permute-start(bf16[512,1024]{1,0:T(8,128)(2,1)S(1)} %get-tuple-element.129), channel_id=1, source_target_pairs={{0,2},{1,3},{2,0},{3,1},{4,6},{5,7},{6,4},{7,5},{8,10},{9,11},{10,... | collective-permute-start | bytes 3145736 | tf_op jit(solution)/shard_map/grad_middle_across/ppermute | solution.py:624
  314.6 7.5 %collective-permute-start.18 = (bf16[512,1024]{1,0:T(8,128)(2,1)S(1)}, bf16[512,1024]{1,0:T(8,128)(2,1)S(1)}, u32[]{:S(2)}, u32[]{:S(2)}) collective-permute-start(bf16[512,1024]{1,0:T(8,128)(2,1)S(1)} %get-tuple-element.144), channel_id=1, source_target_pairs={{0,1},{1,0},{2,3},{3,2},{4,5},{5,4},{6,7},{7,6},{8,9},{9,8},{10,11... | collective-permute-start | bytes 3145736 | tf_op jit(solution)/shard_map/part/ppermute | solution.py:624
  325.1 21.2 %collective-permute-start.25 = (bf16[4,2,2,16,1024]{4,3,0,1,2:T(8,128)(2,1)S(1)}, bf16[4,2,2,16,1024]{4,3,0,1,2:T(8,128)(2,1)S(1)}, u32[]{:S(2)}, u32[]{:S(2)}) collective-permute-start(bf16[4,2,2,16,1024]{4,3,0,1,2:T(8,128)(2,1)S(1)} %bitcast.145), channel_id=1, source_target_pairs={{0,4},{4,0},{8,12},{12,8},{16,20},{20,16},{24,28},{28,24},{1,5},{5... | collective-permute-start | bytes 1572872 | tf_op jit(solution)/shard_map/part/ppermute | solution.py:624
  325.8 30.8 %collective-permute-start.20 = (bf16[2,2,128,512]{3,2,0,1:T(8,128)(2,1)S(1)}, bf16[2,2,128,512]{3,2,0,1:T(8,128)(2,1)S(1)}, u32[]{:S(2)}, u32[]{:S(2)}) collective-permute-start(bf16[2,2,128,512]{3,2,0,1:T(8,128)(2,1)S(1)} %bitcast.146), channel_id=1, source_target_pairs={{0,4},{4,0},{8,12},{12,8},{16,20},{20,16},{24,28},{28,24},{1,5},{5... | collective-permute-start | bytes 1572872 | tf_op jit(solution)/shard_map/part/ppermute | solution.py:624
  327.8 29.0 %collective-permute-start.19 = (bf16[2,2,144,512]{3,2,0,1:T(8,128)(2,1)S(1)}, bf16[2,2,144,512]{3,2,0,1:T(8,128)(2,1)S(1)}, u32[]{:S(2)}, u32[]{:S(2)}) collective-permute-start(bf16[2,2,144,512]{3,2,0,1:T(8,128)(2,1)S(1)} %dynamic-slice_bitcast_fusion), channel_id=1, source_target_pairs={{0,8},{4,12},{8,0},{12,4},{16,24},{20,28},{24,16},{28,20},{1,9},{5... | collective-permute-start | bytes 1769480 | tf_op jit(solution)/shard_map/part/ppermute | solution.py:624
  327.8 50.9 %collective-permute-start.21 = (bf16[512,1024]{1,0:T(8,128)(2,1)S(1)}, bf16[512,1024]{1,0:T(8,128)(2,1)S(1)}, u32[]{:S(2)}, u32[]{:S(2)}) collective-permute-start(bf16[512,1024]{1,0:T(8,128)(2,1)S(1)} %add_convert_fusion.2), channel_id=1, source_target_pairs={{0,2},{1,3},{2,0},{3,1},{4,6},{5,7},{6,4},{7,5},{8,10},{9,11},{10,... | collective-permute-start | bytes 3145736 | tf_op jit(solution)/shard_map/back_across/ppermute | solution.py:624
  328.0 50.3 %collective-permute-start.22 = (bf16[512,1024]{1,0:T(8,128)(2,1)S(1)}, bf16[512,1024]{1,0:T(8,128)(2,1)S(1)}, u32[]{:S(2)}, u32[]{:S(2)}) collective-permute-start(bf16[512,1024]{1,0:T(8,128)(2,1)S(1)} %copy-done.20), channel_id=1, source_target_pairs={{0,1},{1,0},{2,3},{3,2},{4,5},{5,4},{6,7},{7,6},{8,9},{9,8},{10,11... | collective-permute-start | bytes 3145736 | tf_op jit(solution)/shard_map/part/ppermute | solution.py:624
  346.3 33.3 %collective-permute-start.32 = (bf16[512,1024]{1,0:T(8,128)(2,1)S(1)}, bf16[512,1024]{1,0:T(8,128)(2,1)S(1)}, u32[]{:S(2)}, u32[]{:S(2)}) collective-permute-start(bf16[512,1024]{1,0:T(8,128)(2,1)S(1)} %get-tuple-element.173), channel_id=1, source_target_pairs={{0,1},{1,0},{2,3},{3,2},{4,5},{5,4},{6,7},{7,6},{8,9},{9,8},{10,11... | collective-permute-start | bytes 3145736 | tf_op jit(solution)/shard_map/part/ppermute | solution.py:624
  356.6 21.6 %collective-permute-start.26 = (bf16[4,2,16,1024]{3,2,0,1:T(8,128)(2,1)S(1)}, bf16[4,2,16,1024]{3,2,0,1:T(8,128)(2,1)S(1)}, u32[]{:S(2)}, u32[]{:S(2)}) collective-permute-start(bf16[4,2,16,1024]{3,2,0,1:T(8,128)(2,1)S(1)} %fusion.21), channel_id=1, source_target_pairs={{0,8},{4,12},{8,0},{12,4},{16,24},{20,28},{24,16},{28,20},{1,9},{5... | collective-permute-start | bytes 786440 | tf_op jit(solution)/shard_map/part/ppermute | solution.py:624
  378.8 9.3 %collective-permute-start.24 = (bf16[2,128,512]{2,1,0:T(8,128)(2,1)S(1)}, bf16[2,128,512]{2,1,0:T(8,128)(2,1)S(1)}, u32[]{:S(2)}, u32[]{:S(2)}) collective-permute-start(bf16[2,128,512]{2,1,0:T(8,128)(2,1)S(1)} %fusion.20), channel_id=1, source_target_pairs={{0,8},{4,12},{8,0},{12,4},{16,24},{20,28},{24,16},{28,20},{1,9},{5... | collective-permute-start | bytes 786440 | tf_op jit(solution)/shard_map/part/ppermute | solution.py:624
  378.9 9.2 %collective-permute-start.23 = (bf16[2,144,512]{2,1,0:T(8,128)(2,1)S(1)}, bf16[2,144,512]{2,1,0:T(8,128)(2,1)S(1)}, u32[]{:S(2)}, u32[]{:S(2)}) collective-permute-start(bf16[2,144,512]{2,1,0:T(8,128)(2,1)S(1)} %fusion.18), channel_id=1, source_target_pairs={{0,4},{4,0},{8,12},{12,8},{16,20},{20,16},{24,28},{28,24},{1,5},{5... | collective-permute-start | bytes 884744 | tf_op jit(solution)/shard_map/part/ppermute | solution.py:624
  379.5 8.7 %collective-permute-start.30 = (bf16[512,1024]{1,0:T(8,128)(2,1)S(1)}, bf16[512,1024]{1,0:T(8,128)(2,1)S(1)}, u32[]{:S(2)}, u32[]{:S(2)}) collective-permute-start(bf16[512,1024]{1,0:T(8,128)(2,1)S(1)} %copy-done.18), channel_id=1, source_target_pairs={{0,1},{1,0},{2,3},{3,2},{4,5},{5,4},{6,7},{7,6},{8,9},{9,8},{10,11... | collective-permute-start | bytes 3145736 | tf_op jit(solution)/shard_map/part/ppermute | solution.py:624
  379.5 25.6 %collective-permute-start.31 = (bf16[512,1024]{1,0:T(8,128)(2,1)S(1)}, bf16[512,1024]{1,0:T(8,128)(2,1)S(1)}, u32[]{:S(2)}, u32[]{:S(2)}) collective-permute-start(bf16[512,1024]{1,0:T(8,128)(2,1)S(1)} %add_convert_fusion.1), channel_id=1, source_target_pairs={{0,2},{1,3},{2,0},{3,1},{4,6},{5,7},{6,4},{7,5},{8,10},{9,11},{10,... | collective-permute-start | bytes 3145736 | tf_op jit(solution)/shard_map/mlp_across/ppermute | solution.py:624
  410.3 16.4 %collective-permute-start.29 = (bf16[4,16,1024]{2,1,0:T(8,128)(2,1)}, bf16[4,16,1024]{2,1,0:T(8,128)(2,1)}, u32[]{:S(2)}, u32[]{:S(2)}) collective-permute-start(bf16[4,16,1024]{2,1,0:T(8,128)(2,1)} %fusion.24), channel_id=1, source_target_pairs={{0,16},{4,20},{8,24},{12,28},{16,0},{20,4},{24,8},{28,12},{1,17},{... | collective-permute-start | bytes 393224 | tf_op jit(solution)/shard_map/part/ppermute | solution.py:624
  412.2 17.3 %collective-permute-start.28 = (bf16[128,512]{1,0:T(8,128)(2,1)}, bf16[128,512]{1,0:T(8,128)(2,1)}, u32[]{:S(2)}, u32[]{:S(2)}) collective-permute-start(bf16[128,512]{1,0:T(8,128)(2,1)} %fusion.23), channel_id=1, source_target_pairs={{0,16},{4,20},{8,24},{12,28},{16,0},{20,4},{24,8},{28,12},{1,17},{... | collective-permute-start | bytes 393224 | tf_op jit(solution)/shard_map/part/ppermute | solution.py:624
  413.9 17.5 %collective-permute-start.27 = (bf16[144,512]{1,0:T(8,128)(2,1)}, bf16[144,512]{1,0:T(8,128)(2,1)}, u32[]{:S(2)}, u32[]{:S(2)}) collective-permute-start(bf16[144,512]{1,0:T(8,128)(2,1)} %fusion.22), channel_id=1, source_target_pairs={{0,16},{4,20},{8,24},{12,28},{16,0},{20,4},{24,8},{28,12},{1,17},{... | collective-permute-start | bytes 442376 | tf_op jit(solution)/shard_map/part/ppermute | solution.py:624
  432.4 7.7 %collective-permute-start.35 = (f32[288]{0:T(512)S(1)}, f32[288]{0:T(512)S(1)}, u32[]{:S(2)}, u32[]{:S(2)}) collective-permute-start(f32[288]{0:T(512)S(1)} %slice_reduce_fusion), channel_id=1, source_target_pairs={{0,3},{1,2},{2,1},{3,0},{4,7},{5,6},{6,5},{7,4},{8,11},{9,10},{10,... | collective-permute-start | bytes 3464 | tf_op jit(solution)/shard_map/part/ppermute | solution.py:624
  432.4 7.6 %collective-permute-start.34 = (f32[288]{0:T(512)S(1)}, f32[288]{0:T(512)S(1)}, u32[]{:S(2)}, u32[]{:S(2)}) collective-permute-start(f32[288]{0:T(512)S(1)} %slice_reduce_fusion), channel_id=1, source_target_pairs={{0,2},{1,3},{2,0},{3,1},{4,6},{5,7},{6,4},{7,5},{8,10},{9,11},{10,... | collective-permute-start | bytes 3464 | tf_op jit(solution)/shard_map/part/ppermute | solution.py:624
  433.0 7.1 %collective-permute-start.33 = (f32[288]{0:T(512)S(1)}, f32[288]{0:T(512)S(1)}, u32[]{:S(2)}, u32[]{:S(2)}) collective-permute-start(f32[288]{0:T(512)S(1)} %slice_reduce_fusion), channel_id=1, source_target_pairs={{0,1},{1,0},{2,3},{3,2},{4,5},{5,4},{6,7},{7,6},{8,9},{9,8},{10,11... | collective-permute-start | bytes 3464 | tf_op jit(solution)/shard_map/part/ppermute | solution.py:624
  (65 other events, 620.0 us)
Sparse Core Ops, SparseCore 0:
  11.2 66.2 all-gather.4
  80.2 78.4 all-gather.6
  270.7 113.6 reduce-scatter.1

commit v10 on v7

--- a/solution.py
+++ b/solution.py
@@ -817,13 +817,13 @@
         sum_one, sum_two = halved(sum_one, 1, 2), halved(sum_two, 2, 1)
         sum_out = grad_out_w.reshape((out_heads,) + cube + (out_depth, MODEL_WIDTH))
         sum_out = halved(sum_out, 3, 1)
-        sum_one, sum_two, back_across, sum_0, sum_1, near_mlp = together(
-            sum_one, sum_two, back_across, sum_0, sum_1, near_mlp
+        sum_one, sum_two, back_across, sum_0, sum_1, near_mlp, feed_sum = together(
+            sum_one, sum_two, back_across, sum_0, sum_1, near_mlp, feed_sum
         )
         mlp_across = flipped(near_mlp, "tensor", 2, "mlp_across")
         sum_one, sum_two = halved(sum_one, 1, 1), halved(sum_two, 1, 2)
         sum_out = halved(sum_out, 2, 2)
-        sum_one, sum_two, sum_out, feed_sum = together(sum_one, sum_two, sum_out, feed_sum)
+        sum_one, sum_two, sum_out = together(sum_one, sum_two, sum_out)
         sum_one, sum_two = halved(sum_one, 0, 4), halved(sum_two, 0, 4)
         sum_out = halved(sum_out, 1, 4)
         sum_one, sum_two, sum_out, mlp_across = together(sum_one, sum_two, sum_out, mlp_across)

time: 420 us -> 438 us (1.043)
  waiting for transfers between devices: 113 us -> 127 us
  local copies, waits for them, and re-layouts: 27.4 us -> 35.2 us
    ppermute x36, waiting for transfers between devices: 77.3 us -> 88.8 us  [flipped(): lax.ppermute(value, axis, [(i, i ^ bit) for i in range(lax.axis_size(axis...]
    unnamed x123 -> x145, local copies, waits for them, and re-layouts: 9.3 us -> 10.9 us
  transfers between devices with their start and end apart: 39 -> 39, of which waited for: 19 -> 17; matrix products, arithmetic and copies ran while one was open for 22% -> 24% of each run, Pallas kernels for 32% -> 30%
where the time goes in v10:
time: 438 us; the launch traced here: 432 us
  Pallas kernels  145 us (33%)
  waiting for transfers between devices  127 us (29%)
  other arithmetic  65 us (15%)
  local copies, waits for them, and re-layouts  35.2 us (8%)
  starting transfers between devices  27.6 us (6%)
  matrix products  17.5 us (4%)
  between operations  15.4 us (4%)
    ppermute x36, waiting for transfers between devices, flipped(): lax.ppermute(value, axis, [(i, i ^ bit) for i in range(lax.axis_size(axis...  88.8 us
    pallas_call x2, Pallas kernels, feed(): pl.pallas_call(lambda *refs: feed_kernel(packs, *refs), grid=(rows // BLO...  33.6 us
    all_gather x1, waiting for transfers between devices, per_device(): lax.all_gather(pack_one, 'dp', axis=0, tiled=False)  28.6 us
    pallas_call x2, Pallas kernels, attend(): pl.pallas_call(lambda *refs: attend_kernel(half * n // BLOCK, *refs), gri...  27.6 us
    ppermute x36, starting transfers between devices, flipped(): lax.ppermute(value, axis, [(i, i ^ bit) for i in range(lax.axis_size(axis...  27.5 us
    pallas_call x1, Pallas kernels, attend_back_other(): pl.pallas_call(back_other_kernel, grid_spec=pltpu.PrefetchScalarGridSpec(...  25.2 us
    pallas_call x1, Pallas kernels, attend_back_own(): pl.pallas_call(back_own_kernel, grid_spec=pltpu.PrefetchScalarGridSpec(nu...  17.9 us
    pallas_call x1, Pallas kernels, feed_weights(): pl.pallas_call(lambda *refs: feed_weights_kernel(packs, pieces, *refs), g...  16.6 us
  transfers between devices with their start and end apart: 39, of which 17 were waited for; matrix products, arithmetic and copies ran while one was open for 24% of the time, Pallas kernels for 30%

profile of v10, /device:TPU:0, one launch (start us, length us, event | category | flops | bytes accessed | tf_op | source)
XLA Modules:
  0.0 432.3 jit_solution(5638044341961760433)
XLA Ops:
  13.0 3.0 collective-permute-start.1
  16.8 23.4 %collective-permute-done.1 = bf16[512,1024]{1,0:T(8,128)(2,1)} collective-permute-done((bf16[512,1024]{1,0:T(8,128)(2,1)S(1)}, bf16[512,1024]{1,0:T(8,128)(2,1)}, u32[]{:S(2)}, u32[]{:S(2)}) %collective-permute-start.1) | collective-permute-done | bytes 1048608 | tf_op jit(solution)/shard_map/tokens_across/ppermute | solution.py:588
  40.1 3.7 fusion.17
  44.6 4.3 pad_maximum_fusion.x
  48.8 28.6 %all-gather.5.cloned.1.call-done = bf16[1664,1024]{1,0:T(8,128)(2,1)} async-done(((bf16[208,1024]{1,0:T(8,128)(2,1)}), bf16[1664,1024]{1,0:T(8,128)(2,1)}) %all-gather.5.cloned.1.call-update) | async-done | bytes 3407888 | tf_op jit(solution)/shard_map/all_gather | solution.py:654
  78.8 3.1 slice.70
  83.9 13.4 %project.1 = (bf16[1024,2048]{1,0:T(8,128)(2,1)}, f32[2048,512]{1,0:T(8,128)}, f32[2048,256]{1,0:T(8,128)}, bf16[2048,512]{1,0:T(8,128)(2,1)}, bf16[2048,256]{1,...) custom-call(bf16[2048,1024]{1,0:T(8,128)(2,1)} %pad_maximum_fusion.x, ...), custom_call_target="tpu_custom_call" | custom-call | flops 156250000 | bytes 1000 | tf_op jit(solution)/shard_map/project/pallas_call | solution.py:397
  97.3 15.1 %attend.2 = (bf16[1024,512]{1,0:T(8,128)(2,1)S(1)}, bf16[512,1024]{1,0:T(8,128)(2,1)S(1)}, f32[2,2,1024]{2,1,0:T(2,128)S(1)}) custom-call(s32[17]{0:T(128)S(1)} %pad_add_fusion.refs_0_.info, bf16[2048,512]{1,0:T(8,128)(2,1)} %get-tuple-element.100.refs_1_.q, bf16[256,2048]{1,0:T(8,128)(2,1)S(1)} %get-tuple-element.96.refs_2_.k_turned, ...), custom_call_target="tpu_custom_call" | custom-call | flops 281249984 | bytes 1000 | tf_op jit(solution)/shard_map/attend/pallas_call | solution.py:438
  116.8 12.5 %attend.3 = (bf16[1024,512]{1,0:T(8,128)(2,1)S(1)}, bf16[512,1024]{1,0:T(8,128)(2,1)S(1)}, f32[2,2,1024]{2,1,0:T(2,128)S(1)}) custom-call(s32[17]{0:T(128)S(1)} %pad_add_fusion.refs_0_.info, bf16[2048,512]{1,0:T(8,128)(2,1)} %get-tuple-element.100.refs_1_.q, bf16[256,2048]{1,0:T(8,128)(2,1)S(1)} %get-tuple-element.96.refs_2_.k_turned, ...), custom_call_target="tpu_custom_call" | custom-call | flops 281249984 | bytes 1000 | tf_op jit(solution)/shard_map/attend/pallas_call | solution.py:438
  129.3 12.7 %collective-permute-done.5 = bf16[512,1024]{1,0:T(8,128)(2,1)S(1)} collective-permute-done((bf16[512,1024]{1,0:T(8,128)(2,1)S(1)}, bf16[512,1024]{1,0:T(8,128)(2,1)S(1)}, u32[]{:S(2)}, u32[]{:S(2)}) %collective-permute-start.5) | collective-permute-done | bytes 1048608 | tf_op jit(solution)/shard_map/attn_across/ppermute | solution.py:588
  149.2 9.5 %all-gather.7.cloned.1.call-done = bf16[4608,512]{1,0:T(8,128)(2,1)} async-done(((bf16[576,512]{1,0:T(8,128)(2,1)}), bf16[4608,512]{1,0:T(8,128)(2,1)}) %all-gather.7.cloned.1.call-update) | async-done | bytes 4718608 | tf_op jit(solution)/shard_map/all_gather | solution.py:656
  168.9 16.8 %feed.2 = (bf16[1024,1024]{1,0:T(8,128)(2,1)}, bf16[768,1024]{1,0:T(8,128)(2,1)S(1)}, bf16[1024,1536]{1,0:T(8,128)(2,1)}, bf16[512,1024]{1,0:T(8,128)(2,1)S(1)},...) custom-call(bf16[1024,1024]{1,0:T(8,128)(2,1)} %pad_maximum_fusion.1.refs_0_, ...), custom_call_target="tpu_custom_call" | custom-call | flops 250000000 | bytes 1000 | tf_op jit(solution)/shard_map/feed/pallas_call | solution.py:533
  192.4 16.8 %feed.3 = (bf16[1024,1024]{1,0:T(8,128)(2,1)}, bf16[768,1024]{1,0:T(8,128)(2,1)S(1)}, bf16[1024,1536]{1,0:T(8,128)(2,1)}, bf16[512,1024]{1,0:T(8,128)(2,1)S(1)},...) custom-call(bf16[1024,1024]{1,0:T(8,128)(2,1)} %pad_maximum_fusion.2.refs_0_, ...), custom_call_target="tpu_custom_call" | custom-call | flops 250000000 | bytes 1000 | tf_op jit(solution)/shard_map/feed/pallas_call | solution.py:533
  216.8 16.6 %feed_weights.1 = bf16[8,576,512]{2,1,0:T(8,128)(2,1)} custom-call(bf16[1024,1024]{1,0:T(8,128)(2,1)S(1)} %copy-done.12, bf16[1024,1024]{1,0:T(8,128)(2,1)} %get-tuple-element.120.refs_1_, bf16[1024,1536]{1,0:T(8,128)(2,1)} %get-tuple-element.121.refs_2_, bf16[1024,1536]{1,0:T(8,128)(2,1)} %get-tuple-element.122.refs_3_, ...), custom_call_target="tpu_custom_call" | custom-call | flops 250000000 | bytes 1000 | tf_op jit(solution)/shard_map/feed_weights/pallas_call | solution.py:558
  233.4 7.5 %collective-permute-done.14 = bf16[512,1024]{1,0:T(8,128)(2,1)} collective-permute-done((bf16[512,1024]{1,0:T(8,128)(2,1)}, bf16[512,1024]{1,0:T(8,128)(2,1)}, u32[]{:S(2)}, u32[]{:S(2)}) %collective-permute-start.14) | collective-permute-done | bytes 1048608 | tf_op jit(solution)/shard_map/back_across/ppermute | solution.py:588
  240.9 3.2 multiply_reduce_fusion.1
  244.1 4.2 fusion.35
  253.4 17.9 %attend_back_own.1 = (bf16[1024,512]{1,0:T(8,128)(2,1)S(1)}, f32[2048,256]{1,0:T(8,128)}, f32[2048,256]{1,0:T(8,128)}, f32[2,1,128]{2,1,0:T(1,128)S(1)}) custom-call(s32[17]{0:T(128)S(1)} %pad_add_fusion.refs_0_.info, bf16[2048,512]{1,0:T(8,128)(2,1)} %get-tuple-element.100.refs_1_.q, bf16[2048,256]{1,0:T(8,128)(2,1)S(1)} %copy-done.8, ...), custom_call_target="tpu_custom_call" | custom-call | flops 390624992 | bytes 1000 | tf_op jit(solution)/shard_map/attend_back_own/pallas_call | solution.py:458
  282.5 25.2 %attend_back_other.1 = (bf16[2048,1024]{1,0:T(8,128)(2,1)}, f32[2,2,128]{2,1,0:T(2,128)S(1)}) custom-call(s32[17]{0:T(128)S(1)} %pad_add_fusion.refs_0_.info, bf16[2048,512]{1,0:T(8,128)(2,1)} %get-tuple-element.100.refs_1_.q, bf16[2048,256]{1,0:T(8,128)(2,1)S(1)} %copy-done.9, bf16[2048,256]{1,0:T(8,128)(2,1)S(1)} %copy-done.4, ...), custom_call_target="tpu_custom_call" | custom-call | flops 437500000 | bytes 1000 | tf_op jit(solution)/shard_map/attend_back_other/pallas_call | solution.py:489
  307.8 4.7 %unproject.2 = (bf16[512,1024]{1,0:T(8,128)(2,1)S(1)}, bf16[512,1024]{1,0:T(8,128)(2,1)S(1)}) custom-call(bf16[2048,1024]{1,0:T(8,128)(2,1)} %get-tuple-element.165.grad, bf16[1024,1024]{1,0:T(8,128)(2,1)S(1)} %bitcast.108), custom_call_target="tpu_custom_call" | custom-call | flops 62500000 | bytes 1000 | tf_op jit(solution)/shard_map/unproject/pallas_call | solution.py:576
  312.7 6.3 %fusion.40 = f32[1024,1024]{1,0:T(8,128)S(1)} fusion(bf16[1024,2048]{1,0:T(8,128)(2,1)} %get-tuple-element.142, bf16[2048,1024]{1,0:T(8,128)(2,1)S(1)} %copy-done.31), kind=kOutput, calls=%fused_computation.143 | convolution fusion | flops 4294967296 | bytes 12582912 | tf_op jit(solution)/shard_map/dot_general | solution.py:64
  330.5 3.8 collective-permute-start.19
  334.3 5.6 %unproject.3 = (bf16[512,1024]{1,0:T(8,128)(2,1)S(1)}, bf16[512,1024]{1,0:T(8,128)(2,1)}) custom-call(bf16[2048,1024]{1,0:T(8,128)(2,1)} %get-tuple-element.165.grad, bf16[1024,1024]{1,0:T(8,128)(2,1)S(1)} %bitcast.109), custom_call_target="tpu_custom_call" | custom-call | flops 62500000 | bytes 1000 | tf_op jit(solution)/shard_map/unproject/pallas_call | solution.py:576
  341.8 7.1 %collective-permute-done.20 = bf16[2,2,128,512]{3,2,0,1:T(8,128)(2,1)S(1)} collective-permute-done((bf16[2,2,128,512]{3,2,0,1:T(8,128)(2,1)}, bf16[2,2,128,512]{3,2,0,1:T(8,128)(2,1)S(1)}, u32[]{:S(2)}, u32[]{:S(2)}) %collective-permute-start.20) | collective-permute-done | bytes 524320 | tf_op jit(solution)/shard_map/part/ppermute | solution.py:588
  348.9 3.4 collective-permute-start.27
  354.7 3.8 collective-permute-done.27
  379.0 5.2 %multiply_subtract_fusion = (f32[128,2,768]{2,1,0:T(2,128)}, f32[128,2,768]{2,1,0:T(2,128)}, f32[128,2,768]{2,1,0:T(2,128)}) fusion(f32[128,2,768]{2,1,0:T(2,128)} %param.23, f32[128,2,768]{2,1,0:T(2,128)} %copy.94, f32[128,2,768]{2,1,0:T(2,128)} %param.28, f32[128,2,768]{2,1,0:T(2,128)} %param.33), kind=kLoop, calls=%fused_computation.48 | loop fusion | flops 2949120 | bytes 5505024 | tf_op jit(solution)/shard_map/sub | solution.py:53
  384.2 3.8 fusion.4
  395.2 12.6 %collective-permute-done.29 = bf16[128,512]{1,0:T(8,128)(2,1)S(1)} collective-permute-done((bf16[128,512]{1,0:T(8,128)(2,1)S(1)}, bf16[128,512]{1,0:T(8,128)(2,1)S(1)}, u32[]{:S(2)}, u32[]{:S(2)}) %collective-permute-start.29) | collective-permute-done | bytes 131104 | tf_op jit(solution)/shard_map/part/ppermute | solution.py:588
  407.9 5.5 %collective-permute-done.30 = bf16[4,16,1024]{2,1,0:T(8,128)(2,1)S(1)} collective-permute-done((bf16[4,16,1024]{2,1,0:T(8,128)(2,1)S(1)}, bf16[4,16,1024]{2,1,0:T(8,128)(2,1)S(1)}, u32[]{:S(2)}, u32[]{:S(2)}) %collective-permute-start.30) | collective-permute-done | bytes 131104 | tf_op jit(solution)/shard_map/part/ppermute | solution.py:588
  416.2 4.0 multiply_subtract_fusion.1
  420.3 3.4 add_convert_fusion
  (308 shorter events, 110.3 us)
Async XLA Ops:
  7.2 70.3 %all-gather.5.cloned.1.call-start = ((), (), s32[]{:S(2)}) async-start(), calls=%async_computation.2 | async-start | bytes 3833856 | tf_op jit(solution)/shard_map/all_gather | solution.py:654
  11.1 147.6 %all-gather.7.cloned.1.call-start = ((), (), s32[]{:S(2)}) async-start(), calls=%async_computation.3 | async-start | bytes 5308416 | tf_op jit(solution)/shard_map/all_gather | solution.py:656
  12.9 347.9 %reduce-scatter.2.cloned.1.call-start = ((), (), s32[]{:S(2)}) async-start(), calls=%async_computation.1 | async-start | bytes 5308416 | tf_op jit(solution)/shard_map/reduce_scatter | solution.py:762
  13.0 27.1 %collective-permute-start.1 = (bf16[512,1024]{1,0:T(8,128)(2,1)S(1)}, bf16[512,1024]{1,0:T(8,128)(2,1)}, u32[]{:S(2)}, u32[]{:S(2)}) collective-permute-start(bf16[512,1024]{1,0:T(8,128)(2,1)S(1)} %copy-done.32), channel_id=1, source_target_pairs={{0,2},{1,3},{2,0},{3,1},{4,6},{5,7},{6,4},{7,5},{8,10},{9,11},{10,... | collective-permute-start | bytes 3145736 | tf_op jit(solution)/shard_map/tokens_across/ppermute | solution.py:588
  16.0 28.6 %collective-permute-start = (bf16[512,1024]{1,0:T(8,128)(2,1)S(1)}, bf16[512,1024]{1,0:T(8,128)(2,1)}, u32[]{:S(2)}, u32[]{:S(2)}) collective-permute-start(bf16[512,1024]{1,0:T(8,128)(2,1)S(1)} %copy-done.32), channel_id=1, source_target_pairs={{0,1},{1,0},{2,3},{3,2},{4,5},{5,4},{6,7},{7,6},{8,9},{9,8},{10,11... | collective-permute-start | bytes 3145736 | tf_op jit(solution)/shard_map/part/ppermute | solution.py:588
  16.0 96.5 %collective-permute-start.3 = (bf16[512,1024]{1,0:T(8,128)(2,1)}, bf16[512,1024]{1,0:T(8,128)(2,1)}, u32[]{:S(2)}, u32[]{:S(2)}) collective-permute-start(bf16[512,1024]{1,0:T(8,128)(2,1)} %param.19), channel_id=1, source_target_pairs={{0,2},{1,3},{2,0},{3,1},{4,6},{5,7},{6,4},{7,5},{8,10},{9,11},{10,... | collective-permute-start | bytes 3145736 | tf_op jit(solution)/shard_map/grad_across/ppermute | solution.py:588
  40.1 4.5 %collective-permute-start.2 = (bf16[512,1024]{1,0:T(8,128)(2,1)}, bf16[512,1024]{1,0:T(8,128)(2,1)}, u32[]{:S(2)}, u32[]{:S(2)}) collective-permute-start(bf16[512,1024]{1,0:T(8,128)(2,1)} %collective-permute-done.1), channel_id=1, source_target_pairs={{0,1},{1,0},{2,3},{3,2},{4,5},{5,4},{6,7},{7,6},{8,9},{9,8},{10,11... | collective-permute-start | bytes 3145736 | tf_op jit(solution)/shard_map/part/ppermute | solution.py:588
  116.7 25.3 %collective-permute-start.5 = (bf16[512,1024]{1,0:T(8,128)(2,1)S(1)}, bf16[512,1024]{1,0:T(8,128)(2,1)S(1)}, u32[]{:S(2)}, u32[]{:S(2)}) collective-permute-start(bf16[512,1024]{1,0:T(8,128)(2,1)S(1)} %add_convert_fusion.5), channel_id=1, source_target_pairs={{0,2},{1,3},{2,0},{3,1},{4,6},{5,7},{6,4},{7,5},{8,10},{9,11},{10,... | collective-permute-start | bytes 3145736 | tf_op jit(solution)/shard_map/attn_across/ppermute | solution.py:588
  143.8 21.8 %collective-permute-start.9 = (bf16[512,1024]{1,0:T(8,128)(2,1)}, bf16[512,1024]{1,0:T(8,128)(2,1)}, u32[]{:S(2)}, u32[]{:S(2)}) collective-permute-start(bf16[512,1024]{1,0:T(8,128)(2,1)} %param.19), channel_id=1, source_target_pairs={{0,1},{1,0},{2,3},{3,2},{4,5},{5,4},{6,7},{7,6},{8,9},{9,8},{10,11... | collective-permute-start | bytes 3145736 | tf_op jit(solution)/shard_map/part/ppermute | solution.py:588
  162.7 25.6 %collective-permute-start.7 = (bf16[512,1024]{1,0:T(8,128)(2,1)S(1)}, bf16[512,1024]{1,0:T(8,128)(2,1)S(1)}, u32[]{:S(2)}, u32[]{:S(2)}) collective-permute-start(bf16[512,1024]{1,0:T(8,128)(2,1)S(1)} %multiply_convert_fusion), channel_id=1, source_target_pairs={{0,2},{1,3},{2,0},{3,1},{4,6},{5,7},{6,4},{7,5},{8,10},{9,11},{10,... | collective-permute-start | bytes 3145736 | tf_op jit(solution)/shard_map/normed_across/ppermute | solution.py:588
  166.9 22.7 %collective-permute-start.12 = (bf16[512,1024]{1,0:T(8,128)(2,1)}, bf16[512,1024]{1,0:T(8,128)(2,1)S(1)}, u32[]{:S(2)}, u32[]{:S(2)}) collective-permute-start(bf16[512,1024]{1,0:T(8,128)(2,1)} %collective-permute-done.3), channel_id=1, source_target_pairs={{0,1},{1,0},{2,3},{3,2},{4,5},{5,4},{6,7},{7,6},{8,9},{9,8},{10,11... | collective-permute-start | bytes 3145736 | tf_op jit(solution)/shard_map/part/ppermute | solution.py:588
  215.3 25.5 %collective-permute-start.14 = (bf16[512,1024]{1,0:T(8,128)(2,1)}, bf16[512,1024]{1,0:T(8,128)(2,1)}, u32[]{:S(2)}, u32[]{:S(2)}) collective-permute-start(bf16[512,1024]{1,0:T(8,128)(2,1)} %add_convert_fusion.4), channel_id=1, source_target_pairs={{0,2},{1,3},{2,0},{3,1},{4,6},{5,7},{6,4},{7,5},{8,10},{9,11},{10,... | collective-permute-start | bytes 3145736 | tf_op jit(solution)/shard_map/back_across/ppermute | solution.py:588
  216.8 24.1 %collective-permute-start.10 = (bf16[512,1024]{1,0:T(8,128)(2,1)S(1)}, bf16[512,1024]{1,0:T(8,128)(2,1)}, u32[]{:S(2)}, u32[]{:S(2)}) collective-permute-start(bf16[512,1024]{1,0:T(8,128)(2,1)S(1)} %get-tuple-element.112), channel_id=1, source_target_pairs={{0,1},{1,0},{2,3},{3,2},{4,5},{5,4},{6,7},{7,6},{8,9},{9,8},{10,11... | collective-permute-start | bytes 3145736 | tf_op jit(solution)/shard_map/part/ppermute | solution.py:588
  248.4 25.7 %collective-permute-start.16 = (bf16[512,1024]{1,0:T(8,128)(2,1)S(1)}, bf16[512,1024]{1,0:T(8,128)(2,1)}, u32[]{:S(2)}, u32[]{:S(2)}) collective-permute-start(bf16[512,1024]{1,0:T(8,128)(2,1)S(1)} %get-tuple-element.192), channel_id=1, source_target_pairs={{0,2},{1,3},{2,0},{3,1},{4,6},{5,7},{6,4},{7,5},{8,10},{9,11},{10,... | collective-permute-start | bytes 3145736 | tf_op jit(solution)/shard_map/grad_middle_across/ppermute | solution.py:588
  312.5 6.6 %collective-permute-start.18 = (bf16[512,1024]{1,0:T(8,128)(2,1)S(1)}, bf16[512,1024]{1,0:T(8,128)(2,1)S(1)}, u32[]{:S(2)}, u32[]{:S(2)}) collective-permute-start(bf16[512,1024]{1,0:T(8,128)(2,1)S(1)} %get-tuple-element.140), channel_id=1, source_target_pairs={{0,1},{1,0},{2,3},{3,2},{4,5},{5,4},{6,7},{7,6},{8,9},{9,8},{10,11... | collective-permute-start | bytes 3145736 | tf_op jit(solution)/shard_map/part/ppermute | solution.py:588
  322.2 17.7 %collective-permute-start.26 = (bf16[4,2,2,16,1024]{4,3,0,1,2:T(8,128)(2,1)}, bf16[4,2,2,16,1024]{4,3,0,1,2:T(8,128)(2,1)}, u32[]{:S(2)}, u32[]{:S(2)}) collective-permute-start(bf16[4,2,2,16,1024]{4,3,0,1,2:T(8,128)(2,1)} %bitcast.106), channel_id=1, source_target_pairs={{0,4},{4,0},{8,12},{12,8},{16,20},{20,16},{24,28},{28,24},{1,5},{5... | collective-permute-start | bytes 1572872 | tf_op jit(solution)/shard_map/part/ppermute | solution.py:588
  328.4 20.5 %collective-permute-start.20 = (bf16[2,2,128,512]{3,2,0,1:T(8,128)(2,1)}, bf16[2,2,128,512]{3,2,0,1:T(8,128)(2,1)S(1)}, u32[]{:S(2)}, u32[]{:S(2)}) collective-permute-start(bf16[2,2,128,512]{3,2,0,1:T(8,128)(2,1)} %fusion.10), channel_id=1, source_target_pairs={{0,4},{4,0},{8,12},{12,8},{16,20},{20,16},{24,28},{28,24},{1,5},{5... | collective-permute-start | bytes 1572872 | tf_op jit(solution)/shard_map/part/ppermute | solution.py:588
  330.5 23.0 %collective-permute-start.19 = (bf16[2,2,144,512]{3,2,0,1:T(8,128)(2,1)S(1)}, bf16[2,2,144,512]{3,2,0,1:T(8,128)(2,1)S(1)}, u32[]{:S(2)}, u32[]{:S(2)}) collective-permute-start(bf16[2,2,144,512]{3,2,0,1:T(8,128)(2,1)S(1)} %fusion.8), channel_id=1, source_target_pairs={{0,8},{4,12},{8,0},{12,4},{16,24},{20,28},{24,16},{28,20},{1,9},{5... | collective-permute-start | bytes 1769480 | tf_op jit(solution)/shard_map/part/ppermute | solution.py:588
  334.3 27.8 %collective-permute-start.21 = (bf16[512,1024]{1,0:T(8,128)(2,1)}, bf16[512,1024]{1,0:T(8,128)(2,1)}, u32[]{:S(2)}, u32[]{:S(2)}) collective-permute-start(bf16[512,1024]{1,0:T(8,128)(2,1)} %add_convert_fusion.2), channel_id=1, source_target_pairs={{0,2},{1,3},{2,0},{3,1},{4,6},{5,7},{6,4},{7,5},{8,10},{9,11},{10,... | collective-permute-start | bytes 3145736 | tf_op jit(solution)/shard_map/back_across/ppermute | solution.py:588
  334.3 25.1 %collective-permute-start.22 = (bf16[512,1024]{1,0:T(8,128)(2,1)S(1)}, bf16[512,1024]{1,0:T(8,128)(2,1)S(1)}, u32[]{:S(2)}, u32[]{:S(2)}) collective-permute-start(bf16[512,1024]{1,0:T(8,128)(2,1)S(1)} %copy-done.23), channel_id=1, source_target_pairs={{0,1},{1,0},{2,3},{3,2},{4,5},{5,4},{6,7},{7,6},{8,9},{9,8},{10,11... | collective-permute-start | bytes 3145736 | tf_op jit(solution)/shard_map/part/ppermute | solution.py:588
  339.9 29.3 %collective-permute-start.32 = (bf16[512,1024]{1,0:T(8,128)(2,1)}, bf16[512,1024]{1,0:T(8,128)(2,1)}, u32[]{:S(2)}, u32[]{:S(2)}) collective-permute-start(bf16[512,1024]{1,0:T(8,128)(2,1)} %get-tuple-element.167), channel_id=1, source_target_pairs={{0,1},{1,0},{2,3},{3,2},{4,5},{5,4},{6,7},{7,6},{8,9},{9,8},{10,11... | collective-permute-start | bytes 3145736 | tf_op jit(solution)/shard_map/part/ppermute | solution.py:588
  348.9 9.7 %collective-permute-start.27 = (bf16[4,2,16,1024]{3,2,0,1:T(8,128)(2,1)S(1)}, bf16[4,2,16,1024]{3,2,0,1:T(8,128)(2,1)S(1)}, u32[]{:S(2)}, u32[]{:S(2)}) collective-permute-start(bf16[4,2,16,1024]{3,2,0,1:T(8,128)(2,1)S(1)} %fusion.21), channel_id=1, source_target_pairs={{0,8},{4,12},{8,0},{12,4},{16,24},{20,28},{24,16},{28,20},{1,9},{5... | collective-permute-start | bytes 786440 | tf_op jit(solution)/shard_map/part/ppermute | solution.py:588
  365.2 25.5 %collective-permute-start.24 = (bf16[2,144,512]{2,1,0:T(8,128)(2,1)}, bf16[2,144,512]{2,1,0:T(8,128)(2,1)}, u32[]{:S(2)}, u32[]{:S(2)}) collective-permute-start(bf16[2,144,512]{2,1,0:T(8,128)(2,1)} %fusion.18), channel_id=1, source_target_pairs={{0,4},{4,0},{8,12},{12,8},{16,20},{20,16},{24,28},{28,24},{1,5},{5... | collective-permute-start | bytes 884744 | tf_op jit(solution)/shard_map/part/ppermute | solution.py:588
  367.4 21.8 %collective-permute-start.25 = (bf16[2,128,512]{2,1,0:T(8,128)(2,1)}, bf16[2,128,512]{2,1,0:T(8,128)(2,1)}, u32[]{:S(2)}, u32[]{:S(2)}) collective-permute-start(bf16[2,128,512]{2,1,0:T(8,128)(2,1)} %fusion.20), channel_id=1, source_target_pairs={{0,8},{4,12},{8,0},{12,4},{16,24},{20,28},{24,16},{28,20},{1,9},{5... | collective-permute-start | bytes 786440 | tf_op jit(solution)/shard_map/part/ppermute | solution.py:588
  369.2 44.3 %collective-permute-start.31 = (bf16[512,1024]{1,0:T(8,128)(2,1)}, bf16[512,1024]{1,0:T(8,128)(2,1)}, u32[]{:S(2)}, u32[]{:S(2)}) collective-permute-start(bf16[512,1024]{1,0:T(8,128)(2,1)} %add_convert_fusion.1), channel_id=1, source_target_pairs={{0,2},{1,3},{2,0},{3,1},{4,6},{5,7},{6,4},{7,5},{8,10},{9,11},{10,... | collective-permute-start | bytes 3145736 | tf_op jit(solution)/shard_map/mlp_across/ppermute | solution.py:588
  369.2 51.1 %collective-permute-start.23 = (bf16[512,1024]{1,0:T(8,128)(2,1)S(1)}, bf16[512,1024]{1,0:T(8,128)(2,1)}, u32[]{:S(2)}, u32[]{:S(2)}) collective-permute-start(bf16[512,1024]{1,0:T(8,128)(2,1)S(1)} %copy-done.21), channel_id=1, source_target_pairs={{0,1},{1,0},{2,3},{3,2},{4,5},{5,4},{6,7},{7,6},{8,9},{9,8},{10,11... | collective-permute-start | bytes 3145736 | tf_op jit(solution)/shard_map/part/ppermute | solution.py:588
  391.8 16.0 %collective-permute-start.29 = (bf16[128,512]{1,0:T(8,128)(2,1)S(1)}, bf16[128,512]{1,0:T(8,128)(2,1)S(1)}, u32[]{:S(2)}, u32[]{:S(2)}) collective-permute-start(bf16[128,512]{1,0:T(8,128)(2,1)S(1)} %fusion.23), channel_id=1, source_target_pairs={{0,16},{4,20},{8,24},{12,28},{16,0},{20,4},{24,8},{28,12},{1,17},{... | collective-permute-start | bytes 393224 | tf_op jit(solution)/shard_map/part/ppermute | solution.py:588
  392.1 21.3 %collective-permute-start.28 = (bf16[144,512]{1,0:T(8,128)(2,1)S(1)}, bf16[144,512]{1,0:T(8,128)(2,1)S(1)}, u32[]{:S(2)}, u32[]{:S(2)}) collective-permute-start(bf16[144,512]{1,0:T(8,128)(2,1)S(1)} %fusion.22), channel_id=1, source_target_pairs={{0,16},{4,20},{8,24},{12,28},{16,0},{20,4},{24,8},{28,12},{1,17},{... | collective-permute-start | bytes 442376 | tf_op jit(solution)/shard_map/part/ppermute | solution.py:588
  394.9 18.5 %collective-permute-start.30 = (bf16[4,16,1024]{2,1,0:T(8,128)(2,1)S(1)}, bf16[4,16,1024]{2,1,0:T(8,128)(2,1)S(1)}, u32[]{:S(2)}, u32[]{:S(2)}) collective-permute-start(bf16[4,16,1024]{2,1,0:T(8,128)(2,1)S(1)} %fusion.24), channel_id=1, source_target_pairs={{0,16},{4,20},{8,24},{12,28},{16,0},{20,4},{24,8},{28,12},{1,17},{... | collective-permute-start | bytes 393224 | tf_op jit(solution)/shard_map/part/ppermute | solution.py:588
  413.5 11.2 %collective-permute-start.35 = (f32[288]{0:T(512)S(1)}, f32[288]{0:T(512)S(1)}, u32[]{:S(2)}, u32[]{:S(2)}) collective-permute-start(f32[288]{0:T(512)S(1)} %slice_reduce_fusion), channel_id=1, source_target_pairs={{0,3},{1,2},{2,1},{3,0},{4,7},{5,6},{6,5},{7,4},{8,11},{9,10},{10,... | collective-permute-start | bytes 3464 | tf_op jit(solution)/shard_map/part/ppermute | solution.py:588
  415.0 9.7 %collective-permute-start.33 = (f32[288]{0:T(512)S(1)}, f32[288]{0:T(512)S(1)}, u32[]{:S(2)}, u32[]{:S(2)}) collective-permute-start(f32[288]{0:T(512)S(1)} %slice_reduce_fusion), channel_id=1, source_target_pairs={{0,1},{1,0},{2,3},{3,2},{4,5},{5,4},{6,7},{7,6},{8,9},{9,8},{10,11... | collective-permute-start | bytes 3464 | tf_op jit(solution)/shard_map/part/ppermute | solution.py:588
  415.4 9.3 %collective-permute-start.34 = (f32[288]{0:T(512)S(1)}, f32[288]{0:T(512)S(1)}, u32[]{:S(2)}, u32[]{:S(2)}) collective-permute-start(f32[288]{0:T(512)S(1)} %slice_reduce_fusion), channel_id=1, source_target_pairs={{0,2},{1,3},{2,0},{3,1},{4,6},{5,7},{6,4},{7,5},{8,10},{9,11},{10,... | collective-permute-start | bytes 3464 | tf_op jit(solution)/shard_map/part/ppermute | solution.py:588
  (77 other events, 627.3 us)
Sparse Core Ops, SparseCore 0:
  11.2 66.2 all-gather.4
  80.2 78.4 all-gather.6
  241.0 93.5 reduce-scatter.1

commit v11 on v10

--- a/solution.py
+++ b/solution.py
@@ -823,7 +823,7 @@
         mlp_across = flipped(near_mlp, "tensor", 2, "mlp_across")
         sum_one, sum_two = halved(sum_one, 1, 1), halved(sum_two, 1, 2)
         sum_out = halved(sum_out, 2, 2)
-        sum_one, sum_two, sum_out = together(sum_one, sum_two, sum_out)
+        sum_one, sum_two, sum_out, feed_sum = together(sum_one, sum_two, sum_out, feed_sum)
         sum_one, sum_two = halved(sum_one, 0, 4), halved(sum_two, 0, 4)
         sum_out = halved(sum_out, 1, 4)
         sum_one, sum_two, sum_out, mlp_across = together(sum_one, sum_two, sum_out, mlp_across)

time: 438 us -> 422 us (0.963)
  waiting for transfers between devices: 127 us -> 117 us
  starting transfers between devices: 27.6 us -> 20.6 us
  Pallas kernels: 145 us -> 150 us
  local copies, waits for them, and re-layouts: 35.2 us -> 30.7 us
    ppermute x36, waiting for transfers between devices: 88.8 us -> 81.1 us  [flipped(): lax.ppermute(value, axis, [(i, i ^ bit) for i in range(lax.axis_size(axis...]
    ppermute x36, starting transfers between devices: 27.5 us -> 20.5 us  [flipped(): lax.ppermute(value, axis, [(i, i ^ bit) for i in range(lax.axis_size(axis...]
    unnamed x145 -> x149, local copies, waits for them, and re-layouts: 10.9 us -> 11 us
  transfers between devices with their start and end apart: 39 -> 39, of which waited for: 17 -> 19; matrix products, arithmetic and copies ran while one was open for 24% -> 24% of each run, Pallas kernels for 30% -> 32%
where the time goes in v11:
time: 422 us; the launch traced here: 416 us
  Pallas kernels  150 us (36%)
  waiting for transfers between devices  117 us (28%)
  other arithmetic  65.2 us (15%)
  local copies, waits for them, and re-layouts  30.7 us (7%)
  starting transfers between devices  20.6 us (5%)
  matrix products  17.5 us (4%)
  between operations  15.4 us (4%)
    ppermute x36, waiting for transfers between devices, flipped(): lax.ppermute(value, axis, [(i, i ^ bit) for i in range(lax.axis_size(axis...  81.1 us
    pallas_call x2, Pallas kernels, feed(): pl.pallas_call(lambda *refs: feed_kernel(packs, *refs), grid=(rows // BLO...  33.6 us
    pallas_call x2, Pallas kernels, attend(): pl.pallas_call(lambda *refs: attend_kernel(half * n // BLOCK, *refs), gri...  30.2 us
    all_gather x1, waiting for transfers between devices, per_device(): lax.all_gather(pack_one, 'dp', axis=0, tiled=False)  28.6 us
    pallas_call x1, Pallas kernels, attend_back_other(): pl.pallas_call(back_other_kernel, grid_spec=pltpu.PrefetchScalarGridSpec(...  28.2 us
    ppermute x36, starting transfers between devices, flipped(): lax.ppermute(value, axis, [(i, i ^ bit) for i in range(lax.axis_size(axis...  20.5 us
    pallas_call x1, Pallas kernels, attend_back_own(): pl.pallas_call(back_own_kernel, grid_spec=pltpu.PrefetchScalarGridSpec(nu...  17.9 us
    pallas_call x1, Pallas kernels, feed_weights(): pl.pallas_call(lambda *refs: feed_weights_kernel(packs, pieces, *refs), g...  16.5 us
  transfers between devices with their start and end apart: 39, of which 19 were waited for; matrix products, arithmetic and copies ran while one was open for 24% of the time, Pallas kernels for 32%

profile of v11, /device:TPU:0, one launch (start us, length us, event | category | flops | bytes accessed | tf_op | source)
XLA Modules:
  0.0 416.2 jit_solution(2117362863860914499)
XLA Ops:
  13.0 3.0 collective-permute-start.1
  16.8 23.4 %collective-permute-done.1 = bf16[512,1024]{1,0:T(8,128)(2,1)} collective-permute-done((bf16[512,1024]{1,0:T(8,128)(2,1)S(1)}, bf16[512,1024]{1,0:T(8,128)(2,1)}, u32[]{:S(2)}, u32[]{:S(2)}) %collective-permute-start.1) | collective-permute-done | bytes 1048608 | tf_op jit(solution)/shard_map/tokens_across/ppermute | solution.py:588
  40.1 3.7 fusion.17
  44.6 4.3 %pad_maximum_fusion.x = bf16[2048,1024]{1,0:T(8,128)(2,1)} fusion(bf16[512,1024]{1,0:T(8,128)(2,1)} %collective-permute-done.2, bf16[512,1024]{1,0:T(8,128)(2,1)} %collective-permute-done.1, bf16[512,1024]{1,0:T(8,128)(2,1)} %collective-permute-done, bf16[512,1024]{1,0:T(8,128)(2,1)S(1)} %copy-done.32), kind=kLoop, calls=%fused_computation | loop fusion | flops 16777216 | bytes 8388608 | tf_op jit(solution)/shard_map/concatenate | solution.py:692
  48.9 28.6 %all-gather.5.cloned.1.call-done = bf16[1664,1024]{1,0:T(8,128)(2,1)} async-done(((bf16[208,1024]{1,0:T(8,128)(2,1)}), bf16[1664,1024]{1,0:T(8,128)(2,1)}) %all-gather.5.cloned.1.call-update) | async-done | bytes 3407888 | tf_op jit(solution)/shard_map/all_gather | solution.py:654
  78.8 3.1 slice.70
  83.9 13.5 %project.1 = (bf16[1024,2048]{1,0:T(8,128)(2,1)}, f32[2048,512]{1,0:T(8,128)}, f32[2048,256]{1,0:T(8,128)}, bf16[2048,512]{1,0:T(8,128)(2,1)}, bf16[2048,256]{1,...) custom-call(bf16[2048,1024]{1,0:T(8,128)(2,1)} %pad_maximum_fusion.x, ...), custom_call_target="tpu_custom_call" | custom-call | flops 156250000 | bytes 1000 | tf_op jit(solution)/shard_map/project/pallas_call | solution.py:397
  97.4 17.7 %attend.2 = (bf16[1024,512]{1,0:T(8,128)(2,1)S(1)}, bf16[512,1024]{1,0:T(8,128)(2,1)S(1)}, f32[2,2,1024]{2,1,0:T(2,128)S(1)}) custom-call(s32[17]{0:T(128)S(1)} %pad_add_fusion.refs_0_.info, bf16[2048,512]{1,0:T(8,128)(2,1)} %get-tuple-element.101.refs_1_.q, bf16[256,2048]{1,0:T(8,128)(2,1)S(1)} %get-tuple-element.97.refs_2_.k_turned, ...), custom_call_target="tpu_custom_call" | custom-call | flops 281249984 | bytes 1000 | tf_op jit(solution)/shard_map/attend/pallas_call | solution.py:438
  116.0 2.6 collective-permute-done.4
  119.5 12.5 %attend.3 = (bf16[1024,512]{1,0:T(8,128)(2,1)S(1)}, bf16[512,1024]{1,0:T(8,128)(2,1)S(1)}, f32[2,2,1024]{2,1,0:T(2,128)S(1)}) custom-call(s32[17]{0:T(128)S(1)} %pad_add_fusion.refs_0_.info, bf16[2048,512]{1,0:T(8,128)(2,1)} %get-tuple-element.101.refs_1_.q, bf16[256,2048]{1,0:T(8,128)(2,1)S(1)} %get-tuple-element.97.refs_2_.k_turned, ...), custom_call_target="tpu_custom_call" | custom-call | flops 281249984 | bytes 1000 | tf_op jit(solution)/shard_map/attend/pallas_call | solution.py:438
  132.0 12.7 %collective-permute-done.5 = bf16[512,1024]{1,0:T(8,128)(2,1)S(1)} collective-permute-done((bf16[512,1024]{1,0:T(8,128)(2,1)S(1)}, bf16[512,1024]{1,0:T(8,128)(2,1)S(1)}, u32[]{:S(2)}, u32[]{:S(2)}) %collective-permute-start.5) | collective-permute-done | bytes 1048608 | tf_op jit(solution)/shard_map/attn_across/ppermute | solution.py:588
  146.9 2.9 collective-permute-done.6
  151.8 6.9 %all-gather.7.cloned.1.call-done = bf16[4608,512]{1,0:T(8,128)(2,1)} async-done(((bf16[576,512]{1,0:T(8,128)(2,1)}), bf16[4608,512]{1,0:T(8,128)(2,1)}) %all-gather.7.cloned.1.call-update) | async-done | bytes 4718608 | tf_op jit(solution)/shard_map/all_gather | solution.py:656
  168.9 16.7 %feed.2 = (bf16[1024,1024]{1,0:T(8,128)(2,1)}, bf16[768,1024]{1,0:T(8,128)(2,1)S(1)}, bf16[1024,1536]{1,0:T(8,128)(2,1)}, bf16[512,1024]{1,0:T(8,128)(2,1)S(1)},...) custom-call(bf16[1024,1024]{1,0:T(8,128)(2,1)} %pad_maximum_fusion.1.refs_0_, ...), custom_call_target="tpu_custom_call" | custom-call | flops 250000000 | bytes 1000 | tf_op jit(solution)/shard_map/feed/pallas_call | solution.py:533
  185.6 2.7 collective-permute-done.7
  192.5 16.9 %feed.3 = (bf16[1024,1024]{1,0:T(8,128)(2,1)}, bf16[768,1024]{1,0:T(8,128)(2,1)S(1)}, bf16[1024,1536]{1,0:T(8,128)(2,1)}, bf16[512,1024]{1,0:T(8,128)(2,1)S(1)},...) custom-call(bf16[1024,1024]{1,0:T(8,128)(2,1)} %pad_maximum_fusion.2.refs_0_, ...), custom_call_target="tpu_custom_call" | custom-call | flops 250000000 | bytes 1000 | tf_op jit(solution)/shard_map/feed/pallas_call | solution.py:533
  216.9 16.5 %feed_weights.1 = bf16[8,576,512]{2,1,0:T(8,128)(2,1)} custom-call(bf16[1024,1024]{1,0:T(8,128)(2,1)S(1)} %copy-done.12, bf16[1024,1024]{1,0:T(8,128)(2,1)} %get-tuple-element.121.refs_1_, bf16[1024,1536]{1,0:T(8,128)(2,1)} %get-tuple-element.122.refs_2_, bf16[1024,1536]{1,0:T(8,128)(2,1)} %get-tuple-element.123.refs_3_, ...), custom_call_target="tpu_custom_call" | custom-call | flops 250000000 | bytes 1000 | tf_op jit(solution)/shard_map/feed_weights/pallas_call | solution.py:558
  233.5 7.5 %collective-permute-done.14 = bf16[512,1024]{1,0:T(8,128)(2,1)} collective-permute-done((bf16[512,1024]{1,0:T(8,128)(2,1)}, bf16[512,1024]{1,0:T(8,128)(2,1)}, u32[]{:S(2)}, u32[]{:S(2)}) %collective-permute-start.14) | collective-permute-done | bytes 1048608 | tf_op jit(solution)/shard_map/back_across/ppermute | solution.py:588
  241.0 3.2 multiply_reduce_fusion.1
  244.2 4.1 fusion.35
  253.4 17.9 %attend_back_own.1 = (bf16[1024,512]{1,0:T(8,128)(2,1)S(1)}, f32[2048,256]{1,0:T(8,128)}, f32[2048,256]{1,0:T(8,128)}, f32[2,1,128]{2,1,0:T(1,128)S(1)}) custom-call(s32[17]{0:T(128)S(1)} %pad_add_fusion.refs_0_.info, bf16[2048,512]{1,0:T(8,128)(2,1)} %get-tuple-element.101.refs_1_.q, bf16[2048,256]{1,0:T(8,128)(2,1)S(1)} %copy-done.8, ...), custom_call_target="tpu_custom_call" | custom-call | flops 390624992 | bytes 1000 | tf_op jit(solution)/shard_map/attend_back_own/pallas_call | solution.py:458
  282.6 28.2 %attend_back_other.1 = (bf16[2048,1024]{1,0:T(8,128)(2,1)}, f32[2,2,128]{2,1,0:T(2,128)S(1)}) custom-call(s32[17]{0:T(128)S(1)} %pad_add_fusion.refs_0_.info, bf16[2048,512]{1,0:T(8,128)(2,1)} %get-tuple-element.101.refs_1_.q, bf16[2048,256]{1,0:T(8,128)(2,1)S(1)} %copy-done.9, bf16[2048,256]{1,0:T(8,128)(2,1)S(1)} %copy-done.4, ...), custom_call_target="tpu_custom_call" | custom-call | flops 437500000 | bytes 1000 | tf_op jit(solution)/shard_map/attend_back_other/pallas_call | solution.py:489
  310.8 4.7 %unproject.2 = (bf16[512,1024]{1,0:T(8,128)(2,1)S(1)}, bf16[512,1024]{1,0:T(8,128)(2,1)S(1)}) custom-call(bf16[2048,1024]{1,0:T(8,128)(2,1)} %get-tuple-element.167.grad, bf16[1024,1024]{1,0:T(8,128)(2,1)S(1)} %bitcast.108), custom_call_target="tpu_custom_call" | custom-call | flops 62500000 | bytes 1000 | tf_op jit(solution)/shard_map/unproject/pallas_call | solution.py:576
  315.7 6.3 %fusion.40 = f32[1024,1024]{1,0:T(8,128)S(1)} fusion(bf16[1024,2048]{1,0:T(8,128)(2,1)} %get-tuple-element.143, bf16[2048,1024]{1,0:T(8,128)(2,1)S(1)} %copy-done.31), kind=kOutput, calls=%fused_computation.143 | convolution fusion | flops 4294967296 | bytes 12582912 | tf_op jit(solution)/shard_map/dot_general | solution.py:64
  333.1 5.6 %unproject.3 = (bf16[512,1024]{1,0:T(8,128)(2,1)S(1)}, bf16[512,1024]{1,0:T(8,128)(2,1)}) custom-call(bf16[2048,1024]{1,0:T(8,128)(2,1)} %get-tuple-element.167.grad, bf16[1024,1024]{1,0:T(8,128)(2,1)S(1)} %bitcast.109), custom_call_target="tpu_custom_call" | custom-call | flops 62500000 | bytes 1000 | tf_op jit(solution)/shard_map/unproject/pallas_call | solution.py:576
  341.5 9.3 %collective-permute-done.20 = bf16[2,2,128,512]{3,2,0,1:T(8,128)(2,1)S(1)} collective-permute-done((bf16[2,2,128,512]{3,2,0,1:T(8,128)(2,1)}, bf16[2,2,128,512]{3,2,0,1:T(8,128)(2,1)S(1)}, u32[]{:S(2)}, u32[]{:S(2)}) %collective-permute-start.20) | collective-permute-done | bytes 524320 | tf_op jit(solution)/shard_map/part/ppermute | solution.py:588
  353.2 5.4 %collective-permute-done.27 = bf16[4,2,16,1024]{3,2,0,1:T(8,128)(2,1)S(1)} collective-permute-done((bf16[4,2,16,1024]{3,2,0,1:T(8,128)(2,1)S(1)}, bf16[4,2,16,1024]{3,2,0,1:T(8,128)(2,1)S(1)}, u32[]{:S(2)}, u32[]{:S(2)}) %collective-permute-start.27) | collective-permute-done | bytes 262176 | tf_op jit(solution)/shard_map/part/ppermute | solution.py:588
  369.5 3.9 fusion.4
  382.3 4.9 %multiply_subtract_fusion = (f32[128,2,768]{2,1,0:T(2,128)}, f32[128,2,768]{2,1,0:T(2,128)}, f32[128,2,768]{2,1,0:T(2,128)}) fusion(f32[128,2,768]{2,1,0:T(2,128)S(1)} %copy-done.47, f32[128,2,768]{2,1,0:T(2,128)S(1)} %copy.94, f32[128,2,768]{2,1,0:T(2,128)} %param.28, f32[128,2,768]{2,1,0:T(2,128)} %param.33), kind=kLoop, calls=%fused_computation.48 | loop fusion | flops 2949120 | bytes 5505024 | tf_op jit(solution)/shard_map/sub | solution.py:53
  390.5 3.4 collective-permute-done.29
  400.1 4.0 multiply_subtract_fusion.1
  404.2 3.4 add_convert_fusion
  (312 shorter events, 101.4 us)
Async XLA Ops:
  7.2 70.3 %all-gather.5.cloned.1.call-start = ((), (), s32[]{:S(2)}) async-start(), calls=%async_computation.2 | async-start | bytes 3833856 | tf_op jit(solution)/shard_map/all_gather | solution.py:654
  11.1 147.6 %all-gather.7.cloned.1.call-start = ((), (), s32[]{:S(2)}) async-start(), calls=%async_computation.3 | async-start | bytes 5308416 | tf_op jit(solution)/shard_map/all_gather | solution.py:656
  12.9 347.9 %reduce-scatter.2.cloned.1.call-start = ((), (), s32[]{:S(2)}) async-start(), calls=%async_computation.1 | async-start | bytes 5308416 | tf_op jit(solution)/shard_map/reduce_scatter | solution.py:762
  13.0 27.1 %collective-permute-start.1 = (bf16[512,1024]{1,0:T(8,128)(2,1)S(1)}, bf16[512,1024]{1,0:T(8,128)(2,1)}, u32[]{:S(2)}, u32[]{:S(2)}) collective-permute-start(bf16[512,1024]{1,0:T(8,128)(2,1)S(1)} %copy-done.32), channel_id=1, source_target_pairs={{0,2},{1,3},{2,0},{3,1},{4,6},{5,7},{6,4},{7,5},{8,10},{9,11},{10,... | collective-permute-start | bytes 3145736 | tf_op jit(solution)/shard_map/tokens_across/ppermute | solution.py:588
  16.0 28.6 %collective-permute-start = (bf16[512,1024]{1,0:T(8,128)(2,1)S(1)}, bf16[512,1024]{1,0:T(8,128)(2,1)}, u32[]{:S(2)}, u32[]{:S(2)}) collective-permute-start(bf16[512,1024]{1,0:T(8,128)(2,1)S(1)} %copy-done.32), channel_id=1, source_target_pairs={{0,1},{1,0},{2,3},{3,2},{4,5},{5,4},{6,7},{7,6},{8,9},{9,8},{10,11... | collective-permute-start | bytes 3145736 | tf_op jit(solution)/shard_map/part/ppermute | solution.py:588
  16.0 99.2 %collective-permute-start.3 = (bf16[512,1024]{1,0:T(8,128)(2,1)}, bf16[512,1024]{1,0:T(8,128)(2,1)}, u32[]{:S(2)}, u32[]{:S(2)}) collective-permute-start(bf16[512,1024]{1,0:T(8,128)(2,1)} %param.19), channel_id=1, source_target_pairs={{0,2},{1,3},{2,0},{3,1},{4,6},{5,7},{6,4},{7,5},{8,10},{9,11},{10,... | collective-permute-start | bytes 3145736 | tf_op jit(solution)/shard_map/grad_across/ppermute | solution.py:588
  40.1 4.5 %collective-permute-start.2 = (bf16[512,1024]{1,0:T(8,128)(2,1)}, bf16[512,1024]{1,0:T(8,128)(2,1)}, u32[]{:S(2)}, u32[]{:S(2)}) collective-permute-start(bf16[512,1024]{1,0:T(8,128)(2,1)} %collective-permute-done.1), channel_id=1, source_target_pairs={{0,1},{1,0},{2,3},{3,2},{4,5},{5,4},{6,7},{7,6},{8,9},{9,8},{10,11... | collective-permute-start | bytes 3145736 | tf_op jit(solution)/shard_map/part/ppermute | solution.py:588
  119.4 25.3 %collective-permute-start.5 = (bf16[512,1024]{1,0:T(8,128)(2,1)S(1)}, bf16[512,1024]{1,0:T(8,128)(2,1)S(1)}, u32[]{:S(2)}, u32[]{:S(2)}) collective-permute-start(bf16[512,1024]{1,0:T(8,128)(2,1)S(1)} %add_convert_fusion.5), channel_id=1, source_target_pairs={{0,2},{1,3},{2,0},{3,1},{4,6},{5,7},{6,4},{7,5},{8,10},{9,11},{10,... | collective-permute-start | bytes 3145736 | tf_op jit(solution)/shard_map/attn_across/ppermute | solution.py:588
  146.4 19.1 %collective-permute-start.9 = (bf16[512,1024]{1,0:T(8,128)(2,1)}, bf16[512,1024]{1,0:T(8,128)(2,1)}, u32[]{:S(2)}, u32[]{:S(2)}) collective-permute-start(bf16[512,1024]{1,0:T(8,128)(2,1)} %param.19), channel_id=1, source_target_pairs={{0,1},{1,0},{2,3},{3,2},{4,5},{5,4},{6,7},{7,6},{8,9},{9,8},{10,11... | collective-permute-start | bytes 3145736 | tf_op jit(solution)/shard_map/part/ppermute | solution.py:588
  162.7 25.6 %collective-permute-start.7 = (bf16[512,1024]{1,0:T(8,128)(2,1)S(1)}, bf16[512,1024]{1,0:T(8,128)(2,1)S(1)}, u32[]{:S(2)}, u32[]{:S(2)}) collective-permute-start(bf16[512,1024]{1,0:T(8,128)(2,1)S(1)} %multiply_convert_fusion), channel_id=1, source_target_pairs={{0,2},{1,3},{2,0},{3,1},{4,6},{5,7},{6,4},{7,5},{8,10},{9,11},{10,... | collective-permute-start | bytes 3145736 | tf_op jit(solution)/shard_map/normed_across/ppermute | solution.py:588
  166.9 22.7 %collective-permute-start.12 = (bf16[512,1024]{1,0:T(8,128)(2,1)}, bf16[512,1024]{1,0:T(8,128)(2,1)S(1)}, u32[]{:S(2)}, u32[]{:S(2)}) collective-permute-start(bf16[512,1024]{1,0:T(8,128)(2,1)} %collective-permute-done.3), channel_id=1, source_target_pairs={{0,1},{1,0},{2,3},{3,2},{4,5},{5,4},{6,7},{7,6},{8,9},{9,8},{10,11... | collective-permute-start | bytes 3145736 | tf_op jit(solution)/shard_map/part/ppermute | solution.py:588
  215.5 25.5 %collective-permute-start.14 = (bf16[512,1024]{1,0:T(8,128)(2,1)}, bf16[512,1024]{1,0:T(8,128)(2,1)}, u32[]{:S(2)}, u32[]{:S(2)}) collective-permute-start(bf16[512,1024]{1,0:T(8,128)(2,1)} %add_convert_fusion.4), channel_id=1, source_target_pairs={{0,2},{1,3},{2,0},{3,1},{4,6},{5,7},{6,4},{7,5},{8,10},{9,11},{10,... | collective-permute-start | bytes 3145736 | tf_op jit(solution)/shard_map/back_across/ppermute | solution.py:588
  216.9 24.1 %collective-permute-start.10 = (bf16[512,1024]{1,0:T(8,128)(2,1)S(1)}, bf16[512,1024]{1,0:T(8,128)(2,1)}, u32[]{:S(2)}, u32[]{:S(2)}) collective-permute-start(bf16[512,1024]{1,0:T(8,128)(2,1)S(1)} %get-tuple-element.113), channel_id=1, source_target_pairs={{0,1},{1,0},{2,3},{3,2},{4,5},{5,4},{6,7},{7,6},{8,9},{9,8},{10,11... | collective-permute-start | bytes 3145736 | tf_op jit(solution)/shard_map/part/ppermute | solution.py:588
  248.5 25.7 %collective-permute-start.16 = (bf16[512,1024]{1,0:T(8,128)(2,1)S(1)}, bf16[512,1024]{1,0:T(8,128)(2,1)}, u32[]{:S(2)}, u32[]{:S(2)}) collective-permute-start(bf16[512,1024]{1,0:T(8,128)(2,1)S(1)} %get-tuple-element.194), channel_id=1, source_target_pairs={{0,2},{1,3},{2,0},{3,1},{4,6},{5,7},{6,4},{7,5},{8,10},{9,11},{10,... | collective-permute-start | bytes 3145736 | tf_op jit(solution)/shard_map/grad_middle_across/ppermute | solution.py:588
  315.5 6.6 %collective-permute-start.18 = (bf16[512,1024]{1,0:T(8,128)(2,1)S(1)}, bf16[512,1024]{1,0:T(8,128)(2,1)S(1)}, u32[]{:S(2)}, u32[]{:S(2)}) collective-permute-start(bf16[512,1024]{1,0:T(8,128)(2,1)S(1)} %get-tuple-element.141), channel_id=1, source_target_pairs={{0,1},{1,0},{2,3},{3,2},{4,5},{5,4},{6,7},{7,6},{8,9},{9,8},{10,11... | collective-permute-start | bytes 3145736 | tf_op jit(solution)/shard_map/part/ppermute | solution.py:588
  325.1 15.1 %collective-permute-start.26 = (bf16[4,2,2,16,1024]{4,3,0,1,2:T(8,128)(2,1)}, bf16[4,2,2,16,1024]{4,3,0,1,2:T(8,128)(2,1)}, u32[]{:S(2)}, u32[]{:S(2)}) collective-permute-start(bf16[4,2,2,16,1024]{4,3,0,1,2:T(8,128)(2,1)} %bitcast.106), channel_id=1, source_target_pairs={{0,4},{4,0},{8,12},{12,8},{16,20},{20,16},{24,28},{28,24},{1,5},{5... | collective-permute-start | bytes 1572872 | tf_op jit(solution)/shard_map/part/ppermute | solution.py:588
  330.1 20.6 %collective-permute-start.20 = (bf16[2,2,128,512]{3,2,0,1:T(8,128)(2,1)}, bf16[2,2,128,512]{3,2,0,1:T(8,128)(2,1)S(1)}, u32[]{:S(2)}, u32[]{:S(2)}) collective-permute-start(bf16[2,2,128,512]{3,2,0,1:T(8,128)(2,1)} %fusion.10), channel_id=1, source_target_pairs={{0,4},{4,0},{8,12},{12,8},{16,20},{20,16},{24,28},{28,24},{1,5},{5... | collective-permute-start | bytes 1572872 | tf_op jit(solution)/shard_map/part/ppermute | solution.py:588
  332.8 19.2 %collective-permute-start.19 = (bf16[2,2,144,512]{3,2,0,1:T(8,128)(2,1)S(1)}, bf16[2,2,144,512]{3,2,0,1:T(8,128)(2,1)S(1)}, u32[]{:S(2)}, u32[]{:S(2)}) collective-permute-start(bf16[2,2,144,512]{3,2,0,1:T(8,128)(2,1)S(1)} %fusion.8), channel_id=1, source_target_pairs={{0,8},{4,12},{8,0},{12,4},{16,24},{20,28},{24,16},{28,20},{1,9},{5... | collective-permute-start | bytes 1769480 | tf_op jit(solution)/shard_map/part/ppermute | solution.py:588
  332.9 29.3 %collective-permute-start.21 = (bf16[512,1024]{1,0:T(8,128)(2,1)}, bf16[512,1024]{1,0:T(8,128)(2,1)}, u32[]{:S(2)}, u32[]{:S(2)}) collective-permute-start(bf16[512,1024]{1,0:T(8,128)(2,1)} %add_convert_fusion.2), channel_id=1, source_target_pairs={{0,2},{1,3},{2,0},{3,1},{4,6},{5,7},{6,4},{7,5},{8,10},{9,11},{10,... | collective-permute-start | bytes 3145736 | tf_op jit(solution)/shard_map/back_across/ppermute | solution.py:588
  333.1 26.4 %collective-permute-start.22 = (bf16[512,1024]{1,0:T(8,128)(2,1)S(1)}, bf16[512,1024]{1,0:T(8,128)(2,1)S(1)}, u32[]{:S(2)}, u32[]{:S(2)}) collective-permute-start(bf16[512,1024]{1,0:T(8,128)(2,1)S(1)} %copy-done.23), channel_id=1, source_target_pairs={{0,1},{1,0},{2,3},{3,2},{4,5},{5,4},{6,7},{7,6},{8,9},{9,8},{10,11... | collective-permute-start | bytes 3145736 | tf_op jit(solution)/shard_map/part/ppermute | solution.py:588
  340.2 26.7 %collective-permute-start.32 = (bf16[512,1024]{1,0:T(8,128)(2,1)}, bf16[512,1024]{1,0:T(8,128)(2,1)}, u32[]{:S(2)}, u32[]{:S(2)}) collective-permute-start(bf16[512,1024]{1,0:T(8,128)(2,1)} %get-tuple-element.169), channel_id=1, source_target_pairs={{0,1},{1,0},{2,3},{3,2},{4,5},{5,4},{6,7},{7,6},{8,9},{9,8},{10,11... | collective-permute-start | bytes 3145736 | tf_op jit(solution)/shard_map/part/ppermute | solution.py:588
  350.7 7.8 %collective-permute-start.27 = (bf16[4,2,16,1024]{3,2,0,1:T(8,128)(2,1)S(1)}, bf16[4,2,16,1024]{3,2,0,1:T(8,128)(2,1)S(1)}, u32[]{:S(2)}, u32[]{:S(2)}) collective-permute-start(bf16[4,2,16,1024]{3,2,0,1:T(8,128)(2,1)S(1)} %fusion.21), channel_id=1, source_target_pairs={{0,8},{4,12},{8,0},{12,4},{16,24},{20,28},{24,16},{28,20},{1,9},{5... | collective-permute-start | bytes 786440 | tf_op jit(solution)/shard_map/part/ppermute | solution.py:588
  363.7 9.8 %collective-permute-start.24 = (bf16[2,144,512]{2,1,0:T(8,128)(2,1)S(1)}, bf16[2,144,512]{2,1,0:T(8,128)(2,1)S(1)}, u32[]{:S(2)}, u32[]{:S(2)}) collective-permute-start(bf16[2,144,512]{2,1,0:T(8,128)(2,1)S(1)} %fusion.18), channel_id=1, source_target_pairs={{0,4},{4,0},{8,12},{12,8},{16,20},{20,16},{24,28},{28,24},{1,5},{5... | collective-permute-start | bytes 884744 | tf_op jit(solution)/shard_map/part/ppermute | solution.py:588
  366.5 7.0 %collective-permute-start.25 = (bf16[2,128,512]{2,1,0:T(8,128)(2,1)S(1)}, bf16[2,128,512]{2,1,0:T(8,128)(2,1)S(1)}, u32[]{:S(2)}, u32[]{:S(2)}) collective-permute-start(bf16[2,128,512]{2,1,0:T(8,128)(2,1)S(1)} %fusion.20), channel_id=1, source_target_pairs={{0,8},{4,12},{8,0},{12,4},{16,24},{20,28},{24,16},{28,20},{1,9},{5... | collective-permute-start | bytes 786440 | tf_op jit(solution)/shard_map/part/ppermute | solution.py:588
  366.9 30.3 %collective-permute-start.31 = (bf16[512,1024]{1,0:T(8,128)(2,1)}, bf16[512,1024]{1,0:T(8,128)(2,1)}, u32[]{:S(2)}, u32[]{:S(2)}) collective-permute-start(bf16[512,1024]{1,0:T(8,128)(2,1)} %add_convert_fusion.1), channel_id=1, source_target_pairs={{0,2},{1,3},{2,0},{3,1},{4,6},{5,7},{6,4},{7,5},{8,10},{9,11},{10,... | collective-permute-start | bytes 3145736 | tf_op jit(solution)/shard_map/mlp_across/ppermute | solution.py:588
  366.9 37.2 %collective-permute-start.23 = (bf16[512,1024]{1,0:T(8,128)(2,1)S(1)}, bf16[512,1024]{1,0:T(8,128)(2,1)}, u32[]{:S(2)}, u32[]{:S(2)}) collective-permute-start(bf16[512,1024]{1,0:T(8,128)(2,1)S(1)} %copy-done.21), channel_id=1, source_target_pairs={{0,1},{1,0},{2,3},{3,2},{4,5},{5,4},{6,7},{7,6},{8,9},{9,8},{10,11... | collective-permute-start | bytes 3145736 | tf_op jit(solution)/shard_map/part/ppermute | solution.py:588
  374.5 22.7 %collective-permute-start.28 = (bf16[144,512]{1,0:T(8,128)(2,1)}, bf16[144,512]{1,0:T(8,128)(2,1)S(1)}, u32[]{:S(2)}, u32[]{:S(2)}) collective-permute-start(bf16[144,512]{1,0:T(8,128)(2,1)} %fusion.22), channel_id=1, source_target_pairs={{0,16},{4,20},{8,24},{12,28},{16,0},{20,4},{24,8},{28,12},{1,17},{... | collective-permute-start | bytes 442376 | tf_op jit(solution)/shard_map/part/ppermute | solution.py:588
  376.9 17.1 %collective-permute-start.29 = (bf16[128,512]{1,0:T(8,128)(2,1)}, bf16[128,512]{1,0:T(8,128)(2,1)}, u32[]{:S(2)}, u32[]{:S(2)}) collective-permute-start(bf16[128,512]{1,0:T(8,128)(2,1)} %fusion.23), channel_id=1, source_target_pairs={{0,16},{4,20},{8,24},{12,28},{16,0},{20,4},{24,8},{28,12},{1,17},{... | collective-permute-start | bytes 393224 | tf_op jit(solution)/shard_map/part/ppermute | solution.py:588
  379.7 16.5 %collective-permute-start.30 = (bf16[4,16,1024]{2,1,0:T(8,128)(2,1)}, bf16[4,16,1024]{2,1,0:T(8,128)(2,1)}, u32[]{:S(2)}, u32[]{:S(2)}) collective-permute-start(bf16[4,16,1024]{2,1,0:T(8,128)(2,1)} %fusion.24), channel_id=1, source_target_pairs={{0,16},{4,20},{8,24},{12,28},{16,0},{20,4},{24,8},{28,12},{1,17},{... | collective-permute-start | bytes 393224 | tf_op jit(solution)/shard_map/part/ppermute | solution.py:588
  397.3 11.2 %collective-permute-start.35 = (f32[288]{0:T(512)S(1)}, f32[288]{0:T(512)S(1)}, u32[]{:S(2)}, u32[]{:S(2)}) collective-permute-start(f32[288]{0:T(512)S(1)} %slice_reduce_fusion), channel_id=1, source_target_pairs={{0,3},{1,2},{2,1},{3,0},{4,7},{5,6},{6,5},{7,4},{8,11},{9,10},{10,... | collective-permute-start | bytes 3464 | tf_op jit(solution)/shard_map/part/ppermute | solution.py:588
  398.7 9.9 %collective-permute-start.33 = (f32[288]{0:T(512)S(1)}, f32[288]{0:T(512)S(1)}, u32[]{:S(2)}, u32[]{:S(2)}) collective-permute-start(f32[288]{0:T(512)S(1)} %slice_reduce_fusion), channel_id=1, source_target_pairs={{0,1},{1,0},{2,3},{3,2},{4,5},{5,4},{6,7},{7,6},{8,9},{9,8},{10,11... | collective-permute-start | bytes 3464 | tf_op jit(solution)/shard_map/part/ppermute | solution.py:588
  399.5 9.1 %collective-permute-start.34 = (f32[288]{0:T(512)S(1)}, f32[288]{0:T(512)S(1)}, u32[]{:S(2)}, u32[]{:S(2)}) collective-permute-start(f32[288]{0:T(512)S(1)} %slice_reduce_fusion), channel_id=1, source_target_pairs={{0,2},{1,3},{2,0},{3,1},{4,6},{5,7},{6,4},{7,5},{8,10},{9,11},{10,... | collective-permute-start | bytes 3464 | tf_op jit(solution)/shard_map/part/ppermute | solution.py:588
  (79 other events, 656.8 us)
Sparse Core Ops, SparseCore 0:
  11.2 66.2 all-gather.4
  80.2 78.4 all-gather.6
  241.1 93.4 reduce-scatter.1
